TPU v7x, 128 devices: a whole 4x4x4 slice. The times are simulated.
128 devices in a mesh: tm: 32 (over z, y, core), rows: 4 (over x).
Axes of the slice: x: 4, y: 4, z: 4, core: 2. Of those that a mesh axis runs over, the one named last changes fastest.
Arguments:
- inputs: bfloat16 [64, 32, 80, 256], P('tm', 'rows'), may hold values from -64 to 64
- cotangent: bfloat16 [64, 32, 80, 256], P('tm', 'rows'), may hold values from -64 to 64
- gain_one: float32 [256], replicated, may hold values from 0.1 to 1.9
- gain_two: float32 [256], replicated, may hold values from 0.1 to 1.9
- weight_one: bfloat16 [6912, 256], replicated, may hold values from -4 to 4
- weight_two: bfloat16 [6912, 256], replicated, may hold values from -4 to 4
- first_one: float32 [1769472], P(('tm', 'rows')), may hold values from -6 to 6
- second_one: float32 [1769472], P(('tm', 'rows')), may hold values from 1 to 10
- first_two: float32 [1769472], P(('tm', 'rows')), may hold values from -6 to 6
- second_two: float32 [1769472], P(('tm', 'rows')), may hold values from 1 to 10
Outputs:
- input_grad: bfloat16 [64, 32, 80, 256], P('tm', 'rows')
- new_weight_one: bfloat16 [6912, 256], replicated
- new_weight_two: bfloat16 [6912, 256], replicated
- new_first_one: float32 [1769472], P(('tm', 'rows'))
- new_second_one: float32 [1769472], P(('tm', 'rows'))
- new_first_two: float32 [1769472], P(('tm', 'rows'))
- new_second_two: float32 [1769472], P(('tm', 'rows'))
All inputs are finite; a program needn't handle non-finite values.
Results may differ from a plain program's by a relative error of at most 0.018.
Values may be sent and summed in bfloat16 or wider, within the bound.
No kernel may reach another device: no remote copies, remote signals or barrier semaphores. Data moves between devices by JAX's collectives and lax.ppermute only.
A program may use at most 128 MiB of HBM per device.

v0:
```python
import jax
import jax.numpy as jnp
from jax import lax
from jax.sharding import PartitionSpec as P

GROUPS = 32


norm_eps = 1e-05
learn_rate = 0.25
beta_one = 0.9
beta_two = 0.95
decay_rate = 0.1
adam_eps = 1e-08
first_fix = 1.0 - 0.9**10
second_fix = 1.0 - 0.95**10


def shifted(value, axis, steps):
    count = lax.axis_size(axis)
    leading, last = (max(0, -steps), min(count, count - steps))
    return lax.ppermute(value, axis, [(source, source + steps) for source in range(leading, last)])


def with_halo(array, sides, width):
    for axis, dim in sides:
        count, length = (lax.axis_size(axis), array.shape[dim])
        up = [(i, (i + 1) % count) for i in range(count - 1)]
        down = [(j, i) for i, j in up]
        last = lax.slice_in_dim(array, length - width, length, axis=dim)
        leading = lax.slice_in_dim(array, 0, width, axis=dim)
        before = lax.ppermute(last, axis, up)
        after = lax.ppermute(leading, axis, down)
        array = jnp.concatenate([before, array, after], axis=dim)
    return array


def summed(pieces):
    return lax.psum(pieces, ("tm", "rows"))


def per_group(values):
    channels = values.shape[-1]
    per_channel = jnp.sum(values.reshape(-1, channels), axis=0)
    return jnp.sum(per_channel.reshape(GROUPS, -1), axis=1)


def broaden(statistic, channels):
    return jnp.repeat(statistic, channels // GROUPS)


def normalize(values, cell_count):
    channels = values.shape[-1]
    center = broaden(summed(per_group(values)) / cell_count, channels)
    centered = values - center
    inverse = lax.rsqrt(summed(per_group(centered * centered)) / cell_count + norm_eps)
    inverse_wide = broaden(inverse, channels)
    return (centered * inverse_wide, inverse_wide)


def norm_backward(slope, normed, inverse_wide, cell_count):
    channels = slope.shape[-1]
    mean_sum, cross_sum = summed((per_group(slope), per_group(slope * normed)))
    return inverse_wide * (
        slope
        - broaden(mean_sum / cell_count, channels)
        - normed * broaden(cross_sum / cell_count, channels)
    )


def extend(volume, upcoming):
    edge_frames = volume if upcoming else volume
    arrived = shifted(edge_frames, "tm", -1 if upcoming else 1)
    joined = jnp.concatenate((volume, arrived) if upcoming else (arrived, volume), axis=0)
    rimmed = with_halo(joined, (("rows", 1),), 1)
    return jnp.pad(rimmed, ((0, 0), (0, 0), (1, 1), (0, 0)))


def patches(extended, backward, frames, rows_here, columns):
    pieces = []
    for tap_index in range(27):
        time_off, row_off, col_off = (tap_index // 9, tap_index // 3 % 3, tap_index % 3)
        if backward:
            time_off, row_off, col_off = (2 - time_off, 2 - row_off, 2 - col_off)
        pieces.append(
            extended[
                time_off : time_off + frames,
                row_off : row_off + rows_here,
                col_off : col_off + columns,
            ]
        )
    return jnp.concatenate(pieces, axis=-1).reshape(frames * rows_here * columns, -1)


def flipped(weight, channels):
    return (
        weight.reshape(27, channels, channels).transpose(0, 2, 1).reshape(27 * channels, channels)
    )


def reduce_grad(local_grad):
    flattened = local_grad.reshape(-1)
    return lax.psum_scatter(flattened, ("tm", "rows"), scatter_dimension=0, tiled=True)


def adamw_share(weight, gradient, first, second):
    share_len = first.shape[0]
    own_share = lax.dynamic_slice_in_dim(
        weight.reshape(-1), lax.axis_index(("tm", "rows")) * share_len, share_len
    ).astype(jnp.float32)
    first_new = beta_one * first + (1.0 - beta_one) * gradient
    second_new = beta_two * second + (1.0 - beta_two) * gradient * gradient
    updated = own_share * (1.0 - learn_rate * decay_rate) - learn_rate * (first_new / first_fix) / (
        jnp.sqrt(second_new / second_fix) + adam_eps
    )
    return (updated.astype(jnp.bfloat16), first_new, second_new)


def local(
    inputs,
    cotangent,
    gain_one,
    gain_two,
    weight_one,
    weight_two,
    first_one,
    second_one,
    first_two,
    second_two,
):
    frames, rows_here, columns, channels = inputs.shape
    cell_count = float(
        frames
        * rows_here
        * columns
        * lax.axis_size("tm")
        * lax.axis_size("rows")
        * (channels // GROUPS)
    )
    conv_scale = (27.0 * channels) ** (-0.5)
    in_val = inputs.astype(jnp.float32)
    in_hat, inv_one = normalize(in_val, cell_count)
    pre_one = in_hat * gain_one
    gate_one = jax.nn.sigmoid(pre_one)
    hidden_one = (pre_one * gate_one).astype(jnp.bfloat16)
    patch_one = patches(extend(hidden_one, False), False, frames, rows_here, columns)
    middle = (
        jnp.dot(patch_one, weight_one, preferred_element_type=jnp.float32) * conv_scale
    ).astype(jnp.bfloat16)
    mid_hat, inv_two = normalize(middle.astype(jnp.float32).reshape(inputs.shape), cell_count)
    pre_two = mid_hat * gain_two
    gate_two = jax.nn.sigmoid(pre_two)
    hidden_two = (pre_two * gate_two).astype(jnp.bfloat16)
    patch_two = patches(extend(hidden_two, False), False, frames, rows_here, columns)
    grad_two = (
        lax.dot_general(
            patch_two,
            cotangent.reshape(-1, channels),
            (((0,), (0,)), ((), ())),
            preferred_element_type=jnp.float32,
        )
        * conv_scale
    )
    share_two = reduce_grad(grad_two)
    patch_back = patches(extend(cotangent, True), True, frames, rows_here, columns)
    back_two = (
        jnp.dot(patch_back, flipped(weight_two, channels), preferred_element_type=jnp.float32)
        * conv_scale
    ).reshape(inputs.shape)
    slope_two = back_two * gate_two * (1.0 + pre_two * (1.0 - gate_two)) * gain_two
    mid_grad = norm_backward(slope_two, mid_hat, inv_two, cell_count).astype(jnp.bfloat16)
    grad_one = (
        lax.dot_general(
            patch_one,
            mid_grad.reshape(-1, channels),
            (((0,), (0,)), ((), ())),
            preferred_element_type=jnp.float32,
        )
        * conv_scale
    )
    share_one = reduce_grad(grad_one)
    patch_mid = patches(extend(mid_grad, True), True, frames, rows_here, columns)
    back_one = (
        jnp.dot(patch_mid, flipped(weight_one, channels), preferred_element_type=jnp.float32)
        * conv_scale
    ).reshape(inputs.shape)
    slope_one = back_one * gate_one * (1.0 + pre_one * (1.0 - gate_one)) * gain_one
    input_grad = (
        cotangent.astype(jnp.float32) + norm_backward(slope_one, in_hat, inv_one, cell_count)
    ).astype(jnp.bfloat16)
    part_one, new_first_one, new_second_one = adamw_share(
        weight_one, share_one, first_one, second_one
    )
    part_two, new_first_two, new_second_two = adamw_share(
        weight_two, share_two, first_two, second_two
    )
    whole_one, whole_two = (
        lax.all_gather(part_one, ("tm", "rows"), axis=0, tiled=True),
        lax.all_gather(part_two, ("tm", "rows"), axis=0, tiled=True),
    )
    new_weight_one = whole_one.reshape(weight_one.shape)
    new_weight_two = whole_two.reshape(weight_two.shape)
    return (
        input_grad,
        new_weight_one,
        new_weight_two,
        new_first_one,
        new_second_one,
        new_first_two,
        new_second_two,
    )


def solution(mesh):
    return jax.shard_map(
        local,
        mesh=mesh,
        in_specs=(
            P("tm", "rows", None, None),
            P("tm", "rows", None, None),
            P(),
            P(),
            P(),
            P(),
            P(("tm", "rows")),
            P(("tm", "rows")),
            P(("tm", "rows")),
            P(("tm", "rows")),
        ),
        out_specs=(
            P("tm", "rows", None, None),
            P(),
            P(),
            P(("tm", "rows")),
            P(("tm", "rows")),
            P(("tm", "rows")),
            P(("tm", "rows")),
        ),
        check_vma=False,
    )
```

profile of v0, /device:TPU:1, one launch (start us, length us, event | category | flops | bytes accessed | tf_op | source)
XLA Modules:
  0.0 941.9 jit_solution(6844223563028410496)
XLA Ops:
  7.2 1.3 convert_reduce_fusion
  8.7 68.7 %psum.56 = f32[32]{0:T(128)S(1)} all-reduce(f32[32]{0:T(128)S(1)} %reduce_sum.145), channel_id=1, replica_groups=mesh['tm'=32,'rows'=4] {'tm','rows'}, use_global_device_ids=true, to_apply=%region_2.0 | all-reduce | flops 32 | bytes 256 | tf_op jit(solution)/shard_map/psum | solution.py:39
  77.6 1.3 fusion.42
  79.1 2.8 collective-permute-start.3
  81.9 65.2 %psum.57 = f32[32]{0:T(128)S(1)} all-reduce(f32[32]{0:T(128)S(1)} %reduce_sum.147), channel_id=1, replica_groups=mesh['tm'=32,'rows'=4] {'tm','rows'}, use_global_device_ids=true, to_apply=%region_5.0 | all-reduce | flops 32 | bytes 256 | tf_op jit(solution)/shard_map/psum | solution.py:39
  147.2 1.5 fusion.33
  148.8 3.6 collective-permute-start
  152.3 1.1 constant_dynamic-update-slice_fusion.3
  154.4 1.7 collective-permute-start.4
  156.1 1.3 collective-permute-start.5
  157.4 5.7 copy.21
  163.2 4.0 collective-permute-start.1
  167.2 1.8 collective-permute-start.2
  169.0 1.0 fusion.20
  174.0 5.6 copy-done.22
  184.4 1.2 copy-done.6
  185.7 5.9 fusion.64
  191.8 1.1 slice_dynamic-update-slice_fusion.49
  192.9 65.7 %psum.58 = f32[32]{0:T(128)S(1)} all-reduce(f32[32]{0:T(128)S(1)} %reduce_sum.149), channel_id=1, replica_groups=mesh['tm'=32,'rows'=4] {'tm','rows'}, use_global_device_ids=true, to_apply=%region_8.9 | all-reduce | flops 32 | bytes 256 | tf_op jit(solution)/shard_map/psum | solution.py:39
  258.8 1.5 multiply_reduce_fusion.1
  262.4 64.0 %psum.59 = f32[32]{0:T(128)S(1)} all-reduce(f32[32]{0:T(128)S(1)} %reduce_sum.151), channel_id=1, replica_groups=mesh['tm'=32,'rows'=4] {'tm','rows'}, use_global_device_ids=true, to_apply=%region_11.12 | all-reduce | flops 32 | bytes 256 | tf_op jit(solution)/shard_map/psum | solution.py:39
  326.6 13.9 %fusion.59 = (f32[256]{0:T(256)S(1)}, f32[256]{0:T(256)S(1)}, f32[1280,256]{1,0:T(8,128)}) fusion(f32[256]{0:T(256)S(1)} %mul.222, f32[1280,256]{1,0:T(8,128)} %get-tuple-element.41, f32[256]{0:T(256)S(1)} %sub.72, f32[256]{0:T(256)S(1)} %copy-done.24, bf16[1280,6912]{1,0:T(8,128)(2,1)} %bitcast.64, bf16[6912,256]{1,0:T(8,128)(2,1)} %bitcast.59), kind=kOutput, calls=%fused_computation.220 | convolution fusion | flops 4535091200 | bytes 23860224 | tf_op jit(solution)/shard_map/dot_general | solution.py:167
  340.9 62.5 %all-reduce.7 = (f32[32]{0:T(128)S(1)}, f32[32]{0:T(128)S(1)}) all-reduce(f32[32]{0:T(128)S(1)} %reduce_sum.155, f32[32]{0:T(128)S(1)} %reduce_sum.153), channel_id=1, replica_groups=mesh['tm'=32,'rows'=4] {'tm','rows'}, use_global_device_ids=true, to_apply=%region_17.18 | all-reduce | flops 64 | bytes 512 | tf_op jit(solution)/shard_map/psum | solution.py:39
  403.8 2.1 multiply_convert_fusion
  405.9 3.5 collective-permute-start.9
  409.4 7.5 collective-permute-done.9
  417.0 1.3 collective-permute-start.10
  418.3 1.5 collective-permute-start.11
  419.8 13.7 %fusion.3 = f32[864,2,8,128]{3,2,1,0:T(8,128)} fusion(bf16[2,8,80,6912]{3,2,1,0:T(8,128)(2,1)} %copy-done.21, bf16[2,8,80,256]{3,2,1,0:T(8,128)(2,1)S(1)} %get-tuple-element.25), kind=kOutput, calls=%fused_computation.7 | convolution fusion | flops 4531617792 | bytes 25427968 | tf_op jit(solution)/shard_map/dot_general | solution.py:173
  433.5 9.6 %copy.26 = f32[864,2,8,128]{3,1,2,0:T(2,128)} copy(f32[864,2,8,128]{3,2,1,0:T(8,128)} %fusion.3) | data formatting | bytes 14155776
  443.0 1.2 select_maximum_fusion
  447.8 7.0 fusion.4
  454.8 9.6 %copy.28 = f32[864,2,8,128]{3,1,2,0:T(2,128)} copy(f32[864,2,8,128]{3,2,1,0:T(8,128)} %fusion.4) | data formatting | bytes 14155776
  464.5 7.4 copy.27
  471.9 167.6 %all-reduce.11.cloned.1.call-done = (f32[1769472]{0:T(1024)}, f32[1769472]{0:T(1024)}) async-done(((f32[1769472]{0:T(1024)}, f32[1769472]{0:T(1024)}), (f32[1769472]{0:T(1024)}, f32[1769472]{0:T(1024)})) %all-reduce.11.cloned.1.call-update) | async-done | bytes 14155792
  639.5 1.6 subtract_convert_fusion
  641.8 2.4 collective-permute-start.6
  644.2 9.5 %collective-permute-done.6 = bf16[2,8,80,256]{3,2,1,0:T(8,128)(2,1)S(1)} collective-permute-done((bf16[2,8,80,256]{3,2,1,0:T(8,128)(2,1)S(1)}, bf16[2,8,80,256]{3,2,1,0:T(8,128)(2,1)S(1)}, u32[]{:S(2)}, u32[]{:S(2)}) %collective-permute-start.6) | collective-permute-done | bytes 655392 | tf_op jit(solution)/shard_map/ppermute | solution.py:22
  653.7 2.3 collective-permute-start.7
  656.0 1.5 collective-permute-start.8
  657.5 7.4 copy.25
  664.9 5.7 copy.22
  671.7 1.1 slice_dynamic-update-slice_fusion.47
  672.8 1.0 slice_dynamic-update-slice_fusion.46
  674.7 1.1 slice_dynamic-update-slice_fusion.44
  677.7 1.2 slice_dynamic-update-slice_fusion.42
  680.8 1.6 subtract_convert_fusion.1
  683.1 1.2 slice_dynamic-update-slice_fusion.39
  684.3 2.1 slice_dynamic-update-slice_fusion.38
  687.3 1.1 slice_dynamic-update-slice_fusion.36
  690.3 1.1 slice_dynamic-update-slice_fusion.34
  693.3 1.1 slice_dynamic-update-slice_fusion.31
  694.5 2.0 slice_dynamic-update-slice_fusion.30
  697.4 1.1 slice_dynamic-update-slice_fusion.28
  698.5 1.0 constant_dynamic-update-slice_fusion.6
  700.4 1.1 slice_dynamic-update-slice_fusion.26
  701.5 1.0 slice_dynamic-update-slice_fusion.25
  703.4 8.8 convolution_multiply_fusion
  713.5 68.4 %all-reduce.6 = (f32[32]{0:T(128)S(1)}, f32[32]{0:T(128)S(1)}) all-reduce(f32[32]{0:T(128)S(1)} %reduce_sum.159, f32[32]{0:T(128)S(1)} %reduce_sum.157), channel_id=1, replica_groups=mesh['tm'=32,'rows'=4] {'tm','rows'}, use_global_device_ids=true, to_apply=%region_23.24 | all-reduce | flops 64 | bytes 512 | tf_op jit(solution)/shard_map/psum | solution.py:39
  782.2 1.2 fusion.41
  783.4 69.1 %reduce.5 = bf16[128,13824]{1,0:T(8,128)(2,1)S(1)} reduce(bf16[128,1,13824]{2,1,0:T(2,128)(2,1)} %all-gather.7.cloned.1.call-done, bf16[]{:T(256)} %constant.77), dimensions={1}, to_apply=%all-gather.1.reduce_sub_computation | reduce | bytes 7077890 | tf_op jit(solution)/shard_map/all_gather | solution.py:199
  852.6 6.7 reshape.129
  859.3 69.1 %reduce.4 = bf16[128,13824]{1,0:T(8,128)(2,1)S(1)} reduce(bf16[128,1,13824]{2,1,0:T(2,128)(2,1)} %all-gather.5.cloned.1.call-done, bf16[]{:T(256)} %constant.77), dimensions={1}, to_apply=%all-gather.reduce_sub_computation | reduce | bytes 7077890 | tf_op jit(solution)/shard_map/all_gather | solution.py:198
  928.4 6.7 reshape.126
  (211 shorter events, 33.0 us)
Async XLA Ops:
  7.2 632.3 %all-reduce.11.cloned.1.call-start = ((), (), s32[]{:S(2)}) async-start(), calls=%async_computation.2 | async-start | bytes 28311552
  79.1 74.4 %collective-permute-start.3 = (bf16[2,8,80,256]{3,2,1,0:T(8,128)(2,1)}, bf16[2,8,80,256]{3,2,1,0:T(8,128)(2,1)S(1)}, u32[]{:S(2)}, u32[]{:S(2)}) collective-permute-start(bf16[2,8,80,256]{3,2,1,0:T(8,128)(2,1)} %param.11), channel_id=1, source_target_pairs={{4,0},{8,4},{12,8},{16,12},{20,16},{24,20},{28,24},{32,28},{36,32}... | collective-permute-start | bytes 1966088 | tf_op jit(solution)/shard_map/ppermute | solution.py:22
  148.8 14.4 %copy-start.2 = (bf16[2,8,80,256]{3,2,1,0:T(8,128)(2,1)}, bf16[2,8,80,256]{3,2,1,0:T(8,128)(2,1)S(1)}, u32[]{:S(2)}) copy-start(bf16[2,8,80,256]{3,2,1,0:T(8,128)(2,1)S(1)} %fusion.33) | copy-start | bytes 1966084
  148.8 14.4 %collective-permute-start = (bf16[2,8,80,256]{3,2,1,0:T(8,128)(2,1)S(1)}, bf16[2,8,80,256]{3,2,1,0:T(8,128)(2,1)S(1)}, u32[]{:S(2)}, u32[]{:S(2)}) collective-permute-start(bf16[2,8,80,256]{3,2,1,0:T(8,128)(2,1)S(1)} %fusion.33), channel_id=1, source_target_pairs={{0,4},{4,8},{8,12},{12,16},{16,20},{20,24},{24,28},{28,32},{32,36}... | collective-permute-start | bytes 1966088 | tf_op jit(solution)/shard_map/ppermute | solution.py:22
  153.5 1.0 copy-start.15
  154.4 14.6 %collective-permute-start.4 = (bf16[4,1,80,256]{3,2,1,0:T(8,128)(2,1)}, bf16[4,1,80,256]{3,2,1,0:T(8,128)(2,1)S(1)}, u32[]{:S(2)}, u32[]{:S(2)}) collective-permute-start(bf16[4,1,80,256]{3,2,1,0:T(8,128)(2,1)} %get-tuple-element.38), channel_id=1, source_target_pairs={{0,1},{1,2},{2,3},{4,5},{5,6},{6,7},{8,9},{9,10},{10,11},{12,13},{... | collective-permute-start | bytes 491528 | tf_op jit(solution)/shard_map/ppermute | solution.py:32
  156.1 12.9 %collective-permute-start.5 = (bf16[4,1,80,256]{3,2,1,0:T(8,128)(2,1)}, bf16[4,1,80,256]{3,2,1,0:T(8,128)(2,1)S(1)}, u32[]{:S(2)}, u32[]{:S(2)}) collective-permute-start(bf16[4,1,80,256]{3,2,1,0:T(8,128)(2,1)} %get-tuple-element.39), channel_id=1, source_target_pairs={{1,0},{2,1},{3,2},{5,4},{6,5},{7,6},{9,8},{10,9},{11,10},{13,12},{... | collective-permute-start | bytes 491528 | tf_op jit(solution)/shard_map/ppermute | solution.py:33
  163.2 5.8 copy-start.4
  163.2 10.4 %collective-permute-start.1 = (bf16[4,1,80,256]{3,2,1,0:T(8,128)(2,1)S(1)}, bf16[4,1,80,256]{3,2,1,0:T(8,128)(2,1)S(1)}, u32[]{:S(2)}, u32[]{:S(2)}) collective-permute-start(bf16[4,1,80,256]{3,2,1,0:T(8,128)(2,1)S(1)} %get-tuple-element.36), channel_id=1, source_target_pairs={{0,1},{1,2},{2,3},{4,5},{5,6},{6,7},{8,9},{9,10},{10,11},{12,13},{... | collective-permute-start | bytes 491528 | tf_op jit(solution)/shard_map/ppermute | solution.py:32
  167.2 6.8 collective-permute-start.2
  170.0 1.1 copy-start.16
  172.4 1.1 copy-start.10
  172.7 6.9 copy-start.3
  172.7 6.9 copy-start.5
  173.6 6.0 copy-start.22
  182.3 1.1 copy-start
  182.4 1.1 copy-start.23
  183.4 2.2 copy-start.6
  184.4 7.2 copy-start.21
  191.6 135.0 %copy-start.24 = (f32[256]{0:T(256)S(1)}, f32[256]{0:T(256)}, u32[]{:S(2)}) copy-start(f32[256]{0:T(256)} %param.13) | copy-start | bytes 3076
  326.6 77.2 %copy-start.13 = (f32[1280,256]{1,0:T(8,128)S(1)}, f32[1280,256]{1,0:T(8,128)}, u32[]{:S(2)}) copy-start(f32[1280,256]{1,0:T(8,128)} %get-tuple-element.41) | copy-start | bytes 3932164
  405.9 11.0 %collective-permute-start.9 = (bf16[2,8,80,256]{3,2,1,0:T(8,128)(2,1)S(1)}, bf16[2,8,80,256]{3,2,1,0:T(8,128)(2,1)S(1)}, u32[]{:S(2)}, u32[]{:S(2)}) collective-permute-start(bf16[2,8,80,256]{3,2,1,0:T(8,128)(2,1)S(1)} %get-tuple-element.24), channel_id=1, source_target_pairs={{0,4},{4,8},{8,12},{12,16},{16,20},{20,24},{24,28},{28,32},{32,36}... | collective-permute-start | bytes 1966088 | tf_op jit(solution)/shard_map/ppermute | solution.py:22
  417.0 26.0 %collective-permute-start.10 = (bf16[4,1,80,256]{3,2,1,0:T(8,128)(2,1)S(1)}, bf16[4,1,80,256]{3,2,1,0:T(8,128)(2,1)S(1)}, u32[]{:S(2)}, u32[]{:S(2)}) collective-permute-start(bf16[4,1,80,256]{3,2,1,0:T(8,128)(2,1)S(1)} %get-tuple-element.28), channel_id=1, source_target_pairs={{0,1},{1,2},{2,3},{4,5},{5,6},{6,7},{8,9},{9,10},{10,11},{12,13},{... | collective-permute-start | bytes 491528 | tf_op jit(solution)/shard_map/ppermute | solution.py:32
  418.3 24.7 %collective-permute-start.11 = (bf16[4,1,80,256]{3,2,1,0:T(8,128)(2,1)S(1)}, bf16[4,1,80,256]{3,2,1,0:T(8,128)(2,1)S(1)}, u32[]{:S(2)}, u32[]{:S(2)}) collective-permute-start(bf16[4,1,80,256]{3,2,1,0:T(8,128)(2,1)S(1)} %get-tuple-element.29), channel_id=1, source_target_pairs={{1,0},{2,1},{3,2},{5,4},{6,5},{7,6},{9,8},{10,9},{11,10},{13,12},{... | collective-permute-start | bytes 491528 | tf_op jit(solution)/shard_map/ppermute | solution.py:33
  446.7 1.1 copy-start.11
  464.4 175.1 %copy-start.17 = (f32[13824]{0:T(1024)S(1)}, f32[13824]{0:T(1024)}, u32[]{:S(2)}) copy-start(f32[13824]{0:T(1024)} %param.18) | copy-start | bytes 165892
  464.4 175.1 %copy-start.18 = (f32[13824]{0:T(1024)S(1)}, f32[13824]{0:T(1024)}, u32[]{:S(2)}) copy-start(f32[13824]{0:T(1024)} %param.19) | copy-start | bytes 165892
  464.4 319.1 %all-gather.7.cloned.1.call-start = ((), (), s32[]{:S(2)}) async-start(), calls=%async_computation.1 | async-start | bytes 7133184 | tf_op jit(solution)/shard_map/all_gather | solution.py:199
  641.7 217.6 %all-gather.5.cloned.1.call-start = ((), (), s32[]{:S(2)}) async-start(), calls=%async_computation | async-start | bytes 7133184 | tf_op jit(solution)/shard_map/all_gather | solution.py:198
  641.8 11.9 %collective-permute-start.6 = (bf16[2,8,80,256]{3,2,1,0:T(8,128)(2,1)S(1)}, bf16[2,8,80,256]{3,2,1,0:T(8,128)(2,1)S(1)}, u32[]{:S(2)}, u32[]{:S(2)}) collective-permute-start(bf16[2,8,80,256]{3,2,1,0:T(8,128)(2,1)S(1)} %get-tuple-element.25), channel_id=1, source_target_pairs={{4,0},{8,4},{12,8},{16,12},{20,16},{24,20},{28,24},{32,28},{36,32}... | collective-permute-start | bytes 1966088 | tf_op jit(solution)/shard_map/ppermute | solution.py:22
  653.7 16.9 %collective-permute-start.7 = (bf16[4,1,80,256]{3,2,1,0:T(8,128)(2,1)S(1)}, bf16[4,1,80,256]{3,2,1,0:T(8,128)(2,1)S(1)}, u32[]{:S(2)}, u32[]{:S(2)}) collective-permute-start(bf16[4,1,80,256]{3,2,1,0:T(8,128)(2,1)S(1)} %get-tuple-element.32), channel_id=1, source_target_pairs={{0,1},{1,2},{2,3},{4,5},{5,6},{6,7},{8,9},{9,10},{10,11},{12,13},{... | collective-permute-start | bytes 491528 | tf_op jit(solution)/shard_map/ppermute | solution.py:32
  656.0 14.6 %collective-permute-start.8 = (bf16[4,1,80,256]{3,2,1,0:T(8,128)(2,1)S(1)}, bf16[4,1,80,256]{3,2,1,0:T(8,128)(2,1)S(1)}, u32[]{:S(2)}, u32[]{:S(2)}) collective-permute-start(bf16[4,1,80,256]{3,2,1,0:T(8,128)(2,1)S(1)} %get-tuple-element.33), channel_id=1, source_target_pairs={{1,0},{2,1},{3,2},{5,4},{6,5},{7,6},{9,8},{10,9},{11,10},{13,12},{... | collective-permute-start | bytes 491528 | tf_op jit(solution)/shard_map/ppermute | solution.py:33
  670.9 3.8 copy-start.9
  670.9 8.0 copy-start.7
  675.8 5.0 copy-start.19
  675.8 5.0 copy-start.20
  686.3 5.1 copy-start.8
  698.5 4.9 copy-start.14
  703.4 8.9 copy-start.1
  712.3 69.9 %copy-start.12 = (bf16[2,8,80,256]{3,2,1,0:T(8,128)(2,1)S(1)}, bf16[2,8,80,256]{3,2,1,0:T(8,128)(2,1)}, u32[]{:S(2)}) copy-start(bf16[2,8,80,256]{3,2,1,0:T(8,128)(2,1)} %param.11) | copy-start | bytes 1966084
Sparse Core Ops, SparseCore 0:
  464.5 174.9 all-reduce.10
  642.9 67.4 all-gather.6
  714.4 66.7 all-gather.4
where the time goes:
time: 947 us; the launch traced here: 942 us
  blocking collectives  394 us (42%)
  waiting for transfers between devices  185 us (20%)
  other arithmetic  159 us (17%)
  local copies, waits for them, and re-layouts  111 us (12%)
  matrix products  49.3 us (5%)
  starting transfers between devices  27.8 us (3%)
  between operations  15.1 us (2%)
    psum x6, blocking collectives, summed(): return lax.psum(pieces, ('tm', 'rows'))  394 us
    unnamed x4, waiting for transfers between devices  168 us
    unnamed x151, local copies, waits for them, and re-layouts  81 us
    all_gather x1, other arithmetic, local(): lax.all_gather(part_two, ('tm', 'rows'), axis=0, tiled=True)  69.1 us
    all_gather x1, other arithmetic, local(): lax.all_gather(part_one, ('tm', 'rows'), axis=0, tiled=True)  69.1 us
  transfers between devices with their start and end apart: 15, of which 4 were waited for; matrix products, arithmetic and copies ran while one was open for 19% of the time, Pallas kernels for 0%

commit v1 on v0

--- a/solution.py
+++ b/solution.py
@@ -35,8 +35,27 @@
     return array
 
 
-def summed(pieces):
-    return lax.psum(pieces, ("tm", "rows"))
+def coordinates(index):
+    return (index >> 5, index >> 3 & 3, index >> 2 & 1, index & 3)
+
+
+def flat_index(z, y, core, x):
+    return ((z * 4 + y) * 2 + core) * 4 + x
+
+
+CHIP_GROUPS = [
+    [flat_index(z, y, core, x) for z in range(4) for y in range(4) for x in range(4)]
+    for core in range(2)
+]
+CORE_PAIRS = [(i, i ^ 4) for i in range(128)]
+BOTH = ("tm", "rows")
+
+
+def from_everyone(first, second):
+    row = jnp.concatenate([first, second, jnp.zeros((64,), jnp.float32)])
+    spread = jnp.broadcast_to(row[None], (128, 128))
+    arrived = lax.all_to_all(spread, BOTH, 0, 0, tiled=True)
+    return arrived[:, :GROUPS], arrived[:, GROUPS : 2 * GROUPS]
 
 
 def per_group(values):
@@ -51,16 +70,22 @@
 
 def normalize(values, cell_count):
     channels = values.shape[-1]
-    center = broaden(summed(per_group(values)) / cell_count, channels)
-    centered = values - center
-    inverse = lax.rsqrt(summed(per_group(centered * centered)) / cell_count + norm_eps)
-    inverse_wide = broaden(inverse, channels)
-    return (centered * inverse_wide, inverse_wide)
+    here_count = cell_count / 128.0
+    here_mean = per_group(values) / here_count
+    centered = values - broaden(here_mean, channels)
+    means, squares = from_everyone(here_mean, per_group(centered * centered))
+    center = jnp.mean(means, axis=0)
+    offsets = means - center
+    spread = jnp.sum(squares, axis=0) + here_count * jnp.sum(offsets * offsets, axis=0)
+    inverse_wide = broaden(lax.rsqrt(spread / cell_count + norm_eps), channels)
+    center_wide = broaden(center, channels)
+    return center_wide, inverse_wide
 
 
 def norm_backward(slope, normed, inverse_wide, cell_count):
     channels = slope.shape[-1]
-    mean_sum, cross_sum = summed((per_group(slope), per_group(slope * normed)))
+    means, crosses = from_everyone(per_group(slope), per_group(slope * normed))
+    mean_sum, cross_sum = jnp.sum(means, axis=0), jnp.sum(crosses, axis=0)
     return inverse_wide * (
         slope
         - broaden(mean_sum / cell_count, channels)
@@ -99,8 +124,28 @@
 
 
 def reduce_grad(local_grad):
-    flattened = local_grad.reshape(-1)
-    return lax.psum_scatter(flattened, ("tm", "rows"), scatter_dimension=0, tiled=True)
+    core = lax.axis_index("tm") % 2
+    halves = local_grad.astype(jnp.bfloat16).reshape(16, 2, 216, 256)
+    kept = lax.dynamic_index_in_dim(halves, core, 1, keepdims=False)
+    given = lax.dynamic_index_in_dim(halves, 1 - core, 1, keepdims=False)
+    taken = lax.ppermute(given, BOTH, CORE_PAIRS)
+    pair_sum = (kept.astype(jnp.float32) + taken.astype(jnp.float32)).astype(jnp.bfloat16)
+    arrived = lax.all_to_all(
+        pair_sum.reshape(64, 54, 256), BOTH, 0, 0, axis_index_groups=CHIP_GROUPS, tiled=True
+    )
+    return jnp.sum(arrived.astype(jnp.float32), axis=0).reshape(-1)
+
+
+def gather_weights(part_one, part_two):
+    core = lax.axis_index("tm") % 2
+    both = jnp.concatenate([part_one.reshape(54, 256), part_two.reshape(54, 256)], axis=0)
+    spread = jnp.broadcast_to(both[None], (64, 108, 256))
+    own = lax.all_to_all(spread, BOTH, 0, 0, axis_index_groups=CHIP_GROUPS, tiled=True)
+    other = lax.ppermute(own, BOTH, CORE_PAIRS)
+    low = jnp.where(core == 0, own, other).reshape(16, 1, 4, 108, 256)
+    high = jnp.where(core == 0, other, own).reshape(16, 1, 4, 108, 256)
+    whole = jnp.concatenate([low, high], axis=1)
+    return (whole[:, :, :, :54].reshape(6912, 256), whole[:, :, :, 54:].reshape(6912, 256))
 
 
 def adamw_share(weight, gradient, first, second):
@@ -139,7 +184,8 @@
     )
     conv_scale = (27.0 * channels) ** (-0.5)
     in_val = inputs.astype(jnp.float32)
-    in_hat, inv_one = normalize(in_val, cell_count)
+    center_one, inv_one = normalize(in_val, cell_count)
+    in_hat = (in_val - center_one) * inv_one
     pre_one = in_hat * gain_one
     gate_one = jax.nn.sigmoid(pre_one)
     hidden_one = (pre_one * gate_one).astype(jnp.bfloat16)
@@ -147,7 +193,9 @@
     middle = (
         jnp.dot(patch_one, weight_one, preferred_element_type=jnp.float32) * conv_scale
     ).astype(jnp.bfloat16)
-    mid_hat, inv_two = normalize(middle.astype(jnp.float32).reshape(inputs.shape), cell_count)
+    mid_val = middle.astype(jnp.float32).reshape(inputs.shape)
+    center_two, inv_two = normalize(mid_val, cell_count)
+    mid_hat = (mid_val - center_two) * inv_two
     pre_two = mid_hat * gain_two
     gate_two = jax.nn.sigmoid(pre_two)
     hidden_two = (pre_two * gate_two).astype(jnp.bfloat16)
@@ -194,12 +242,7 @@
     part_two, new_first_two, new_second_two = adamw_share(
         weight_two, share_two, first_two, second_two
     )
-    whole_one, whole_two = (
-        lax.all_gather(part_one, ("tm", "rows"), axis=0, tiled=True),
-        lax.all_gather(part_two, ("tm", "rows"), axis=0, tiled=True),
-    )
-    new_weight_one = whole_one.reshape(weight_one.shape)
-    new_weight_two = whole_two.reshape(weight_two.shape)
+    new_weight_one, new_weight_two = gather_weights(part_one, part_two)
     return (
         input_grad,
         new_weight_one,

time: 947 us -> 407 us (0.43)
  blocking collectives: 394 us -> 0 us
  other arithmetic: 159 us -> 42.9 us
  waiting for transfers between devices: 185 us -> 78.9 us
  starting transfers between devices: 27.8 us -> 92.1 us
  local copies, waits for them, and re-layouts: 111 us -> 133 us
  between operations: 15.1 us -> 2.33 us
    psum x6 -> x0, blocking collectives: 394 us -> none  [summed(): return lax.psum(pieces, ('tm', 'rows'))]
    unnamed x4 -> x0, waiting for transfers between devices: 168 us -> none
    all_gather x2 -> x0, other arithmetic: 138 us -> none  [the longest x1 69.1 us: local(): lax.all_gather(part_two, ('tm', 'rows'), axis=0, tiled=True)]
    all_to_all x0 -> x7, waiting for transfers between devices: none -> 78.4 us  [the longest x2 27.5 us: reduce_grad(): lax.all_to_all(pair_sum.reshape(64, 54, 256), BOTH, 0, 0, axis_index_grou...]
    all_to_all x0 -> x7, starting transfers between devices: none -> 57.1 us  [the longest x4 32.1 us: from_everyone(): arrived = lax.all_to_all(spread, BOTH, 0, 0, tiled=True)]
    ppermute x4, waiting for transfers between devices: 17 us -> 0.01 us  [shifted(): lax.ppermute(value, axis, [(source, source + steps) for source in range(l...]
    unnamed x151 -> x145, local copies, waits for them, and re-layouts: 81 us -> 85.9 us
  transfers between devices with their start and end apart: 15 -> 22, of which waited for: 4 -> 7; matrix products, arithmetic and copies ran while one was open for 19% -> 37% of each run, Pallas kernels for 0% -> 0%
where the time goes in v1:
time: 407 us; the launch traced here: 400 us
  local copies, waits for them, and re-layouts  133 us (33%)
  starting transfers between devices  92.1 us (23%)
  waiting for transfers between devices  78.9 us (19%)
  matrix products  50 us (12%)
  other arithmetic  42.9 us (11%)
    unnamed x145, local copies, waits for them, and re-layouts  85.9 us
    all_to_all x4, starting transfers between devices, from_everyone(): arrived = lax.all_to_all(spread, BOTH, 0, 0, tiled=True)  32.1 us
    all_to_all x2, waiting for transfers between devices, reduce_grad(): lax.all_to_all(pair_sum.reshape(64, 54, 256), BOTH, 0, 0, axis_index_grou...  27.5 us
    all_to_all x1, waiting for transfers between devices, gather_weights(): lax.all_to_all(spread, BOTH, 0, 0, axis_index_groups=CHIP_GROUPS, tiled=T...  26 us
    all_to_all x4, waiting for transfers between devices, from_everyone(): arrived = lax.all_to_all(spread, BOTH, 0, 0, tiled=True)  24.9 us
    all_to_all x2, starting transfers between devices, reduce_grad(): lax.all_to_all(pair_sum.reshape(64, 54, 256), BOTH, 0, 0, axis_index_grou...  19 us
    dot_general x1, matrix products, local(): jnp.dot(patch_back, flipped(weight_two, channels), preferred_element_type...  13.9 us
    ppermute x4, starting transfers between devices, with_halo(): before = lax.ppermute(last, axis, up)  13.3 us
  transfers between devices with their start and end apart: 22, of which 7 were waited for; matrix products, arithmetic and copies ran while one was open for 37% of the time, Pallas kernels for 0%

profile of v1, /device:TPU:1, one launch (start us, length us, event | category | flops | bytes accessed | tf_op | source)
XLA Modules:
  0.0 399.6 jit_solution(16850012817574624717)
XLA Ops:
  0.6 1.3 convert_reduce_fusion.2
  2.3 1.3 fusion.26
  4.6 11.5 %all-to-all-start = ((f32[128,1,128]{2,1,0:T(1,128)}), f32[128,1,128]{2,1,0:T(1,128)S(1)}, u32[]{:S(2)}, u32[]{:S(2)}) async-start(f32[128,1,128]{2,1,0:T(1,128)} %broadcast_in_dim.31), calls=%async_computation | async-start | bytes 131072 | tf_op jit(solution)/shard_map/all_to_all | solution.py:57
  16.1 3.0 collective-permute-start.3
  19.1 6.6 %all-to-all-done = f32[128,1,128]{2,1,0:T(1,128)S(1)} async-done(((f32[128,1,128]{2,1,0:T(1,128)}), f32[128,1,128]{2,1,0:T(1,128)S(1)}, u32[]{:S(2)}, u32[]{:S(2)}) %all-to-all-start) | async-done | bytes 65568 | tf_op jit(solution)/shard_map/all_to_all | solution.py:57
  26.5 1.5 fusion.37
  28.0 2.8 collective-permute-start
  33.1 2.2 collective-permute-start.4
  35.3 1.3 collective-permute-start.5
  36.6 5.7 %copy.68 = bf16[27,256,256]{2,1,0:T(8,128)(2,1)} copy(bf16[27,256,256]{1,2,0:T(8,128)(2,1)} %bitcast.72) | data formatting | bytes 7077888 | tf_op jit(solution)/shard_map/transpose | solution.py:122
  42.4 4.0 collective-permute-start.1
  46.4 1.3 collective-permute-start.2
  53.6 5.5 %copy-done.21 = bf16[2,8,80,6912]{3,2,1,0:T(8,128)(2,1)} copy-done((bf16[2,8,80,6912]{3,2,1,0:T(8,128)(2,1)}, bf16[2,8,80,6912]{3,2,1,0:T(8,128)(2,1)S(1)}, u32[]{:S(2)}) %copy-start.21) | copy-done | bytes 17694744
  65.4 5.9 %fusion.67 = (f32[256]{0:T(256)S(1)}, f32[1280,256]{1,0:T(8,128)}) fusion(bf16[1280,6912]{1,0:T(8,128)(2,1)S(1)} %bitcast.93, bf16[6912,256]{1,0:T(8,128)(2,1)S(1)} %copy-done.8), kind=kOutput, calls=%fused_computation.255 | convolution fusion | flops 4531159040 | bytes 22545408 | tf_op jit(solution)/shard_map/dot_general | solution.py:194
  71.7 1.5 multiply_reduce_fusion.1
  74.2 9.9 %all-to-all-start.1 = ((f32[128,1,128]{2,1,0:T(1,128)}), f32[128,1,128]{2,1,0:T(1,128)S(1)}, u32[]{:S(2)}, u32[]{:S(2)}) async-start(f32[128,1,128]{2,1,0:T(1,128)} %broadcast_in_dim.35), calls=%async_computation.1 | async-start | bytes 131072 | tf_op jit(solution)/shard_map/all_to_all | solution.py:57
  85.0 8.7 %all-to-all-done.1 = f32[128,1,128]{2,1,0:T(1,128)S(1)} async-done(((f32[128,1,128]{2,1,0:T(1,128)}), f32[128,1,128]{2,1,0:T(1,128)S(1)}, u32[]{:S(2)}, u32[]{:S(2)}) %all-to-all-start.1) | async-done | bytes 65568 | tf_op jit(solution)/shard_map/all_to_all | solution.py:57
  94.5 13.9 %fusion.62 = (f32[256]{0:T(256)S(1)}, f32[256]{0:T(256)S(1)}, f32[1280,256]{1,0:T(8,128)}) fusion(f32[256]{0:T(256)S(1)} %mul.238, f32[1280,256]{1,0:T(8,128)} %get-tuple-element.47, f32[256]{0:T(256)S(1)} %sub.122, f32[256]{0:T(256)S(1)} %copy-done.23, bf16[1280,6912]{1,0:T(8,128)(2,1)} %bitcast.94, bf16[6912,256]{1,0:T(8,128)(2,1)} %bitcast.80), kind=kOutput, calls=%fused_computation.253 | convolution fusion | flops 4535091200 | bytes 23860224 | tf_op jit(solution)/shard_map/dot_general | solution.py:215
  109.5 4.8 %all-to-all-start.2 = ((f32[128,1,128]{2,1,0:T(1,128)}), f32[128,1,128]{2,1,0:T(1,128)S(1)}, u32[]{:S(2)}, u32[]{:S(2)}) async-start(f32[128,1,128]{2,1,0:T(1,128)} %broadcast_in_dim.74), calls=%async_computation.2 | async-start | bytes 131072 | tf_op jit(solution)/shard_map/all_to_all | solution.py:57
  114.4 7.5 %copy.89 = bf16[864,2,8,128]{3,1,2,0:T(2,128)(2,1)} copy(bf16[864,2,8,128]{3,2,1,0:T(8,128)(2,1)} %bitcast.74) | data formatting | bytes 7077888
  121.9 5.4 %copy.90 = bf16[864,2,8,128]{3,1,2,0:T(2,128)(2,1)} copy(bf16[864,2,8,128]{3,2,1,0:T(8,128)(2,1)S(1)} %bitcast.73) | data formatting | bytes 7077888
  127.4 5.8 %copy.71 = bf16[27,256,256]{2,1,0:T(8,128)(2,1)} copy(bf16[27,256,256]{1,2,0:T(8,128)(2,1)} %bitcast.75) | data formatting | bytes 7077888 | tf_op jit(solution)/shard_map/transpose | solution.py:122
  133.7 2.1 multiply_convert_fusion
  135.8 3.5 collective-permute-start.10
  139.3 2.1 collective-permute-start.6
  141.4 10.8 %fusion.2 = bf16[6912,256]{1,0:T(8,128)(2,1)S(1)} fusion(bf16[2,8,80,6912]{3,2,1,0:T(8,128)(2,1)} %copy-done.20, bf16[2,8,80,256]{3,2,1,0:T(8,128)(2,1)S(1)} %get-tuple-element.31), kind=kOutput, calls=%fused_computation.4 | convolution fusion | flops 4533387264 | bytes 21889024 | tf_op jit(solution)/shard_map/dot_general | solution.py:221
  152.3 3.1 collective-permute-start.11
  155.4 1.3 collective-permute-start.12
  157.0 4.0 collective-permute-start.7
  161.0 1.5 collective-permute-start.8
  190.9 10.8 %fusion.3 = bf16[6912,256]{1,0:T(8,128)(2,1)S(1)} fusion(bf16[2,8,80,6912]{3,2,1,0:T(8,128)(2,1)} %slice_dynamic-update-slice_fusion, bf16[2,8,80,256]{3,2,1,0:T(8,128)(2,1)S(1)} %copy-done.10), kind=kOutput, calls=%fused_computation.5 | convolution fusion | flops 4533387264 | bytes 21889024 | tf_op jit(solution)/shard_map/dot_general | solution.py:204
  201.8 1.4 dynamic-slice_bitcast_fusion
  204.0 1.8 maximum_maximum_fusion.1
  206.3 1.5 reshape.187
  207.8 12.8 %all-to-all-start.4 = ((bf16[64,54,256]{2,1,0:T(8,128)(2,1)}), bf16[64,54,256]{2,1,0:T(8,128)(2,1)}, u32[]{:S(2)}, u32[]{:S(2)}) async-start(bf16[64,54,256]{2,1,0:T(8,128)(2,1)} %reshape.187), calls=%async_computation.4 | async-start | bytes 3670016 | tf_op jit(solution)/shard_map/all_to_all | solution.py:133
  220.5 1.9 select_maximum_fusion.3
  223.6 2.1 slice_dynamic-update-slice_fusion.46
  227.7 3.1 fusion.6
  230.8 3.7 reshape.192
  234.5 12.5 %all-to-all-done.4 = bf16[64,54,256]{2,1,0:T(8,128)(2,1)} async-done(((bf16[64,54,256]{2,1,0:T(8,128)(2,1)}), bf16[64,54,256]{2,1,0:T(8,128)(2,1)}, u32[]{:S(2)}, u32[]{:S(2)}) %all-to-all-start.4) | async-done | bytes 1769504 | tf_op jit(solution)/shard_map/all_to_all | solution.py:133
  247.0 6.2 %all-to-all-start.5 = ((bf16[64,54,256]{2,1,0:T(8,128)(2,1)}), bf16[64,54,256]{2,1,0:T(8,128)(2,1)}, u32[]{:S(2)}, u32[]{:S(2)}) async-start(bf16[64,54,256]{2,1,0:T(8,128)(2,1)} %reshape.192), calls=%async_computation.5 | async-start | bytes 3670016 | tf_op jit(solution)/shard_map/all_to_all | solution.py:133
  253.2 2.0 constant_dynamic-update-slice_fusion.7
  257.4 2.1 slice_dynamic-update-slice_fusion.41
  260.4 1.8 convert_reduce_fusion.1
  262.2 1.4 subtract_convert_fusion.1
  263.7 15.0 %all-to-all-done.5 = bf16[64,54,256]{2,1,0:T(8,128)(2,1)} async-done(((bf16[64,54,256]{2,1,0:T(8,128)(2,1)}), bf16[64,54,256]{2,1,0:T(8,128)(2,1)}, u32[]{:S(2)}, u32[]{:S(2)}) %all-to-all-start.5) | async-done | bytes 1769504 | tf_op jit(solution)/shard_map/all_to_all | solution.py:133
  278.7 1.8 convert_reduce_fusion
  280.6 1.4 subtract_convert_fusion
  282.0 2.0 broadcast_in_dim.80
  284.1 6.1 %all-to-all-start.6 = ((bf16[64,108,256]{2,1,0:T(8,128)(2,1)}), bf16[64,108,256]{2,1,0:T(8,128)(2,1)}, u32[]{:S(2)}, u32[]{:S(2)}) async-start(bf16[64,108,256]{2,1,0:T(8,128)(2,1)} %broadcast_in_dim.80), calls=%async_computation.6 | async-start | bytes 7340032 | tf_op jit(solution)/shard_map/all_to_all | solution.py:143
  291.4 2.1 slice_dynamic-update-slice_fusion.38
  298.5 2.0 slice_dynamic-update-slice_fusion.33
  302.7 2.0 slice_dynamic-update-slice_fusion.30
  308.6 26.0 %all-to-all-done.6 = bf16[64,108,256]{2,1,0:T(8,128)(2,1)} async-done(((bf16[64,108,256]{2,1,0:T(8,128)(2,1)}), bf16[64,108,256]{2,1,0:T(8,128)(2,1)}, u32[]{:S(2)}, u32[]{:S(2)}) %all-to-all-start.6) | async-done | bytes 3538976 | tf_op jit(solution)/shard_map/all_to_all | solution.py:143
  334.6 5.1 %copy.76 = bf16[64,108,256]{2,0,1:T(8,128)(2,1)} copy(bf16[64,108,256]{2,1,0:T(8,128)(2,1)} %all-to-all-done.6) | data formatting | bytes 7077888 | tf_op jit(solution)/shard_map/all_to_all | solution.py:143
  339.6 4.1 %collective-permute-start.14 = (bf16[64,108,256]{2,0,1:T(8,128)(2,1)}, bf16[64,108,256]{2,0,1:T(8,128)(2,1)}, u32[]{:S(2)}, u32[]{:S(2)}) collective-permute-start(bf16[64,108,256]{2,0,1:T(8,128)(2,1)} %copy.76), channel_id=1, source_target_pairs={{0,4},{1,5},{2,6},{3,7},{4,0},{5,1},{6,2},{7,3},{8,12},{9,13},{10,... | collective-permute-start | bytes 10616840 | tf_op jit(solution)/shard_map/ppermute | solution.py:144
  344.8 2.0 slice_dynamic-update-slice_fusion.25
  347.8 8.5 %convolution_multiply_fusion = f32[1280,256]{1,0:T(8,128)S(1)} fusion(bf16[1280,6912]{1,0:T(8,128)(2,1)} %bitcast.10, bf16[6912,256]{1,0:T(8,128)(2,1)S(1)} %bitcast.79), kind=kOutput, calls=%fused_computation.21 | convolution fusion | flops 4530176000 | bytes 22544384 | tf_op jit(solution)/shard_map/dot_general | solution.py:232
  358.3 5.9 %all-to-all-start.3 = ((f32[128,1,128]{2,1,0:T(1,128)}), f32[128,1,128]{2,1,0:T(1,128)S(1)}, u32[]{:S(2)}, u32[]{:S(2)}) async-start(f32[128,1,128]{2,1,0:T(1,128)} %broadcast_in_dim.77), calls=%async_computation.3 | async-start | bytes 131072 | tf_op jit(solution)/shard_map/all_to_all | solution.py:57
  364.1 9.6 %all-to-all-done.3 = f32[128,1,128]{2,1,0:T(1,128)S(1)} async-done(((f32[128,1,128]{2,1,0:T(1,128)}), f32[128,1,128]{2,1,0:T(1,128)S(1)}, u32[]{:S(2)}, u32[]{:S(2)}) %all-to-all-start.3) | async-done | bytes 65568 | tf_op jit(solution)/shard_map/all_to_all | solution.py:57
  375.4 7.4 %broadcast_select_fusion = (bf16[64,108,256]{2,1,0:T(8,128)(2,1)S(1)}, bf16[64,108,256]{2,1,0:T(8,128)(2,1)S(1)}) fusion(bf16[64,108,256]{2,1,0:T(8,128)(2,1)} %all-to-all-done.6, pred[]{:T(512)S(6)} %eq.8, bf16[64,108,256]{2,0,1:T(8,128)(2,1)} %collective-permute-done.14), kind=kLoop, calls=%fused_computation.14 | loop fusion | flops 3538944 | bytes 14155777 | tf_op jit(solution)/shard_map/jit(_where)/select_n | solution.py:146
  382.8 3.8 pad_maximum_fusion
  386.7 6.2 %reshape.197 = bf16[6912,256]{1,0:T(8,128)(2,1)} reshape(bf16[16,2,4,54,256]{4,3,2,1,0:T(8,128)(2,1)} %get-tuple-element.27) | data formatting | bytes 7077888 | tf_op jit(solution)/shard_map/reshape | solution.py:148
  392.9 6.2 %reshape.198 = bf16[6912,256]{1,0:T(8,128)(2,1)} reshape(bf16[16,2,4,54,256]{4,3,2,1,0:T(8,128)(2,1)} %get-tuple-element.26) | data formatting | bytes 7077888 | tf_op jit(solution)/shard_map/reshape | solution.py:148
  (248 shorter events, 74.8 us)
Async XLA Ops:
  4.6 21.1 %all-to-all-start = ((f32[128,1,128]{2,1,0:T(1,128)}), f32[128,1,128]{2,1,0:T(1,128)S(1)}, u32[]{:S(2)}, u32[]{:S(2)}) async-start(f32[128,1,128]{2,1,0:T(1,128)} %broadcast_in_dim.31), calls=%async_computation | async-start | bytes 131072 | tf_op jit(solution)/shard_map/all_to_all | solution.py:57
  16.1 15.9 %collective-permute-start.3 = (bf16[2,8,80,256]{3,2,1,0:T(8,128)(2,1)}, bf16[2,8,80,256]{3,2,1,0:T(8,128)(2,1)}, u32[]{:S(2)}, u32[]{:S(2)}) collective-permute-start(bf16[2,8,80,256]{3,2,1,0:T(8,128)(2,1)} %param.11), channel_id=1, source_target_pairs={{4,0},{8,4},{12,8},{16,12},{20,16},{24,20},{28,24},{32,28},{36,32}... | collective-permute-start | bytes 1966088 | tf_op jit(solution)/shard_map/ppermute | solution.py:22
  28.0 14.4 %copy-start.3 = (bf16[2,8,80,256]{3,2,1,0:T(8,128)(2,1)}, bf16[2,8,80,256]{3,2,1,0:T(8,128)(2,1)S(1)}, u32[]{:S(2)}) copy-start(bf16[2,8,80,256]{3,2,1,0:T(8,128)(2,1)S(1)} %fusion.37) | copy-start | bytes 1966084
  28.0 14.4 %collective-permute-start = (bf16[2,8,80,256]{3,2,1,0:T(8,128)(2,1)S(1)}, bf16[2,8,80,256]{3,2,1,0:T(8,128)(2,1)S(1)}, u32[]{:S(2)}, u32[]{:S(2)}) collective-permute-start(bf16[2,8,80,256]{3,2,1,0:T(8,128)(2,1)S(1)} %fusion.37), channel_id=1, source_target_pairs={{0,4},{4,8},{8,12},{12,16},{16,20},{20,24},{24,28},{28,32},{32,36}... | collective-permute-start | bytes 1966088 | tf_op jit(solution)/shard_map/ppermute | solution.py:22
  33.1 14.6 %collective-permute-start.4 = (bf16[4,1,80,256]{3,2,1,0:T(8,128)(2,1)S(1)}, bf16[4,1,80,256]{3,2,1,0:T(8,128)(2,1)S(1)}, u32[]{:S(2)}, u32[]{:S(2)}) collective-permute-start(bf16[4,1,80,256]{3,2,1,0:T(8,128)(2,1)S(1)} %get-tuple-element.44), channel_id=1, source_target_pairs={{0,1},{1,2},{2,3},{4,5},{5,6},{6,7},{8,9},{9,10},{10,11},{12,13},{... | collective-permute-start | bytes 491528 | tf_op jit(solution)/shard_map/ppermute | solution.py:32
  35.3 12.4 %collective-permute-start.5 = (bf16[4,1,80,256]{3,2,1,0:T(8,128)(2,1)S(1)}, bf16[4,1,80,256]{3,2,1,0:T(8,128)(2,1)S(1)}, u32[]{:S(2)}, u32[]{:S(2)}) collective-permute-start(bf16[4,1,80,256]{3,2,1,0:T(8,128)(2,1)S(1)} %get-tuple-element.45), channel_id=1, source_target_pairs={{1,0},{2,1},{3,2},{5,4},{6,5},{7,6},{9,8},{10,9},{11,10},{13,12},{... | collective-permute-start | bytes 491528 | tf_op jit(solution)/shard_map/ppermute | solution.py:33
  42.4 5.4 %copy-start.5 = (bf16[2,8,80,256]{3,2,1,0:T(8,128)(2,1)}, bf16[2,8,80,256]{3,2,1,0:T(8,128)(2,1)S(1)}, u32[]{:S(2)}) copy-start(bf16[2,8,80,256]{3,2,1,0:T(8,128)(2,1)S(1)} %collective-permute-done) | copy-start | bytes 1966084
  42.4 10.7 %collective-permute-start.1 = (bf16[4,1,80,256]{3,2,1,0:T(8,128)(2,1)S(1)}, bf16[4,1,80,256]{3,2,1,0:T(8,128)(2,1)S(1)}, u32[]{:S(2)}, u32[]{:S(2)}) collective-permute-start(bf16[4,1,80,256]{3,2,1,0:T(8,128)(2,1)S(1)} %get-tuple-element.42), channel_id=1, source_target_pairs={{0,1},{1,2},{2,3},{4,5},{5,6},{6,7},{8,9},{9,10},{10,11},{12,13},{... | collective-permute-start | bytes 491528 | tf_op jit(solution)/shard_map/ppermute | solution.py:32
  46.4 7.2 %collective-permute-start.2 = (bf16[4,1,80,256]{3,2,1,0:T(8,128)(2,1)S(1)}, bf16[4,1,80,256]{3,2,1,0:T(8,128)(2,1)S(1)}, u32[]{:S(2)}, u32[]{:S(2)}) collective-permute-start(bf16[4,1,80,256]{3,2,1,0:T(8,128)(2,1)S(1)} %get-tuple-element.43), channel_id=1, source_target_pairs={{1,0},{2,1},{3,2},{5,4},{6,5},{7,6},{9,8},{10,9},{11,10},{13,12},{... | collective-permute-start | bytes 491528 | tf_op jit(solution)/shard_map/ppermute | solution.py:33
  51.7 1.1 copy-start.9
  52.1 7.1 %copy-start.4 = (bf16[2,8,80,256]{3,2,1,0:T(8,128)(2,1)S(1)}, bf16[2,8,80,256]{3,2,1,0:T(8,128)(2,1)}, u32[]{:S(2)}) copy-start(bf16[2,8,80,256]{3,2,1,0:T(8,128)(2,1)} %copy-done.3) | copy-start | bytes 1966084
  52.1 7.1 %copy-start.6 = (bf16[2,8,80,256]{3,2,1,0:T(8,128)(2,1)S(1)}, bf16[2,8,80,256]{3,2,1,0:T(8,128)(2,1)}, u32[]{:S(2)}) copy-start(bf16[2,8,80,256]{3,2,1,0:T(8,128)(2,1)} %copy-done.5) | copy-start | bytes 1966084
  53.1 6.0 %copy-start.21 = (bf16[2,8,80,6912]{3,2,1,0:T(8,128)(2,1)}, bf16[2,8,80,6912]{3,2,1,0:T(8,128)(2,1)S(1)}, u32[]{:S(2)}) copy-start(bf16[2,8,80,6912]{3,2,1,0:T(8,128)(2,1)S(1)} %fusion.56) | copy-start | bytes 53084164
  62.1 1.1 copy-start
  62.1 1.1 copy-start.22
  63.2 2.2 copy-start.8
  64.1 7.2 %copy-start.20 = (bf16[2,8,80,6912]{3,2,1,0:T(8,128)(2,1)}, bf16[2,8,80,6912]{3,2,1,0:T(8,128)(2,1)S(1)}, u32[]{:S(2)}) copy-start(bf16[2,8,80,6912]{3,2,1,0:T(8,128)(2,1)S(1)} %slice_dynamic-update-slice_fusion.67) | copy-start | bytes 53084164
  65.4 29.1 %copy-start.23 = (f32[256]{0:T(256)S(1)}, f32[256]{0:T(256)}, u32[]{:S(2)}) copy-start(f32[256]{0:T(256)} %param.13) | copy-start | bytes 3076
  74.2 19.5 %all-to-all-start.1 = ((f32[128,1,128]{2,1,0:T(1,128)}), f32[128,1,128]{2,1,0:T(1,128)S(1)}, u32[]{:S(2)}, u32[]{:S(2)}) async-start(f32[128,1,128]{2,1,0:T(1,128)} %broadcast_in_dim.35), calls=%async_computation.1 | async-start | bytes 131072 | tf_op jit(solution)/shard_map/all_to_all | solution.py:57
  109.5 23.7 %all-to-all-start.2 = ((f32[128,1,128]{2,1,0:T(1,128)}), f32[128,1,128]{2,1,0:T(1,128)S(1)}, u32[]{:S(2)}, u32[]{:S(2)}) async-start(f32[128,1,128]{2,1,0:T(1,128)} %broadcast_in_dim.74), calls=%async_computation.2 | async-start | bytes 131072 | tf_op jit(solution)/shard_map/all_to_all | solution.py:57
  114.4 7.6 %copy-start.7 = (bf16[6912,256]{1,0:T(8,128)(2,1)S(1)}, bf16[6912,256]{1,0:T(8,128)(2,1)}, u32[]{:S(2)}) copy-start(bf16[6912,256]{1,0:T(8,128)(2,1)} %param.15) | copy-start | bytes 10616836
  127.4 6.3 %copy-start.12 = (f32[1280,256]{1,0:T(8,128)S(1)}, f32[1280,256]{1,0:T(8,128)}, u32[]{:S(2)}) copy-start(f32[1280,256]{1,0:T(8,128)} %get-tuple-element.47) | copy-start | bytes 3932164
  135.8 16.5 %collective-permute-start.10 = (bf16[2,8,80,256]{3,2,1,0:T(8,128)(2,1)S(1)}, bf16[2,8,80,256]{3,2,1,0:T(8,128)(2,1)S(1)}, u32[]{:S(2)}, u32[]{:S(2)}) collective-permute-start(bf16[2,8,80,256]{3,2,1,0:T(8,128)(2,1)S(1)} %get-tuple-element.30), channel_id=1, source_target_pairs={{0,4},{4,8},{8,12},{12,16},{16,20},{20,24},{24,28},{28,32},{32,36}... | collective-permute-start | bytes 1966088 | tf_op jit(solution)/shard_map/ppermute | solution.py:22
  139.3 17.6 %collective-permute-start.6 = (bf16[2,8,80,256]{3,2,1,0:T(8,128)(2,1)S(1)}, bf16[2,8,80,256]{3,2,1,0:T(8,128)(2,1)S(1)}, u32[]{:S(2)}, u32[]{:S(2)}) collective-permute-start(bf16[2,8,80,256]{3,2,1,0:T(8,128)(2,1)S(1)} %get-tuple-element.31), channel_id=1, source_target_pairs={{4,0},{8,4},{12,8},{16,12},{20,16},{24,20},{28,24},{32,28},{36,32}... | collective-permute-start | bytes 1966088 | tf_op jit(solution)/shard_map/ppermute | solution.py:22
  152.3 10.2 %collective-permute-start.11 = (bf16[4,1,80,256]{3,2,1,0:T(8,128)(2,1)S(1)}, bf16[4,1,80,256]{3,2,1,0:T(8,128)(2,1)S(1)}, u32[]{:S(2)}, u32[]{:S(2)}) collective-permute-start(bf16[4,1,80,256]{3,2,1,0:T(8,128)(2,1)S(1)} %get-tuple-element.34), channel_id=1, source_target_pairs={{0,1},{1,2},{2,3},{4,5},{5,6},{6,7},{8,9},{9,10},{10,11},{12,13},{... | collective-permute-start | bytes 491528 | tf_op jit(solution)/shard_map/ppermute | solution.py:32
  155.4 7.1 %collective-permute-start.12 = (bf16[4,1,80,256]{3,2,1,0:T(8,128)(2,1)S(1)}, bf16[4,1,80,256]{3,2,1,0:T(8,128)(2,1)S(1)}, u32[]{:S(2)}, u32[]{:S(2)}) collective-permute-start(bf16[4,1,80,256]{3,2,1,0:T(8,128)(2,1)S(1)} %get-tuple-element.35), channel_id=1, source_target_pairs={{1,0},{2,1},{3,2},{5,4},{6,5},{7,6},{9,8},{10,9},{11,10},{13,12},{... | collective-permute-start | bytes 491528 | tf_op jit(solution)/shard_map/ppermute | solution.py:33
  156.9 48.9 %collective-permute-start.9 = (bf16[16,216,256]{2,1,0:T(8,128)(2,1)S(1)}, bf16[16,216,256]{2,1,0:T(8,128)(2,1)S(1)}, u32[]{:S(2)}, u32[]{:S(2)}) collective-permute-start(bf16[16,216,256]{2,1,0:T(8,128)(2,1)S(1)} %dynamic-slice_bitcast_fusion.1), channel_id=1, source_target_pairs={{0,4},{1,5},{2,6},{3,7},{4,0},{5,1},{6,2},{7,3},{8,12},{9,13},{10,... | collective-permute-start | bytes 5308424 | tf_op jit(solution)/shard_map/ppermute | solution.py:131
  157.0 47.0 %copy-start.1 = (bf16[2,8,80,256]{3,2,1,0:T(8,128)(2,1)}, bf16[2,8,80,256]{3,2,1,0:T(8,128)(2,1)S(1)}, u32[]{:S(2)}) copy-start(bf16[2,8,80,256]{3,2,1,0:T(8,128)(2,1)S(1)} %collective-permute-done.6) | copy-start | bytes 1966084
  157.0 46.9 %collective-permute-start.7 = (bf16[4,1,80,256]{3,2,1,0:T(8,128)(2,1)S(1)}, bf16[4,1,80,256]{3,2,1,0:T(8,128)(2,1)S(1)}, u32[]{:S(2)}, u32[]{:S(2)}) collective-permute-start(bf16[4,1,80,256]{3,2,1,0:T(8,128)(2,1)S(1)} %get-tuple-element.38), channel_id=1, source_target_pairs={{0,1},{1,2},{2,3},{4,5},{5,6},{6,7},{8,9},{9,10},{10,11},{12,13},{... | collective-permute-start | bytes 491528 | tf_op jit(solution)/shard_map/ppermute | solution.py:32
  161.0 42.9 %collective-permute-start.8 = (bf16[4,1,80,256]{3,2,1,0:T(8,128)(2,1)S(1)}, bf16[4,1,80,256]{3,2,1,0:T(8,128)(2,1)S(1)}, u32[]{:S(2)}, u32[]{:S(2)}) collective-permute-start(bf16[4,1,80,256]{3,2,1,0:T(8,128)(2,1)S(1)} %get-tuple-element.39), channel_id=1, source_target_pairs={{1,0},{2,1},{3,2},{5,4},{6,5},{7,6},{9,8},{10,9},{11,10},{13,12},{... | collective-permute-start | bytes 491528 | tf_op jit(solution)/shard_map/ppermute | solution.py:33
  184.9 6.0 %copy-start.10 = (bf16[2,8,80,256]{3,2,1,0:T(8,128)(2,1)S(1)}, bf16[2,8,80,256]{3,2,1,0:T(8,128)(2,1)}, u32[]{:S(2)}) copy-start(bf16[2,8,80,256]{3,2,1,0:T(8,128)(2,1)} %param.11) | copy-start | bytes 1966084
  201.7 4.0 %copy-start.14 = (bf16[6912,256]{1,0:T(8,128)(2,1)}, bf16[6912,256]{1,0:T(8,128)(2,1)S(1)}, u32[]{:S(2)}) copy-start(bf16[6912,256]{1,0:T(8,128)(2,1)S(1)} %fusion.3) | copy-start | bytes 10616836
  203.2 24.5 %collective-permute-start.13 = (bf16[16,216,256]{2,1,0:T(8,128)(2,1)}, bf16[16,216,256]{2,1,0:T(8,128)(2,1)}, u32[]{:S(2)}, u32[]{:S(2)}) collective-permute-start(bf16[16,216,256]{2,1,0:T(8,128)(2,1)} %dynamic-slice_bitcast_fusion), channel_id=1, source_target_pairs={{0,4},{1,5},{2,6},{3,7},{4,0},{5,1},{6,2},{7,3},{8,12},{9,13},{10,... | collective-permute-start | bytes 5308424 | tf_op jit(solution)/shard_map/ppermute | solution.py:131
  207.8 39.2 %all-to-all-start.4 = ((bf16[64,54,256]{2,1,0:T(8,128)(2,1)}), bf16[64,54,256]{2,1,0:T(8,128)(2,1)}, u32[]{:S(2)}, u32[]{:S(2)}) async-start(bf16[64,54,256]{2,1,0:T(8,128)(2,1)} %reshape.187), calls=%async_computation.4 | async-start | bytes 3670016 | tf_op jit(solution)/shard_map/all_to_all | solution.py:133
  220.5 7.1 %copy-start.15 = (bf16[6912,256]{1,0:T(8,128)(2,1)S(1)}, bf16[6912,256]{1,0:T(8,128)(2,1)}, u32[]{:S(2)}) copy-start(bf16[6912,256]{1,0:T(8,128)(2,1)} %copy-done.14) | copy-start | bytes 10616836
  247.0 31.7 %all-to-all-start.5 = ((bf16[64,54,256]{2,1,0:T(8,128)(2,1)}), bf16[64,54,256]{2,1,0:T(8,128)(2,1)}, u32[]{:S(2)}, u32[]{:S(2)}) async-start(bf16[64,54,256]{2,1,0:T(8,128)(2,1)} %reshape.192), calls=%async_computation.5 | async-start | bytes 3670016 | tf_op jit(solution)/shard_map/all_to_all | solution.py:133
  255.3 7.0 %copy-start.16 = (f32[13824]{0:T(1024)S(1)}, f32[13824]{0:T(1024)}, u32[]{:S(2)}) copy-start(f32[13824]{0:T(1024)} %param.16) | copy-start | bytes 165892
  255.3 7.0 %copy-start.17 = (f32[13824]{0:T(1024)S(1)}, f32[13824]{0:T(1024)}, u32[]{:S(2)}) copy-start(f32[13824]{0:T(1024)} %param.17) | copy-start | bytes 165892
  257.4 23.2 %copy-start.18 = (f32[13824]{0:T(1024)S(1)}, f32[13824]{0:T(1024)}, u32[]{:S(2)}) copy-start(f32[13824]{0:T(1024)} %param.18) | copy-start | bytes 165892
  257.4 23.2 %copy-start.19 = (f32[13824]{0:T(1024)S(1)}, f32[13824]{0:T(1024)}, u32[]{:S(2)}) copy-start(f32[13824]{0:T(1024)} %param.19) | copy-start | bytes 165892
  284.1 50.5 %all-to-all-start.6 = ((bf16[64,108,256]{2,1,0:T(8,128)(2,1)}), bf16[64,108,256]{2,1,0:T(8,128)(2,1)}, u32[]{:S(2)}, u32[]{:S(2)}) async-start(bf16[64,108,256]{2,1,0:T(8,128)(2,1)} %broadcast_in_dim.80), calls=%async_computation.6 | async-start | bytes 7340032 | tf_op jit(solution)/shard_map/all_to_all | solution.py:143
  290.2 5.4 %copy-start.2 = (bf16[2,8,80,256]{3,2,1,0:T(8,128)(2,1)S(1)}, bf16[2,8,80,256]{3,2,1,0:T(8,128)(2,1)}, u32[]{:S(2)}) copy-start(bf16[2,8,80,256]{3,2,1,0:T(8,128)(2,1)} %copy-done.1) | copy-start | bytes 1966084
  339.6 8.2 %copy-start.13 = (bf16[27,256,256]{2,1,0:T(8,128)(2,1)S(1)}, bf16[27,256,256]{2,1,0:T(8,128)(2,1)}, u32[]{:S(2)}) copy-start(bf16[27,256,256]{2,1,0:T(8,128)(2,1)} %copy.71) | copy-start | bytes 10616836
  339.6 35.8 %collective-permute-start.14 = (bf16[64,108,256]{2,0,1:T(8,128)(2,1)}, bf16[64,108,256]{2,0,1:T(8,128)(2,1)}, u32[]{:S(2)}, u32[]{:S(2)}) collective-permute-start(bf16[64,108,256]{2,0,1:T(8,128)(2,1)} %copy.76), channel_id=1, source_target_pairs={{0,4},{1,5},{2,6},{3,7},{4,0},{5,1},{6,2},{7,3},{8,12},{9,13},{10,... | collective-permute-start | bytes 10616840 | tf_op jit(solution)/shard_map/ppermute | solution.py:144
  356.3 17.9 %copy-start.11 = (bf16[2,8,80,256]{3,2,1,0:T(8,128)(2,1)S(1)}, bf16[2,8,80,256]{3,2,1,0:T(8,128)(2,1)}, u32[]{:S(2)}) copy-start(bf16[2,8,80,256]{3,2,1,0:T(8,128)(2,1)} %param.11) | copy-start | bytes 1966084
  358.3 15.5 %all-to-all-start.3 = ((f32[128,1,128]{2,1,0:T(1,128)}), f32[128,1,128]{2,1,0:T(1,128)S(1)}, u32[]{:S(2)}, u32[]{:S(2)}) async-start(f32[128,1,128]{2,1,0:T(1,128)} %broadcast_in_dim.77), calls=%async_computation.3 | async-start | bytes 131072 | tf_op jit(solution)/shard_map/all_to_all | solution.py:57

commit v2 on v0

v2 whole, which is shorter than its diff:
```python
import jax
import jax.numpy as jnp
from jax import lax
from jax.experimental import pallas as pl
from jax.experimental.pallas import tpu as pltpu
from jax.sharding import PartitionSpec as P

C = 256
COLS = 80
ROWS = 8
FR = 2
CELLS = FR * ROWS * COLS
EXT = (FR + 2) * (ROWS + 2) * COLS
BAND = ROWS * COLS
norm_eps = 1e-05
F32 = jnp.float32
BF16 = jnp.bfloat16
HERE = float(CELLS * 8)
TOTAL = HERE * 128.0
SCALE = (27.0 * C) ** (-0.5)
SHARE = 108
PIECE = 112
BLOCK = 432
BOTH = ("tm", "rows")
CORE_PAIRS = [(i, i ^ 4) for i in range(128)]
CHIP_GROUPS = [
    [((z * 4 + y) * 2 + core) * 4 + x for z in range(4) for y in range(4) for x in range(4)]
    for core in range(2)
]
learn_rate = 0.25
beta_one = 0.9
beta_two = 0.95
decay_rate = 0.1
adam_eps = 1e-08
first_fix = 1.0 - 0.9**10
second_fix = 1.0 - 0.95**10


def mixed(value, matrix):
    return jnp.dot(value, matrix, precision=lax.Precision.HIGHEST, preferred_element_type=F32)


def iotas(shape):
    return lax.broadcasted_iota(jnp.int32, shape, 0), lax.broadcasted_iota(jnp.int32, shape, 1)


def spread_matrix(offset):
    lane, channel = iotas((128, C))
    return jnp.where(lane == (channel >> 3) + offset, 1.0, 0.0).astype(F32)


def pack_row(first, second):
    channel, lane = iotas((C, 128))
    head = jnp.where((channel >> 3) == lane, 1.0, 0.0).astype(F32)
    tail = jnp.where((channel >> 3) + 32 == lane, 1.0, 0.0).astype(F32)
    wide = jnp.broadcast_to(first, (8, C)), jnp.broadcast_to(second, (8, C))
    row = mixed(wide[0], head) + mixed(wide[1], tail)
    return jnp.broadcast_to(row[0:1], (128, 128))


def read_norm(table):
    total = jnp.sum(table, axis=0, keepdims=True)
    center = total / 128.0
    offset = table - center
    square = jnp.sum(offset * offset, axis=0, keepdims=True)
    low, high = spread_matrix(0), spread_matrix(32)
    wide = lambda v, m: mixed(jnp.broadcast_to(v, (8, 128)), m)[0:1]
    spread = wide(total, high) + HERE * wide(square, low)
    return wide(center, low), lax.rsqrt(spread / TOTAL + norm_eps)


def read_sums(table):
    total = jnp.sum(table, axis=0, keepdims=True) / TOTAL
    wide = lambda m: mixed(jnp.broadcast_to(total, (8, 128)), m)[0:1]
    return wide(spread_matrix(0)), wide(spread_matrix(32))


def folded(values):
    return jnp.sum(values.reshape(-1, 8, C), axis=0)


def chunk(index, size=COLS):
    return pl.ds(pl.multiple_of(index * size, size), size)


def local_moments(read, count):
    zero = jnp.zeros((8, C), F32)
    sums = lax.fori_loop(0, count, lambda i, s: s + folded(read(i)), zero)
    ch_sum = jnp.sum(sums, axis=0, keepdims=True)
    r, c = iotas((C, C))
    same = jnp.where((r >> 3) == (c >> 3), 1.0, 0.0).astype(F32)
    mean = mixed(jnp.broadcast_to(ch_sum, (8, C)), same)[0:1] / HERE

    def squares(i, s):
        off = read(i) - mean
        return s + folded(off * off)

    ch_sq = jnp.sum(lax.fori_loop(0, count, squares, zero), axis=0, keepdims=True)
    return pack_row(mean / 8.0, ch_sq)


def store_shifted(target, rows, value, backward):
    col = lax.broadcasted_iota(jnp.int32, value.shape, 0)
    left = jnp.where(col == 0, 0.0, pltpu.roll(value, 1, 0))
    right = jnp.where(col == COLS - 1, 0.0, pltpu.roll(value, COLS - 1, 0))
    one, three = (right, left) if backward else (left, right)
    target[rows, 0:C] = one.astype(BF16)
    target[rows, C : 2 * C] = value.astype(BF16)
    target[rows, 2 * C : 3 * C] = three.astype(BF16)


def each_row(own, frames, above, below, ok, upcoming, target, make, backward):
    own_at, halo_at = (0, FR) if upcoming else (FR, 0)

    def body(source, at, flag):
        def step(i, _):
            frame, row = at + i // ROWS, i % ROWS
            value = make(source[chunk(i), :].astype(F32))
            if flag is not None:
                value = value * flag
            store_shifted(target, chunk(frame * (ROWS + 2) + row + 1), value, backward)
            return 0

        lax.fori_loop(0, FR * ROWS, step, 0)

    body(own, own_at, None)
    body(frames, halo_at, ok[0])

    def edge(i, _):
        flag = jnp.where((i < FR) == (halo_at == 0), ok[0], 1.0)
        top = make(above[chunk(i), :].astype(F32)) * (flag * ok[1])
        store_shifted(target, chunk(i * (ROWS + 2)), top, backward)
        low = make(below[chunk(i), :].astype(F32)) * (flag * ok[2])
        store_shifted(target, chunk(i * (ROWS + 2) + ROWS + 1), low, backward)
        return 0

    lax.fori_loop(0, FR + 2, edge, 0)


def conv(patches, weight, write, backward):
    for t in range(FR):
        total = None
        for a in range(3):
            for b in range(3):
                f, r = (t + 2 - a, 2 - b) if backward else (t + a, b)
                at = (f * (ROWS + 2) + r) * COLS
                left = patches[at : at + BAND, :]
                tap = (9 * a + 3 * b) * C
                if backward:
                    right = jnp.concatenate([weight[tap + k * C : tap + (k + 1) * C, :] for k in range(3)], axis=1)
                    part = lax.dot_general(left, right, (((1,), (1,)), ((), ())), preferred_element_type=F32)
                else:
                    part = jnp.dot(left, weight[tap : tap + 3 * C, :], preferred_element_type=F32)
                total = part if total is None else total + part
        write(t, total * SCALE)


def wgrad(patches, grad, whole):
    for a in range(3):
        for b in range(3):
            total = None
            for t in range(FR):
                at = ((t + a) * (ROWS + 2) + b) * COLS
                part = lax.dot_general(
                    patches[at : at + BAND, :],
                    grad[t * BAND : (t + 1) * BAND, :],
                    (((0,), (0,)), ((), ())),
                    preferred_element_type=F32,
                )
                total = part if total is None else total + part
            tap = (9 * a + 3 * b) * C
            whole[tap : tap + 3 * C, :] = total * SCALE


def cut_pieces(whole, core, flat, kept, given):
    flat[...] = jnp.zeros_like(flat)

    def block(i, _):
        for side, out in ((core, kept), (1 - core, given)):
            at = pl.multiple_of(i * BLOCK + side * (BLOCK // 2), 8)
            slab = whole[pl.ds(at, BLOCK // 2), :]
            flat[pl.ds(0, BLOCK // 2, 2), :] = slab[:, :128]
            flat[pl.ds(1, BLOCK // 2, 2), :] = slab[:, 128:]
            for x in range(4):
                out[i * 4 + x] = flat[x * SHARE : x * SHARE + PIECE, :].astype(BF16)
        return 0

    lax.fori_loop(0, 16, block, 0)


def silu_parts(value, center, inverse, gain):
    hat = (value - center) * inverse
    pre = hat * gain
    return hat, pre, jax.nn.sigmoid(pre)


def stats_kernel(inputs, row):
    row[...] = local_moments(lambda i: inputs[chunk(i), :].astype(F32), FR * ROWS)


def conv_kernel(ok, inputs, frames, above, below, table, gain, weight, patches, middle, row):
    center, inverse = read_norm(table[...])

    def hidden(value):
        _, pre, gate = silu_parts(value, center, inverse, gain[...])
        return pre * gate

    each_row(inputs, frames, above, below, ok, False, patches, hidden, False)

    def write(t, value):
        middle[t * BAND : (t + 1) * BAND, :] = value.astype(BF16)

    conv(patches, weight, write, False)
    row[...] = local_moments(lambda i: middle[chunk(i), :].astype(F32), FR * ROWS)


def back_two_kernel(ok, cotangent, frames, above, below, weight, back, patches):
    each_row(cotangent, frames, above, below, ok, True, patches, lambda v: v, True)

    def write(t, value):
        back[t * BAND : (t + 1) * BAND, :] = value

    conv(patches, weight, write, True)


def slopes(read, back, center, inverse, gain, slope):
    def step(i, sums):
        hat, pre, gate = silu_parts(read(i), center, inverse, gain)
        here = back[chunk(i), :] * gate * (1.0 + pre * (1.0 - gate)) * gain
        slope[chunk(i), :] = here
        return sums[0] + folded(here), sums[1] + folded(here * hat)

    zero = jnp.zeros((8, C), F32)
    plain, cross = lax.fori_loop(0, FR * ROWS, step, (zero, zero))
    return pack_row(jnp.sum(plain, axis=0, keepdims=True), jnp.sum(cross, axis=0, keepdims=True))


def slope_kernel(middle, table, gain, back, slope, row):
    center, inverse = read_norm(table[...])
    read = lambda i: middle[chunk(i), :].astype(F32)
    row[...] = slopes(read, back, center, inverse, gain[...], slope)


def grad_two_kernel(ok, core, middle, frames, above, below, table, gain, cotangent, kept, given, patches, whole, flat):
    center, inverse = read_norm(table[...])

    def hidden(value):
        _, pre, gate = silu_parts(value, center, inverse, gain[...])
        return pre * gate

    each_row(middle, frames, above, below, ok, False, patches, hidden, False)
    wgrad(patches, cotangent, whole)
    cut_pieces(whole, core[0], flat, kept, given)


def grad_one_kernel(core, slope, middle, table, sums, patches, mid_grad, kept, given, whole, flat):
    center, inverse = read_norm(table[...])
    mean, cross = read_sums(sums[...])

    def step(i, _):
        hat = (middle[chunk(i), :].astype(F32) - center) * inverse
        mid_grad[chunk(i), :] = (inverse * (slope[chunk(i), :] - mean - hat * cross)).astype(BF16)
        return 0

    lax.fori_loop(0, FR * ROWS, step, 0)
    wgrad(patches, mid_grad, whole)
    cut_pieces(whole, core[0], flat, kept, given)


def back_one_kernel(ok, mid_grad, frames, above, below, weight, inputs, table, gain, slope, row, patches, back):
    each_row(mid_grad, frames, above, below, ok, True, patches, lambda v: v, True)

    def write(t, value):
        back[t * BAND : (t + 1) * BAND, :] = value

    conv(patches, weight, write, True)
    center, inverse = read_norm(table[...])
    read = lambda i: inputs[chunk(i), :].astype(F32)
    row[...] = slopes(read, back, center, inverse, gain[...], slope)


def final_kernel(slope, inputs, table, sums, cotangent, result):
    center, inverse = read_norm(table[...])
    mean, cross = read_sums(sums[...])

    def step(i, _):
        hat = (inputs[chunk(i), :].astype(F32) - center) * inverse
        grad = inverse * (slope[chunk(i), :] - mean - hat * cross)
        result[chunk(i), :] = (cotangent[chunk(i), :].astype(F32) + grad).astype(BF16)
        return 0

    lax.fori_loop(0, FR * ROWS, step, 0)


def adam_kernel(arrived, own, first, second, first_new, second_new, spread):
    add = lambda i, s: s + arrived[i].astype(F32)
    gradient = lax.fori_loop(0, 64, add, jnp.zeros((PIECE, 128), F32))[:SHARE]
    one = beta_one * first[...] + (1.0 - beta_one) * gradient
    two = beta_two * second[...] + (1.0 - beta_two) * gradient * gradient
    first_new[...] = one
    second_new[...] = two
    updated = own[...].astype(F32) * (1.0 - learn_rate * decay_rate) - learn_rate * (one / first_fix) / (
        jnp.sqrt(two / second_fix) + adam_eps
    )
    piece = jnp.concatenate([updated, jnp.zeros((PIECE - SHARE, 128), F32)], axis=0).astype(BF16)

    def copy(i, _):
        spread[i] = piece
        return 0

    lax.fori_loop(0, 64, copy, 0)


def assemble_kernel(core, own, other, weight, flat):
    def fill(low, high):
        def block(i, _):
            for s in range(8):
                piece = (low if s < 4 else high)[i * 4 + s % 4]
                flat[s * SHARE : s * SHARE + PIECE, :] = piece.astype(F32)
            rows = pl.ds(pl.multiple_of(i * BLOCK, BLOCK), BLOCK)
            weight[rows, 0:128] = flat[pl.ds(0, BLOCK, 2), :].astype(BF16)
            weight[rows, 128:256] = flat[pl.ds(1, BLOCK, 2), :].astype(BF16)
            return 0

        lax.fori_loop(0, 16, block, 0)

    @pl.when(core[0] == 0)
    def _():
        fill(own, other)

    @pl.when(core[0] != 0)
    def _():
        fill(other, own)


def run(kernel, scalars, arrays, outs, scratch=(), mib=24, flops=0):
    vmem = pl.BlockSpec(memory_space=pltpu.VMEM)
    size = sum(x.size * x.dtype.itemsize for x in (*arrays, *outs))
    return pl.pallas_call(
        kernel,
        out_shape=tuple(outs),
        in_specs=[pl.BlockSpec(memory_space=pltpu.SMEM)] * len(scalars) + [vmem] * len(arrays),
        out_specs=tuple(vmem for _ in outs),
        scratch_shapes=list(scratch),
        compiler_params=pltpu.CompilerParams(vmem_limit_bytes=mib * 1024 * 1024),
        cost_estimate=pl.CostEstimate(flops=flops, bytes_accessed=size, transcendentals=0),
    )(*scalars, *arrays)


def everyone(row):
    return lax.all_to_all(row, BOTH, 0, 0, tiled=True)


def halo(block, upcoming):
    steps, bands = lax.axis_size("tm"), lax.axis_size("rows")
    forward = [(i, i + 1) for i in range(steps - 1)]
    backward = [(j, i) for i, j in forward]
    frames = lax.ppermute(block, "tm", backward if upcoming else forward)
    pair = lambda r: (block[:, r], frames[:, r]) if upcoming else (frames[:, r], block[:, r])
    down = [(i, i + 1) for i in range(bands - 1)]
    up = [(j, i) for i, j in down]
    above = lax.ppermute(jnp.concatenate(pair(ROWS - 1), axis=0), "rows", down)
    below = lax.ppermute(jnp.concatenate(pair(0), axis=0), "rows", up)
    return frames.reshape(CELLS, C), above.reshape(-1, C), below.reshape(-1, C)


def cells(array):
    return array.reshape(FR, ROWS, COLS, C)


def scatter_sum(kept, given):
    taken = lax.ppermute(given, BOTH, CORE_PAIRS)
    pair_sum = (kept.astype(F32) + taken.astype(F32)).astype(BF16)
    return lax.all_to_all(pair_sum, BOTH, 0, 0, axis_index_groups=CHIP_GROUPS, tiled=True)


def own_share(weight):
    place = lax.axis_index(BOTH) * (SHARE // 2)
    return lax.dynamic_slice_in_dim(weight, place, SHARE // 2, axis=0).reshape(SHARE, 128)


def local(
    inputs,
    cotangent,
    gain_one,
    gain_two,
    weight_one,
    weight_two,
    first_one,
    second_one,
    first_two,
    second_two,
):
    shape = jax.ShapeDtypeStruct
    step, band = lax.axis_index("tm"), lax.axis_index("rows")
    core = (step % 2).astype(jnp.int32).reshape(1)
    inside = lambda *tests: jnp.stack([jnp.where(t, 1.0, 0.0).astype(F32) for t in tests])
    above_ok, below_ok = band > 0, band < lax.axis_size("rows") - 1
    ok_before = inside(step > 0, above_ok, below_ok)
    ok_after = inside(step < lax.axis_size("tm") - 1, above_ok, below_ok)
    gain_one, gain_two = gain_one.reshape(1, C), gain_two.reshape(1, C)
    flat_inputs, flat_cot = inputs.reshape(CELLS, C), cotangent.reshape(CELLS, C)

    row_type = shape((128, 128), F32)
    act_type, wide_type = shape((CELLS, C), BF16), shape((CELLS, C), F32)
    patch_type = shape((EXT, 3 * C), BF16)
    piece_type = shape((64, PIECE, 128), BF16)
    moment_type = shape((SHARE, 128), F32)
    patch_scratch = pltpu.VMEM((EXT, 3 * C), BF16)
    whole_scratch = pltpu.VMEM((27 * C, C), F32)
    flat_scratch = pltpu.VMEM((BLOCK + 8, 128), F32)
    work = 2 * CELLS * 27 * C * C

    (row_one,) = run(stats_kernel, (), (flat_inputs,), (row_type,))
    table_one = everyone(row_one)
    halo_in = halo(inputs, False)
    halo_cot = halo(cotangent, True)
    (back_two,) = run(
        back_two_kernel, (ok_after,), (flat_cot, *halo_cot, weight_two), (wide_type,), (patch_scratch,), flops=work
    )
    patch_one, middle, row_two = run(
        conv_kernel,
        (ok_before,),
        (flat_inputs, *halo_in, table_one, gain_one, weight_one),
        (patch_type, act_type, row_type),
        flops=work,
    )
    table_two = everyone(row_two)
    halo_mid = halo(cells(middle), False)
    slope_two, row_three = run(
        slope_kernel, (), (middle, table_two, gain_two, back_two), (wide_type, row_type)
    )
    table_three = everyone(row_three)
    kept_two, given_two = run(
        grad_two_kernel,
        (ok_before, core),
        (middle, *halo_mid, table_two, gain_two, flat_cot),
        (piece_type, piece_type),
        (patch_scratch, whole_scratch, flat_scratch),
        flops=work,
    )
    mid_grad, kept_one, given_one = run(
        grad_one_kernel,
        (core,),
        (slope_two, middle, table_two, table_three, patch_one),
        (act_type, piece_type, piece_type),
        (whole_scratch, flat_scratch),
        flops=work,
    )
    arrived_two = scatter_sum(kept_two, given_two)
    arrived_one = scatter_sum(kept_one, given_one)
    halo_grad = halo(cells(mid_grad), True)
    slope_one, row_four = run(
        back_one_kernel,
        (ok_after,),
        (mid_grad, *halo_grad, weight_one, flat_inputs, table_one, gain_one),
        (wide_type, row_type),
        (patch_scratch, pltpu.VMEM((CELLS, C), F32)),
        flops=work,
    )
    table_four = everyone(row_four)
    (input_grad,) = run(
        final_kernel, (), (slope_one, flat_inputs, table_one, table_four, flat_cot), (act_type,)
    )

    def update(arrived, weight, first, second):
        first_new, second_new, spread = run(
            adam_kernel,
            (),
            (arrived, own_share(weight), first.reshape(SHARE, 128), second.reshape(SHARE, 128)),
            (moment_type, moment_type, piece_type),
        )
        own = lax.all_to_all(spread, BOTH, 0, 0, axis_index_groups=CHIP_GROUPS, tiled=True)
        other = lax.ppermute(own, BOTH, CORE_PAIRS)
        (whole,) = run(
            assemble_kernel,
            (core,),
            (own, other),
            (shape((27 * C, C), BF16),),
            (pltpu.VMEM((2 * BLOCK + 8, 128), F32),),
        )
        return whole, first_new.reshape(-1), second_new.reshape(-1)

    new_weight_two, new_first_two, new_second_two = update(arrived_two, weight_two, first_two, second_two)
    new_weight_one, new_first_one, new_second_one = update(arrived_one, weight_one, first_one, second_one)
    return (
        cells(input_grad),
        new_weight_one,
        new_weight_two,
        new_first_one,
        new_second_one,
        new_first_two,
        new_second_two,
    )


def solution(mesh):
    split, share = P("tm", "rows", None, None), P(("tm", "rows"))
    return jax.shard_map(
        local,
        mesh=mesh,
        in_specs=(split, split, P(), P(), P(), P(), share, share, share, share),
        out_specs=(split, P(), P(), share, share, share, share),
        check_vma=False,
    )
```

time: 947 us -> 333 us (0.35)
  blocking collectives: 394 us -> 15.8 us
  other arithmetic: 159 us -> 7.2 us
  local copies, waits for them, and re-layouts: 111 us -> 29.3 us
  starting transfers between devices: 27.8 us -> 95 us
  waiting for transfers between devices: 185 us -> 124 us
  Pallas kernels: 0 us -> 59.6 us
  matrix products: 49.3 us -> 0 us
  between operations: 15.1 us -> 1.16 us
    psum x6 -> x0, blocking collectives: 394 us -> none  [summed(): return lax.psum(pieces, ('tm', 'rows'))]
    unnamed x4 -> x0, waiting for transfers between devices: 168 us -> none
    all_gather x2 -> x0, other arithmetic: 138 us -> none  [the longest x1 69.1 us: local(): lax.all_gather(part_two, ('tm', 'rows'), axis=0, tiled=True)]
    all_to_all x0 -> x7, waiting for transfers between devices: none -> 93.6 us  [the longest x2 43.4 us: scatter_sum(): lax.all_to_all(pair_sum, BOTH, 0, 0, axis_index_groups=CHIP_GROUPS, tiled...]
    pallas_call x0 -> x12, Pallas kernels: none -> 59.6 us  [run(): pl.pallas_call(kernel, out_shape=tuple(outs), in_specs=[pl.BlockSpec(memo...]
    all_to_all x0 -> x7, starting transfers between devices: none -> 58.6 us  [the longest x3 31.1 us: everyone(): return lax.all_to_all(row, BOTH, 0, 0, tiled=True)]
    unnamed x151 -> x62, local copies, waits for them, and re-layouts: 81 us -> 25.5 us
    dot_general x5 -> x0, matrix products: 49.3 us -> none  [the longest x1 13.9 us: local(): jnp.dot(patch_back, flipped(weight_two, channels), preferred_element_type...]
  transfers between devices with their start and end apart: 15 -> 23, of which waited for: 4 -> 12; matrix products, arithmetic and copies ran while one was open for 19% -> 3% of each run, Pallas kernels for 0% -> 14%
where the time goes in v2:
time: 333 us; the launch traced here: 332 us
  waiting for transfers between devices  124 us (37%)
  starting transfers between devices  95 us (29%)
  Pallas kernels  59.6 us (18%)
  local copies, waits for them, and re-layouts  29.3 us (9%)
  blocking collectives  15.8 us (5%)
  other arithmetic  7.2 us (2%)
    pallas_call x12, Pallas kernels, run(): pl.pallas_call(kernel, out_shape=tuple(outs), in_specs=[pl.BlockSpec(memo...  59.6 us
    all_to_all x2, waiting for transfers between devices, scatter_sum(): lax.all_to_all(pair_sum, BOTH, 0, 0, axis_index_groups=CHIP_GROUPS, tiled...  43.4 us
    all_to_all x2, waiting for transfers between devices, update(): lax.all_to_all(spread, BOTH, 0, 0, axis_index_groups=CHIP_GROUPS, tiled=T...  40.6 us
    all_to_all x3, starting transfers between devices, everyone(): return lax.all_to_all(row, BOTH, 0, 0, tiled=True)  31.1 us
    unnamed x62, local copies, waits for them, and re-layouts  25.5 us
    ppermute x4, waiting for transfers between devices, halo(): frames = lax.ppermute(block, 'tm', backward if upcoming else forward)  20.9 us
    all_to_all x2, starting transfers between devices, scatter_sum(): lax.all_to_all(pair_sum, BOTH, 0, 0, axis_index_groups=CHIP_GROUPS, tiled...  16.1 us
    all_to_all x1, blocking collectives, everyone(): return lax.all_to_all(row, BOTH, 0, 0, tiled=True)  15.8 us
  transfers between devices with their start and end apart: 23, of which 12 were waited for; matrix products, arithmetic and copies ran while one was open for 3% of the time, Pallas kernels for 14%

profile of v2, /device:TPU:1, one launch (start us, length us, event | category | flops | bytes accessed | tf_op | source)
XLA Modules:
  0.0 331.6 jit_solution(2432338950895917648)
XLA Ops:
  0.6 4.6 %collective-permute-start = (bf16[2,8,80,256]{3,2,1,0:T(8,128)(2,1)}, bf16[2,8,80,256]{3,2,1,0:T(8,128)(2,1)S(1)}, u32[]{:S(2)}, u32[]{:S(2)}) collective-permute-start(bf16[2,8,80,256]{3,2,1,0:T(8,128)(2,1)} %param.10), channel_id=1, source_target_pairs={{0,4},{4,8},{8,12},{12,16},{16,20},{20,24},{24,28},{28,32},{32,36}... | collective-permute-start | bytes 1966088 | tf_op jit(solution)/shard_map/ppermute | solution.py:358
  5.3 1.1 copy-done.4
  6.3 1.9 shard_map.153
  8.2 9.8 %all-to-all-start = ((f32[128,1,128]{2,1,0:T(1,128)}), f32[128,1,128]{2,1,0:T(1,128)S(1)}, u32[]{:S(2)}, u32[]{:S(2)}) async-start(f32[128,1,128]{2,1,0:T(1,128)} %bitcast.14), calls=%async_computation | async-start | bytes 131072 | tf_op jit(solution)/shard_map/all_to_all | solution.py:351
  18.0 3.0 collective-permute-start.3
  21.2 0.9 slice_bitcast_fusion.14
  22.1 0.9 slice_bitcast_fusion.12
  23.1 2.6 collective-permute-start.1
  25.8 1.3 collective-permute-start.2
  27.1 3.1 collective-permute-done.3
  30.9 4.2 %collective-permute-start.4 = (bf16[4,80,256]{2,1,0:T(8,128)(2,1)}, bf16[4,80,256]{2,1,0:T(8,128)(2,1)}, u32[]{:S(2)}, u32[]{:S(2)}) collective-permute-start(bf16[4,80,256]{2,1,0:T(8,128)(2,1)} %pad_maximum_fusion.2), channel_id=1, source_target_pairs={{0,1},{1,2},{2,3},{4,5},{5,6},{6,7},{8,9},{9,10},{10,11},{12,13},{... | collective-permute-start | bytes 491528 | tf_op jit(solution)/shard_map/ppermute | solution.py:362
  35.8 1.3 collective-permute-start.5
  38.5 2.0 copy-done.20
  40.5 0.9 copy-done.25
  42.3 9.1 %shard_map.154 = (bf16[3200,768]{1,0:T(8,128)(2,1)S(1)}, bf16[1280,256]{1,0:T(8,128)(2,1)S(1)}, f32[128,128]{1,0:T(8,128)}) custom-call(f32[3]{0:T(128)S(1)} %maximum_maximum_fusion.1.ok, bf16[1280,256]{1,0:T(8,128)(2,1)S(1)} %bitcast.91, bf16[1280,256]{1,0:T(8,128)(2,1)S(1)} %bitcast.115, bf16[320,256]{1,0:T(8,128)(2,1)S(1)} %bitcast.118, ...), custom_call_target="tpu_custom_call" | custom-call | flops 4529848320 | bytes 10880000 | tf_op jit(solution)/shard_map/pallas_call | solution.py:339
  51.5 2.2 copy-done.29
  53.7 11.5 %all-to-all-start.1 = ((f32[128,1,128]{2,1,0:T(1,128)}), f32[128,1,128]{2,1,0:T(1,128)S(1)}, u32[]{:S(2)}, u32[]{:S(2)}) async-start(f32[128,1,128]{2,1,0:T(1,128)} %bitcast.18), calls=%async_computation.1 | async-start | bytes 131072 | tf_op jit(solution)/shard_map/all_to_all | solution.py:351
  65.2 1.1 copy-done.17
  66.3 2.0 copy-done.19
  68.3 6.8 %shard_map.155.back = f32[1280,256]{1,0:T(8,128)S(1)} custom-call(f32[3]{0:T(128)S(1)} %maximum_maximum_fusion.ok, bf16[1280,256]{1,0:T(8,128)(2,1)S(1)} %bitcast.96, bf16[1280,256]{1,0:T(8,128)(2,1)S(1)} %bitcast.114, bf16[320,256]{1,0:T(8,128)(2,1)} %bitcast.25.above, bf16[320,256]{1,0:T(8,128)(2,1)} %bitcast.28.below, bf16[6912,256]{1,0:T(8,128)(2,1)S(1)} %copy-done.19), custom_call_target="tpu_custom_call" | custom-call | flops 4529848320 | bytes 6488064 | tf_op jit(solution)/shard_map/pallas_call | solution.py:339
  75.2 2.1 shard_map.156
  77.3 1.1 copy-done.22
  78.4 9.8 %all-to-all-start.2 = ((f32[128,1,128]{2,1,0:T(1,128)}), f32[128,1,128]{2,1,0:T(1,128)S(1)}, u32[]{:S(2)}, u32[]{:S(2)}) async-start(f32[128,1,128]{2,1,0:T(1,128)} %bitcast.30), calls=%async_computation.2 | async-start | bytes 131072 | tf_op jit(solution)/shard_map/all_to_all | solution.py:351
  88.1 9.6 %all-to-all-done.2 = f32[128,1,128]{2,1,0:T(1,128)S(1)} async-done(((f32[128,1,128]{2,1,0:T(1,128)}), f32[128,1,128]{2,1,0:T(1,128)S(1)}, u32[]{:S(2)}, u32[]{:S(2)}) %all-to-all-start.2) | async-done | bytes 65568 | tf_op jit(solution)/shard_map/all_to_all | solution.py:351
  97.7 1.3 copy-done.23
  99.1 2.4 copy-done.30
  101.5 7.5 %shard_map.157 = (bf16[1280,256]{1,0:T(8,128)(2,1)S(1)}, bf16[64,112,128]{2,1,0:T(8,128)(2,1)S(1)}, bf16[64,112,128]{2,1,0:T(8,128)(2,1)S(1)}) custom-call(s32[1]{0:T(128)} %bitcast.3.core, f32[1280,256]{1,0:T(8,128)S(1)} %copy-done.23, bf16[1280,256]{1,0:T(8,128)(2,1)S(1)} %get-tuple-element.25.middle, f32[128,128]{1,0:T(8,128)S(1)} %bitcast.102, ...), custom_call_target="tpu_custom_call" | custom-call | flops 4529848320 | bytes 11337728 | tf_op jit(solution)/shard_map/pallas_call | solution.py:339
  109.8 2.3 collective-permute-start.11
  112.1 7.5 %collective-permute-done.11 = bf16[2,8,80,256]{3,2,0,1:T(8,128)(2,1)S(1)} collective-permute-done((bf16[2,8,80,256]{3,2,0,1:T(8,128)(2,1)S(1)}, bf16[2,8,80,256]{3,2,0,1:T(8,128)(2,1)S(1)}, u32[]{:S(2)}, u32[]{:S(2)}) %collective-permute-start.11) | collective-permute-done | bytes 655392 | tf_op jit(solution)/shard_map/ppermute | solution.py:358
  119.7 2.2 collective-permute-start.12
  121.9 1.5 collective-permute-start.13
  124.1 3.9 %collective-permute-done.13 = bf16[4,80,256]{2,1,0:T(8,128)(2,1)S(1)} collective-permute-done((bf16[4,80,256]{2,1,0:T(8,128)(2,1)S(1)}, bf16[4,80,256]{2,1,0:T(8,128)(2,1)S(1)}, u32[]{:S(2)}, u32[]{:S(2)}) %collective-permute-start.13) | collective-permute-done | bytes 163872 | tf_op jit(solution)/shard_map/ppermute | solution.py:363
  128.0 10.5 %shard_map.162 = (bf16[64,112,128]{2,1,0:T(8,128)(2,1)S(1)}, bf16[64,112,128]{2,1,0:T(8,128)(2,1)}) custom-call(f32[3]{0:T(128)S(1)} %maximum_maximum_fusion.1.ok, s32[1]{0:T(128)} %bitcast.3.core, bf16[1280,256]{1,0:T(8,128)(2,1)S(1)} %get-tuple-element.25.middle, bf16[1280,256]{1,0:T(8,128)(2,1)S(1)} %bitcast.99, bf16[320,256]{1,0:T(8,128)(2,1)S(1)} %bitcast.120, ...), custom_call_target="tpu_custom_call" | custom-call | flops 4529848320 | bytes 6030336 | tf_op jit(solution)/shard_map/pallas_call | solution.py:339
  138.4 1.2 copy-done.8
  139.7 1.8 add_convert_fusion.1
  141.5 10.3 %all-to-all-start.4 = ((bf16[64,112,128]{2,1,0:T(8,128)(2,1)}), bf16[64,112,128]{2,1,0:T(8,128)(2,1)S(1)}, u32[]{:S(2)}, u32[]{:S(2)}) async-start(bf16[64,112,128]{2,1,0:T(8,128)(2,1)} %add_convert_fusion.1), calls=%async_computation.4 | async-start | bytes 3670016 | tf_op jit(solution)/shard_map/all_to_all | solution.py:374
  151.8 3.8 %add_convert_fusion = bf16[64,112,128]{2,1,0:T(8,128)(2,1)} fusion(bf16[64,112,128]{2,1,0:T(8,128)(2,1)} %collective-permute-done.14, bf16[64,112,128]{2,1,0:T(8,128)(2,1)} %copy-done.8), kind=kLoop, calls=%fused_computation | loop fusion | flops 3670016 | bytes 5505024 | tf_op jit(solution)/shard_map/convert_element_type | solution.py:373
  155.6 23.0 %all-to-all-done.4.arrived = bf16[64,112,128]{2,1,0:T(8,128)(2,1)S(1)} async-done(((bf16[64,112,128]{2,1,0:T(8,128)(2,1)}), bf16[64,112,128]{2,1,0:T(8,128)(2,1)S(1)}, u32[]{:S(2)}, u32[]{:S(2)}) %all-to-all-start.4) | async-done | bytes 1835040 | tf_op jit(solution)/shard_map/all_to_all | solution.py:374
  178.6 1.2 copy-done.2
  179.8 5.8 %all-to-all-start.6 = ((bf16[64,112,128]{2,1,0:T(8,128)(2,1)}), bf16[64,112,128]{2,1,0:T(8,128)(2,1)S(1)}, u32[]{:S(2)}, u32[]{:S(2)}) async-start(bf16[64,112,128]{2,1,0:T(8,128)(2,1)} %add_convert_fusion), calls=%async_computation.6 | async-start | bytes 3670016 | tf_op jit(solution)/shard_map/all_to_all | solution.py:374
  186.4 1.5 copy-done.3
  187.9 1.7 shard_map.160
  189.6 1.2 copy-done.6
  190.8 20.4 %all-to-all-done.6.arrived = bf16[64,112,128]{2,1,0:T(8,128)(2,1)S(1)} async-done(((bf16[64,112,128]{2,1,0:T(8,128)(2,1)}), bf16[64,112,128]{2,1,0:T(8,128)(2,1)S(1)}, u32[]{:S(2)}, u32[]{:S(2)}) %all-to-all-start.6) | async-done | bytes 1835040 | tf_op jit(solution)/shard_map/all_to_all | solution.py:374
  211.2 1.2 copy-done
  212.4 6.0 %all-to-all-start.5 = ((bf16[64,112,128]{2,1,0:T(8,128)(2,1)}), bf16[64,112,128]{2,1,0:T(8,128)(2,1)S(1)}, u32[]{:S(2)}, u32[]{:S(2)}) async-start(bf16[64,112,128]{2,1,0:T(8,128)(2,1)} %copy-done.6), calls=%async_computation.5 | async-start | bytes 3670016 | tf_op jit(solution)/shard_map/all_to_all | solution.py:473
  219.3 1.5 copy-done.1
  220.8 1.7 shard_map.163
  222.5 1.2 copy-done.7
  223.7 19.7 %all-to-all-done.5.own = bf16[64,112,128]{2,1,0:T(8,128)(2,1)S(1)} async-done(((bf16[64,112,128]{2,1,0:T(8,128)(2,1)}), bf16[64,112,128]{2,1,0:T(8,128)(2,1)S(1)}, u32[]{:S(2)}, u32[]{:S(2)}) %all-to-all-start.5) | async-done | bytes 1835040 | tf_op jit(solution)/shard_map/all_to_all | solution.py:473
  243.4 5.5 %all-to-all-start.7 = ((bf16[64,112,128]{2,1,0:T(8,128)(2,1)}), bf16[64,112,128]{2,1,0:T(8,128)(2,1)}, u32[]{:S(2)}, u32[]{:S(2)}) async-start(bf16[64,112,128]{2,1,0:T(8,128)(2,1)} %copy-done.7), calls=%async_computation.7 | async-start | bytes 3670016 | tf_op jit(solution)/shard_map/all_to_all | solution.py:473
  248.9 3.2 collective-permute-start.10
  252.2 20.8 %all-to-all-done.7.own = bf16[64,112,128]{2,1,0:T(8,128)(2,1)} async-done(((bf16[64,112,128]{2,1,0:T(8,128)(2,1)}), bf16[64,112,128]{2,1,0:T(8,128)(2,1)}, u32[]{:S(2)}, u32[]{:S(2)}) %all-to-all-start.7) | async-done | bytes 1835040 | tf_op jit(solution)/shard_map/all_to_all | solution.py:473
  273.0 3.9 %collective-permute-start.15 = (bf16[64,112,128]{2,1,0:T(8,128)(2,1)}, bf16[64,112,128]{2,1,0:T(8,128)(2,1)S(1)}, u32[]{:S(2)}, u32[]{:S(2)}) collective-permute-start(bf16[64,112,128]{2,1,0:T(8,128)(2,1)} %all-to-all-done.7.own), channel_id=1, source_target_pairs={{0,4},{1,5},{2,6},{3,7},{4,0},{5,1},{6,2},{7,3},{8,12},{9,13},{10,... | collective-permute-start | bytes 5505032 | tf_op jit(solution)/shard_map/ppermute | solution.py:474
  277.0 2.2 collective-permute-start.6
  279.2 10.2 %collective-permute-done.6 = bf16[2,8,80,256]{3,2,0,1:T(8,128)(2,1)S(1)} collective-permute-done((bf16[2,8,80,256]{3,2,0,1:T(8,128)(2,1)S(1)}, bf16[2,8,80,256]{3,2,0,1:T(8,128)(2,1)S(1)}, u32[]{:S(2)}, u32[]{:S(2)}) %collective-permute-start.6) | collective-permute-done | bytes 655392 | tf_op jit(solution)/shard_map/ppermute | solution.py:358
  289.5 2.0 collective-permute-start.7
  291.5 1.3 collective-permute-start.8
  293.7 3.9 %collective-permute-done.8 = bf16[4,80,256]{2,1,0:T(8,128)(2,1)S(1)} collective-permute-done((bf16[4,80,256]{2,1,0:T(8,128)(2,1)S(1)}, bf16[4,80,256]{2,1,0:T(8,128)(2,1)S(1)}, u32[]{:S(2)}, u32[]{:S(2)}) %collective-permute-start.8) | collective-permute-done | bytes 163872 | tf_op jit(solution)/shard_map/ppermute | solution.py:363
  297.5 7.7 %shard_map.158 = (f32[1280,256]{1,0:T(8,128)S(1)}, f32[128,128]{1,0:T(8,128)S(1)}) custom-call(f32[3]{0:T(128)S(1)} %maximum_maximum_fusion.ok, bf16[1280,256]{1,0:T(8,128)(2,1)S(1)} %get-tuple-element.30.mid_grad, bf16[1280,256]{1,0:T(8,128)(2,1)S(1)} %bitcast.100, bf16[320,256]{1,0:T(8,128)(2,1)S(1)} %bitcast.121, bf16[320,256]{1,0:T(8,128)(2,1)S(1)} %bitcast.123, ...), custom_call_target="tpu_custom_call" | custom-call | flops 4529848320 | bytes 7275520 | tf_op jit(solution)/shard_map/pallas_call | solution.py:339
  305.2 15.8 %all_to_all.64 = f32[128,1,128]{2,1,0:T(1,128)S(1)} all-to-all(f32[128,1,128]{2,1,0:T(1,128)S(1)} %bitcast.109), channel_id=1, replica_groups=mesh['tm'=32,'rows'=4] {'tm','rows'}, dimensions={0} | all-to-all | bytes 131072 | tf_op jit(solution)/shard_map/all_to_all | solution.py:351
  321.0 1.8 shard_map.159
  322.8 4.4 %shard_map.161 = bf16[6912,256]{1,0:T(8,128)(2,1)} custom-call(s32[1]{0:T(128)} %bitcast.3.core, bf16[64,112,128]{2,1,0:T(8,128)(2,1)S(1)} %all-to-all-done.5.own, bf16[64,112,128]{2,1,0:T(8,128)(2,1)} %collective-permute-done.10.other), custom_call_target="tpu_custom_call" | custom-call | bytes 7208960 | tf_op jit(solution)/shard_map/pallas_call | solution.py:339
  327.2 4.4 %shard_map.164 = bf16[6912,256]{1,0:T(8,128)(2,1)} custom-call(s32[1]{0:T(128)} %bitcast.3.core, bf16[64,112,128]{2,1,0:T(8,128)(2,1)} %all-to-all-done.7.own, bf16[64,112,128]{2,1,0:T(8,128)(2,1)S(1)} %collective-permute-done.15.other), custom_call_target="tpu_custom_call" | custom-call | bytes 7208960 | tf_op jit(solution)/shard_map/pallas_call | solution.py:339
  (85 shorter events, 8.1 us)
Async XLA Ops:
  0.6 37.8 %copy-start.28 = (f32[256]{0:T(256)S(1)}, f32[256]{0:T(256)}, u32[]{:S(2)}) copy-start(f32[256]{0:T(256)} %param.12) | copy-start | bytes 3076
  0.6 22.4 %collective-permute-start = (bf16[2,8,80,256]{3,2,1,0:T(8,128)(2,1)}, bf16[2,8,80,256]{3,2,1,0:T(8,128)(2,1)S(1)}, u32[]{:S(2)}, u32[]{:S(2)}) collective-permute-start(bf16[2,8,80,256]{3,2,1,0:T(8,128)(2,1)} %param.10), channel_id=1, source_target_pairs={{0,4},{4,8},{8,12},{12,16},{16,20},{20,24},{24,28},{28,32},{32,36}... | collective-permute-start | bytes 1966088 | tf_op jit(solution)/shard_map/ppermute | solution.py:358
  5.2 1.1 copy-start.4
  6.3 32.1 %copy-start.5 = (bf16[2,8,80,256]{3,2,1,0:T(8,128)(2,1)S(1)}, bf16[2,8,80,256]{3,2,1,0:T(8,128)(2,1)}, u32[]{:S(2)}) copy-start(bf16[2,8,80,256]{3,2,1,0:T(8,128)(2,1)} %param.10) | copy-start | bytes 1966084
  8.2 28.9 %all-to-all-start = ((f32[128,1,128]{2,1,0:T(1,128)}), f32[128,1,128]{2,1,0:T(1,128)S(1)}, u32[]{:S(2)}, u32[]{:S(2)}) async-start(f32[128,1,128]{2,1,0:T(1,128)} %bitcast.14), calls=%async_computation | async-start | bytes 131072 | tf_op jit(solution)/shard_map/all_to_all | solution.py:351
  18.0 12.2 %collective-permute-start.3 = (bf16[2,8,80,256]{3,2,1,0:T(8,128)(2,1)}, bf16[2,8,80,256]{3,2,1,0:T(8,128)(2,1)S(1)}, u32[]{:S(2)}, u32[]{:S(2)}) collective-permute-start(bf16[2,8,80,256]{3,2,1,0:T(8,128)(2,1)} %param.11), channel_id=1, source_target_pairs={{4,0},{8,4},{12,8},{16,12},{20,16},{24,20},{28,24},{32,28},{36,32}... | collective-permute-start | bytes 1966088 | tf_op jit(solution)/shard_map/ppermute | solution.py:358
  23.1 14.0 %collective-permute-start.1 = (bf16[4,80,256]{2,1,0:T(8,128)(2,1)S(1)}, bf16[4,80,256]{2,1,0:T(8,128)(2,1)S(1)}, u32[]{:S(2)}, u32[]{:S(2)}) collective-permute-start(bf16[4,80,256]{2,1,0:T(8,128)(2,1)S(1)} %pad_maximum_fusion), channel_id=1, source_target_pairs={{0,1},{1,2},{2,3},{4,5},{5,6},{6,7},{8,9},{9,10},{10,11},{12,13},{... | collective-permute-start | bytes 491528 | tf_op jit(solution)/shard_map/ppermute | solution.py:362
  25.8 12.0 %collective-permute-start.2 = (bf16[4,80,256]{2,1,0:T(8,128)(2,1)S(1)}, bf16[4,80,256]{2,1,0:T(8,128)(2,1)S(1)}, u32[]{:S(2)}, u32[]{:S(2)}) collective-permute-start(bf16[4,80,256]{2,1,0:T(8,128)(2,1)S(1)} %pad_maximum_fusion.1), channel_id=1, source_target_pairs={{1,0},{2,1},{3,2},{5,4},{6,5},{7,6},{9,8},{10,9},{11,10},{13,12},{... | collective-permute-start | bytes 491528 | tf_op jit(solution)/shard_map/ppermute | solution.py:363
  30.2 21.3 %copy-start.16 = (bf16[2,8,80,256]{3,2,1,0:T(8,128)(2,1)}, bf16[2,8,80,256]{3,2,1,0:T(8,128)(2,1)S(1)}, u32[]{:S(2)}) copy-start(bf16[2,8,80,256]{3,2,1,0:T(8,128)(2,1)S(1)} %collective-permute-done.3) | copy-start | bytes 1966084
  30.9 34.3 %collective-permute-start.4 = (bf16[4,80,256]{2,1,0:T(8,128)(2,1)}, bf16[4,80,256]{2,1,0:T(8,128)(2,1)}, u32[]{:S(2)}, u32[]{:S(2)}) collective-permute-start(bf16[4,80,256]{2,1,0:T(8,128)(2,1)} %pad_maximum_fusion.2), channel_id=1, source_target_pairs={{0,1},{1,2},{2,3},{4,5},{5,6},{6,7},{8,9},{9,10},{10,11},{12,13},{... | collective-permute-start | bytes 491528 | tf_op jit(solution)/shard_map/ppermute | solution.py:362
  35.8 29.4 %collective-permute-start.5 = (bf16[4,80,256]{2,1,0:T(8,128)(2,1)}, bf16[4,80,256]{2,1,0:T(8,128)(2,1)}, u32[]{:S(2)}, u32[]{:S(2)}) collective-permute-start(bf16[4,80,256]{2,1,0:T(8,128)(2,1)} %pad_maximum_fusion.3), channel_id=1, source_target_pairs={{1,0},{2,1},{3,2},{5,4},{6,5},{7,6},{9,8},{10,9},{11,10},{13,12},{... | collective-permute-start | bytes 491528 | tf_op jit(solution)/shard_map/ppermute | solution.py:363
  37.1 0.7 copy-start.24
  37.8 0.7 copy-start.26
  38.5 2.0 copy-start.20
  40.5 0.9 copy-start.25
  41.4 0.9 copy-start.27
  42.3 22.9 %copy-start.9 = (bf16[2,8,80,256]{3,2,1,0:T(8,128)(2,1)S(1)}, bf16[2,8,80,256]{3,2,1,0:T(8,128)(2,1)}, u32[]{:S(2)}) copy-start(bf16[2,8,80,256]{3,2,1,0:T(8,128)(2,1)} %param.11) | copy-start | bytes 1966084
  51.4 2.2 copy-start.29
  53.7 21.5 %all-to-all-start.1 = ((f32[128,1,128]{2,1,0:T(1,128)}), f32[128,1,128]{2,1,0:T(1,128)S(1)}, u32[]{:S(2)}, u32[]{:S(2)}) async-start(f32[128,1,128]{2,1,0:T(1,128)} %bitcast.18), calls=%async_computation.1 | async-start | bytes 131072 | tf_op jit(solution)/shard_map/all_to_all | solution.py:351
  65.2 1.1 copy-start.17
  66.3 2.0 copy-start.19
  68.3 6.9 %copy-start.18 = (f32[256]{0:T(256)S(1)}, f32[256]{0:T(256)}, u32[]{:S(2)}) copy-start(f32[256]{0:T(256)} %param.13) | copy-start | bytes 3076
  77.3 1.1 copy-start.22
  78.4 19.4 %all-to-all-start.2 = ((f32[128,1,128]{2,1,0:T(1,128)}), f32[128,1,128]{2,1,0:T(1,128)S(1)}, u32[]{:S(2)}, u32[]{:S(2)}) async-start(f32[128,1,128]{2,1,0:T(1,128)} %bitcast.30), calls=%async_computation.2 | async-start | bytes 131072 | tf_op jit(solution)/shard_map/all_to_all | solution.py:351
  97.7 1.3 copy-start.23
  99.1 2.4 copy-start.30
  109.0 30.7 %collective-permute-start.9 = (bf16[64,112,128]{2,1,0:T(8,128)(2,1)S(1)}, bf16[64,112,128]{2,1,0:T(8,128)(2,1)S(1)}, u32[]{:S(2)}, u32[]{:S(2)}) collective-permute-start(bf16[64,112,128]{2,1,0:T(8,128)(2,1)S(1)} %get-tuple-element.34), channel_id=1, source_target_pairs={{0,4},{1,5},{2,6},{3,7},{4,0},{5,1},{6,2},{7,3},{8,12},{9,13},{10,... | collective-permute-start | bytes 5505032 | tf_op jit(solution)/shard_map/ppermute | solution.py:372
  109.8 18.2 %copy-start.10 = (bf16[2,8,80,256]{3,2,1,0:T(8,128)(2,1)S(1)}, bf16[2,8,80,256]{3,2,1,0:T(8,128)(2,1)}, u32[]{:S(2)}) copy-start(bf16[2,8,80,256]{3,2,1,0:T(8,128)(2,1)} %param.11) | copy-start | bytes 1966084
  109.8 9.8 %collective-permute-start.11 = (bf16[2,8,80,256]{3,2,0,1:T(8,128)(2,1)S(1)}, bf16[2,8,80,256]{3,2,0,1:T(8,128)(2,1)S(1)}, u32[]{:S(2)}, u32[]{:S(2)}) collective-permute-start(bf16[2,8,80,256]{3,2,0,1:T(8,128)(2,1)S(1)} %copy.41), channel_id=1, source_target_pairs={{0,4},{4,8},{8,12},{12,16},{16,20},{20,24},{24,28},{28,32},{32,36}... | collective-permute-start | bytes 1966088 | tf_op jit(solution)/shard_map/ppermute | solution.py:358
  119.7 4.5 %collective-permute-start.12 = (bf16[4,80,256]{2,1,0:T(8,128)(2,1)S(1)}, bf16[4,80,256]{2,1,0:T(8,128)(2,1)S(1)}, u32[]{:S(2)}, u32[]{:S(2)}) collective-permute-start(bf16[4,80,256]{2,1,0:T(8,128)(2,1)S(1)} %pad_maximum_fusion.6), channel_id=1, source_target_pairs={{0,1},{1,2},{2,3},{4,5},{5,6},{6,7},{8,9},{9,10},{10,11},{12,13},{... | collective-permute-start | bytes 491528 | tf_op jit(solution)/shard_map/ppermute | solution.py:362
  121.9 6.1 %collective-permute-start.13 = (bf16[4,80,256]{2,1,0:T(8,128)(2,1)S(1)}, bf16[4,80,256]{2,1,0:T(8,128)(2,1)S(1)}, u32[]{:S(2)}, u32[]{:S(2)}) collective-permute-start(bf16[4,80,256]{2,1,0:T(8,128)(2,1)S(1)} %pad_maximum_fusion.7), channel_id=1, source_target_pairs={{1,0},{2,1},{3,2},{5,4},{6,5},{7,6},{9,8},{10,9},{11,10},{13,12},{... | collective-permute-start | bytes 491528 | tf_op jit(solution)/shard_map/ppermute | solution.py:363
  138.4 1.2 copy-start.8
  139.7 12.1 %collective-permute-start.14 = (bf16[64,112,128]{2,1,0:T(8,128)(2,1)}, bf16[64,112,128]{2,1,0:T(8,128)(2,1)}, u32[]{:S(2)}, u32[]{:S(2)}) collective-permute-start(bf16[64,112,128]{2,1,0:T(8,128)(2,1)} %get-tuple-element.37), channel_id=1, source_target_pairs={{0,4},{1,5},{2,6},{3,7},{4,0},{5,1},{6,2},{7,3},{8,12},{9,13},{10,... | collective-permute-start | bytes 5505032 | tf_op jit(solution)/shard_map/ppermute | solution.py:372
  141.5 37.1 %all-to-all-start.4 = ((bf16[64,112,128]{2,1,0:T(8,128)(2,1)}), bf16[64,112,128]{2,1,0:T(8,128)(2,1)S(1)}, u32[]{:S(2)}, u32[]{:S(2)}) async-start(bf16[64,112,128]{2,1,0:T(8,128)(2,1)} %add_convert_fusion.1), calls=%async_computation.4 | async-start | bytes 3670016 | tf_op jit(solution)/shard_map/all_to_all | solution.py:374
  155.6 30.8 %copy-start.12 = (f32[13824]{0:T(1024)S(1)}, f32[13824]{0:T(1024)}, u32[]{:S(2)}) copy-start(f32[13824]{0:T(1024)} %param.16) | copy-start | bytes 165892
  155.6 30.8 %copy-start.13 = (f32[13824]{0:T(1024)S(1)}, f32[13824]{0:T(1024)}, u32[]{:S(2)}) copy-start(f32[13824]{0:T(1024)} %param.17) | copy-start | bytes 165892
  178.6 1.2 copy-start.2
  179.8 31.4 %all-to-all-start.6 = ((bf16[64,112,128]{2,1,0:T(8,128)(2,1)}), bf16[64,112,128]{2,1,0:T(8,128)(2,1)S(1)}, u32[]{:S(2)}, u32[]{:S(2)}) async-start(bf16[64,112,128]{2,1,0:T(8,128)(2,1)} %add_convert_fusion), calls=%async_computation.6 | async-start | bytes 3670016 | tf_op jit(solution)/shard_map/all_to_all | solution.py:374
  186.4 1.5 copy-start.3
  189.6 1.2 copy-start.6
  211.2 1.2 copy-start
  212.4 6.8 %copy-start.14 = (f32[13824]{0:T(1024)S(1)}, f32[13824]{0:T(1024)}, u32[]{:S(2)}) copy-start(f32[13824]{0:T(1024)} %param.18) | copy-start | bytes 165892
  212.4 6.8 %copy-start.15 = (f32[13824]{0:T(1024)S(1)}, f32[13824]{0:T(1024)}, u32[]{:S(2)}) copy-start(f32[13824]{0:T(1024)} %param.19) | copy-start | bytes 165892
  212.4 31.0 %all-to-all-start.5 = ((bf16[64,112,128]{2,1,0:T(8,128)(2,1)}), bf16[64,112,128]{2,1,0:T(8,128)(2,1)S(1)}, u32[]{:S(2)}, u32[]{:S(2)}) async-start(bf16[64,112,128]{2,1,0:T(8,128)(2,1)} %copy-done.6), calls=%async_computation.5 | async-start | bytes 3670016 | tf_op jit(solution)/shard_map/all_to_all | solution.py:473
  219.2 1.5 copy-start.1
  222.4 1.2 copy-start.7
  243.4 29.6 %all-to-all-start.7 = ((bf16[64,112,128]{2,1,0:T(8,128)(2,1)}), bf16[64,112,128]{2,1,0:T(8,128)(2,1)}, u32[]{:S(2)}, u32[]{:S(2)}) async-start(bf16[64,112,128]{2,1,0:T(8,128)(2,1)} %copy-done.7), calls=%async_computation.7 | async-start | bytes 3670016 | tf_op jit(solution)/shard_map/all_to_all | solution.py:473
  248.9 73.9 %collective-permute-start.10 = (bf16[64,112,128]{2,1,0:T(8,128)(2,1)S(1)}, bf16[64,112,128]{2,1,0:T(8,128)(2,1)}, u32[]{:S(2)}, u32[]{:S(2)}) collective-permute-start(bf16[64,112,128]{2,1,0:T(8,128)(2,1)S(1)} %all-to-all-done.5.own), channel_id=1, source_target_pairs={{0,4},{1,5},{2,6},{3,7},{4,0},{5,1},{6,2},{7,3},{8,12},{9,13},{10,... | collective-permute-start | bytes 5505032 | tf_op jit(solution)/shard_map/ppermute | solution.py:474
  273.0 54.2 %collective-permute-start.15 = (bf16[64,112,128]{2,1,0:T(8,128)(2,1)}, bf16[64,112,128]{2,1,0:T(8,128)(2,1)S(1)}, u32[]{:S(2)}, u32[]{:S(2)}) collective-permute-start(bf16[64,112,128]{2,1,0:T(8,128)(2,1)} %all-to-all-done.7.own), channel_id=1, source_target_pairs={{0,4},{1,5},{2,6},{3,7},{4,0},{5,1},{6,2},{7,3},{8,12},{9,13},{10,... | collective-permute-start | bytes 5505032 | tf_op jit(solution)/shard_map/ppermute | solution.py:474
  276.9 20.6 %copy-start.21 = (bf16[6912,256]{1,0:T(8,128)(2,1)S(1)}, bf16[6912,256]{1,0:T(8,128)(2,1)}, u32[]{:S(2)}) copy-start(bf16[6912,256]{1,0:T(8,128)(2,1)} %weight.5) | copy-start | bytes 10616836
  277.0 12.5 %collective-permute-start.6 = (bf16[2,8,80,256]{3,2,0,1:T(8,128)(2,1)S(1)}, bf16[2,8,80,256]{3,2,0,1:T(8,128)(2,1)S(1)}, u32[]{:S(2)}, u32[]{:S(2)}) collective-permute-start(bf16[2,8,80,256]{3,2,0,1:T(8,128)(2,1)S(1)} %copy.36), channel_id=1, source_target_pairs={{4,0},{8,4},{12,8},{16,12},{20,16},{24,20},{28,24},{32,28},{36,32}... | collective-permute-start | bytes 1966088 | tf_op jit(solution)/shard_map/ppermute | solution.py:358
  289.5 4.2 %collective-permute-start.7 = (bf16[4,80,256]{2,1,0:T(8,128)(2,1)S(1)}, bf16[4,80,256]{2,1,0:T(8,128)(2,1)S(1)}, u32[]{:S(2)}, u32[]{:S(2)}) collective-permute-start(bf16[4,80,256]{2,1,0:T(8,128)(2,1)S(1)} %pad_maximum_fusion.4), channel_id=1, source_target_pairs={{0,1},{1,2},{2,3},{4,5},{5,6},{6,7},{8,9},{9,10},{10,11},{12,13},{... | collective-permute-start | bytes 491528 | tf_op jit(solution)/shard_map/ppermute | solution.py:362
  291.5 6.1 %collective-permute-start.8 = (bf16[4,80,256]{2,1,0:T(8,128)(2,1)S(1)}, bf16[4,80,256]{2,1,0:T(8,128)(2,1)S(1)}, u32[]{:S(2)}, u32[]{:S(2)}) collective-permute-start(bf16[4,80,256]{2,1,0:T(8,128)(2,1)S(1)} %pad_maximum_fusion.5), channel_id=1, source_target_pairs={{1,0},{2,1},{3,2},{5,4},{6,5},{7,6},{9,8},{10,9},{11,10},{13,12},{... | collective-permute-start | bytes 491528 | tf_op jit(solution)/shard_map/ppermute | solution.py:363
  297.5 23.5 %copy-start.11 = (bf16[2,8,80,256]{3,2,1,0:T(8,128)(2,1)S(1)}, bf16[2,8,80,256]{3,2,1,0:T(8,128)(2,1)}, u32[]{:S(2)}) copy-start(bf16[2,8,80,256]{3,2,1,0:T(8,128)(2,1)} %param.11) | copy-start | bytes 1966084

commit v3 on v2

v3 whole, which is shorter than its diff:
```python
import jax
import jax.numpy as jnp
from jax import lax
from jax.experimental import pallas as pl
from jax.experimental.pallas import tpu as pltpu
from jax.sharding import PartitionSpec as P

C = 256
COLS = 80
ROWS = 8
FR = 2
CELLS = FR * ROWS * COLS
EXT = (FR + 2) * (ROWS + 2) * COLS
BAND = ROWS * COLS
norm_eps = 1e-05
F32 = jnp.float32
BF16 = jnp.bfloat16
HERE = float(CELLS * 8)
TOTAL = HERE * 128.0
SCALE = (27.0 * C) ** (-0.5)
SHARE = 108
PIECE = 112
BLOCK = 432
BOTH = ("tm", "rows")
CORE_PAIRS = [(i, i ^ 4) for i in range(128)]
CHIP_GROUPS = [
    [((z * 4 + y) * 2 + core) * 4 + x for z in range(4) for y in range(4) for x in range(4)]
    for core in range(2)
]
learn_rate = 0.25
beta_one = 0.9
beta_two = 0.95
decay_rate = 0.1
adam_eps = 1e-08
first_fix = 1.0 - 0.9**10
second_fix = 1.0 - 0.95**10


def mixed(value, matrix):
    return jnp.dot(value, matrix, precision=lax.Precision.HIGHEST, preferred_element_type=F32)


def iotas(shape):
    return lax.broadcasted_iota(jnp.int32, shape, 0), lax.broadcasted_iota(jnp.int32, shape, 1)


def spread_matrix(offset):
    lane, channel = iotas((128, C))
    return jnp.where(lane == (channel >> 3) + offset, 1.0, 0.0).astype(F32)


def pack_row(first, second):
    channel, lane = iotas((C, 128))
    head = jnp.where((channel >> 3) == lane, 1.0, 0.0).astype(F32)
    tail = jnp.where((channel >> 3) + 32 == lane, 1.0, 0.0).astype(F32)
    wide = jnp.broadcast_to(first, (8, C)), jnp.broadcast_to(second, (8, C))
    row = mixed(wide[0], head) + mixed(wide[1], tail)
    return jnp.broadcast_to(row[0:1], (128, 128))


def read_norm(table):
    total = jnp.sum(table, axis=0, keepdims=True)
    center = total / 128.0
    offset = table - center
    square = jnp.sum(offset * offset, axis=0, keepdims=True)
    low, high = spread_matrix(0), spread_matrix(32)
    wide = lambda v, m: mixed(jnp.broadcast_to(v, (8, 128)), m)[0:1]
    spread = wide(total, high) + HERE * wide(square, low)
    return wide(center, low), lax.rsqrt(spread / TOTAL + norm_eps)


def read_sums(table):
    total = jnp.sum(table, axis=0, keepdims=True) / TOTAL
    wide = lambda m: mixed(jnp.broadcast_to(total, (8, 128)), m)[0:1]
    return wide(spread_matrix(0)), wide(spread_matrix(32))


def folded(values):
    return jnp.sum(values.reshape(-1, 8, C), axis=0)


def chunk(index, size=COLS):
    return pl.ds(pl.multiple_of(index * size, size), size)


def local_moments(read, count):
    zero = jnp.zeros((8, C), F32)
    sums = lax.fori_loop(0, count, lambda i, s: s + folded(read(i)), zero)
    ch_sum = jnp.sum(sums, axis=0, keepdims=True)
    r, c = iotas((C, C))
    same = jnp.where((r >> 3) == (c >> 3), 1.0, 0.0).astype(F32)
    mean = mixed(jnp.broadcast_to(ch_sum, (8, C)), same)[0:1] / HERE

    def squares(i, s):
        off = read(i) - mean
        return s + folded(off * off)

    ch_sq = jnp.sum(lax.fori_loop(0, count, squares, zero), axis=0, keepdims=True)
    return pack_row(mean / 8.0, ch_sq)


def store_shifted(target, rows, value, backward):
    col = lax.broadcasted_iota(jnp.int32, value.shape, 0)
    left = jnp.where(col == 0, 0.0, pltpu.roll(value, 1, 0))
    right = jnp.where(col == COLS - 1, 0.0, pltpu.roll(value, COLS - 1, 0))
    one, three = (right, left) if backward else (left, right)
    target[rows, 0:C] = one.astype(BF16)
    target[rows, C : 2 * C] = value.astype(BF16)
    target[rows, 2 * C : 3 * C] = three.astype(BF16)


def each_row(own, above, below, frames, ok, upcoming, target, make, backward):
    own_at, halo_at = (0, FR) if upcoming else (FR, 0)

    def put(source, i, frame, row, flag):
        value = make(source[chunk(i), :].astype(F32))
        if flag is not None:
            value = value * flag
        store_shifted(target, chunk(frame * (ROWS + 2) + row), value, backward)

    def inner(i, _):
        put(own, i, own_at + i // ROWS, i % ROWS + 1, None)
        return 0

    def edge(i, _):
        put(above, i, own_at + i, 0, ok[1])
        put(below, i, own_at + i, ROWS + 1, ok[2])
        return 0

    def outer(i, _):
        row = i % (ROWS + 2)
        flag = ok[0] * jnp.where(row == 0, ok[1], jnp.where(row == ROWS + 1, ok[2], 1.0))
        put(frames, i, halo_at + i // (ROWS + 2), row, flag)
        return 0

    lax.fori_loop(0, FR * ROWS, inner, 0)
    lax.fori_loop(0, FR, edge, 0)
    lax.fori_loop(0, FR * (ROWS + 2), outer, 0)


def conv(patches, weight, write, backward):
    for t in range(FR):
        total = None
        for a in range(3):
            for b in range(3):
                f, r = (t + 2 - a, 2 - b) if backward else (t + a, b)
                at = (f * (ROWS + 2) + r) * COLS
                left = patches[at : at + BAND, :]
                tap = (9 * a + 3 * b) * C
                if backward:
                    right = jnp.concatenate([weight[tap + k * C : tap + (k + 1) * C, :] for k in range(3)], axis=1)
                    part = lax.dot_general(left, right, (((1,), (1,)), ((), ())), preferred_element_type=F32)
                else:
                    part = jnp.dot(left, weight[tap : tap + 3 * C, :], preferred_element_type=F32)
                total = part if total is None else total + part
        write(t, total * SCALE)


def both_frames(patches, place):
    starts = [(f * (ROWS + 2) + r) * COLS for f, r in map(place, range(FR))]
    return jnp.concatenate([patches[at : at + BAND, :] for at in starts], axis=0)


def wgrad(patches, grad, whole):
    for a in range(3):
        ready = patches.get(a + FR - 1)
        for b in range(3):
            left = both_frames(ready, lambda t: (t + a, b))
            total = lax.dot_general(
                left, grad[...], (((0,), (0,)), ((), ())), preferred_element_type=F32
            )
            tap = (9 * a + 3 * b) * C
            whole[tap : tap + 3 * C, :] = total * SCALE


def cut_pieces(whole, core, flat, kept, given):
    flat[...] = jnp.zeros_like(flat)
    for side, out in ((1 - core, given), (core, kept)):

        def block(i, _):
            at = pl.multiple_of(i * BLOCK + side * (BLOCK // 2), 8)
            slab = whole[pl.ds(at, BLOCK // 2), :]
            flat[pl.ds(0, BLOCK // 2, 2), :] = slab[:, :128]
            flat[pl.ds(1, BLOCK // 2, 2), :] = slab[:, 128:]
            for x in range(4):
                out.ref[i * 4 + x] = flat[x * SHARE : x * SHARE + PIECE, :].astype(BF16)
            return 0

        lax.fori_loop(0, 16, block, 0)
        out.send()


def silu_parts(value, center, inverse, gain):
    hat = (value - center) * inverse
    pre = hat * gain
    return hat, pre, jax.nn.sigmoid(pre)


def stats_kernel(inputs, row):
    inputs = inputs.get()
    row.ref[...] = local_moments(lambda i: inputs[chunk(i), :].astype(F32), FR * ROWS)


def conv_kernel(ok, inputs, above, below, frames, table, gain, weight, patches, middle, row):
    center, inverse = read_norm(table.get()[...])
    gain = gain.get()[...]

    def hidden(value):
        _, pre, gate = silu_parts(value, center, inverse, gain)
        return pre * gate

    each_row(inputs.get(), above.get(), below.get(), frames.get(), ok, False, patches.ref, hidden, False)
    patches.send()

    def write(t, value):
        middle.ref[t * BAND : (t + 1) * BAND, :] = value.astype(BF16)

    conv(patches.ref, weight.get(), write, False)
    middle.send()
    row.ref[...] = local_moments(lambda i: middle.ref[chunk(i), :].astype(F32), FR * ROWS)


def slopes(read, back, center, inverse, gain, slope, hidden=None):
    def step(i, sums):
        hat, pre, gate = silu_parts(read(i), center, inverse, gain)
        if hidden is not None:
            hidden[chunk(i), :] = (pre * gate).astype(BF16)
        here = back[chunk(i), :] * gate * (1.0 + pre * (1.0 - gate)) * gain
        slope[chunk(i), :] = here
        return sums[0] + folded(here), sums[1] + folded(here * hat)

    zero = jnp.zeros((8, C), F32)
    plain, cross = lax.fori_loop(0, FR * ROWS, step, (zero, zero))
    return pack_row(jnp.sum(plain, axis=0, keepdims=True), jnp.sum(cross, axis=0, keepdims=True))


def second_kernel(
    ok, core, cotangent, above, below, frames, weight, middle, table, gain, slope, row, kept, given, patches, back, hidden, whole, flat
):
    each_row(cotangent.get(), above.get(), below.get(), frames.get(), ok, True, patches, lambda v: v, True)

    def write(t, value):
        back[t * BAND : (t + 1) * BAND, :] = value

    conv(patches, weight.get(), write, True)
    center, inverse = read_norm(table.get()[...])
    middle = middle.get()
    read = lambda i: middle[chunk(i), :].astype(F32)
    row.ref[...] = slopes(read, back, center, inverse, gain.get()[...], slope.ref, hidden)
    slope.send()
    turned = hidden[...].astype(F32).T.astype(BF16)
    for a in range(3):
        for b in range(3):
            right = both_frames(patches, lambda t: (t + 2 - a, 2 - b))
            total = jnp.dot(turned, right, preferred_element_type=F32)
            total = total * SCALE
            for c in range(3):
                tap = (9 * a + 3 * b + c) * C
                whole[tap : tap + C, :] = total[:, c * C : (c + 1) * C]
    cut_pieces(whole, core[0], flat, kept, given)


def grad_one_kernel(core, slope, middle, patches, table, sums, mid_grad, kept, given, whole, flat):
    center, inverse = read_norm(table.get()[...])
    mean, cross = read_sums(sums.get()[...])
    slope, middle = slope.get(), middle.get()

    def step(i, _):
        hat = (middle[chunk(i), :].astype(F32) - center) * inverse
        mid_grad.ref[chunk(i), :] = (inverse * (slope[chunk(i), :] - mean - hat * cross)).astype(BF16)
        return 0

    lax.fori_loop(0, FR * ROWS, step, 0)
    mid_grad.send()
    wgrad(patches, mid_grad.ref, whole)
    cut_pieces(whole, core[0], flat, kept, given)


def back_one_kernel(ok, mid_grad, above, below, frames, weight, inputs, table, gain, slope, row, patches, back):
    each_row(mid_grad.get(), above.get(), below.get(), frames.get(), ok, True, patches, lambda v: v, True)

    def write(t, value):
        back[t * BAND : (t + 1) * BAND, :] = value

    conv(patches, weight.get(), write, True)
    center, inverse = read_norm(table.get()[...])
    inputs = inputs.get()
    read = lambda i: inputs[chunk(i), :].astype(F32)
    row.ref[...] = slopes(read, back, center, inverse, gain.get()[...], slope.ref)


def final_kernel(slope, inputs, table, sums, cotangent, result):
    center, inverse = read_norm(table.get()[...])
    mean, cross = read_sums(sums.get()[...])
    slope, inputs, cotangent = slope.get(), inputs.get(), cotangent.get()

    def step(i, _):
        hat = (inputs[chunk(i), :].astype(F32) - center) * inverse
        grad = inverse * (slope[chunk(i), :] - mean - hat * cross)
        result.ref[chunk(i), :] = (cotangent[chunk(i), :].astype(F32) + grad).astype(BF16)
        return 0

    lax.fori_loop(0, FR * ROWS, step, 0)


def adam_step(arrived, own, first, second, first_new, second_new):
    gradient = jnp.zeros((PIECE, 128), F32)
    for k in range(4):
        ready = arrived.get(k)
        gradient = lax.fori_loop(16 * k, 16 * k + 16, lambda i, s: s + ready[i].astype(F32), gradient)
    gradient = gradient[:SHARE]
    one = beta_one * first.get()[...] + (1.0 - beta_one) * gradient
    two = beta_two * second.get()[...] + (1.0 - beta_two) * gradient * gradient
    first_new.ref[...] = one
    second_new.ref[...] = two
    updated = own.get()[...].astype(F32) * (1.0 - learn_rate * decay_rate) - learn_rate * (one / first_fix) / (
        jnp.sqrt(two / second_fix) + adam_eps
    )
    return jnp.concatenate([updated, jnp.zeros((PIECE - SHARE, 128), F32)], axis=0).astype(BF16)


def adam_two_kernel(arrived, own, first, second, first_new, second_new, part):
    part.ref[0] = adam_step(arrived, own, first, second, first_new, second_new)


def adam_one_kernel(arrived, own, first, second, first_new, second_new, spread):
    piece = adam_step(arrived, own, first, second, first_new, second_new)

    def copy(i, _):
        spread.ref[i] = piece
        return 0

    for k in range(4):
        lax.fori_loop(16 * k, 16 * k + 16, copy, 0)
        spread.send(k)


def assemble(block, piece, weight, flat):
    for s in range(8):
        flat[s * SHARE : s * SHARE + PIECE, :] = piece(s).astype(F32)
    rows = pl.ds(pl.multiple_of(block * BLOCK, BLOCK), BLOCK)
    weight[rows, 0:128] = flat[pl.ds(0, BLOCK, 2), :].astype(BF16)
    weight[rows, 128:256] = flat[pl.ds(1, BLOCK, 2), :].astype(BF16)


def assemble_kernel(core, own, other, weight, flat, halves, arrive):
    parts = 4
    copies = [
        [
            pltpu.make_async_copy(
                source.at[pl.ds(16 * k, 16)], halves.at[place, pl.ds(16 * k, 16)], arrive.at[n, k]
            )
            for n, (source, place) in enumerate(((own, core[0]), (other, 1 - core[0])))
        ]
        for k in range(parts)
    ]
    for pair in copies:
        for copy in pair:
            copy.start()

    for k in range(parts):
        for copy in copies[k]:
            copy.wait()

        def block(i, _):
            assemble(i, lambda s: halves[s // 4, i * 4 + s % 4], weight.ref, flat)
            return 0

        lax.fori_loop(4 * k, 4 * k + 4, block, 0)
        weight.send(k)


def assemble_all_kernel(gathered, weight, flat):
    for k in range(4):
        ready = gathered.get(k)

        def block(i, _):
            assemble(i, lambda s: ready[i * 8 + s], weight.ref, flat)
            return 0

        lax.fori_loop(4 * k, 4 * k + 4, block, 0)
        weight.send(k)


class Coming:
    def __init__(self, ref, copies=()):
        self.ref, self.copies = ref, list(copies)
        for copy in self.copies:
            copy.start()
        self.parts = len(self.copies)

    def get(self, part=None):
        last = self.parts - 1 if part is None else part
        while self.copies and self.parts - len(self.copies) <= last:
            self.copies.pop(0).wait()
        return self.ref


class Going:
    def __init__(self, ref, copies=()):
        self.ref, self.copies, self.sent = ref, list(copies), set()

    def send(self, part=None):
        for k in range(len(self.copies)) if part is None else (part,):
            if k not in self.sent:
                self.copies[k].start()
                self.sent.add(k)

    def finish(self):
        self.send()
        for copy in self.copies:
            copy.wait()


SMALL = 80 * 1024


def run(kernel, scalars, arrays, outs, scratch=(), mib=60, parts=(), raw=()):
    parts, count = dict(parts), len(arrays)
    vmem, hbm = pl.BlockSpec(memory_space=pltpu.VMEM), pl.BlockSpec(memory_space=pltpu.HBM)
    every = [*arrays, *outs]
    large = [x.size * x.dtype.itemsize > SMALL for x in every]
    staged = [n for n in range(len(every)) if large[n] and n not in raw]
    buffers = [pltpu.VMEM(every[n].shape, every[n].dtype) for n in staged]
    semaphores = [pltpu.SemaphoreType.DMA((parts.get(n, 1),)) for n in staged]

    def body(*refs):
        lead, rest = refs[: len(scalars)], refs[len(scalars) :]
        places, rest = rest[: len(every)], rest[len(every) :]
        own, rest = rest[: len(scratch)], rest[len(scratch) :]
        boxes = []
        for n, place in enumerate(places):
            if n in raw:
                boxes.append(place)
                continue
            kind = Coming if n < count else Going
            if not large[n]:
                boxes.append(kind(place))
                continue
            at = staged.index(n)
            buffer, arrive, cuts = rest[at], rest[len(staged) + at], parts.get(n, 1)
            size = every[n].shape[0] // cuts
            copies = []
            for k in range(cuts):
                ends = [place.at[pl.ds(k * size, size)], buffer.at[pl.ds(k * size, size)]]
                source, target = ends if n < count else ends[::-1]
                copies.append(pltpu.make_async_copy(source, target, arrive.at[k]))
            boxes.append(kind(buffer, copies))
        kernel(*lead, *boxes, *own)
        for n, box in enumerate(boxes):
            if n not in raw:
                box.get() if n < count else box.finish()

    return pl.pallas_call(
        body,
        out_shape=tuple(outs),
        in_specs=[pl.BlockSpec(memory_space=pltpu.SMEM)] * len(scalars)
        + [hbm if large[n] else vmem for n in range(count)],
        out_specs=tuple(hbm if large[n] else vmem for n in range(count, len(every))),
        scratch_shapes=[*scratch, *buffers, *semaphores],
        compiler_params=pltpu.CompilerParams(vmem_limit_bytes=mib * 1024 * 1024),
        cost_estimate=pl.CostEstimate(flops=1024, bytes_accessed=1024, transcendentals=0),
    )(*scalars, *arrays)


def everyone(row):
    return lax.all_to_all(row, BOTH, 0, 0, tiled=True)


def after(value, *others):
    return lax.optimization_barrier((value, *others))[0]


def neighbours(axis):
    forward = [(i, i + 1) for i in range(lax.axis_size(axis) - 1)]
    return forward, [(j, i) for i, j in forward]


def edge_rows(blocks):
    down, up = neighbours("rows")
    last = jnp.concatenate([block[:, ROWS - 1] for block in blocks], axis=0)
    leading = jnp.concatenate([block[:, 0] for block in blocks], axis=0)
    above, below = lax.ppermute(last, "rows", down), lax.ppermute(leading, "rows", up)
    return [(above[k : k + FR], below[k : k + FR]) for k in range(0, FR * len(blocks), FR)]


def join_edges(block, edges):
    return jnp.concatenate([edges[0][:, None], block, edges[1][:, None]], axis=1)


def frame_halo(block, edges, perm):
    return lax.ppermute(join_edges(block, edges), "tm", perm).reshape(-1, C)


def flat(edges):
    return [edge.reshape(-1, C) for edge in edges]


def cells(array):
    return array.reshape(FR, ROWS, COLS, C)


def pair_sum(kept, given):
    taken = lax.ppermute(given, BOTH, CORE_PAIRS)
    return (kept.astype(F32) + taken.astype(F32)).astype(BF16)


def over_chips(pieces):
    return lax.all_to_all(pieces, BOTH, 0, 0, axis_index_groups=CHIP_GROUPS, tiled=True)


def own_share(weight):
    place = lax.axis_index(BOTH) * (SHARE // 2)
    return lax.dynamic_slice_in_dim(weight, place, SHARE // 2, axis=0).reshape(SHARE, 128)


def local(
    inputs,
    cotangent,
    gain_one,
    gain_two,
    weight_one,
    weight_two,
    first_one,
    second_one,
    first_two,
    second_two,
):
    shape = jax.ShapeDtypeStruct
    step, band = lax.axis_index("tm"), lax.axis_index("rows")
    core = (step % 2).astype(jnp.int32).reshape(1)
    inside = lambda *tests: jnp.stack([jnp.where(t, 1.0, 0.0).astype(F32) for t in tests])
    above_ok, below_ok = band > 0, band < lax.axis_size("rows") - 1
    ok_before = inside(step > 0, above_ok, below_ok)
    ok_after = inside(step < lax.axis_size("tm") - 1, above_ok, below_ok)
    gain_one, gain_two = gain_one.reshape(1, C), gain_two.reshape(1, C)
    flat_inputs, flat_cot = inputs.reshape(CELLS, C), cotangent.reshape(CELLS, C)

    row_type = shape((128, 128), F32)
    act_type, wide_type = shape((CELLS, C), BF16), shape((CELLS, C), F32)
    patch_type = shape((EXT, 3 * C), BF16)
    piece_type = shape((64, PIECE, 128), BF16)
    moment_type = shape((SHARE, 128), F32)
    patch_scratch = pltpu.VMEM((EXT, 3 * C), BF16)
    whole_scratch = pltpu.VMEM((27 * C, C), F32)
    flat_scratch = pltpu.VMEM((BLOCK + 8, 128), F32)

    def update(kernel, arrived, weight, first, second, more, part_types):
        first_new, second_new, *part = run(
            kernel,
            (),
            (*arrived, own_share(weight), first.reshape(SHARE, 128), second.reshape(SHARE, 128), *more),
            (moment_type, moment_type, *part_types),
            parts={0: 4, 6: 4} if part_types[0] is piece_type else {0: 4},
        )
        return part, first_new.reshape(-1), second_new.reshape(-1)

    forward, backward = neighbours("tm")
    edges_in, edges_cot = edge_rows((inputs, cotangent))
    (row_one,) = run(stats_kernel, (), (flat_inputs,), (row_type,))
    frames_in = frame_halo(after(inputs, row_one), edges_in, forward)
    frames_cot = frame_halo(after(cotangent, row_one), edges_cot, backward)
    table_one = everyone(row_one)
    patch_one, middle, row_two = run(
        conv_kernel,
        (ok_before,),
        (flat_inputs, *flat(edges_in), frames_in, table_one, gain_one, weight_one),
        (patch_type, act_type, row_type),
    )
    table_two = everyone(row_two)
    slope_two, row_three, kept_two, given_two = run(
        second_kernel,
        (ok_after, core),
        (flat_cot, *flat(edges_cot), frames_cot, weight_two, middle, table_two, gain_two),
        (wide_type, row_type, piece_type, piece_type),
        (patch_scratch, pltpu.VMEM((CELLS, C), F32), pltpu.VMEM((CELLS, C), BF16), whole_scratch, flat_scratch),
    )
    table_three = everyone(row_three)
    pair_two = pair_sum(kept_two, given_two)
    mid_grad, kept_one, given_one = run(
        grad_one_kernel,
        (core,),
        (after(slope_two, pair_two), middle, patch_one, table_two, table_three),
        (act_type, piece_type, piece_type),
        (whole_scratch, flat_scratch),
        parts={2: 4},
    )
    edges_grad = edge_rows((cells(mid_grad),))[0]
    frames_grad = frame_halo(cells(mid_grad), edges_grad, backward)
    arrived_two = over_chips(pair_two)
    part_two, new_first_two, new_second_two = update(
        adam_two_kernel,
        (after(arrived_two, given_one),),
        weight_two,
        first_two,
        second_two,
        (),
        (shape((1, PIECE, 128), BF16),),
    )
    gathered_two = lax.all_gather(part_two[0], BOTH, axis=0, tiled=True)
    pair_one = pair_sum(kept_one, after(given_one, part_two[0]))
    arrived_one = over_chips(pair_one)
    (part_one,), new_first_one, new_second_one = update(
        adam_one_kernel,
        (after(arrived_one, frames_grad),),
        weight_one,
        first_one,
        second_one,
        (),
        (piece_type,),
    )
    slope_one, row_four = run(
        back_one_kernel,
        (ok_after,),
        (
            after(mid_grad, part_one),
            *flat(edges_grad),
            frames_grad,
            weight_one,
            flat_inputs,
            table_one,
            gain_one,
        ),
        (wide_type, row_type),
        (patch_scratch, pltpu.VMEM((CELLS, C), F32)),
    )
    own_one = over_chips(part_one)
    other_one = lax.ppermute(after(own_one, row_four), BOTH, CORE_PAIRS)
    table_four = everyone(after(row_four, own_one))
    (input_grad,) = run(
        final_kernel, (), (slope_one, flat_inputs, table_one, table_four, flat_cot), (act_type,)
    )
    weight_type = shape((27 * C, C), BF16)
    assemble_scratch = pltpu.VMEM((2 * BLOCK + 8, 128), F32)
    (new_weight_one,) = run(
        assemble_kernel,
        (core,),
        (own_one, other_one),
        (weight_type,),
        (assemble_scratch, pltpu.VMEM((2, 64, PIECE, 128), BF16), pltpu.SemaphoreType.DMA((2, 4))),
        parts={2: 4},
        raw=(0, 1),
    )
    (new_weight_two,) = run(
        assemble_all_kernel, (), (gathered_two,), (weight_type,), (assemble_scratch,), parts={0: 4, 1: 4}
    )
    return (
        cells(input_grad),
        new_weight_one,
        new_weight_two,
        new_first_one,
        new_second_one,
        new_first_two,
        new_second_two,
    )


def solution(mesh):
    split, share = P("tm", "rows", None, None), P(("tm", "rows"))
    return jax.shard_map(
        local,
        mesh=mesh,
        in_specs=(split, split, P(), P(), P(), P(), share, share, share, share),
        out_specs=(split, P(), P(), share, share, share, share),
        check_vma=False,
    )
```

time: 333 us -> 272 us (0.82)
  waiting for transfers between devices: 124 us -> 85.5 us
  starting transfers between devices: 95 us -> 62.3 us
  local copies, waits for them, and re-layouts: 29.3 us -> 12.6 us
  between operations: 1.16 us -> 14.4 us
  Pallas kernels: 59.6 us -> 72.7 us
    all_to_all x4 -> x3, waiting for transfers between devices: 83.9 us -> 27.7 us  [over_chips(): lax.all_to_all(pieces, BOTH, 0, 0, axis_index_groups=CHIP_GROUPS, tiled=T...]
    unnamed x62 -> x26, local copies, waits for them, and re-layouts: 25.5 us -> 5.07 us
    all_to_all x3, waiting for transfers between devices: 9.61 us -> 24.5 us  [everyone(): return lax.all_to_all(row, BOTH, 0, 0, tiled=True)]
    ppermute x16 -> x10, starting transfers between devices: 36.3 us -> 22.9 us  [the longest x3 10.3 us: frame_halo(): return lax.ppermute(join_edges(block, edges), 'tm', perm).reshape(-1, C)]
    pallas_call x12 -> x10, Pallas kernels: 59.6 us -> 72.7 us  [run(): pl.pallas_call(body, out_shape=tuple(outs), in_specs=[pl.BlockSpec(memory...]
    all_to_all x3, starting transfers between devices: 31.1 us -> 18.3 us  [everyone(): return lax.all_to_all(row, BOTH, 0, 0, tiled=True)]
    all_to_all x4 -> x3, starting transfers between devices: 27.6 us -> 20.8 us  [over_chips(): lax.all_to_all(pieces, BOTH, 0, 0, axis_index_groups=CHIP_GROUPS, tiled=T...]
    ppermute x16 -> x10, waiting for transfers between devices: 30.1 us -> 33.2 us  [the longest x2 16.8 us: edge_rows(): lax.ppermute(last, 'rows', down)]
  transfers between devices with their start and end apart: 23 -> 17, of which waited for: 12 -> 10; matrix products, arithmetic and copies ran while one was open for 3% -> 5% of each run, Pallas kernels for 14% -> 18%
where the time goes in v3:
time: 272 us; the launch traced here: 270 us
  waiting for transfers between devices  85.5 us (31%)
  Pallas kernels  72.7 us (27%)
  starting transfers between devices  62.3 us (23%)
  blocking collectives  14.9 us (5%)
  between operations  14.4 us (5%)
  local copies, waits for them, and re-layouts  12.6 us (5%)
  other arithmetic  7.96 us (3%)
    pallas_call x10, Pallas kernels, run(): pl.pallas_call(body, out_shape=tuple(outs), in_specs=[pl.BlockSpec(memory...  72.7 us
    all_to_all x3, waiting for transfers between devices, over_chips(): lax.all_to_all(pieces, BOTH, 0, 0, axis_index_groups=CHIP_GROUPS, tiled=T...  27.7 us
    all_to_all x3, waiting for transfers between devices, everyone(): return lax.all_to_all(row, BOTH, 0, 0, tiled=True)  24.5 us
    all_to_all x3, starting transfers between devices, over_chips(): lax.all_to_all(pieces, BOTH, 0, 0, axis_index_groups=CHIP_GROUPS, tiled=T...  20.8 us
    all_to_all x3, starting transfers between devices, everyone(): return lax.all_to_all(row, BOTH, 0, 0, tiled=True)  18.3 us
    ppermute x2, waiting for transfers between devices, edge_rows(): lax.ppermute(last, 'rows', down)  16.8 us
    all_to_all x1, blocking collectives, everyone(): return lax.all_to_all(row, BOTH, 0, 0, tiled=True)  14.9 us
    ppermute x3, starting transfers between devices, frame_halo(): return lax.ppermute(join_edges(block, edges), 'tm', perm).reshape(-1, C)  10.3 us
  transfers between devices with their start and end apart: 17, of which 10 were waited for; matrix products, arithmetic and copies ran while one was open for 5% of the time, Pallas kernels for 18%

profile of v3, /device:TPU:1, one launch (start us, length us, event | category | flops | bytes accessed | tf_op | source)
XLA Modules:
  0.0 270.2 jit_solution(5350572857372074143)
XLA Ops:
  7.2 0.0 copy-start
  7.2 1.0 slice_bitcast_fusion.3
  8.2 0.9 slice_bitcast_fusion.2
  9.2 4.0 %collective-permute-start = (bf16[4,80,256]{2,1,0:T(8,128)(2,1)S(1)}, bf16[4,80,256]{2,1,0:T(8,128)(2,1)S(1)}, u32[]{:S(2)}, u32[]{:S(2)}) collective-permute-start(bf16[4,80,256]{2,1,0:T(8,128)(2,1)S(1)} %pad_maximum_fusion.3), channel_id=1, source_target_pairs={{0,1},{1,2},{2,3},{4,5},{5,6},{6,7},{8,9},{9,10},{10,11},{12,13},{... | collective-permute-start | bytes 491528 | tf_op jit(solution)/shard_map/ppermute | solution.py:483
  13.1 0.0 copy-start.4
  13.2 1.4 collective-permute-start.1
  14.6 3.0 %shard_map.153 = f32[128,128]{1,0:T(8,128)} custom-call(bf16[1280,256]{1,0:T(8,128)(2,1)} %bitcast.82), custom_call_target="tpu_custom_call" | custom-call | flops 1024 | bytes 1024 | tf_op jit(solution)/shard_map/pallas_call | solution.py:454
  17.6 0.0 collective-permute-done
  17.6 0.7 slice_bitcast_fusion.7
  18.2 1.7 collective-permute-done.1
  19.9 0.7 slice_bitcast_fusion.6
  20.6 0.1 pad_maximum_fusion.1
  20.7 5.0 %collective-permute-start.3 = (bf16[2,10,80,256]{3,2,1,0:T(8,128)(2,1)S(1)}, bf16[2,10,80,256]{3,2,1,0:T(8,128)(2,1)}, u32[]{:S(2)}, u32[]{:S(2)}) collective-permute-start(bf16[2,10,80,256]{3,2,1,0:T(8,128)(2,1)S(1)} %pad_maximum_fusion.1), channel_id=1, source_target_pairs={{0,4},{4,8},{8,12},{12,16},{16,20},{20,24},{24,28},{28,32},{32,36}... | collective-permute-start | bytes 2457608 | tf_op jit(solution)/shard_map/ppermute | solution.py:492
  25.7 0.1 pad_maximum_fusion
  25.8 1.9 collective-permute-start.2
  27.7 10.3 %all-to-all-start = ((f32[128,1,128]{2,1,0:T(1,128)}), f32[128,1,128]{2,1,0:T(1,128)S(1)}, u32[]{:S(2)}, u32[]{:S(2)}) async-start(f32[128,1,128]{2,1,0:T(1,128)} %bitcast.24), calls=%async_computation | async-start | bytes 131072 | tf_op jit(solution)/shard_map/all_to_all | solution.py:467
  38.0 0.6 maximum_maximum_fusion.1.refs_0_
  38.7 8.9 %all-to-all-done = f32[128,1,128]{2,1,0:T(1,128)S(1)} async-done(((f32[128,1,128]{2,1,0:T(1,128)}), f32[128,1,128]{2,1,0:T(1,128)S(1)}, u32[]{:S(2)}, u32[]{:S(2)}) %all-to-all-start) | async-done | bytes 65568 | tf_op jit(solution)/shard_map/all_to_all | solution.py:467
  47.6 0.0 collective-permute-done.3
  47.6 0.6 copy-done.6
  48.2 10.6 %shard_map.154 = (bf16[3200,768]{1,0:T(8,128)(2,1)}, bf16[1280,256]{1,0:T(8,128)(2,1)}, f32[128,128]{1,0:T(8,128)}) custom-call(f32[3]{0:T(128)} %maximum_maximum_fusion.1.refs_0_, bf16[1280,256]{1,0:T(8,128)(2,1)} %bitcast.83, bf16[160,256]{1,0:T(8,128)(2,1)} %bitcast.104, bf16[160,256]{1,0:T(8,128)(2,1)} %bitcast.105, bf16[1600,256]{1,0:T(8,128)(2,1)} %bitcast.22.refs_4_, ...), custom_call_target="tpu_custom_call" | custom-call | flops 1024 | bytes 1024 | tf_op jit(solution)/shard_map/pallas_call | solution.py:454
  58.8 4.4 %all-to-all-start.1 = ((f32[128,1,128]{2,1,0:T(1,128)}), f32[128,1,128]{2,1,0:T(1,128)S(1)}, u32[]{:S(2)}, u32[]{:S(2)}) async-start(f32[128,1,128]{2,1,0:T(1,128)} %bitcast.109), calls=%async_computation.1 | async-start | bytes 131072 | tf_op jit(solution)/shard_map/all_to_all | solution.py:467
  63.2 0.6 maximum_maximum_fusion.refs_0_
  63.8 9.1 %all-to-all-done.1 = f32[128,1,128]{2,1,0:T(1,128)S(1)} async-done(((f32[128,1,128]{2,1,0:T(1,128)}), f32[128,1,128]{2,1,0:T(1,128)S(1)}, u32[]{:S(2)}, u32[]{:S(2)}) %all-to-all-start.1) | async-done | bytes 65568 | tf_op jit(solution)/shard_map/all_to_all | solution.py:467
  72.9 0.6 copy-done.9
  73.5 17.4 %shard_map.155 = (f32[1280,256]{1,0:T(8,128)}, f32[128,128]{1,0:T(8,128)}, bf16[64,112,128]{2,1,0:T(8,128)(2,1)}, bf16[64,112,128]{2,1,0:T(8,128)(2,1)}) custom-call(f32[3]{0:T(128)} %maximum_maximum_fusion.refs_0_, s32[1]{0:T(128)} %bitcast.3.refs_1_.refs_0_, bf16[1280,256]{1,0:T(8,128)(2,1)} %bitcast.86, bf16[160,256]{1,0:T(8,128)(2,1)} %bitcast.102, ...), custom_call_target="tpu_custom_call" | custom-call | flops 1024 | bytes 1024 | tf_op jit(solution)/shard_map/pallas_call | solution.py:454
  90.9 0.8 collective-permute-start.4
  91.7 3.7 %all-to-all-start.2 = ((f32[128,1,128]{2,1,0:T(1,128)}), f32[128,1,128]{2,1,0:T(1,128)S(1)}, u32[]{:S(2)}, u32[]{:S(2)}) async-start(f32[128,1,128]{2,1,0:T(1,128)} %bitcast.108), calls=%async_computation.2 | async-start | bytes 131072 | tf_op jit(solution)/shard_map/all_to_all | solution.py:467
  95.4 3.2 %add_convert_fusion.1 = bf16[64,112,128]{2,1,0:T(8,128)(2,1)} fusion(bf16[64,112,128]{2,1,0:T(8,128)(2,1)S(1)} %collective-permute-done.4, bf16[64,112,128]{2,1,0:T(8,128)(2,1)} %get-tuple-element.39), kind=kLoop, calls=%fused_computation.1 | loop fusion | flops 3670016 | bytes 5505024 | tf_op jit(solution)/shard_map/convert_element_type | solution.py:505
  98.6 6.4 %all-to-all-done.2 = f32[128,1,128]{2,1,0:T(1,128)S(1)} async-done(((f32[128,1,128]{2,1,0:T(1,128)}), f32[128,1,128]{2,1,0:T(1,128)S(1)}, u32[]{:S(2)}, u32[]{:S(2)}) %all-to-all-start.2) | async-done | bytes 65568 | tf_op jit(solution)/shard_map/all_to_all | solution.py:467
  105.1 0.6 copy-done.12
  105.7 4.8 %all-to-all-start.3 = ((bf16[64,112,128]{2,1,0:T(8,128)(2,1)}), bf16[64,112,128]{2,1,0:T(8,128)(2,1)S(1)}, u32[]{:S(2)}, u32[]{:S(2)}) async-start(bf16[64,112,128]{2,1,0:T(8,128)(2,1)} %add_convert_fusion.1), calls=%async_computation.3 | async-start | bytes 3670016 | tf_op jit(solution)/shard_map/all_to_all | solution.py:509
  110.5 0.3 all-gather.2.cloned.1.call-start
  110.8 0.8 constant_dynamic-slice_fusion.1
  111.6 0.6 reshape.112.refs_1_
  112.2 12.5 %shard_map.156 = (bf16[1280,256]{1,0:T(8,128)(2,1)}, bf16[64,112,128]{2,1,0:T(8,128)(2,1)}, bf16[64,112,128]{2,1,0:T(8,128)(2,1)}) custom-call(s32[1]{0:T(128)} %bitcast.3.refs_1_.refs_0_, f32[1280,256]{1,0:T(8,128)} %get-tuple-element.41.refs_1_, bf16[1280,256]{1,0:T(8,128)(2,1)} %get-tuple-element.36.refs_7_.refs_2_, ...), custom_call_target="tpu_custom_call" | custom-call | flops 1024 | bytes 1024 | tf_op jit(solution)/shard_map/pallas_call | solution.py:454
  124.7 11.8 %all-to-all-done.3.refs_0_ = bf16[64,112,128]{2,1,0:T(8,128)(2,1)S(1)} async-done(((bf16[64,112,128]{2,1,0:T(8,128)(2,1)}), bf16[64,112,128]{2,1,0:T(8,128)(2,1)S(1)}, u32[]{:S(2)}, u32[]{:S(2)}) %all-to-all-start.3) | async-done | bytes 1835040 | tf_op jit(solution)/shard_map/all_to_all | solution.py:509
  136.5 1.3 copy-done.3
  137.8 3.1 %shard_map.157 = (f32[108,128]{1,0:T(8,128)}, f32[108,128]{1,0:T(8,128)}, bf16[1,112,128]{2,1,0:T(8,128)(2,1)}) custom-call(bf16[64,112,128]{2,1,0:T(8,128)(2,1)} %copy-done.3, bf16[108,128]{1,0:T(8,128)(2,1)} %reshape.112.refs_1_, f32[108,128]{1,0:T(8,128)} %bitcast.111, f32[108,128]{1,0:T(8,128)} %bitcast.112), custom_call_target="tpu_custom_call" | custom-call | flops 1024 | bytes 1024 | tf_op jit(solution)/shard_map/pallas_call | solution.py:454
  140.9 2.3 collective-permute-start.5
  143.2 0.0 all-gather.2.cloned.1.call-update
  143.2 3.6 %collective-permute-done.5 = bf16[64,112,128]{2,1,0:T(8,128)(2,1)S(1)} collective-permute-done((bf16[64,112,128]{2,1,0:T(8,128)(2,1)}, bf16[64,112,128]{2,1,0:T(8,128)(2,1)S(1)}, u32[]{:S(2)}, u32[]{:S(2)}) %collective-permute-start.5) | collective-permute-done | bytes 1835040 | tf_op jit(solution)/shard_map/ppermute | solution.py:504
  146.8 3.2 %add_convert_fusion = bf16[64,112,128]{2,1,0:T(8,128)(2,1)} fusion(bf16[64,112,128]{2,1,0:T(8,128)(2,1)S(1)} %collective-permute-done.5, bf16[64,112,128]{2,1,0:T(8,128)(2,1)} %get-tuple-element.45), kind=kLoop, calls=%fused_computation | loop fusion | flops 3670016 | bytes 5505024 | tf_op jit(solution)/shard_map/convert_element_type | solution.py:505
  150.0 5.4 %all-to-all-start.4 = ((bf16[64,112,128]{2,1,0:T(8,128)(2,1)}), bf16[64,112,128]{2,1,0:T(8,128)(2,1)S(1)}, u32[]{:S(2)}, u32[]{:S(2)}) async-start(bf16[64,112,128]{2,1,0:T(8,128)(2,1)} %add_convert_fusion), calls=%async_computation.4 | async-start | bytes 3670016 | tf_op jit(solution)/shard_map/all_to_all | solution.py:509
  155.5 2.9 %collective-permute-start.6 = (bf16[2,80,256]{2,1,0:T(8,128)(2,1)S(1)}, bf16[2,80,256]{2,1,0:T(8,128)(2,1)S(1)}, u32[]{:S(2)}, u32[]{:S(2)}) collective-permute-start(bf16[2,80,256]{2,1,0:T(8,128)(2,1)S(1)} %get-tuple-element.61), channel_id=1, source_target_pairs={{0,1},{1,2},{2,3},{4,5},{5,6},{6,7},{8,9},{9,10},{10,11},{12,13},{... | collective-permute-start | bytes 245768 | tf_op jit(solution)/shard_map/ppermute | solution.py:483
  158.4 1.3 collective-permute-start.7
  159.7 16.8 %collective-permute-done.6 = bf16[2,80,256]{2,1,0:T(8,128)(2,1)S(1)} collective-permute-done((bf16[2,80,256]{2,1,0:T(8,128)(2,1)S(1)}, bf16[2,80,256]{2,1,0:T(8,128)(2,1)S(1)}, u32[]{:S(2)}, u32[]{:S(2)}) %collective-permute-start.6) | collective-permute-done | bytes 81952 | tf_op jit(solution)/shard_map/ppermute | solution.py:483
  176.5 1.5 collective-permute-done.7
  178.0 0.6 copy-done.11
  178.6 0.1 pad_maximum_fusion.2
  178.7 3.4 %collective-permute-start.8 = (bf16[2,10,80,256]{3,2,1,0:T(8,128)(2,1)S(1)}, bf16[2,10,80,256]{3,2,1,0:T(8,128)(2,1)S(1)}, u32[]{:S(2)}, u32[]{:S(2)}) collective-permute-start(bf16[2,10,80,256]{3,2,1,0:T(8,128)(2,1)S(1)} %pad_maximum_fusion.2), channel_id=1, source_target_pairs={{4,0},{8,4},{12,8},{16,12},{20,16},{24,20},{28,24},{32,28},{36,32}... | collective-permute-start | bytes 2457608 | tf_op jit(solution)/shard_map/ppermute | solution.py:492
  182.1 1.4 constant_dynamic-slice_fusion
  183.5 1.4 reshape.117.refs_1_
  184.9 9.6 %collective-permute-done.8 = bf16[2,10,80,256]{3,2,1,0:T(8,128)(2,1)S(1)} collective-permute-done((bf16[2,10,80,256]{3,2,1,0:T(8,128)(2,1)S(1)}, bf16[2,10,80,256]{3,2,1,0:T(8,128)(2,1)S(1)}, u32[]{:S(2)}, u32[]{:S(2)}) %collective-permute-start.8) | collective-permute-done | bytes 819232 | tf_op jit(solution)/shard_map/ppermute | solution.py:492
  194.5 1.3 copy-done.2
  195.8 4.5 %shard_map.158 = (f32[108,128]{1,0:T(8,128)}, f32[108,128]{1,0:T(8,128)}, bf16[64,112,128]{2,1,0:T(8,128)(2,1)}) custom-call(bf16[64,112,128]{2,1,0:T(8,128)(2,1)} %copy-done.2, bf16[108,128]{1,0:T(8,128)(2,1)} %reshape.117.refs_1_, f32[108,128]{1,0:T(8,128)} %bitcast.113, f32[108,128]{1,0:T(8,128)} %bitcast.114), custom_call_target="tpu_custom_call" | custom-call | flops 1024 | bytes 1024 | tf_op jit(solution)/shard_map/pallas_call | solution.py:454
  200.3 10.5 %all-to-all-start.5 = ((bf16[64,112,128]{2,1,0:T(8,128)(2,1)}), bf16[64,112,128]{2,1,0:T(8,128)(2,1)S(1)}, u32[]{:S(2)}, u32[]{:S(2)}) async-start(bf16[64,112,128]{2,1,0:T(8,128)(2,1)} %get-tuple-element.51), calls=%async_computation.5 | async-start | bytes 3670016 | tf_op jit(solution)/shard_map/all_to_all | solution.py:509
  210.9 11.0 %shard_map.159 = (f32[1280,256]{1,0:T(8,128)}, f32[128,128]{1,0:T(8,128)}) custom-call(f32[3]{0:T(128)} %maximum_maximum_fusion.refs_0_, bf16[1280,256]{1,0:T(8,128)(2,1)} %get-tuple-element.52.refs_1_, bf16[160,256]{1,0:T(8,128)(2,1)} %bitcast.99, bf16[160,256]{1,0:T(8,128)(2,1)} %bitcast.101, bf16[1600,256]{1,0:T(8,128)(2,1)} %bitcast.93, ...), custom_call_target="tpu_custom_call" | custom-call | flops 1024 | bytes 1024 | tf_op jit(solution)/shard_map/pallas_call | solution.py:454
  221.9 15.9 %all-to-all-done.5.refs_1_ = bf16[64,112,128]{2,1,0:T(8,128)(2,1)S(1)} async-done(((bf16[64,112,128]{2,1,0:T(8,128)(2,1)}), bf16[64,112,128]{2,1,0:T(8,128)(2,1)S(1)}, u32[]{:S(2)}, u32[]{:S(2)}) %all-to-all-start.5) | async-done | bytes 1835040 | tf_op jit(solution)/shard_map/all_to_all | solution.py:509
  237.8 14.9 %all_to_all.59 = f32[128,1,128]{2,1,0:T(1,128)} all-to-all(f32[128,1,128]{2,1,0:T(1,128)} %bitcast.110), channel_id=1, replica_groups=mesh['tm'=32,'rows'=4] {'tm','rows'}, dimensions={0} | all-to-all | bytes 131072 | tf_op jit(solution)/shard_map/all_to_all | solution.py:467
  252.7 4.0 %shard_map.160 = bf16[1280,256]{1,0:T(8,128)(2,1)} custom-call(f32[1280,256]{1,0:T(8,128)} %get-tuple-element.53.refs_0_, bf16[1280,256]{1,0:T(8,128)(2,1)} %bitcast.85, f32[128,128]{1,0:T(8,128)} %bitcast.92, f32[128,128]{1,0:T(8,128)} %bitcast.107, bf16[1280,256]{1,0:T(8,128)(2,1)} %bitcast.87), custom_call_target="tpu_custom_call" | custom-call | flops 1024 | bytes 1024 | tf_op jit(solution)/shard_map/pallas_call | solution.py:454
  256.7 0.0 all-gather.2.cloned.1.call-done.refs_0_
  256.7 3.3 %shard_map.162 = bf16[6912,256]{1,0:T(8,128)(2,1)} custom-call(bf16[128,112,128]{2,1,0:T(8,128)(2,1)} %all-gather.2.cloned.1.call-done.refs_0_), custom_call_target="tpu_custom_call" | custom-call | flops 1024 | bytes 1024 | tf_op jit(solution)/shard_map/pallas_call | solution.py:454
  260.1 3.3 %shard_map.161 = bf16[6912,256]{1,0:T(8,128)(2,1)} custom-call(s32[1]{0:T(128)} %bitcast.3.refs_1_.refs_0_, bf16[64,112,128]{2,1,0:T(8,128)(2,1)} %copy-done.1, bf16[64,112,128]{2,1,0:T(8,128)(2,1)} %collective-permute-done.9.refs_2_), custom_call_target="tpu_custom_call" | custom-call | flops 1024 | bytes 1024 | tf_op jit(solution)/shard_map/pallas_call | solution.py:454
  (26 shorter events, 0.1 us)
Async XLA Ops:
  7.2 13.5 %copy-start = (bf16[2,8,80,256]{3,2,1,0:T(8,128)(2,1)S(1)}, bf16[2,8,80,256]{3,2,1,0:T(8,128)(2,1)}, u32[]{:S(2)}) copy-start(bf16[2,8,80,256]{3,2,1,0:T(8,128)(2,1)} %param.10) | copy-start | bytes 1966084
  9.2 8.4 %collective-permute-start = (bf16[4,80,256]{2,1,0:T(8,128)(2,1)S(1)}, bf16[4,80,256]{2,1,0:T(8,128)(2,1)S(1)}, u32[]{:S(2)}, u32[]{:S(2)}) collective-permute-start(bf16[4,80,256]{2,1,0:T(8,128)(2,1)S(1)} %pad_maximum_fusion.3), channel_id=1, source_target_pairs={{0,1},{1,2},{2,3},{4,5},{5,6},{6,7},{8,9},{9,10},{10,11},{12,13},{... | collective-permute-start | bytes 491528 | tf_op jit(solution)/shard_map/ppermute | solution.py:483
  13.1 12.6 %copy-start.4 = (bf16[2,8,80,256]{3,2,1,0:T(8,128)(2,1)S(1)}, bf16[2,8,80,256]{3,2,1,0:T(8,128)(2,1)}, u32[]{:S(2)}) copy-start(bf16[2,8,80,256]{3,2,1,0:T(8,128)(2,1)} %param.11) | copy-start | bytes 1966084
  13.2 6.8 %collective-permute-start.1 = (bf16[4,80,256]{2,1,0:T(8,128)(2,1)S(1)}, bf16[4,80,256]{2,1,0:T(8,128)(2,1)S(1)}, u32[]{:S(2)}, u32[]{:S(2)}) collective-permute-start(bf16[4,80,256]{2,1,0:T(8,128)(2,1)S(1)} %pad_maximum_fusion.4), channel_id=1, source_target_pairs={{1,0},{2,1},{3,2},{5,4},{6,5},{7,6},{9,8},{10,9},{11,10},{13,12},{... | collective-permute-start | bytes 491528 | tf_op jit(solution)/shard_map/ppermute | solution.py:483
  20.7 26.9 %collective-permute-start.3 = (bf16[2,10,80,256]{3,2,1,0:T(8,128)(2,1)S(1)}, bf16[2,10,80,256]{3,2,1,0:T(8,128)(2,1)}, u32[]{:S(2)}, u32[]{:S(2)}) collective-permute-start(bf16[2,10,80,256]{3,2,1,0:T(8,128)(2,1)S(1)} %pad_maximum_fusion.1), channel_id=1, source_target_pairs={{0,4},{4,8},{8,12},{12,16},{16,20},{20,24},{24,28},{28,32},{32,36}... | collective-permute-start | bytes 2457608 | tf_op jit(solution)/shard_map/ppermute | solution.py:492
  25.8 38.0 %collective-permute-start.2 = (bf16[2,10,80,256]{3,2,1,0:T(8,128)(2,1)S(1)}, bf16[2,10,80,256]{3,2,1,0:T(8,128)(2,1)S(1)}, u32[]{:S(2)}, u32[]{:S(2)}) collective-permute-start(bf16[2,10,80,256]{3,2,1,0:T(8,128)(2,1)S(1)} %pad_maximum_fusion), channel_id=1, source_target_pairs={{4,0},{8,4},{12,8},{16,12},{20,16},{24,20},{28,24},{32,28},{36,32}... | collective-permute-start | bytes 2457608 | tf_op jit(solution)/shard_map/ppermute | solution.py:492
  27.7 19.9 %all-to-all-start = ((f32[128,1,128]{2,1,0:T(1,128)}), f32[128,1,128]{2,1,0:T(1,128)S(1)}, u32[]{:S(2)}, u32[]{:S(2)}) async-start(f32[128,1,128]{2,1,0:T(1,128)} %bitcast.24), calls=%async_computation | async-start | bytes 131072 | tf_op jit(solution)/shard_map/all_to_all | solution.py:467
  47.6 0.6 copy-start.6
  58.8 14.1 %all-to-all-start.1 = ((f32[128,1,128]{2,1,0:T(1,128)}), f32[128,1,128]{2,1,0:T(1,128)S(1)}, u32[]{:S(2)}, u32[]{:S(2)}) async-start(f32[128,1,128]{2,1,0:T(1,128)} %bitcast.109), calls=%async_computation.1 | async-start | bytes 131072 | tf_op jit(solution)/shard_map/all_to_all | solution.py:467
  63.8 9.1 %copy-start.8 = (bf16[2,10,80,256]{3,2,1,0:T(8,128)(2,1)}, bf16[2,10,80,256]{3,2,1,0:T(8,128)(2,1)S(1)}, u32[]{:S(2)}) copy-start(bf16[2,10,80,256]{3,2,1,0:T(8,128)(2,1)S(1)} %collective-permute-done.2) | copy-start | bytes 2457604
  72.9 0.6 copy-start.9
  90.9 4.5 %collective-permute-start.4 = (bf16[64,112,128]{2,1,0:T(8,128)(2,1)}, bf16[64,112,128]{2,1,0:T(8,128)(2,1)S(1)}, u32[]{:S(2)}, u32[]{:S(2)}) collective-permute-start(bf16[64,112,128]{2,1,0:T(8,128)(2,1)} %get-tuple-element.40), channel_id=1, source_target_pairs={{0,4},{1,5},{2,6},{3,7},{4,0},{5,1},{6,2},{7,3},{8,12},{9,13},{10,... | collective-permute-start | bytes 5505032 | tf_op jit(solution)/shard_map/ppermute | solution.py:504
  91.7 13.4 %all-to-all-start.2 = ((f32[128,1,128]{2,1,0:T(1,128)}), f32[128,1,128]{2,1,0:T(1,128)S(1)}, u32[]{:S(2)}, u32[]{:S(2)}) async-start(f32[128,1,128]{2,1,0:T(1,128)} %bitcast.108), calls=%async_computation.2 | async-start | bytes 131072 | tf_op jit(solution)/shard_map/all_to_all | solution.py:467
  105.1 0.6 copy-start.12
  105.7 30.8 %all-to-all-start.3 = ((bf16[64,112,128]{2,1,0:T(8,128)(2,1)}), bf16[64,112,128]{2,1,0:T(8,128)(2,1)S(1)}, u32[]{:S(2)}, u32[]{:S(2)}) async-start(bf16[64,112,128]{2,1,0:T(8,128)(2,1)} %add_convert_fusion.1), calls=%async_computation.3 | async-start | bytes 3670016 | tf_op jit(solution)/shard_map/all_to_all | solution.py:509
  110.5 146.2 %all-gather.2.cloned.1.call-start = ((), (), s32[]{:S(2)}) async-start(), calls=%async_computation.7 | async-start | bytes 3698688 | tf_op jit(solution)/shard_map/all_gather | solution.py:600
  136.5 1.3 copy-start.3
  140.9 5.9 %collective-permute-start.5 = (bf16[64,112,128]{2,1,0:T(8,128)(2,1)}, bf16[64,112,128]{2,1,0:T(8,128)(2,1)S(1)}, u32[]{:S(2)}, u32[]{:S(2)}) collective-permute-start(bf16[64,112,128]{2,1,0:T(8,128)(2,1)} %get-tuple-element.49), channel_id=1, source_target_pairs={{0,4},{1,5},{2,6},{3,7},{4,0},{5,1},{6,2},{7,3},{8,12},{9,13},{10,... | collective-permute-start | bytes 5505032 | tf_op jit(solution)/shard_map/ppermute | solution.py:504
  150.0 5.4 %copy-start.5 = (bf16[1280,256]{1,0:T(8,128)(2,1)S(1)}, bf16[1280,256]{1,0:T(8,128)(2,1)}, u32[]{:S(2)}) copy-start(bf16[1280,256]{1,0:T(8,128)(2,1)} %get-tuple-element.52.refs_1_) | copy-start | bytes 1966084
  150.0 44.5 %all-to-all-start.4 = ((bf16[64,112,128]{2,1,0:T(8,128)(2,1)}), bf16[64,112,128]{2,1,0:T(8,128)(2,1)S(1)}, u32[]{:S(2)}, u32[]{:S(2)}) async-start(bf16[64,112,128]{2,1,0:T(8,128)(2,1)} %add_convert_fusion), calls=%async_computation.4 | async-start | bytes 3670016 | tf_op jit(solution)/shard_map/all_to_all | solution.py:509
  155.5 21.0 %collective-permute-start.6 = (bf16[2,80,256]{2,1,0:T(8,128)(2,1)S(1)}, bf16[2,80,256]{2,1,0:T(8,128)(2,1)S(1)}, u32[]{:S(2)}, u32[]{:S(2)}) collective-permute-start(bf16[2,80,256]{2,1,0:T(8,128)(2,1)S(1)} %get-tuple-element.61), channel_id=1, source_target_pairs={{0,1},{1,2},{2,3},{4,5},{5,6},{6,7},{8,9},{9,10},{10,11},{12,13},{... | collective-permute-start | bytes 245768 | tf_op jit(solution)/shard_map/ppermute | solution.py:483
  158.4 19.6 %collective-permute-start.7 = (bf16[2,80,256]{2,1,0:T(8,128)(2,1)S(1)}, bf16[2,80,256]{2,1,0:T(8,128)(2,1)S(1)}, u32[]{:S(2)}, u32[]{:S(2)}) collective-permute-start(bf16[2,80,256]{2,1,0:T(8,128)(2,1)S(1)} %get-tuple-element.62), channel_id=1, source_target_pairs={{1,0},{2,1},{3,2},{5,4},{6,5},{7,6},{9,8},{10,9},{11,10},{13,12},{... | collective-permute-start | bytes 245768 | tf_op jit(solution)/shard_map/ppermute | solution.py:483
  176.5 23.8 %copy-start.10 = (bf16[2,80,256]{2,1,0:T(8,128)(2,1)}, bf16[2,80,256]{2,1,0:T(8,128)(2,1)S(1)}, u32[]{:S(2)}) copy-start(bf16[2,80,256]{2,1,0:T(8,128)(2,1)S(1)} %collective-permute-done.6) | copy-start | bytes 245764
  178.0 0.6 copy-start.11
  178.7 15.7 %collective-permute-start.8 = (bf16[2,10,80,256]{3,2,1,0:T(8,128)(2,1)S(1)}, bf16[2,10,80,256]{3,2,1,0:T(8,128)(2,1)S(1)}, u32[]{:S(2)}, u32[]{:S(2)}) collective-permute-start(bf16[2,10,80,256]{3,2,1,0:T(8,128)(2,1)S(1)} %pad_maximum_fusion.2), channel_id=1, source_target_pairs={{4,0},{8,4},{12,8},{16,12},{20,16},{24,20},{28,24},{32,28},{36,32}... | collective-permute-start | bytes 2457608 | tf_op jit(solution)/shard_map/ppermute | solution.py:492
  194.5 16.4 %copy-start.7 = (bf16[2,10,80,256]{3,2,1,0:T(8,128)(2,1)}, bf16[2,10,80,256]{3,2,1,0:T(8,128)(2,1)S(1)}, u32[]{:S(2)}) copy-start(bf16[2,10,80,256]{3,2,1,0:T(8,128)(2,1)S(1)} %collective-permute-done.8) | copy-start | bytes 2457604
  194.5 1.3 copy-start.2
  200.3 37.5 %all-to-all-start.5 = ((bf16[64,112,128]{2,1,0:T(8,128)(2,1)}), bf16[64,112,128]{2,1,0:T(8,128)(2,1)S(1)}, u32[]{:S(2)}, u32[]{:S(2)}) async-start(bf16[64,112,128]{2,1,0:T(8,128)(2,1)} %get-tuple-element.51), calls=%async_computation.5 | async-start | bytes 3670016 | tf_op jit(solution)/shard_map/all_to_all | solution.py:509
  237.8 22.2 %copy-start.1 = (bf16[64,112,128]{2,1,0:T(8,128)(2,1)}, bf16[64,112,128]{2,1,0:T(8,128)(2,1)S(1)}, u32[]{:S(2)}) copy-start(bf16[64,112,128]{2,1,0:T(8,128)(2,1)S(1)} %all-to-all-done.5.refs_1_) | copy-start | bytes 5505028
  237.8 22.2 %collective-permute-start.9 = (bf16[64,112,128]{2,1,0:T(8,128)(2,1)S(1)}, bf16[64,112,128]{2,1,0:T(8,128)(2,1)}, u32[]{:S(2)}, u32[]{:S(2)}) collective-permute-start(bf16[64,112,128]{2,1,0:T(8,128)(2,1)S(1)} %all-to-all-done.5.refs_1_), channel_id=1, source_target_pairs={{0,4},{1,5},{2,6},{3,7},{4,0},{5,1},{6,2},{7,3},{8,12},{9,13},{10,... | collective-permute-start | bytes 5505032 | tf_op jit(solution)/shard_map/ppermute | solution.py:628
Sparse Core Ops, SparseCore 0:
  143.3 83.0 all-gather.1

commit v4 on v3

--- a/solution.py
+++ b/solution.py
@@ -130,12 +130,25 @@
     def outer(i, _):
         row = i % (ROWS + 2)
         flag = ok[0] * jnp.where(row == 0, ok[1], jnp.where(row == ROWS + 1, ok[2], 1.0))
-        put(frames, i, halo_at + i // (ROWS + 2), row, flag)
+        put(frames[0], i, halo_at + i // (ROWS + 2), row, flag)
+        return 0
+
+    def outer_inner(i, _):
+        put(frames[0], i, halo_at + i // ROWS, i % ROWS + 1, ok[0])
+        return 0
+
+    def outer_edge(i, _):
+        put(frames[1], i, halo_at + i, 0, ok[0] * ok[1])
+        put(frames[2], i, halo_at + i, ROWS + 1, ok[0] * ok[2])
         return 0
 
     lax.fori_loop(0, FR * ROWS, inner, 0)
     lax.fori_loop(0, FR, edge, 0)
-    lax.fori_loop(0, FR * (ROWS + 2), outer, 0)
+    if len(frames) == 1:
+        lax.fori_loop(0, FR * (ROWS + 2), outer, 0)
+    else:
+        lax.fori_loop(0, FR * ROWS, outer_inner, 0)
+        lax.fori_loop(0, FR, outer_edge, 0)
 
 
 def conv(patches, weight, write, backward):
@@ -209,7 +222,7 @@
         _, pre, gate = silu_parts(value, center, inverse, gain)
         return pre * gate
 
-    each_row(inputs.get(), above.get(), below.get(), frames.get(), ok, False, patches.ref, hidden, False)
+    each_row(inputs.get(), above.get(), below.get(), (frames.get(),), ok, False, patches.ref, hidden, False)
     patches.send()
 
     def write(t, value):
@@ -234,24 +247,29 @@
     return pack_row(jnp.sum(plain, axis=0, keepdims=True), jnp.sum(cross, axis=0, keepdims=True))
 
 
-def second_kernel(
-    ok, core, cotangent, above, below, frames, weight, middle, table, gain, slope, row, kept, given, patches, back, hidden, whole, flat
-):
-    each_row(cotangent.get(), above.get(), below.get(), frames.get(), ok, True, patches, lambda v: v, True)
+def back_two_kernel(ok, cotangent, above, below, frames, weight, back, patches):
+    each_row(
+        cotangent.get(), above.get(), below.get(), (frames.get(),), ok, True, patches.ref, lambda v: v, True
+    )
+    patches.send()
 
     def write(t, value):
-        back[t * BAND : (t + 1) * BAND, :] = value
-
-    conv(patches, weight.get(), write, True)
+        back.ref[t * BAND : (t + 1) * BAND, :] = value
+
+    conv(patches.ref, weight.get(), write, True)
+
+
+def second_kernel(core, middle, back, patches, table, gain, slope, row, kept, given, hidden, whole, flat):
     center, inverse = read_norm(table.get()[...])
     middle = middle.get()
     read = lambda i: middle[chunk(i), :].astype(F32)
-    row.ref[...] = slopes(read, back, center, inverse, gain.get()[...], slope.ref, hidden)
+    row.ref[...] = slopes(read, back.get(), center, inverse, gain.get()[...], slope.ref, hidden)
     slope.send()
     turned = hidden[...].astype(F32).T.astype(BF16)
-    for a in range(3):
+    for a in (2, 1, 0):
+        ready = patches.get(FR + 1 - a)
         for b in range(3):
-            right = both_frames(patches, lambda t: (t + 2 - a, 2 - b))
+            right = both_frames(ready, lambda t: (t + 2 - a, 2 - b))
             total = jnp.dot(turned, right, preferred_element_type=F32)
             total = total * SCALE
             for c in range(3):
@@ -276,8 +294,11 @@
     cut_pieces(whole, core[0], flat, kept, given)
 
 
-def back_one_kernel(ok, mid_grad, above, below, frames, weight, inputs, table, gain, slope, row, patches, back):
-    each_row(mid_grad.get(), above.get(), below.get(), frames.get(), ok, True, patches, lambda v: v, True)
+def back_one_kernel(
+    ok, mid_grad, above, below, frames, above_frames, below_frames, weight, inputs, table, gain, slope, row, patches, back
+):
+    beyond = (frames.get(), above_frames.get(), below_frames.get())
+    each_row(mid_grad.get(), above.get(), below.get(), beyond, ok, True, patches, lambda v: v, True)
 
     def write(t, value):
         back[t * BAND : (t + 1) * BAND, :] = value
@@ -286,12 +307,29 @@
     center, inverse = read_norm(table.get()[...])
     inputs = inputs.get()
     read = lambda i: inputs[chunk(i), :].astype(F32)
-    row.ref[...] = slopes(read, back, center, inverse, gain.get()[...], slope.ref)
-
-
-def final_kernel(slope, inputs, table, sums, cotangent, result):
+    row.ref[...] = slopes(read, back, center, inverse, gain.get()[...], slope.ref)[: row.ref.shape[0]]
+
+
+def last_kernel(core, own, other, slope, inputs, table, cotangent, weight, result, flat, halves, arrive):
+    copies = []
+    for n, (source, place) in enumerate(((own, core[0]), (other, 1 - core[0]))):
+        copies.append(pltpu.make_async_copy(source, halves.at[place], arrive.at[n]))
+        copies[-1].start()
     center, inverse = read_norm(table.get()[...])
-    mean, cross = read_sums(sums.get()[...])
+    for copy in copies:
+        copy.wait()
+
+    def block(i, _):
+        assemble(i, lambda s: halves[s // 4, i * 4 + s % 4], weight.ref, flat)
+        return 0
+
+    for k in range(4):
+        lax.fori_loop(4 * k, 4 * k + 4, block, 0)
+        weight.send(k)
+
+    add = lambda i, s: s + halves[0, i, 96:, :].astype(F32) + halves[1, i, 96:, :].astype(F32)
+    sums = lax.fori_loop(0, 64, add, jnp.zeros((16, 128), F32))
+    mean, cross = read_sums(sums[SHARE - 96 :])
     slope, inputs, cotangent = slope.get(), inputs.get(), cotangent.get()
 
     def step(i, _):
@@ -303,7 +341,7 @@
     lax.fori_loop(0, FR * ROWS, step, 0)
 
 
-def adam_step(arrived, own, first, second, first_new, second_new):
+def adam_step(arrived, own, first, second, first_new, second_new, extra):
     gradient = jnp.zeros((PIECE, 128), F32)
     for k in range(4):
         ready = arrived.get(k)
@@ -316,15 +354,22 @@
     updated = own.get()[...].astype(F32) * (1.0 - learn_rate * decay_rate) - learn_rate * (one / first_fix) / (
         jnp.sqrt(two / second_fix) + adam_eps
     )
-    return jnp.concatenate([updated, jnp.zeros((PIECE - SHARE, 128), F32)], axis=0).astype(BF16)
+    return jnp.concatenate([updated, extra], axis=0).astype(BF16)
 
 
 def adam_two_kernel(arrived, own, first, second, first_new, second_new, part):
-    part.ref[0] = adam_step(arrived, own, first, second, first_new, second_new)
-
-
-def adam_one_kernel(arrived, own, first, second, first_new, second_new, spread):
-    piece = adam_step(arrived, own, first, second, first_new, second_new)
+    extra = jnp.zeros((PIECE - SHARE, 128), F32)
+    part.ref[0] = adam_step(arrived, own, first, second, first_new, second_new, extra)
+
+
+def adam_one_kernel(arrived, own, first, second, sums, first_new, second_new, spread):
+    rest = sums.get()[0:1, :]
+    terms = []
+    for _ in range(3):
+        terms.append(rest.astype(BF16).astype(F32))
+        rest = rest - terms[-1]
+    extra = jnp.concatenate([*terms, jnp.zeros((1, 128), F32)], axis=0)
+    piece = adam_step(arrived, own, first, second, first_new, second_new, extra)
 
     def copy(i, _):
         spread.ref[i] = piece
@@ -341,33 +386,6 @@
     rows = pl.ds(pl.multiple_of(block * BLOCK, BLOCK), BLOCK)
     weight[rows, 0:128] = flat[pl.ds(0, BLOCK, 2), :].astype(BF16)
     weight[rows, 128:256] = flat[pl.ds(1, BLOCK, 2), :].astype(BF16)
-
-
-def assemble_kernel(core, own, other, weight, flat, halves, arrive):
-    parts = 4
-    copies = [
-        [
-            pltpu.make_async_copy(
-                source.at[pl.ds(16 * k, 16)], halves.at[place, pl.ds(16 * k, 16)], arrive.at[n, k]
-            )
-            for n, (source, place) in enumerate(((own, core[0]), (other, 1 - core[0])))
-        ]
-        for k in range(parts)
-    ]
-    for pair in copies:
-        for copy in pair:
-            copy.start()
-
-    for k in range(parts):
-        for copy in copies[k]:
-            copy.wait()
-
-        def block(i, _):
-            assemble(i, lambda s: halves[s // 4, i * 4 + s % 4], weight.ref, flat)
-            return 0
-
-        lax.fori_loop(4 * k, 4 * k + 4, block, 0)
-        weight.send(k)
 
 
 def assemble_all_kernel(gathered, weight, flat):
@@ -453,7 +471,7 @@
 
     return pl.pallas_call(
         body,
-        out_shape=tuple(outs),
+        out_shape=tuple(jax.ShapeDtypeStruct(x.shape, x.dtype) for x in outs),
         in_specs=[pl.BlockSpec(memory_space=pltpu.SMEM)] * len(scalars)
         + [hbm if large[n] else vmem for n in range(count)],
         out_specs=tuple(hbm if large[n] else vmem for n in range(count, len(every))),
@@ -476,12 +494,22 @@
     return forward, [(j, i) for i, j in forward]
 
 
-def edge_rows(blocks):
+def edge_rows(last, leading, blocks):
     down, up = neighbours("rows")
-    last = jnp.concatenate([block[:, ROWS - 1] for block in blocks], axis=0)
-    leading = jnp.concatenate([block[:, 0] for block in blocks], axis=0)
     above, below = lax.ppermute(last, "rows", down), lax.ppermute(leading, "rows", up)
-    return [(above[k : k + FR], below[k : k + FR]) for k in range(0, FR * len(blocks), FR)]
+    return [(above[k : k + FR], below[k : k + FR]) for k in range(0, FR * blocks, FR)]
+
+
+def five_sides(block):
+    bands, steps = lax.axis_size("rows"), lax.axis_size("tm")
+    last, leading = block[:, ROWS - 1], block[:, 0]
+    _, backward = neighbours("tm")
+    frames = lax.ppermute(block, "tm", backward)
+    place = lambda t, r: t * bands + r
+    falls = [(place(t, r), place(t - 1, r + 1)) for t in range(1, steps) for r in range(bands - 1)]
+    rises = [(place(t, r), place(t - 1, r - 1)) for t in range(1, steps) for r in range(1, bands)]
+    corners = lax.ppermute(last, BOTH, falls), lax.ppermute(leading, BOTH, rises)
+    return ((frames, *corners), *edge_rows(last, leading, 1)[0])
 
 
 def join_edges(block, edges):
@@ -496,13 +524,36 @@
     return [edge.reshape(-1, C) for edge in edges]
 
 
+def over_bands(piece):
+    bands, here = lax.axis_size("rows"), lax.axis_index("rows")
+    turned = [piece]
+    for k in range(1, bands):
+        turned.append(lax.ppermute(piece, "rows", [(i, (i + k) % bands) for i in range(bands)]))
+    ordered = []
+    for band in range(bands):
+        choice = turned[0]
+        for k in range(1, bands):
+            choice = jnp.where((here - band) % bands == k, turned[k], choice)
+        ordered.append(choice)
+    return jnp.concatenate(ordered, axis=0)
+
+
 def cells(array):
     return array.reshape(FR, ROWS, COLS, C)
 
 
+def pair_kernel(kept, taken, result):
+    for k in range(4):
+        first, second = kept.get(k), taken.get(k)
+        for i in range(16 * k, 16 * k + 16):
+            result.ref[i] = (first[i].astype(F32) + second[i].astype(F32)).astype(BF16)
+        result.send(k)
+
+
 def pair_sum(kept, given):
     taken = lax.ppermute(given, BOTH, CORE_PAIRS)
-    return (kept.astype(F32) + taken.astype(F32)).astype(BF16)
+    (total,) = run(pair_kernel, (), (kept, taken), (kept,), parts={0: 4, 1: 4, 2: 4})
+    return total
 
 
 def over_chips(pieces):
@@ -551,12 +602,15 @@
             (),
             (*arrived, own_share(weight), first.reshape(SHARE, 128), second.reshape(SHARE, 128), *more),
             (moment_type, moment_type, *part_types),
-            parts={0: 4, 6: 4} if part_types[0] is piece_type else {0: 4},
+            parts={0: 4, 7: 4} if part_types[0] is piece_type else {0: 4},
         )
         return part, first_new.reshape(-1), second_new.reshape(-1)
 
     forward, backward = neighbours("tm")
-    edges_in, edges_cot = edge_rows((inputs, cotangent))
+    first_edges = [
+        jnp.concatenate([block[:, at] for block in (inputs, cotangent)], axis=0) for at in (ROWS - 1, 0)
+    ]
+    edges_in, edges_cot = edge_rows(*first_edges, 2)
     (row_one,) = run(stats_kernel, (), (flat_inputs,), (row_type,))
     frames_in = frame_halo(after(inputs, row_one), edges_in, forward)
     frames_cot = frame_halo(after(cotangent, row_one), edges_cot, backward)
@@ -568,12 +622,19 @@
         (patch_type, act_type, row_type),
     )
     table_two = everyone(row_two)
+    back_two, patch_cot = run(
+        back_two_kernel,
+        (ok_after,),
+        (after(flat_cot, row_two), *flat(edges_cot), frames_cot, weight_two),
+        (wide_type, patch_type),
+    )
     slope_two, row_three, kept_two, given_two = run(
         second_kernel,
-        (ok_after, core),
-        (flat_cot, *flat(edges_cot), frames_cot, weight_two, middle, table_two, gain_two),
+        (core,),
+        (middle, back_two, patch_cot, table_two, gain_two),
         (wide_type, row_type, piece_type, piece_type),
-        (patch_scratch, pltpu.VMEM((CELLS, C), F32), pltpu.VMEM((CELLS, C), BF16), whole_scratch, flat_scratch),
+        (pltpu.VMEM((CELLS, C), BF16), whole_scratch, flat_scratch),
+        parts={2: 4},
     )
     table_three = everyone(row_three)
     pair_two = pair_sum(kept_two, given_two)
@@ -585,8 +646,7 @@
         (whole_scratch, flat_scratch),
         parts={2: 4},
     )
-    edges_grad = edge_rows((cells(mid_grad),))[0]
-    frames_grad = frame_halo(cells(mid_grad), edges_grad, backward)
+    frames_grad, *edges_grad = five_sides(cells(mid_grad))
     arrived_two = over_chips(pair_two)
     part_two, new_first_two, new_second_two = update(
         adam_two_kernel,
@@ -597,52 +657,48 @@
         (),
         (shape((1, PIECE, 128), BF16),),
     )
-    gathered_two = lax.all_gather(part_two[0], BOTH, axis=0, tiled=True)
-    pair_one = pair_sum(kept_one, after(given_one, part_two[0]))
+    gathered_two = lax.all_gather(over_bands(part_two[0]), "tm", axis=0, tiled=True)
+    pair_one = after(pair_sum(kept_one, after(given_one, arrived_two, *frames_grad, *edges_grad)), part_two[0])
     arrived_one = over_chips(pair_one)
-    (part_one,), new_first_one, new_second_one = update(
-        adam_one_kernel,
-        (after(arrived_one, frames_grad),),
-        weight_one,
-        first_one,
-        second_one,
-        (),
-        (piece_type,),
-    )
     slope_one, row_four = run(
         back_one_kernel,
         (ok_after,),
         (
-            after(mid_grad, part_one),
+            after(mid_grad, pair_one),
             *flat(edges_grad),
-            frames_grad,
+            *flat(frames_grad),
             weight_one,
             flat_inputs,
             table_one,
             gain_one,
         ),
-        (wide_type, row_type),
+        (wide_type, shape((8, 128), F32)),
         (patch_scratch, pltpu.VMEM((CELLS, C), F32)),
     )
+    (part_one,), new_first_one, new_second_one = update(
+        adam_one_kernel,
+        (arrived_one,),
+        weight_one,
+        first_one,
+        second_one,
+        (row_four,),
+        (piece_type,),
+    )
     own_one = over_chips(part_one)
-    other_one = lax.ppermute(after(own_one, row_four), BOTH, CORE_PAIRS)
-    table_four = everyone(after(row_four, own_one))
-    (input_grad,) = run(
-        final_kernel, (), (slope_one, flat_inputs, table_one, table_four, flat_cot), (act_type,)
-    )
+    other_one = lax.ppermute(own_one, BOTH, CORE_PAIRS)
     weight_type = shape((27 * C, C), BF16)
     assemble_scratch = pltpu.VMEM((2 * BLOCK + 8, 128), F32)
-    (new_weight_one,) = run(
-        assemble_kernel,
-        (core,),
-        (own_one, other_one),
-        (weight_type,),
-        (assemble_scratch, pltpu.VMEM((2, 64, PIECE, 128), BF16), pltpu.SemaphoreType.DMA((2, 4))),
-        parts={2: 4},
-        raw=(0, 1),
-    )
     (new_weight_two,) = run(
         assemble_all_kernel, (), (gathered_two,), (weight_type,), (assemble_scratch,), parts={0: 4, 1: 4}
+    )
+    new_weight_one, input_grad = run(
+        last_kernel,
+        (core,),
+        (own_one, other_one, slope_one, flat_inputs, table_one, flat_cot),
+        (weight_type, act_type),
+        (assemble_scratch, pltpu.VMEM((2, 64, PIECE, 128), BF16), pltpu.SemaphoreType.DMA((2,))),
+        parts={6: 4},
+        raw=(0, 1),
     )
     return (
         cells(input_grad),

time: 272 us -> 255 us (0.938)
  waiting for transfers between devices: 85.5 us -> 32.9 us
  blocking collectives: 14.9 us -> 35.4 us
  Pallas kernels: 72.7 us -> 83.2 us
  starting transfers between devices: 62.3 us -> 69.4 us
  other arithmetic: 7.96 us -> 2.87 us
    all_to_all x1, blocking collectives: 14.9 us -> 35.4 us  [over_chips(): lax.all_to_all(pieces, BOTH, 0, 0, axis_index_groups=CHIP_GROUPS, tiled=T...]
    ppermute x2, waiting for transfers between devices: 16.8 us -> 0.01 us  [edge_rows(): lax.ppermute(last, 'rows', down)]
    all_to_all x3 -> x2, waiting for transfers between devices: 27.7 us -> 12.9 us  [over_chips(): lax.all_to_all(pieces, BOTH, 0, 0, axis_index_groups=CHIP_GROUPS, tiled=T...]
    ppermute x1 -> x7, starting transfers between devices: 0.01 us -> 11.6 us  [the longest x3 4.52 us: over_bands(): lax.ppermute(piece, 'rows', [(i, (i + k) % bands) for i in range(bands)])]
    pallas_call x10 -> x12, Pallas kernels: 72.7 us -> 83.2 us  [run(): pl.pallas_call(body, out_shape=tuple((jax.ShapeDtypeStruct(x.shape, x.dty...]
    all_to_all x3, waiting for transfers between devices: 24.5 us -> 14.5 us  [everyone(): return lax.all_to_all(row, BOTH, 0, 0, tiled=True)]
    ppermute x3 -> x2, waiting for transfers between devices: 9.6 us -> 0.01 us  [frame_halo(): return lax.ppermute(join_edges(block, edges), 'tm', perm).reshape(-1, C)]
    convert_element_type x2 -> x0, other arithmetic: 6.42 us -> none  [pair_sum(): return (kept.astype(F32) + taken.astype(F32)).astype(BF16)]
  transfers between devices with their start and end apart: 17 -> 21, of which waited for: 10 -> 8; matrix products, arithmetic and copies ran while one was open for 5% -> 3% of each run, Pallas kernels for 18% -> 25%
where the time goes in v4:
time: 255 us; the launch traced here: 253 us
  Pallas kernels  83.2 us (33%)
  starting transfers between devices  69.4 us (27%)
  blocking collectives  35.4 us (14%)
  waiting for transfers between devices  32.9 us (13%)
  local copies, waits for them, and re-layouts  14.8 us (6%)
  between operations  14.5 us (6%)
  other arithmetic  2.87 us (1%)
    pallas_call x12, Pallas kernels, run(): pl.pallas_call(body, out_shape=tuple((jax.ShapeDtypeStruct(x.shape, x.dty...  83.2 us
    all_to_all x1, blocking collectives, over_chips(): lax.all_to_all(pieces, BOTH, 0, 0, axis_index_groups=CHIP_GROUPS, tiled=T...  35.4 us
    all_to_all x3, starting transfers between devices, everyone(): return lax.all_to_all(row, BOTH, 0, 0, tiled=True)  23.3 us
    all_to_all x2, starting transfers between devices, over_chips(): lax.all_to_all(pieces, BOTH, 0, 0, axis_index_groups=CHIP_GROUPS, tiled=T...  15.8 us
    all_to_all x3, waiting for transfers between devices, everyone(): return lax.all_to_all(row, BOTH, 0, 0, tiled=True)  14.5 us
    all_to_all x2, waiting for transfers between devices, over_chips(): lax.all_to_all(pieces, BOTH, 0, 0, axis_index_groups=CHIP_GROUPS, tiled=T...  12.9 us
    unnamed x32, local copies, waits for them, and re-layouts  7.72 us
    ppermute x2, starting transfers between devices, edge_rows(): lax.ppermute(last, 'rows', down)  7.05 us
  transfers between devices with their start and end apart: 21, of which 8 were waited for; matrix products, arithmetic and copies ran while one was open for 3% of the time, Pallas kernels for 25%

profile of v4, /device:TPU:1, one launch (start us, length us, event | category | flops | bytes accessed | tf_op | source)
XLA Modules:
  0.0 253.1 jit_solution(15114683330273698914)
XLA Ops:
  7.2 1.0 slice_bitcast_fusion.3
  8.2 0.9 slice_bitcast_fusion.2
  9.2 4.0 %collective-permute-start = (bf16[4,80,256]{2,1,0:T(8,128)(2,1)S(1)}, bf16[4,80,256]{2,1,0:T(8,128)(2,1)S(1)}, u32[]{:S(2)}, u32[]{:S(2)}) collective-permute-start(bf16[4,80,256]{2,1,0:T(8,128)(2,1)S(1)} %pad_maximum_fusion.2), channel_id=1, source_target_pairs={{0,1},{1,2},{2,3},{4,5},{5,6},{6,7},{8,9},{9,10},{10,11},{12,13},{... | collective-permute-start | bytes 491528 | tf_op jit(solution)/shard_map/ppermute | solution.py:499
  13.2 1.4 collective-permute-start.1
  14.6 3.0 %shard_map.153 = f32[128,128]{1,0:T(8,128)} custom-call(bf16[1280,256]{1,0:T(8,128)(2,1)} %bitcast.78), custom_call_target="tpu_custom_call" | custom-call | flops 1024 | bytes 1024 | tf_op jit(solution)/shard_map/pallas_call | solution.py:472
  17.6 0.7 slice_bitcast_fusion.7
  18.3 1.7 collective-permute-done.1
  19.9 0.7 slice_bitcast_fusion.6
  20.7 5.0 %collective-permute-start.2 = (bf16[2,10,80,256]{3,2,1,0:T(8,128)(2,1)S(1)}, bf16[2,10,80,256]{3,2,1,0:T(8,128)(2,1)}, u32[]{:S(2)}, u32[]{:S(2)}) collective-permute-start(bf16[2,10,80,256]{3,2,1,0:T(8,128)(2,1)S(1)} %pad_maximum_fusion), channel_id=1, source_target_pairs={{0,4},{4,8},{8,12},{12,16},{16,20},{20,24},{24,28},{28,32},{32,36}... | collective-permute-start | bytes 2457608 | tf_op jit(solution)/shard_map/ppermute | solution.py:520
  25.7 0.1 pad_maximum_fusion.1
  25.8 1.9 collective-permute-start.3
  27.8 10.3 %all-to-all-start = ((f32[128,1,128]{2,1,0:T(1,128)}), f32[128,1,128]{2,1,0:T(1,128)S(1)}, u32[]{:S(2)}, u32[]{:S(2)}) async-start(f32[128,1,128]{2,1,0:T(1,128)} %bitcast.98), calls=%async_computation | async-start | bytes 131072 | tf_op jit(solution)/shard_map/all_to_all | solution.py:485
  38.0 0.6 maximum_maximum_fusion.refs_0_
  38.6 9.0 %all-to-all-done = f32[128,1,128]{2,1,0:T(1,128)S(1)} async-done(((f32[128,1,128]{2,1,0:T(1,128)}), f32[128,1,128]{2,1,0:T(1,128)S(1)}, u32[]{:S(2)}, u32[]{:S(2)}) %all-to-all-start) | async-done | bytes 65568 | tf_op jit(solution)/shard_map/all_to_all | solution.py:485
  47.6 0.6 copy-done.7
  48.2 10.5 %shard_map.154 = (bf16[3200,768]{1,0:T(8,128)(2,1)}, bf16[1280,256]{1,0:T(8,128)(2,1)}, f32[128,128]{1,0:T(8,128)}) custom-call(f32[3]{0:T(128)} %maximum_maximum_fusion.refs_0_, bf16[1280,256]{1,0:T(8,128)(2,1)} %bitcast.79, bf16[160,256]{1,0:T(8,128)(2,1)} %bitcast.95, bf16[160,256]{1,0:T(8,128)(2,1)} %bitcast.96, bf16[1600,256]{1,0:T(8,128)(2,1)} %bitcast.15.refs_4_, ...), custom_call_target="tpu_custom_call" | custom-call | flops 1024 | bytes 1024 | tf_op jit(solution)/shard_map/pallas_call | solution.py:472
  58.8 4.4 %all-to-all-start.1 = ((f32[128,1,128]{2,1,0:T(1,128)}), f32[128,1,128]{2,1,0:T(1,128)S(1)}, u32[]{:S(2)}, u32[]{:S(2)}) async-start(f32[128,1,128]{2,1,0:T(1,128)} %bitcast.103), calls=%async_computation.1 | async-start | bytes 131072 | tf_op jit(solution)/shard_map/all_to_all | solution.py:485
  63.2 0.6 maximum_maximum_fusion.1.refs_0_
  63.8 0.9 copy-done.8
  64.7 9.4 %shard_map.155 = (f32[1280,256]{1,0:T(8,128)}, bf16[3200,768]{1,0:T(8,128)(2,1)}) custom-call(f32[3]{0:T(128)} %maximum_maximum_fusion.1.refs_0_, bf16[1280,256]{1,0:T(8,128)(2,1)} %bitcast.82, bf16[160,256]{1,0:T(8,128)(2,1)} %bitcast.93, bf16[160,256]{1,0:T(8,128)(2,1)} %bitcast.94, bf16[1600,256]{1,0:T(8,128)(2,1)} %bitcast.89, bf16[6912,256]{1,0:T(8,128)(2,1)} %refs_5_.1), custom_call_target="tpu_custom_call" | custom-call | flops 1024 | bytes 1024 | tf_op jit(solution)/shard_map/pallas_call | solution.py:472
  74.1 0.6 copy-done.10
  74.7 13.1 %shard_map.156 = (f32[1280,256]{1,0:T(8,128)}, f32[128,128]{1,0:T(8,128)}, bf16[64,112,128]{2,1,0:T(8,128)(2,1)}, bf16[64,112,128]{2,1,0:T(8,128)(2,1)}) custom-call(s32[1]{0:T(128)} %bitcast.refs_0_, bf16[1280,256]{1,0:T(8,128)(2,1)} %get-tuple-element.38.refs_1_.refs_2_, f32[1280,256]{1,0:T(8,128)} %get-tuple-element.42.refs_2_, ...), custom_call_target="tpu_custom_call" | custom-call | flops 1024 | bytes 1024 | tf_op jit(solution)/shard_map/pallas_call | solution.py:472
  87.8 1.3 collective-permute-start.4
  89.1 8.7 %all-to-all-start.2 = ((f32[128,1,128]{2,1,0:T(1,128)}), f32[128,1,128]{2,1,0:T(1,128)S(1)}, u32[]{:S(2)}, u32[]{:S(2)}) async-start(f32[128,1,128]{2,1,0:T(1,128)} %bitcast.104), calls=%async_computation.2 | async-start | bytes 131072 | tf_op jit(solution)/shard_map/all_to_all | solution.py:485
  97.8 1.2 copy-done.6
  99.1 3.0 %shard_map.157 = bf16[64,112,128]{2,1,0:T(8,128)(2,1)} custom-call(bf16[64,112,128]{2,1,0:T(8,128)(2,1)} %get-tuple-element.45.refs_0_, bf16[64,112,128]{2,1,0:T(8,128)(2,1)} %copy-done.6), custom_call_target="tpu_custom_call" | custom-call | flops 1024 | bytes 1024 | tf_op jit(solution)/shard_map/pallas_call | solution.py:472
  102.0 5.5 %all-to-all-done.2 = f32[128,1,128]{2,1,0:T(1,128)S(1)} async-done(((f32[128,1,128]{2,1,0:T(1,128)}), f32[128,1,128]{2,1,0:T(1,128)S(1)}, u32[]{:S(2)}, u32[]{:S(2)}) %all-to-all-start.2) | async-done | bytes 65568 | tf_op jit(solution)/shard_map/all_to_all | solution.py:485
  107.5 0.6 copy-done.11
  108.1 5.1 %all-to-all-start.3 = ((bf16[64,112,128]{2,1,0:T(8,128)(2,1)}), bf16[64,112,128]{2,1,0:T(8,128)(2,1)S(1)}, u32[]{:S(2)}, u32[]{:S(2)}) async-start(bf16[64,112,128]{2,1,0:T(8,128)(2,1)} %shard_map.157), calls=%async_computation.3 | async-start | bytes 3670016 | tf_op jit(solution)/shard_map/all_to_all | solution.py:560
  113.2 0.3 all-gather.2.cloned.1.call-start
  113.5 12.5 %shard_map.158 = (bf16[1280,256]{1,0:T(8,128)(2,1)}, bf16[64,112,128]{2,1,0:T(8,128)(2,1)}, bf16[64,112,128]{2,1,0:T(8,128)(2,1)}) custom-call(s32[1]{0:T(128)} %bitcast.refs_0_, f32[1280,256]{1,0:T(8,128)} %get-tuple-element.47.refs_1_, bf16[1280,256]{1,0:T(8,128)(2,1)} %get-tuple-element.38.refs_1_.refs_2_, bf16[3200,768]{1,0:T(8,128)(2,1)} %get-tuple-element.48.refs_3_, ...), custom_call_target="tpu_custom_call" | custom-call | flops 1024 | bytes 1024 | tf_op jit(solution)/shard_map/pallas_call | solution.py:472
  126.0 2.5 %collective-permute-start.5 = (bf16[2,8,80,256]{3,2,1,0:T(8,128)(2,1)}, bf16[2,8,80,256]{3,2,1,0:T(8,128)(2,1)S(1)}, u32[]{:S(2)}, u32[]{:S(2)}) collective-permute-start(bf16[2,8,80,256]{3,2,1,0:T(8,128)(2,1)} %bitcast.87), channel_id=1, source_target_pairs={{4,0},{8,4},{12,8},{16,12},{20,16},{24,20},{28,24},{32,28},{36,32}... | collective-permute-start | bytes 1966088 | tf_op jit(solution)/shard_map/ppermute | solution.py:507
  128.6 0.9 slice_bitcast_fusion
  129.5 2.5 collective-permute-start.6
  132.0 3.1 %collective-permute-start.8 = (bf16[2,80,256]{2,1,0:T(8,128)(2,1)S(1)}, bf16[2,80,256]{2,1,0:T(8,128)(2,1)S(1)}, u32[]{:S(2)}, u32[]{:S(2)}) collective-permute-start(bf16[2,80,256]{2,1,0:T(8,128)(2,1)S(1)} %get-tuple-element.68), channel_id=1, source_target_pairs={{0,1},{1,2},{2,3},{4,5},{5,6},{6,7},{8,9},{9,10},{10,11},{12,13},{... | collective-permute-start | bytes 245768 | tf_op jit(solution)/shard_map/ppermute | solution.py:499
  135.1 1.3 collective-permute-start.7
  136.4 1.3 collective-permute-start.9
  137.7 0.8 constant_dynamic-slice_fusion.1
  138.5 0.6 reshape.116.refs_1_
  139.1 0.3 all-to-all-done.3.refs_0_
  139.4 1.3 copy-done.1
  140.7 3.1 %shard_map.160 = (f32[108,128]{1,0:T(8,128)}, f32[108,128]{1,0:T(8,128)}, bf16[1,112,128]{2,1,0:T(8,128)(2,1)}) custom-call(bf16[64,112,128]{2,1,0:T(8,128)(2,1)} %copy-done.1, bf16[108,128]{1,0:T(8,128)(2,1)} %reshape.116.refs_1_, f32[108,128]{1,0:T(8,128)} %bitcast.105, f32[108,128]{1,0:T(8,128)} %bitcast.106), custom_call_target="tpu_custom_call" | custom-call | flops 1024 | bytes 1024 | tf_op jit(solution)/shard_map/pallas_call | solution.py:472
  143.9 2.7 %collective-permute-start.12 = (bf16[1,112,128]{2,1,0:T(8,128)(2,1)}, bf16[1,112,128]{2,1,0:T(8,128)(2,1)S(1)}, u32[]{:S(2)}, u32[]{:S(2)}) collective-permute-start(bf16[1,112,128]{2,1,0:T(8,128)(2,1)} %get-tuple-element.55), channel_id=1, source_target_pairs={{0,3},{1,0},{2,1},{3,2},{4,7},{5,4},{6,5},{7,6},{8,11},{9,8},{10,9... | collective-permute-start | bytes 86024 | tf_op jit(solution)/shard_map/ppermute | solution.py:531
  146.6 1.1 collective-permute-start.13
  147.7 0.8 collective-permute-start.14
  148.4 0.4 collective-permute-start.10
  148.9 2.2 collective-permute-done.13
  151.0 1.2 collective-permute-done.14
  152.2 0.8 select_select_fusion.3
  153.0 0.7 pad_maximum_fusion.4
  153.7 1.2 copy-done.5
  154.9 3.0 %shard_map.159 = bf16[64,112,128]{2,1,0:T(8,128)(2,1)} custom-call(bf16[64,112,128]{2,1,0:T(8,128)(2,1)} %get-tuple-element.50.refs_0_, bf16[64,112,128]{2,1,0:T(8,128)(2,1)} %copy-done.5), custom_call_target="tpu_custom_call" | custom-call | flops 1024 | bytes 1024 | tf_op jit(solution)/shard_map/pallas_call | solution.py:472
  157.9 10.7 %all-to-all-start.4 = ((bf16[64,112,128]{2,1,0:T(8,128)(2,1)}), bf16[64,112,128]{2,1,0:T(8,128)(2,1)S(1)}, u32[]{:S(2)}, u32[]{:S(2)}) async-start(bf16[64,112,128]{2,1,0:T(8,128)(2,1)} %shard_map.159), calls=%async_computation.4 | async-start | bytes 3670016 | tf_op jit(solution)/shard_map/all_to_all | solution.py:560
  168.6 0.8 constant_dynamic-slice_fusion
  169.4 0.6 reshape.119.refs_1_
  170.0 11.0 %shard_map.161 = (f32[1280,256]{1,0:T(8,128)}, f32[8,128]{1,0:T(8,128)}) custom-call(f32[3]{0:T(128)} %maximum_maximum_fusion.1.refs_0_, bf16[1280,256]{1,0:T(8,128)(2,1)} %get-tuple-element.57.refs_1_, bf16[160,256]{1,0:T(8,128)(2,1)} %bitcast.100, bf16[160,256]{1,0:T(8,128)(2,1)} %bitcast.102, bf16[1280,256]{1,0:T(8,128)(2,1)} %bitcast.90, ...), custom_call_target="tpu_custom_call" | custom-call | flops 1024 | bytes 1024 | tf_op jit(solution)/shard_map/pallas_call | solution.py:472
  181.1 12.6 %all-to-all-done.4.refs_0_ = bf16[64,112,128]{2,1,0:T(8,128)(2,1)S(1)} async-done(((bf16[64,112,128]{2,1,0:T(8,128)(2,1)}), bf16[64,112,128]{2,1,0:T(8,128)(2,1)S(1)}, u32[]{:S(2)}, u32[]{:S(2)}) %all-to-all-start.4) | async-done | bytes 1835040 | tf_op jit(solution)/shard_map/all_to_all | solution.py:560
  193.7 1.2 copy-done.2
  194.9 4.5 %shard_map.162 = (f32[108,128]{1,0:T(8,128)}, f32[108,128]{1,0:T(8,128)}, bf16[64,112,128]{2,1,0:T(8,128)(2,1)}) custom-call(bf16[64,112,128]{2,1,0:T(8,128)(2,1)} %copy-done.2, bf16[108,128]{1,0:T(8,128)(2,1)} %reshape.119.refs_1_, f32[108,128]{1,0:T(8,128)} %bitcast.107, f32[108,128]{1,0:T(8,128)} %bitcast.108, f32[8,128]{1,0:T(8,128)} %get-tuple-element.58.refs_4_), custom_call_target="tpu_custom_call" | custom-call | flops 1024 | bytes 1024 | tf_op jit(solution)/shard_map/pallas_call | solution.py:472
  199.4 35.4 %all_to_all.48.refs_1_ = bf16[64,112,128]{2,1,0:T(8,128)(2,1)S(1)} all-to-all(bf16[64,112,128]{2,1,0:T(8,128)(2,1)} %get-tuple-element.59), channel_id=1, replica_groups={{0,1,2,3,8,9,10,11,16,17,18,19,24,25,26,27,32,33,34,35,40,41,42,43,48,4..., dimensions={0} | all-to-all | bytes 3670016 | tf_op jit(solution)/shard_map/all_to_all | solution.py:560
  234.8 0.8 collective-permute-start.11
  235.6 0.5 all-gather.2.cloned.1.call-done.refs_0_
  236.1 3.3 %shard_map.164 = bf16[6912,256]{1,0:T(8,128)(2,1)} custom-call(bf16[128,112,128]{2,1,0:T(8,128)(2,1)} %all-gather.2.cloned.1.call-done.refs_0_), custom_call_target="tpu_custom_call" | custom-call | flops 1024 | bytes 1024 | tf_op jit(solution)/shard_map/pallas_call | solution.py:472
  239.4 6.8 %shard_map.163 = (bf16[6912,256]{1,0:T(8,128)(2,1)}, bf16[1280,256]{1,0:T(8,128)(2,1)}) custom-call(s32[1]{0:T(128)} %bitcast.refs_0_, bf16[64,112,128]{2,1,0:T(8,128)(2,1)} %copy-done.3, bf16[64,112,128]{2,1,0:T(8,128)(2,1)} %collective-permute-done.11.refs_2_, f32[1280,256]{1,0:T(8,128)} %get-tuple-element.60.refs_3_, bf16[1280,256]{1,0:T(8,128)(2,1)} %bitcast.81, ...), custom_call_target="tpu_custom_call" | custom-call | flops 1024 | bytes 1024 | tf_op jit(solution)/shard_map/pallas_call | solution.py:472
  (41 shorter events, 0.2 us)
Async XLA Ops:
  7.2 13.5 %copy-start = (bf16[2,8,80,256]{3,2,1,0:T(8,128)(2,1)S(1)}, bf16[2,8,80,256]{3,2,1,0:T(8,128)(2,1)}, u32[]{:S(2)}) copy-start(bf16[2,8,80,256]{3,2,1,0:T(8,128)(2,1)} %param.10) | copy-start | bytes 1966084
  9.2 8.4 %collective-permute-start = (bf16[4,80,256]{2,1,0:T(8,128)(2,1)S(1)}, bf16[4,80,256]{2,1,0:T(8,128)(2,1)S(1)}, u32[]{:S(2)}, u32[]{:S(2)}) collective-permute-start(bf16[4,80,256]{2,1,0:T(8,128)(2,1)S(1)} %pad_maximum_fusion.2), channel_id=1, source_target_pairs={{0,1},{1,2},{2,3},{4,5},{5,6},{6,7},{8,9},{9,10},{10,11},{12,13},{... | collective-permute-start | bytes 491528 | tf_op jit(solution)/shard_map/ppermute | solution.py:499
  13.1 12.6 %copy-start.4 = (bf16[2,8,80,256]{3,2,1,0:T(8,128)(2,1)S(1)}, bf16[2,8,80,256]{3,2,1,0:T(8,128)(2,1)}, u32[]{:S(2)}) copy-start(bf16[2,8,80,256]{3,2,1,0:T(8,128)(2,1)} %param.11) | copy-start | bytes 1966084
  13.2 6.8 %collective-permute-start.1 = (bf16[4,80,256]{2,1,0:T(8,128)(2,1)S(1)}, bf16[4,80,256]{2,1,0:T(8,128)(2,1)S(1)}, u32[]{:S(2)}, u32[]{:S(2)}) collective-permute-start(bf16[4,80,256]{2,1,0:T(8,128)(2,1)S(1)} %pad_maximum_fusion.3), channel_id=1, source_target_pairs={{1,0},{2,1},{3,2},{5,4},{6,5},{7,6},{9,8},{10,9},{11,10},{13,12},{... | collective-permute-start | bytes 491528 | tf_op jit(solution)/shard_map/ppermute | solution.py:499
  20.7 26.9 %collective-permute-start.2 = (bf16[2,10,80,256]{3,2,1,0:T(8,128)(2,1)S(1)}, bf16[2,10,80,256]{3,2,1,0:T(8,128)(2,1)}, u32[]{:S(2)}, u32[]{:S(2)}) collective-permute-start(bf16[2,10,80,256]{3,2,1,0:T(8,128)(2,1)S(1)} %pad_maximum_fusion), channel_id=1, source_target_pairs={{0,4},{4,8},{8,12},{12,16},{16,20},{20,24},{24,28},{28,32},{32,36}... | collective-permute-start | bytes 2457608 | tf_op jit(solution)/shard_map/ppermute | solution.py:520
  25.8 38.0 %collective-permute-start.3 = (bf16[2,10,80,256]{3,2,1,0:T(8,128)(2,1)S(1)}, bf16[2,10,80,256]{3,2,1,0:T(8,128)(2,1)S(1)}, u32[]{:S(2)}, u32[]{:S(2)}) collective-permute-start(bf16[2,10,80,256]{3,2,1,0:T(8,128)(2,1)S(1)} %pad_maximum_fusion.1), channel_id=1, source_target_pairs={{4,0},{8,4},{12,8},{16,12},{20,16},{24,20},{28,24},{32,28},{36,32}... | collective-permute-start | bytes 2457608 | tf_op jit(solution)/shard_map/ppermute | solution.py:520
  27.8 19.9 %all-to-all-start = ((f32[128,1,128]{2,1,0:T(1,128)}), f32[128,1,128]{2,1,0:T(1,128)S(1)}, u32[]{:S(2)}, u32[]{:S(2)}) async-start(f32[128,1,128]{2,1,0:T(1,128)} %bitcast.98), calls=%async_computation | async-start | bytes 131072 | tf_op jit(solution)/shard_map/all_to_all | solution.py:485
  47.6 0.6 copy-start.7
  58.8 15.3 %all-to-all-start.1 = ((f32[128,1,128]{2,1,0:T(1,128)}), f32[128,1,128]{2,1,0:T(1,128)S(1)}, u32[]{:S(2)}, u32[]{:S(2)}) async-start(f32[128,1,128]{2,1,0:T(1,128)} %bitcast.103), calls=%async_computation.1 | async-start | bytes 131072 | tf_op jit(solution)/shard_map/all_to_all | solution.py:485
  63.8 0.9 copy-start.8
  74.1 0.6 copy-start.10
  87.8 10.0 %collective-permute-start.4 = (bf16[64,112,128]{2,1,0:T(8,128)(2,1)}, bf16[64,112,128]{2,1,0:T(8,128)(2,1)S(1)}, u32[]{:S(2)}, u32[]{:S(2)}) collective-permute-start(bf16[64,112,128]{2,1,0:T(8,128)(2,1)} %get-tuple-element.46), channel_id=1, source_target_pairs={{0,4},{1,5},{2,6},{3,7},{4,0},{5,1},{6,2},{7,3},{8,12},{9,13},{10,... | collective-permute-start | bytes 5505032 | tf_op jit(solution)/shard_map/ppermute | solution.py:554
  89.1 18.4 %all-to-all-start.2 = ((f32[128,1,128]{2,1,0:T(1,128)}), f32[128,1,128]{2,1,0:T(1,128)S(1)}, u32[]{:S(2)}, u32[]{:S(2)}) async-start(f32[128,1,128]{2,1,0:T(1,128)} %bitcast.104), calls=%async_computation.2 | async-start | bytes 131072 | tf_op jit(solution)/shard_map/all_to_all | solution.py:485
  97.8 1.2 copy-start.6
  107.5 0.6 copy-start.11
  108.1 31.3 %all-to-all-start.3 = ((bf16[64,112,128]{2,1,0:T(8,128)(2,1)}), bf16[64,112,128]{2,1,0:T(8,128)(2,1)S(1)}, u32[]{:S(2)}, u32[]{:S(2)}) async-start(bf16[64,112,128]{2,1,0:T(8,128)(2,1)} %shard_map.157), calls=%async_computation.3 | async-start | bytes 3670016 | tf_op jit(solution)/shard_map/all_to_all | solution.py:560
  113.2 122.9 %all-gather.2.cloned.1.call-start = ((), (), s32[]{:S(2)}) async-start(), calls=%async_computation.6 | async-start | bytes 3784704 | tf_op jit(solution)/shard_map/all_gather | solution.py:660
  126.0 22.4 %collective-permute-start.5 = (bf16[2,8,80,256]{3,2,1,0:T(8,128)(2,1)}, bf16[2,8,80,256]{3,2,1,0:T(8,128)(2,1)S(1)}, u32[]{:S(2)}, u32[]{:S(2)}) collective-permute-start(bf16[2,8,80,256]{3,2,1,0:T(8,128)(2,1)} %bitcast.87), channel_id=1, source_target_pairs={{4,0},{8,4},{12,8},{16,12},{20,16},{24,20},{28,24},{32,28},{36,32}... | collective-permute-start | bytes 1966088 | tf_op jit(solution)/shard_map/ppermute | solution.py:507
  129.5 14.4 %collective-permute-start.6 = (bf16[2,80,256]{2,1,0:T(8,128)(2,1)S(1)}, bf16[2,80,256]{2,1,0:T(8,128)(2,1)S(1)}, u32[]{:S(2)}, u32[]{:S(2)}) collective-permute-start(bf16[2,80,256]{2,1,0:T(8,128)(2,1)S(1)} %get-tuple-element.68), channel_id=1, source_target_pairs={{4,1},{5,2},{6,3},{8,5},{9,6},{10,7},{12,9},{13,10},{14,11},{16,13... | collective-permute-start | bytes 245768 | tf_op jit(solution)/shard_map/ppermute | solution.py:511
  132.0 15.7 %collective-permute-start.8 = (bf16[2,80,256]{2,1,0:T(8,128)(2,1)S(1)}, bf16[2,80,256]{2,1,0:T(8,128)(2,1)S(1)}, u32[]{:S(2)}, u32[]{:S(2)}) collective-permute-start(bf16[2,80,256]{2,1,0:T(8,128)(2,1)S(1)} %get-tuple-element.68), channel_id=1, source_target_pairs={{0,1},{1,2},{2,3},{4,5},{5,6},{6,7},{8,9},{9,10},{10,11},{12,13},{... | collective-permute-start | bytes 245768 | tf_op jit(solution)/shard_map/ppermute | solution.py:499
  135.1 11.5 %collective-permute-start.7 = (bf16[2,80,256]{2,1,0:T(8,128)(2,1)S(1)}, bf16[2,80,256]{2,1,0:T(8,128)(2,1)S(1)}, u32[]{:S(2)}, u32[]{:S(2)}) collective-permute-start(bf16[2,80,256]{2,1,0:T(8,128)(2,1)S(1)} %get-tuple-element.67), channel_id=1, source_target_pairs={{5,0},{6,1},{7,2},{9,4},{10,5},{11,6},{13,8},{14,9},{15,10},{17,12... | collective-permute-start | bytes 245768 | tf_op jit(solution)/shard_map/ppermute | solution.py:511
  136.4 12.0 %collective-permute-start.9 = (bf16[2,80,256]{2,1,0:T(8,128)(2,1)S(1)}, bf16[2,80,256]{2,1,0:T(8,128)(2,1)S(1)}, u32[]{:S(2)}, u32[]{:S(2)}) collective-permute-start(bf16[2,80,256]{2,1,0:T(8,128)(2,1)S(1)} %get-tuple-element.67), channel_id=1, source_target_pairs={{1,0},{2,1},{3,2},{5,4},{6,5},{7,6},{9,8},{10,9},{11,10},{13,12},{... | collective-permute-start | bytes 245768 | tf_op jit(solution)/shard_map/ppermute | solution.py:499
  139.4 1.3 copy-start.1
  143.9 14.0 %copy-start.12 = (bf16[2,80,256]{2,1,0:T(8,128)(2,1)}, bf16[2,80,256]{2,1,0:T(8,128)(2,1)S(1)}, u32[]{:S(2)}) copy-start(bf16[2,80,256]{2,1,0:T(8,128)(2,1)S(1)} %collective-permute-done.6) | copy-start | bytes 245764
  143.9 5.0 %collective-permute-start.12 = (bf16[1,112,128]{2,1,0:T(8,128)(2,1)}, bf16[1,112,128]{2,1,0:T(8,128)(2,1)S(1)}, u32[]{:S(2)}, u32[]{:S(2)}) collective-permute-start(bf16[1,112,128]{2,1,0:T(8,128)(2,1)} %get-tuple-element.55), channel_id=1, source_target_pairs={{0,3},{1,0},{2,1},{3,2},{4,7},{5,4},{6,5},{7,6},{8,11},{9,8},{10,9... | collective-permute-start | bytes 86024 | tf_op jit(solution)/shard_map/ppermute | solution.py:531
  146.6 11.3 %copy-start.14 = (bf16[2,80,256]{2,1,0:T(8,128)(2,1)}, bf16[2,80,256]{2,1,0:T(8,128)(2,1)S(1)}, u32[]{:S(2)}) copy-start(bf16[2,80,256]{2,1,0:T(8,128)(2,1)S(1)} %collective-permute-done.7) | copy-start | bytes 245764
  146.6 4.4 %collective-permute-start.13 = (bf16[1,112,128]{2,1,0:T(8,128)(2,1)}, bf16[1,112,128]{2,1,0:T(8,128)(2,1)S(1)}, u32[]{:S(2)}, u32[]{:S(2)}) collective-permute-start(bf16[1,112,128]{2,1,0:T(8,128)(2,1)} %get-tuple-element.55), channel_id=1, source_target_pairs={{0,2},{1,3},{2,0},{3,1},{4,6},{5,7},{6,4},{7,5},{8,10},{9,11},{10,... | collective-permute-start | bytes 86024 | tf_op jit(solution)/shard_map/ppermute | solution.py:531
  147.7 10.3 %copy-start.13 = (bf16[2,80,256]{2,1,0:T(8,128)(2,1)}, bf16[2,80,256]{2,1,0:T(8,128)(2,1)S(1)}, u32[]{:S(2)}) copy-start(bf16[2,80,256]{2,1,0:T(8,128)(2,1)S(1)} %collective-permute-done.8) | copy-start | bytes 245764
  147.7 4.6 %collective-permute-start.14 = (bf16[1,112,128]{2,1,0:T(8,128)(2,1)}, bf16[1,112,128]{2,1,0:T(8,128)(2,1)S(1)}, u32[]{:S(2)}, u32[]{:S(2)}) collective-permute-start(bf16[1,112,128]{2,1,0:T(8,128)(2,1)} %get-tuple-element.55), channel_id=1, source_target_pairs={{0,1},{1,2},{2,3},{3,0},{4,5},{5,6},{6,7},{7,4},{8,9},{9,10},{10,1... | collective-permute-start | bytes 86024 | tf_op jit(solution)/shard_map/ppermute | solution.py:531
  148.4 9.5 %copy-start.15 = (bf16[2,80,256]{2,1,0:T(8,128)(2,1)}, bf16[2,80,256]{2,1,0:T(8,128)(2,1)S(1)}, u32[]{:S(2)}) copy-start(bf16[2,80,256]{2,1,0:T(8,128)(2,1)S(1)} %collective-permute-done.9) | copy-start | bytes 245764
  148.4 21.6 %copy-start.9 = (bf16[2,8,80,256]{3,2,1,0:T(8,128)(2,1)}, bf16[2,8,80,256]{3,2,1,0:T(8,128)(2,1)S(1)}, u32[]{:S(2)}) copy-start(bf16[2,8,80,256]{3,2,1,0:T(8,128)(2,1)S(1)} %collective-permute-done.5) | copy-start | bytes 1966084
  148.4 5.3 %collective-permute-start.10 = (bf16[64,112,128]{2,1,0:T(8,128)(2,1)}, bf16[64,112,128]{2,1,0:T(8,128)(2,1)S(1)}, u32[]{:S(2)}, u32[]{:S(2)}) collective-permute-start(bf16[64,112,128]{2,1,0:T(8,128)(2,1)} %get-tuple-element.53), channel_id=1, source_target_pairs={{0,4},{1,5},{2,6},{3,7},{4,0},{5,1},{6,2},{7,3},{8,12},{9,13},{10,... | collective-permute-start | bytes 5505032 | tf_op jit(solution)/shard_map/ppermute | solution.py:554
  153.7 1.2 copy-start.5
  157.9 35.7 %all-to-all-start.4 = ((bf16[64,112,128]{2,1,0:T(8,128)(2,1)}), bf16[64,112,128]{2,1,0:T(8,128)(2,1)S(1)}, u32[]{:S(2)}, u32[]{:S(2)}) async-start(bf16[64,112,128]{2,1,0:T(8,128)(2,1)} %shard_map.159), calls=%async_computation.4 | async-start | bytes 3670016 | tf_op jit(solution)/shard_map/all_to_all | solution.py:560
  193.7 1.2 copy-start.2
  234.8 4.6 %copy-start.3 = (bf16[64,112,128]{2,1,0:T(8,128)(2,1)}, bf16[64,112,128]{2,1,0:T(8,128)(2,1)S(1)}, u32[]{:S(2)}) copy-start(bf16[64,112,128]{2,1,0:T(8,128)(2,1)S(1)} %all_to_all.48.refs_1_) | copy-start | bytes 5505028
  234.8 4.6 %collective-permute-start.11 = (bf16[64,112,128]{2,1,0:T(8,128)(2,1)S(1)}, bf16[64,112,128]{2,1,0:T(8,128)(2,1)}, u32[]{:S(2)}, u32[]{:S(2)}) collective-permute-start(bf16[64,112,128]{2,1,0:T(8,128)(2,1)S(1)} %all_to_all.48.refs_1_), channel_id=1, source_target_pairs={{0,4},{1,5},{2,6},{3,7},{4,0},{5,1},{6,2},{7,3},{8,12},{9,13},{10,... | collective-permute-start | bytes 5505032 | tf_op jit(solution)/shard_map/ppermute | solution.py:688
Sparse Core Ops, SparseCore 0:
  153.8 82.2 all-gather.1

commit v5 on v4

--- a/solution.py
+++ b/solution.py
@@ -27,6 +27,11 @@
     [((z * 4 + y) * 2 + core) * 4 + x for z in range(4) for y in range(4) for x in range(4)]
     for core in range(2)
 ]
+PLANE_GROUPS = [
+    [((z * 4 + y) * 2 + core) * 4 + x for z in range(4) for y in range(4)]
+    for core in range(2)
+    for x in range(4)
+]
 learn_rate = 0.25
 beta_one = 0.9
 beta_two = 0.95
@@ -36,8 +41,18 @@
 second_fix = 1.0 - 0.95**10
 
 
-def mixed(value, matrix):
-    return jnp.dot(value, matrix, precision=lax.Precision.HIGHEST, preferred_element_type=F32)
+def mixed(values, matrix):
+    terms = []
+    for rest in values:
+        for _ in range(3):
+            terms.append(rest.astype(BF16).astype(F32))
+            rest = rest - terms[-1]
+    row = lax.broadcasted_iota(jnp.int32, (16, terms[0].shape[1]), 0)
+    stack = jnp.zeros(row.shape, F32)
+    for n, term in enumerate(terms):
+        stack = jnp.where(row == n, term, stack)
+    out = jnp.dot(stack.astype(BF16), matrix.astype(BF16), preferred_element_type=F32)
+    return [out[3 * n : 3 * n + 1] + out[3 * n + 1 : 3 * n + 2] + out[3 * n + 2 : 3 * n + 3] for n in range(len(values))]
 
 
 def iotas(shape):
@@ -51,11 +66,11 @@
 
 def pack_row(first, second):
     channel, lane = iotas((C, 128))
-    head = jnp.where((channel >> 3) == lane, 1.0, 0.0).astype(F32)
-    tail = jnp.where((channel >> 3) + 32 == lane, 1.0, 0.0).astype(F32)
-    wide = jnp.broadcast_to(first, (8, C)), jnp.broadcast_to(second, (8, C))
-    row = mixed(wide[0], head) + mixed(wide[1], tail)
-    return jnp.broadcast_to(row[0:1], (128, 128))
+    head = jnp.where((channel >> 3) == (lane & 31), 1.0, 0.0).astype(F32)
+    heads, tails = mixed((first, second), head)
+    lane = lax.broadcasted_iota(jnp.int32, (1, 128), 1)
+    row = jnp.where(lane < 32, heads, jnp.where(lane < 64, tails, 0.0))
+    return jnp.broadcast_to(row, (128, 128))
 
 
 def read_norm(table):
@@ -63,16 +78,16 @@
     center = total / 128.0
     offset = table - center
     square = jnp.sum(offset * offset, axis=0, keepdims=True)
-    low, high = spread_matrix(0), spread_matrix(32)
-    wide = lambda v, m: mixed(jnp.broadcast_to(v, (8, 128)), m)[0:1]
-    spread = wide(total, high) + HERE * wide(square, low)
-    return wide(center, low), lax.rsqrt(spread / TOTAL + norm_eps)
+    both = jnp.concatenate([spread_matrix(0), spread_matrix(32)], axis=1)
+    wide = mixed((center, square, total), both)
+    spread = wide[2][:, C:] + HERE * wide[1][:, :C]
+    return wide[0][:, :C], lax.rsqrt(spread / TOTAL + norm_eps)
 
 
 def read_sums(table):
     total = jnp.sum(table, axis=0, keepdims=True) / TOTAL
-    wide = lambda m: mixed(jnp.broadcast_to(total, (8, 128)), m)[0:1]
-    return wide(spread_matrix(0)), wide(spread_matrix(32))
+    (wide,) = mixed((total,), jnp.concatenate([spread_matrix(0), spread_matrix(32)], axis=1))
+    return wide[:, :C], wide[:, C:]
 
 
 def folded(values):
@@ -85,17 +100,17 @@
 
 def local_moments(read, count):
     zero = jnp.zeros((8, C), F32)
-    sums = lax.fori_loop(0, count, lambda i, s: s + folded(read(i)), zero)
+    sums = lax.fori_loop(0, count, lambda i, s: s + folded(read(i)), zero, unroll=2)
     ch_sum = jnp.sum(sums, axis=0, keepdims=True)
     r, c = iotas((C, C))
     same = jnp.where((r >> 3) == (c >> 3), 1.0, 0.0).astype(F32)
-    mean = mixed(jnp.broadcast_to(ch_sum, (8, C)), same)[0:1] / HERE
+    mean = mixed((ch_sum,), same)[0] / HERE
 
     def squares(i, s):
         off = read(i) - mean
         return s + folded(off * off)
 
-    ch_sq = jnp.sum(lax.fori_loop(0, count, squares, zero), axis=0, keepdims=True)
+    ch_sq = jnp.sum(lax.fori_loop(0, count, squares, zero, unroll=2), axis=0, keepdims=True)
     return pack_row(mean / 8.0, ch_sq)
 
 
@@ -142,10 +157,10 @@
         put(frames[2], i, halo_at + i, ROWS + 1, ok[0] * ok[2])
         return 0
 
-    lax.fori_loop(0, FR * ROWS, inner, 0)
-    lax.fori_loop(0, FR, edge, 0)
+    lax.fori_loop(0, FR * ROWS, inner, 0, unroll=2)
+    lax.fori_loop(0, FR, edge, 0, unroll=2)
     if len(frames) == 1:
-        lax.fori_loop(0, FR * (ROWS + 2), outer, 0)
+        lax.fori_loop(0, FR * (ROWS + 2), outer, 0, unroll=2)
     else:
         lax.fori_loop(0, FR * ROWS, outer_inner, 0)
         lax.fori_loop(0, FR, outer_edge, 0)
@@ -186,21 +201,22 @@
             whole[tap : tap + 3 * C, :] = total * SCALE
 
 
-def cut_pieces(whole, core, flat, kept, given):
-    flat[...] = jnp.zeros_like(flat)
-    for side, out in ((1 - core, given), (core, kept)):
-
-        def block(i, _):
-            at = pl.multiple_of(i * BLOCK + side * (BLOCK // 2), 8)
-            slab = whole[pl.ds(at, BLOCK // 2), :]
-            flat[pl.ds(0, BLOCK // 2, 2), :] = slab[:, :128]
-            flat[pl.ds(1, BLOCK // 2, 2), :] = slab[:, 128:]
-            for x in range(4):
-                out.ref[i * 4 + x] = flat[x * SHARE : x * SHARE + PIECE, :].astype(BF16)
-            return 0
-
-        lax.fori_loop(0, 16, block, 0)
-        out.send()
+def cut_pieces(whole, core, kept, given):
+    whole[27 * C :, :] = jnp.zeros((8, C), F32)
+    for side, outs in ((1 - core, given), (core, kept)):
+        for k, out in enumerate(outs):
+
+            def block(i, _):
+                at = pl.multiple_of((4 * k + i) * BLOCK + side * (BLOCK // 2), 8)
+                slab = whole[pl.ds(at, BLOCK // 2 + 8), :]
+                for x in range(4):
+                    rows = slab[x * (SHARE // 2) : x * (SHARE // 2) + PIECE // 2, :]
+                    piece = jnp.concatenate([rows[:, :128], rows[:, 128:]], axis=0)
+                    out.ref[i * 4 + x] = piece.astype(BF16)
+                return 0
+
+            lax.fori_loop(0, 4, block, 0)
+            out.send()
 
 
 def silu_parts(value, center, inverse, gain):
@@ -243,7 +259,7 @@
         return sums[0] + folded(here), sums[1] + folded(here * hat)
 
     zero = jnp.zeros((8, C), F32)
-    plain, cross = lax.fori_loop(0, FR * ROWS, step, (zero, zero))
+    plain, cross = lax.fori_loop(0, FR * ROWS, step, (zero, zero), unroll=2)
     return pack_row(jnp.sum(plain, axis=0, keepdims=True), jnp.sum(cross, axis=0, keepdims=True))
 
 
@@ -259,7 +275,8 @@
     conv(patches.ref, weight.get(), write, True)
 
 
-def second_kernel(core, middle, back, patches, table, gain, slope, row, kept, given, hidden, whole, flat):
+def second_kernel(core, middle, back, patches, table, gain, slope, row, *refs):
+    kept, given, (hidden, whole) = refs[:4], refs[4:8], refs[8:]
     center, inverse = read_norm(table.get()[...])
     middle = middle.get()
     read = lambda i: middle[chunk(i), :].astype(F32)
@@ -275,10 +292,11 @@
             for c in range(3):
                 tap = (9 * a + 3 * b + c) * C
                 whole[tap : tap + C, :] = total[:, c * C : (c + 1) * C]
-    cut_pieces(whole, core[0], flat, kept, given)
-
-
-def grad_one_kernel(core, slope, middle, patches, table, sums, mid_grad, kept, given, whole, flat):
+    cut_pieces(whole, core[0], kept, given)
+
+
+def grad_one_kernel(core, slope, middle, patches, table, sums, mid_grad, *refs):
+    kept, given, (whole,) = refs[:4], refs[4:8], refs[8:]
     center, inverse = read_norm(table.get()[...])
     mean, cross = read_sums(sums.get()[...])
     slope, middle = slope.get(), middle.get()
@@ -288,10 +306,10 @@
         mid_grad.ref[chunk(i), :] = (inverse * (slope[chunk(i), :] - mean - hat * cross)).astype(BF16)
         return 0
 
-    lax.fori_loop(0, FR * ROWS, step, 0)
+    lax.fori_loop(0, FR * ROWS, step, 0, unroll=2)
     mid_grad.send()
     wgrad(patches, mid_grad.ref, whole)
-    cut_pieces(whole, core[0], flat, kept, given)
+    cut_pieces(whole, core[0], kept, given)
 
 
 def back_one_kernel(
@@ -310,26 +328,35 @@
     row.ref[...] = slopes(read, back, center, inverse, gain.get()[...], slope.ref)[: row.ref.shape[0]]
 
 
-def last_kernel(core, own, other, slope, inputs, table, cotangent, weight, result, flat, halves, arrive):
+def last_kernel(core, band, *refs):
+    lines, (slope, inputs, table, cotangent, weight, result, flat, halves, arrive) = refs[:8], refs[8:]
     copies = []
-    for n, (source, place) in enumerate(((own, core[0]), (other, 1 - core[0]))):
-        copies.append(pltpu.make_async_copy(source, halves.at[place], arrive.at[n]))
-        copies[-1].start()
+    for n in range(2):
+        place = core[0] if n == 0 else 1 - core[0]
+        for k in range(4):
+            x = lax.rem(band[0] - k + 4, 4)
+            copies.append(pltpu.make_async_copy(lines[4 * n + k], halves.at[place, x], arrive.at[n, k]))
+            copies[-1].start()
     center, inverse = read_norm(table.get()[...])
     for copy in copies:
         copy.wait()
 
     def block(i, _):
-        assemble(i, lambda s: halves[s // 4, i * 4 + s % 4], weight.ref, flat)
+        assemble(i, lambda s: halves[s // 4, s % 4, i], weight.ref, flat)
         return 0
 
     for k in range(4):
         lax.fori_loop(4 * k, 4 * k + 4, block, 0)
         weight.send(k)
 
-    add = lambda i, s: s + halves[0, i, 96:, :].astype(F32) + halves[1, i, 96:, :].astype(F32)
-    sums = lax.fori_loop(0, 64, add, jnp.zeros((16, 128), F32))
-    mean, cross = read_sums(sums[SHARE - 96 :])
+    def add(i, sums):
+        for k in range(8):
+            piece = halves[k // 4, k % 4, i, 48:, :].astype(F32)
+            sums = sums + piece[:8] + piece[56:]
+        return sums
+
+    sums = lax.fori_loop(0, 16, add, jnp.zeros((8, 128), F32))
+    mean, cross = read_sums(sums[6:])
     slope, inputs, cotangent = slope.get(), inputs.get(), cotangent.get()
 
     def step(i, _):
@@ -338,15 +365,17 @@
         result.ref[chunk(i), :] = (cotangent[chunk(i), :].astype(F32) + grad).astype(BF16)
         return 0
 
-    lax.fori_loop(0, FR * ROWS, step, 0)
-
-
-def adam_step(arrived, own, first, second, first_new, second_new, extra):
+    lax.fori_loop(0, FR * ROWS, step, 0, unroll=2)
+
+
+def adam_step(arrived, own, first, second, first_new, second_new, extra, flat):
     gradient = jnp.zeros((PIECE, 128), F32)
     for k in range(4):
         ready = arrived.get(k)
         gradient = lax.fori_loop(16 * k, 16 * k + 16, lambda i, s: s + ready[i].astype(F32), gradient)
-    gradient = gradient[:SHARE]
+    flat[pl.ds(0, PIECE // 2, 2), :] = gradient[: PIECE // 2]
+    flat[pl.ds(1, PIECE // 2, 2), :] = gradient[PIECE // 2 :]
+    gradient = flat[:SHARE, :]
     one = beta_one * first.get()[...] + (1.0 - beta_one) * gradient
     two = beta_two * second.get()[...] + (1.0 - beta_two) * gradient * gradient
     first_new.ref[...] = one
@@ -354,46 +383,62 @@
     updated = own.get()[...].astype(F32) * (1.0 - learn_rate * decay_rate) - learn_rate * (one / first_fix) / (
         jnp.sqrt(two / second_fix) + adam_eps
     )
-    return jnp.concatenate([updated, extra], axis=0).astype(BF16)
-
-
-def adam_two_kernel(arrived, own, first, second, first_new, second_new, part):
+    flat[...] = jnp.concatenate([updated, extra], axis=0)
+    halves = [flat[pl.ds(n, PIECE // 2, 2), :] for n in range(2)]
+    return jnp.concatenate(halves, axis=0).astype(BF16)
+
+
+def adam_two_kernel(arrived, own, first, second, first_new, second_new, part, flat):
     extra = jnp.zeros((PIECE - SHARE, 128), F32)
-    part.ref[0] = adam_step(arrived, own, first, second, first_new, second_new, extra)
-
-
-def adam_one_kernel(arrived, own, first, second, sums, first_new, second_new, spread):
+    part.ref[0] = adam_step(arrived, own, first, second, first_new, second_new, extra, flat)
+
+
+def adam_one_kernel(arrived, own, first, second, sums, first_new, second_new, spread, flat):
     rest = sums.get()[0:1, :]
     terms = []
     for _ in range(3):
         terms.append(rest.astype(BF16).astype(F32))
         rest = rest - terms[-1]
     extra = jnp.concatenate([*terms, jnp.zeros((1, 128), F32)], axis=0)
-    piece = adam_step(arrived, own, first, second, first_new, second_new, extra)
+    piece = adam_step(arrived, own, first, second, first_new, second_new, extra, flat)
 
     def copy(i, _):
         spread.ref[i] = piece
         return 0
 
-    for k in range(4):
-        lax.fori_loop(16 * k, 16 * k + 16, copy, 0)
-        spread.send(k)
-
-
-def assemble(block, piece, weight, flat):
+    lax.fori_loop(0, spread.ref.shape[0], copy, 0)
+
+
+def assemble(block, piece, weight, wide):
     for s in range(8):
-        flat[s * SHARE : s * SHARE + PIECE, :] = piece(s).astype(F32)
+        share = piece(s).astype(F32)
+        rows = slice(s * (SHARE // 2), s * (SHARE // 2) + PIECE // 2)
+        wide[rows, :128] = share[: PIECE // 2]
+        wide[rows, 128:] = share[PIECE // 2 :]
     rows = pl.ds(pl.multiple_of(block * BLOCK, BLOCK), BLOCK)
-    weight[rows, 0:128] = flat[pl.ds(0, BLOCK, 2), :].astype(BF16)
-    weight[rows, 128:256] = flat[pl.ds(1, BLOCK, 2), :].astype(BF16)
-
-
-def assemble_all_kernel(gathered, weight, flat):
-    for k in range(4):
-        ready = gathered.get(k)
+    weight[rows, :] = wide[:BLOCK, :].astype(BF16)
+
+
+def assemble_kernel(core, own, other, weight, flat, halves, arrive):
+    parts = 4
+    copies = [
+        [
+            pltpu.make_async_copy(
+                source.at[pl.ds(16 * k, 16)], halves.at[place, pl.ds(16 * k, 16)], arrive.at[n, k]
+            )
+            for n, (source, place) in enumerate(((own, core[0]), (other, 1 - core[0])))
+        ]
+        for k in range(parts)
+    ]
+    for pair in copies:
+        for copy in pair:
+            copy.start()
+    for k in range(parts):
+        for copy in copies[k]:
+            copy.wait()
 
         def block(i, _):
-            assemble(i, lambda s: ready[i * 8 + s], weight.ref, flat)
+            assemble(i, lambda s: halves[s // 4, i * 4 + s % 4], weight.ref, flat)
             return 0
 
         lax.fori_loop(4 * k, 4 * k + 4, block, 0)
@@ -430,14 +475,14 @@
             copy.wait()
 
 
-SMALL = 80 * 1024
+SMALL, SMALL_RESULT = 16 * 1024, 80 * 1024
 
 
 def run(kernel, scalars, arrays, outs, scratch=(), mib=60, parts=(), raw=()):
     parts, count = dict(parts), len(arrays)
-    vmem, hbm = pl.BlockSpec(memory_space=pltpu.VMEM), pl.BlockSpec(memory_space=pltpu.HBM)
+    vmem, hbm = pl.BlockSpec(memory_space=pltpu.VMEM), pl.BlockSpec(memory_space=pl.ANY)
     every = [*arrays, *outs]
-    large = [x.size * x.dtype.itemsize > SMALL for x in every]
+    large = [x.size * x.dtype.itemsize > (SMALL if n < count else SMALL_RESULT) for n, x in enumerate(every)]
     staged = [n for n in range(len(every)) if large[n] and n not in raw]
     buffers = [pltpu.VMEM(every[n].shape, every[n].dtype) for n in staged]
     semaphores = [pltpu.SemaphoreType.DMA((parts.get(n, 1),)) for n in staged]
@@ -446,14 +491,14 @@
         lead, rest = refs[: len(scalars)], refs[len(scalars) :]
         places, rest = rest[: len(every)], rest[len(every) :]
         own, rest = rest[: len(scratch)], rest[len(scratch) :]
-        boxes = []
-        for n, place in enumerate(places):
+        boxes = [None] * len(every)
+        for n in sorted(range(len(every)), key=lambda n: every[n].size > 128 * 128):
+            place, kind = places[n], Coming if n < count else Going
             if n in raw:
-                boxes.append(place)
+                boxes[n] = place
                 continue
-            kind = Coming if n < count else Going
             if not large[n]:
-                boxes.append(kind(place))
+                boxes[n] = kind(place)
                 continue
             at = staged.index(n)
             buffer, arrive, cuts = rest[at], rest[len(staged) + at], parts.get(n, 1)
@@ -463,7 +508,7 @@
                 ends = [place.at[pl.ds(k * size, size)], buffer.at[pl.ds(k * size, size)]]
                 source, target = ends if n < count else ends[::-1]
                 copies.append(pltpu.make_async_copy(source, target, arrive.at[k]))
-            boxes.append(kind(buffer, copies))
+            boxes[n] = kind(buffer, copies)
         kernel(*lead, *boxes, *own)
         for n, box in enumerate(boxes):
             if n not in raw:
@@ -524,11 +569,20 @@
     return [edge.reshape(-1, C) for edge in edges]
 
 
+def over_plane(pieces):
+    return lax.all_to_all(pieces, BOTH, 0, 0, axis_index_groups=PLANE_GROUPS, tiled=True)
+
+
+def over_line(piece):
+    bands = lax.axis_size("rows")
+    return [
+        lax.ppermute(piece, "rows", [(i, (i + k) % bands) for i in range(bands)]) for k in range(1, bands)
+    ]
+
+
 def over_bands(piece):
     bands, here = lax.axis_size("rows"), lax.axis_index("rows")
-    turned = [piece]
-    for k in range(1, bands):
-        turned.append(lax.ppermute(piece, "rows", [(i, (i + k) % bands) for i in range(bands)]))
+    turned = [piece, *over_line(piece)]
     ordered = []
     for band in range(bands):
         choice = turned[0]
@@ -542,17 +596,19 @@
     return array.reshape(FR, ROWS, COLS, C)
 
 
-def pair_kernel(kept, taken, result):
+def pair_kernel(*refs):
+    kept, taken, result = refs[:4], refs[4:8], refs[8]
     for k in range(4):
-        first, second = kept.get(k), taken.get(k)
-        for i in range(16 * k, 16 * k + 16):
-            result.ref[i] = (first[i].astype(F32) + second[i].astype(F32)).astype(BF16)
+        first, second = kept[k].get(), taken[k].get()
+        for i in range(16):
+            result.ref[16 * k + i] = (first[i].astype(F32) + second[i].astype(F32)).astype(BF16)
         result.send(k)
 
 
 def pair_sum(kept, given):
-    taken = lax.ppermute(given, BOTH, CORE_PAIRS)
-    (total,) = run(pair_kernel, (), (kept, taken), (kept,), parts={0: 4, 1: 4, 2: 4})
+    taken = [lax.ppermute(part, BOTH, CORE_PAIRS) for part in given]
+    whole = jax.ShapeDtypeStruct((64, PIECE, 128), BF16)
+    (total,) = run(pair_kernel, (), (*kept, *taken), (whole,), parts={8: 4})
     return total
 
 
@@ -590,11 +646,10 @@
     row_type = shape((128, 128), F32)
     act_type, wide_type = shape((CELLS, C), BF16), shape((CELLS, C), F32)
     patch_type = shape((EXT, 3 * C), BF16)
-    piece_type = shape((64, PIECE, 128), BF16)
+    piece_types = (shape((16, PIECE, 128), BF16),) * 8
     moment_type = shape((SHARE, 128), F32)
     patch_scratch = pltpu.VMEM((EXT, 3 * C), BF16)
-    whole_scratch = pltpu.VMEM((27 * C, C), F32)
-    flat_scratch = pltpu.VMEM((BLOCK + 8, 128), F32)
+    whole_scratch = pltpu.VMEM((27 * C + 8, C), F32)
 
     def update(kernel, arrived, weight, first, second, more, part_types):
         first_new, second_new, *part = run(
@@ -602,7 +657,8 @@
             (),
             (*arrived, own_share(weight), first.reshape(SHARE, 128), second.reshape(SHARE, 128), *more),
             (moment_type, moment_type, *part_types),
-            parts={0: 4, 7: 4} if part_types[0] is piece_type else {0: 4},
+            (pltpu.VMEM((PIECE, 128), F32),),
+            parts={0: 4},
         )
         return part, first_new.reshape(-1), second_new.reshape(-1)
 
@@ -628,38 +684,40 @@
         (after(flat_cot, row_two), *flat(edges_cot), frames_cot, weight_two),
         (wide_type, patch_type),
     )
-    slope_two, row_three, kept_two, given_two = run(
+    slope_two, row_three, *cuts_two = run(
         second_kernel,
         (core,),
         (middle, back_two, patch_cot, table_two, gain_two),
-        (wide_type, row_type, piece_type, piece_type),
-        (pltpu.VMEM((CELLS, C), BF16), whole_scratch, flat_scratch),
+        (wide_type, row_type, *piece_types),
+        (pltpu.VMEM((CELLS, C), BF16), whole_scratch),
         parts={2: 4},
     )
     table_three = everyone(row_three)
-    pair_two = pair_sum(kept_two, given_two)
-    mid_grad, kept_one, given_one = run(
+    pair_two = pair_sum(cuts_two[:4], cuts_two[4:])
+    mid_grad, *cuts_one = run(
         grad_one_kernel,
         (core,),
         (after(slope_two, pair_two), middle, patch_one, table_two, table_three),
-        (act_type, piece_type, piece_type),
-        (whole_scratch, flat_scratch),
+        (act_type, *piece_types),
+        (whole_scratch,),
         parts={2: 4},
     )
     frames_grad, *edges_grad = five_sides(cells(mid_grad))
     arrived_two = over_chips(pair_two)
+    kept_first = after(cuts_one[0], *frames_grad, *edges_grad)
+    pair_one = pair_sum((kept_first, *cuts_one[1:4]), cuts_one[4:])
     part_two, new_first_two, new_second_two = update(
         adam_two_kernel,
-        (after(arrived_two, given_one),),
+        (after(arrived_two, pair_one),),
         weight_two,
         first_two,
         second_two,
         (),
         (shape((1, PIECE, 128), BF16),),
     )
-    gathered_two = lax.all_gather(over_bands(part_two[0]), "tm", axis=0, tiled=True)
-    pair_one = after(pair_sum(kept_one, after(given_one, arrived_two, *frames_grad, *edges_grad)), part_two[0])
     arrived_one = over_chips(pair_one)
+    line_two = over_bands(part_two[0])
+    spread_two = jnp.broadcast_to(line_two.reshape(1, 4 * PIECE, 128), (16, 4 * PIECE, 128))
     slope_one, row_four = run(
         back_one_kernel,
         (ok_after,),
@@ -677,28 +735,40 @@
     )
     (part_one,), new_first_one, new_second_one = update(
         adam_one_kernel,
-        (arrived_one,),
+        (after(arrived_one, line_two),),
         weight_one,
         first_one,
         second_one,
         (row_four,),
-        (piece_type,),
-    )
-    own_one = over_chips(part_one)
-    other_one = lax.ppermute(own_one, BOTH, CORE_PAIRS)
+        (shape((16, PIECE, 128), BF16),),
+    )
+    own_one = over_plane(part_one)
+    lines_one = [own_one, *over_line(own_one)]
+    own_two = over_plane(after(spread_two, own_one))
+    own_two = after(own_two, *lines_one)
+    other_two = lax.ppermute(own_two, BOTH, CORE_PAIRS).reshape(64, PIECE, 128)
+    others_one = [lax.ppermute(line, BOTH, CORE_PAIRS) for line in lines_one]
     weight_type = shape((27 * C, C), BF16)
-    assemble_scratch = pltpu.VMEM((2 * BLOCK + 8, 128), F32)
+    assemble_scratch = pltpu.VMEM((BLOCK + 8, C), F32)
     (new_weight_two,) = run(
-        assemble_all_kernel, (), (gathered_two,), (weight_type,), (assemble_scratch,), parts={0: 4, 1: 4}
+        assemble_kernel,
+        (core,),
+        (own_two.reshape(64, PIECE, 128), other_two),
+        (weight_type,),
+        (assemble_scratch, pltpu.VMEM((2, 64, PIECE, 128), BF16), pltpu.SemaphoreType.DMA((2, 4))),
+        mib=16,
+        parts={2: 4},
+        raw=(0, 1),
     )
     new_weight_one, input_grad = run(
         last_kernel,
-        (core,),
-        (own_one, other_one, slope_one, flat_inputs, table_one, flat_cot),
+        (core, band.astype(jnp.int32).reshape(1)),
+        (*lines_one, *others_one, after(slope_one, new_weight_two), flat_inputs, table_one, flat_cot),
         (weight_type, act_type),
-        (assemble_scratch, pltpu.VMEM((2, 64, PIECE, 128), BF16), pltpu.SemaphoreType.DMA((2,))),
-        parts={6: 4},
-        raw=(0, 1),
+        (assemble_scratch, pltpu.VMEM((2, 4, 16, PIECE, 128), BF16), pltpu.SemaphoreType.DMA((2, 4))),
+        mib=24,
+        parts={12: 4},
+        raw=range(8),
     )
     return (
         cells(input_grad),

time: 255 us -> 246 us (0.965)
  blocking collectives: 35.4 us -> 12.3 us
  starting transfers between devices: 69.4 us -> 87.2 us
  waiting for transfers between devices: 32.9 us -> 46.6 us
  between operations: 14.5 us -> 1.53 us
  Pallas kernels: 83.2 us -> 78.2 us
  local copies, waits for them, and re-layouts: 14.8 us -> 17.4 us
    all_to_all x1, blocking collectives: 35.4 us -> 12.3 us  [over_plane(): lax.all_to_all(pieces, BOTH, 0, 0, axis_index_groups=PLANE_GROUPS, tiled=...]
    ppermute x6 -> x19, waiting for transfers between devices: 3.36 us -> 24.1 us  [the longest x6 21.7 us: over_line(): lax.ppermute(piece, 'rows', [(i, (i + k) % bands) for i in range(bands)])]
    ppermute x6 -> x19, starting transfers between devices: 7.06 us -> 17.3 us  [the longest x6 8.4 us: over_line(): lax.ppermute(piece, 'rows', [(i, (i + k) % bands) for i in range(bands)])]
    all_to_all x2, waiting for transfers between devices: 12.9 us -> 3.21 us  [over_chips(): lax.all_to_all(pieces, BOTH, 0, 0, axis_index_groups=CHIP_GROUPS, tiled=T...]
    pallas_call x12, Pallas kernels: 83.2 us -> 78.2 us  [run(): pl.pallas_call(body, out_shape=tuple((jax.ShapeDtypeStruct(x.shape, x.dty...]
    all_to_all x0 -> x1, starting transfers between devices: none -> 3.71 us  [over_plane(): lax.all_to_all(pieces, BOTH, 0, 0, axis_index_groups=PLANE_GROUPS, tiled=...]
    unnamed x32 -> x50, local copies, waits for them, and re-layouts: 7.72 us -> 8.74 us
  transfers between devices with their start and end apart: 21 -> 34, of which waited for: 8 -> 12; matrix products, arithmetic and copies ran while one was open for 3% -> 2% of each run, Pallas kernels for 25% -> 23%
where the time goes in v5:
time: 246 us; the launch traced here: 245 us
  starting transfers between devices  87.2 us (35%)
  Pallas kernels  78.2 us (32%)
  waiting for transfers between devices  46.6 us (19%)
  local copies, waits for them, and re-layouts  17.4 us (7%)
  blocking collectives  12.3 us (5%)
    pallas_call x12, Pallas kernels, run(): pl.pallas_call(body, out_shape=tuple((jax.ShapeDtypeStruct(x.shape, x.dty...  78.2 us
    all_to_all x3, starting transfers between devices, everyone(): return lax.all_to_all(row, BOTH, 0, 0, tiled=True)  23.6 us
    ppermute x6, waiting for transfers between devices, over_line(): lax.ppermute(piece, 'rows', [(i, (i + k) % bands) for i in range(bands)])  21.7 us
    all_to_all x2, starting transfers between devices, over_chips(): lax.all_to_all(pieces, BOTH, 0, 0, axis_index_groups=CHIP_GROUPS, tiled=T...  18.3 us
    all_to_all x3, waiting for transfers between devices, everyone(): return lax.all_to_all(row, BOTH, 0, 0, tiled=True)  14.4 us
    all_to_all x1, blocking collectives, over_plane(): lax.all_to_all(pieces, BOTH, 0, 0, axis_index_groups=PLANE_GROUPS, tiled=...  12.3 us
    unnamed x50, local copies, waits for them, and re-layouts  8.74 us
    ppermute x6, starting transfers between devices, over_line(): lax.ppermute(piece, 'rows', [(i, (i + k) % bands) for i in range(bands)])  8.4 us
  transfers between devices with their start and end apart: 34, of which 12 were waited for; matrix products, arithmetic and copies ran while one was open for 2% of the time, Pallas kernels for 23%

profile of v5, /device:TPU:1, one launch (start us, length us, event | category | flops | bytes accessed | tf_op | source)
XLA Modules:
  0.0 244.7 jit_solution(17943865634886872535)
XLA Ops:
  0.6 1.0 slice_bitcast_fusion.3
  1.7 0.9 slice_bitcast_fusion.2
  2.6 4.0 %collective-permute-start = (bf16[4,80,256]{2,1,0:T(8,128)(2,1)S(1)}, bf16[4,80,256]{2,1,0:T(8,128)(2,1)S(1)}, u32[]{:S(2)}, u32[]{:S(2)}) collective-permute-start(bf16[4,80,256]{2,1,0:T(8,128)(2,1)S(1)} %pad_maximum_fusion.2), channel_id=1, source_target_pairs={{0,1},{1,2},{2,3},{4,5},{5,6},{6,7},{8,9},{9,10},{10,11},{12,13},{... | collective-permute-start | bytes 491528 | tf_op jit(solution)/shard_map/ppermute | solution.py:544
  6.6 1.4 collective-permute-start.1
  8.1 2.4 shard_map.153
  10.5 0.7 slice_bitcast_fusion.7
  11.2 2.2 collective-permute-done.1
  13.4 0.7 slice_bitcast_fusion.6
  14.2 5.0 %collective-permute-start.2 = (bf16[2,10,80,256]{3,2,1,0:T(8,128)(2,1)S(1)}, bf16[2,10,80,256]{3,2,1,0:T(8,128)(2,1)}, u32[]{:S(2)}, u32[]{:S(2)}) collective-permute-start(bf16[2,10,80,256]{3,2,1,0:T(8,128)(2,1)S(1)} %pad_maximum_fusion), channel_id=1, source_target_pairs={{0,4},{4,8},{8,12},{12,16},{16,20},{20,24},{24,28},{28,32},{32,36}... | collective-permute-start | bytes 2457608 | tf_op jit(solution)/shard_map/ppermute | solution.py:565
  19.3 1.9 collective-permute-start.3
  21.2 10.3 %all-to-all-start = ((f32[128,1,128]{2,1,0:T(1,128)}), f32[128,1,128]{2,1,0:T(1,128)S(1)}, u32[]{:S(2)}, u32[]{:S(2)}) async-start(f32[128,1,128]{2,1,0:T(1,128)} %bitcast.18), calls=%async_computation | async-start | bytes 131072 | tf_op jit(solution)/shard_map/all_to_all | solution.py:530
  32.1 9.0 %all-to-all-done = f32[128,1,128]{2,1,0:T(1,128)S(1)} async-done(((f32[128,1,128]{2,1,0:T(1,128)}), f32[128,1,128]{2,1,0:T(1,128)S(1)}, u32[]{:S(2)}, u32[]{:S(2)}) %all-to-all-start) | async-done | bytes 65568 | tf_op jit(solution)/shard_map/all_to_all | solution.py:530
  41.1 0.6 copy-done.5
  41.7 10.0 %shard_map.154 = (bf16[3200,768]{1,0:T(8,128)(2,1)}, bf16[1280,256]{1,0:T(8,128)(2,1)}, f32[128,128]{1,0:T(8,128)}) custom-call(f32[3]{0:T(128)} %maximum_maximum_fusion.refs_0_, bf16[1280,256]{1,0:T(8,128)(2,1)} %bitcast.83, bf16[160,256]{1,0:T(8,128)(2,1)} %bitcast.102, bf16[160,256]{1,0:T(8,128)(2,1)} %bitcast.103, bf16[1600,256]{1,0:T(8,128)(2,1)} %bitcast.16.refs_4_, ...), custom_call_target="tpu_custom_call" | custom-call | flops 1024 | bytes 1024 | tf_op jit(solution)/shard_map/pallas_call | solution.py:517
  51.7 4.4 %all-to-all-start.1 = ((f32[128,1,128]{2,1,0:T(1,128)}), f32[128,1,128]{2,1,0:T(1,128)S(1)}, u32[]{:S(2)}, u32[]{:S(2)}) async-start(f32[128,1,128]{2,1,0:T(1,128)} %bitcast.110), calls=%async_computation.1 | async-start | bytes 131072 | tf_op jit(solution)/shard_map/all_to_all | solution.py:530
  56.8 0.9 copy-done.9
  57.6 9.0 %shard_map.155 = (f32[1280,256]{1,0:T(8,128)}, bf16[3200,768]{1,0:T(8,128)(2,1)}) custom-call(f32[3]{0:T(128)} %maximum_maximum_fusion.1.refs_0_, bf16[1280,256]{1,0:T(8,128)(2,1)} %bitcast.87, bf16[160,256]{1,0:T(8,128)(2,1)} %bitcast.100, bf16[160,256]{1,0:T(8,128)(2,1)} %bitcast.101, bf16[1600,256]{1,0:T(8,128)(2,1)} %bitcast.95, bf16[6912,256]{1,0:T(8,128)(2,1)} %refs_5_.1), custom_call_target="tpu_custom_call" | custom-call | flops 1024 | bytes 1024 | tf_op jit(solution)/shard_map/pallas_call | solution.py:517
  66.7 0.6 copy-done.11
  67.3 12.5 %shard_map.156 = (f32[1280,256]{1,0:T(8,128)}, f32[128,128]{1,0:T(8,128)}, bf16[16,112,128]{2,1,0:T(8,128)(2,1)}, bf16[16,112,128]{2,1,0:T(8,128)(2,1)}, bf16[16...) custom-call(s32[1]{0:T(128)} %bitcast.refs_0_, ...), custom_call_target="tpu_custom_call" | custom-call | flops 1024 | bytes 1024 | tf_op jit(solution)/shard_map/pallas_call | solution.py:517
  79.9 1.3 collective-permute-start.4
  81.8 8.9 %all-to-all-start.2 = ((f32[128,1,128]{2,1,0:T(1,128)}), f32[128,1,128]{2,1,0:T(1,128)S(1)}, u32[]{:S(2)}, u32[]{:S(2)}) async-start(f32[128,1,128]{2,1,0:T(1,128)} %bitcast.109), calls=%async_computation.2 | async-start | bytes 131072 | tf_op jit(solution)/shard_map/all_to_all | solution.py:530
  90.8 0.7 copy-done.14
  92.0 3.0 %shard_map.157 = bf16[64,112,128]{2,1,0:T(8,128)(2,1)} custom-call(bf16[16,112,128]{2,1,0:T(8,128)(2,1)} %get-tuple-element.60.refs_0_, bf16[16,112,128]{2,1,0:T(8,128)(2,1)} %get-tuple-element.61.refs_1_, bf16[16,112,128]{2,1,0:T(8,128)(2,1)} %get-tuple-element.62.refs_2_, bf16[16,112,128]{2,1,0:T(8,128)(2,1)} %get-tuple-element.63.refs_3_, ...), custom_call_target="tpu_custom_call" | custom-call | flops 1024 | bytes 1024 | tf_op jit(solution)/shard_map/pallas_call | solution.py:517
  95.0 5.4 %all-to-all-done.2 = f32[128,1,128]{2,1,0:T(1,128)S(1)} async-done(((f32[128,1,128]{2,1,0:T(1,128)}), f32[128,1,128]{2,1,0:T(1,128)S(1)}, u32[]{:S(2)}, u32[]{:S(2)}) %all-to-all-start.2) | async-done | bytes 65568 | tf_op jit(solution)/shard_map/all_to_all | solution.py:530
  100.4 0.6 copy-done.19
  101.0 5.3 %all-to-all-start.4 = ((bf16[64,112,128]{2,1,0:T(8,128)(2,1)}), bf16[64,112,128]{2,1,0:T(8,128)(2,1)S(1)}, u32[]{:S(2)}, u32[]{:S(2)}) async-start(bf16[64,112,128]{2,1,0:T(8,128)(2,1)} %shard_map.157), calls=%async_computation.4 | async-start | bytes 3670016 | tf_op jit(solution)/shard_map/all_to_all | solution.py:616
  106.4 11.3 %shard_map.158 = (bf16[1280,256]{1,0:T(8,128)(2,1)}, bf16[16,112,128]{2,1,0:T(8,128)(2,1)}, bf16[16,112,128]{2,1,0:T(8,128)(2,1)}, bf16[16,112,128]{2,1,0:T(8,12...) custom-call(s32[1]{0:T(128)} %bitcast.refs_0_, ...), custom_call_target="tpu_custom_call" | custom-call | flops 1024 | bytes 1024 | tf_op jit(solution)/shard_map/pallas_call | solution.py:517
  117.7 2.5 %collective-permute-start.8 = (bf16[2,8,80,256]{3,2,1,0:T(8,128)(2,1)}, bf16[2,8,80,256]{3,2,1,0:T(8,128)(2,1)S(1)}, u32[]{:S(2)}, u32[]{:S(2)}) collective-permute-start(bf16[2,8,80,256]{3,2,1,0:T(8,128)(2,1)} %bitcast.93), channel_id=1, source_target_pairs={{4,0},{8,4},{12,8},{16,12},{20,16},{24,20},{28,24},{32,28},{36,32}... | collective-permute-start | bytes 1966088 | tf_op jit(solution)/shard_map/ppermute | solution.py:552
  120.2 0.9 slice_bitcast_fusion
  121.2 1.3 collective-permute-start.10
  122.5 3.6 %collective-permute-start.11 = (bf16[2,80,256]{2,1,0:T(8,128)(2,1)S(1)}, bf16[2,80,256]{2,1,0:T(8,128)(2,1)S(1)}, u32[]{:S(2)}, u32[]{:S(2)}) collective-permute-start(bf16[2,80,256]{2,1,0:T(8,128)(2,1)S(1)} %get-tuple-element.98), channel_id=1, source_target_pairs={{0,1},{1,2},{2,3},{4,5},{5,6},{6,7},{8,9},{9,10},{10,11},{12,13},{... | collective-permute-start | bytes 245768 | tf_op jit(solution)/shard_map/ppermute | solution.py:544
  126.1 1.3 collective-permute-start.12
  127.4 3.2 %collective-permute-start.9 = (bf16[2,80,256]{2,1,0:T(8,128)(2,1)S(1)}, bf16[2,80,256]{2,1,0:T(8,128)(2,1)S(1)}, u32[]{:S(2)}, u32[]{:S(2)}) collective-permute-start(bf16[2,80,256]{2,1,0:T(8,128)(2,1)S(1)} %get-tuple-element.98), channel_id=1, source_target_pairs={{4,1},{5,2},{6,3},{8,5},{9,6},{10,7},{12,9},{13,10},{14,11},{16,13... | collective-permute-start | bytes 245768 | tf_op jit(solution)/shard_map/ppermute | solution.py:556
  130.7 0.6 copy-done.21
  132.0 0.6 copy-done.22
  133.1 2.5 %collective-permute-done.8 = bf16[2,8,80,256]{3,2,1,0:T(8,128)(2,1)S(1)} collective-permute-done((bf16[2,8,80,256]{3,2,1,0:T(8,128)(2,1)}, bf16[2,8,80,256]{3,2,1,0:T(8,128)(2,1)S(1)}, u32[]{:S(2)}, u32[]{:S(2)}) %collective-permute-start.8) | collective-permute-done | bytes 655392 | tf_op jit(solution)/shard_map/ppermute | solution.py:552
  135.7 0.8 copy-done.12
  136.7 3.0 %shard_map.159 = bf16[64,112,128]{2,1,0:T(8,128)(2,1)} custom-call(bf16[16,112,128]{2,1,0:T(8,128)(2,1)} %get-tuple-element.73.refs_0_, bf16[16,112,128]{2,1,0:T(8,128)(2,1)} %get-tuple-element.74.refs_1_, bf16[16,112,128]{2,1,0:T(8,128)(2,1)} %get-tuple-element.75.refs_2_, bf16[16,112,128]{2,1,0:T(8,128)(2,1)} %get-tuple-element.76.refs_3_, ...), custom_call_target="tpu_custom_call" | custom-call | flops 1024 | bytes 1024 | tf_op jit(solution)/shard_map/pallas_call | solution.py:517
  139.8 1.2 copy-done.8
  141.0 13.0 %all-to-all-start.3 = ((bf16[64,112,128]{2,1,0:T(8,128)(2,1)}), bf16[64,112,128]{2,1,0:T(8,128)(2,1)S(1)}, u32[]{:S(2)}, u32[]{:S(2)}) async-start(bf16[64,112,128]{2,1,0:T(8,128)(2,1)} %shard_map.159), calls=%async_computation.3 | async-start | bytes 3670016 | tf_op jit(solution)/shard_map/all_to_all | solution.py:616
  154.0 0.8 constant_dynamic-slice_fusion.1
  154.8 0.6 reshape.128.refs_1_
  155.4 2.3 shard_map.160
  157.8 2.3 collective-permute-start.17
  161.2 0.8 constant_dynamic-slice_fusion
  162.7 10.8 %shard_map.161 = (f32[1280,256]{1,0:T(8,128)}, f32[8,128]{1,0:T(8,128)}) custom-call(f32[3]{0:T(128)} %maximum_maximum_fusion.1.refs_0_, bf16[1280,256]{1,0:T(8,128)(2,1)} %get-tuple-element.84.refs_1_, bf16[160,256]{1,0:T(8,128)(2,1)} %bitcast.106, bf16[160,256]{1,0:T(8,128)(2,1)} %bitcast.107, bf16[1280,256]{1,0:T(8,128)(2,1)} %bitcast.96, ...), custom_call_target="tpu_custom_call" | custom-call | flops 1024 | bytes 1024 | tf_op jit(solution)/shard_map/pallas_call | solution.py:517
  173.5 2.0 collective-permute-done.17
  175.5 1.5 collective-permute-done.18
  177.1 3.2 %all-to-all-done.3.refs_0_ = bf16[64,112,128]{2,1,0:T(8,128)(2,1)S(1)} async-done(((bf16[64,112,128]{2,1,0:T(8,128)(2,1)}), bf16[64,112,128]{2,1,0:T(8,128)(2,1)S(1)}, u32[]{:S(2)}, u32[]{:S(2)}) %all-to-all-start.3) | async-done | bytes 1835040 | tf_op jit(solution)/shard_map/all_to_all | solution.py:616
  180.3 1.2 copy-done.7
  181.5 3.9 %shard_map.162 = (f32[108,128]{1,0:T(8,128)}, f32[108,128]{1,0:T(8,128)}, bf16[16,112,128]{2,1,0:T(8,128)(2,1)}) custom-call(bf16[64,112,128]{2,1,0:T(8,128)(2,1)} %copy-done.7, bf16[108,128]{1,0:T(8,128)(2,1)} %reshape.131.refs_1_, f32[108,128]{1,0:T(8,128)} %bitcast.113, f32[108,128]{1,0:T(8,128)} %bitcast.114, f32[8,128]{1,0:T(8,128)} %get-tuple-element.85.refs_4_), custom_call_target="tpu_custom_call" | custom-call | flops 1024 | bytes 1024 | tf_op jit(solution)/shard_map/pallas_call | solution.py:517
  185.4 12.3 %all_to_all.53.refs_2_ = bf16[16,112,128]{2,1,0:T(8,128)(2,1)S(1)} all-to-all(bf16[16,112,128]{2,1,0:T(8,128)(2,1)} %get-tuple-element.86), channel_id=1, replica_groups={{0,8,16,24,32,40,48,56,64,72,80,88,96,104,112,120},{1,9,17,25,33,41,49,..., dimensions={0} | all-to-all | bytes 917504 | tf_op jit(solution)/shard_map/all_to_all | solution.py:573
  197.7 1.6 broadcast_in_dim.24
  199.3 3.7 %all-to-all-start.6 = ((bf16[16,448,128]{2,1,0:T(8,128)(2,1)}), bf16[16,448,128]{2,1,0:T(8,128)(2,1)S(1)}, u32[]{:S(2)}, u32[]{:S(2)}) async-start(bf16[16,448,128]{2,1,0:T(8,128)(2,1)} %broadcast_in_dim.24), calls=%async_computation.6 | async-start | bytes 3670016 | tf_op jit(solution)/shard_map/all_to_all | solution.py:573
  203.0 0.7 collective-permute-start.20
  203.7 2.4 collective-permute-start.21
  206.1 1.9 collective-permute-start.22
  208.0 4.9 %collective-permute-done.20.refs_3_ = bf16[16,112,128]{2,1,0:T(8,128)(2,1)S(1)} collective-permute-done((bf16[16,112,128]{2,1,0:T(8,128)(2,1)S(1)}, bf16[16,112,128]{2,1,0:T(8,128)(2,1)S(1)}, u32[]{:S(2)}, u32[]{:S(2)}) %collective-permute-start.20) | collective-permute-done | bytes 458784 | tf_op jit(solution)/shard_map/ppermute | solution.py:579
  212.9 10.9 %collective-permute-done.21.refs_4_ = bf16[16,112,128]{2,1,0:T(8,128)(2,1)S(1)} collective-permute-done((bf16[16,112,128]{2,1,0:T(8,128)(2,1)S(1)}, bf16[16,112,128]{2,1,0:T(8,128)(2,1)S(1)}, u32[]{:S(2)}, u32[]{:S(2)}) %collective-permute-start.21) | collective-permute-done | bytes 458784 | tf_op jit(solution)/shard_map/ppermute | solution.py:579
  223.8 2.3 collective-permute-done.22.refs_5_
  226.1 4.9 %collective-permute-start.27 = (bf16[16,448,128]{2,1,0:T(8,128)(2,1)S(1)}, bf16[16,448,128]{2,1,0:T(8,128)(2,1)S(1)}, u32[]{:S(2)}, u32[]{:S(2)}) collective-permute-start(bf16[16,448,128]{2,1,0:T(8,128)(2,1)S(1)} %all-to-all-done.6), channel_id=1, source_target_pairs={{0,4},{1,5},{2,6},{3,7},{4,0},{5,1},{6,2},{7,3},{8,12},{9,13},{10,... | collective-permute-start | bytes 5505032 | tf_op jit(solution)/shard_map/ppermute | solution.py:749
  232.1 2.4 collective-permute-done.27
  234.5 4.2 %shard_map.163 = bf16[6912,256]{1,0:T(8,128)(2,1)} custom-call(s32[1]{0:T(128)} %bitcast.refs_0_, bf16[64,112,128]{2,1,0:T(8,128)(2,1)S(1)} %bitcast.86, bf16[64,112,128]{2,1,0:T(8,128)(2,1)S(1)} %bitcast.89), custom_call_target="tpu_custom_call" | custom-call | flops 1024 | bytes 1024 | tf_op jit(solution)/shard_map/pallas_call | solution.py:517
  238.8 5.7 %shard_map.164 = (bf16[6912,256]{1,0:T(8,128)(2,1)}, bf16[1280,256]{1,0:T(8,128)(2,1)}) custom-call(s32[1]{0:T(128)} %bitcast.refs_0_, s32[1]{0:T(128)} %bitcast.1.refs_1_, bf16[16,112,128]{2,1,0:T(8,128)(2,1)S(1)} %all_to_all.53.refs_2_, bf16[16,112,128]{2,1,0:T(8,128)(2,1)S(1)} %collective-permute-done.20.refs_3_, ...), custom_call_target="tpu_custom_call" | custom-call | flops 1024 | bytes 1024 | tf_op jit(solution)/shard_map/pallas_call | solution.py:517
  (85 shorter events, 7.0 us)
Async XLA Ops:
  0.6 13.5 %copy-start = (bf16[2,8,80,256]{3,2,1,0:T(8,128)(2,1)S(1)}, bf16[2,8,80,256]{3,2,1,0:T(8,128)(2,1)}, u32[]{:S(2)}) copy-start(bf16[2,8,80,256]{3,2,1,0:T(8,128)(2,1)} %param.10) | copy-start | bytes 1966084
  2.6 7.8 %collective-permute-start = (bf16[4,80,256]{2,1,0:T(8,128)(2,1)S(1)}, bf16[4,80,256]{2,1,0:T(8,128)(2,1)S(1)}, u32[]{:S(2)}, u32[]{:S(2)}) collective-permute-start(bf16[4,80,256]{2,1,0:T(8,128)(2,1)S(1)} %pad_maximum_fusion.2), channel_id=1, source_target_pairs={{0,1},{1,2},{2,3},{4,5},{5,6},{6,7},{8,9},{9,10},{10,11},{12,13},{... | collective-permute-start | bytes 491528 | tf_op jit(solution)/shard_map/ppermute | solution.py:544
  6.6 12.6 %copy-start.2 = (bf16[2,8,80,256]{3,2,1,0:T(8,128)(2,1)S(1)}, bf16[2,8,80,256]{3,2,1,0:T(8,128)(2,1)}, u32[]{:S(2)}) copy-start(bf16[2,8,80,256]{3,2,1,0:T(8,128)(2,1)} %param.11) | copy-start | bytes 1966084
  6.6 6.8 %collective-permute-start.1 = (bf16[4,80,256]{2,1,0:T(8,128)(2,1)S(1)}, bf16[4,80,256]{2,1,0:T(8,128)(2,1)S(1)}, u32[]{:S(2)}, u32[]{:S(2)}) collective-permute-start(bf16[4,80,256]{2,1,0:T(8,128)(2,1)S(1)} %pad_maximum_fusion.3), channel_id=1, source_target_pairs={{1,0},{2,1},{3,2},{5,4},{6,5},{7,6},{9,8},{10,9},{11,10},{13,12},{... | collective-permute-start | bytes 491528 | tf_op jit(solution)/shard_map/ppermute | solution.py:544
  14.2 26.9 %collective-permute-start.2 = (bf16[2,10,80,256]{3,2,1,0:T(8,128)(2,1)S(1)}, bf16[2,10,80,256]{3,2,1,0:T(8,128)(2,1)}, u32[]{:S(2)}, u32[]{:S(2)}) collective-permute-start(bf16[2,10,80,256]{3,2,1,0:T(8,128)(2,1)S(1)} %pad_maximum_fusion), channel_id=1, source_target_pairs={{0,4},{4,8},{8,12},{12,16},{16,20},{20,24},{24,28},{28,32},{32,36}... | collective-permute-start | bytes 2457608 | tf_op jit(solution)/shard_map/ppermute | solution.py:565
  19.3 37.5 %collective-permute-start.3 = (bf16[2,10,80,256]{3,2,1,0:T(8,128)(2,1)S(1)}, bf16[2,10,80,256]{3,2,1,0:T(8,128)(2,1)S(1)}, u32[]{:S(2)}, u32[]{:S(2)}) collective-permute-start(bf16[2,10,80,256]{3,2,1,0:T(8,128)(2,1)S(1)} %pad_maximum_fusion.1), channel_id=1, source_target_pairs={{4,0},{8,4},{12,8},{16,12},{20,16},{24,20},{28,24},{32,28},{36,32}... | collective-permute-start | bytes 2457608 | tf_op jit(solution)/shard_map/ppermute | solution.py:565
  21.2 19.9 %all-to-all-start = ((f32[128,1,128]{2,1,0:T(1,128)}), f32[128,1,128]{2,1,0:T(1,128)S(1)}, u32[]{:S(2)}, u32[]{:S(2)}) async-start(f32[128,1,128]{2,1,0:T(1,128)} %bitcast.18), calls=%async_computation | async-start | bytes 131072 | tf_op jit(solution)/shard_map/all_to_all | solution.py:530
  41.1 0.6 copy-start.5
  51.7 15.0 %all-to-all-start.1 = ((f32[128,1,128]{2,1,0:T(1,128)}), f32[128,1,128]{2,1,0:T(1,128)S(1)}, u32[]{:S(2)}, u32[]{:S(2)}) async-start(f32[128,1,128]{2,1,0:T(1,128)} %bitcast.110), calls=%async_computation.1 | async-start | bytes 131072 | tf_op jit(solution)/shard_map/all_to_all | solution.py:530
  56.8 0.9 copy-start.9
  66.7 0.6 copy-start.11
  79.9 10.9 %collective-permute-start.4 = (bf16[16,112,128]{2,1,0:T(8,128)(2,1)}, bf16[16,112,128]{2,1,0:T(8,128)(2,1)S(1)}, u32[]{:S(2)}, u32[]{:S(2)}) collective-permute-start(bf16[16,112,128]{2,1,0:T(8,128)(2,1)} %get-tuple-element.64), channel_id=1, source_target_pairs={{0,4},{1,5},{2,6},{3,7},{4,0},{5,1},{6,2},{7,3},{8,12},{9,13},{10,... | collective-permute-start | bytes 1376264 | tf_op jit(solution)/shard_map/ppermute | solution.py:609
  81.2 9.6 %collective-permute-start.5 = (bf16[16,112,128]{2,1,0:T(8,128)(2,1)}, bf16[16,112,128]{2,1,0:T(8,128)(2,1)S(1)}, u32[]{:S(2)}, u32[]{:S(2)}) collective-permute-start(bf16[16,112,128]{2,1,0:T(8,128)(2,1)} %get-tuple-element.65), channel_id=1, source_target_pairs={{0,4},{1,5},{2,6},{3,7},{4,0},{5,1},{6,2},{7,3},{8,12},{9,13},{10,... | collective-permute-start | bytes 1376264 | tf_op jit(solution)/shard_map/ppermute | solution.py:609
  81.3 9.5 %collective-permute-start.6 = (bf16[16,112,128]{2,1,0:T(8,128)(2,1)}, bf16[16,112,128]{2,1,0:T(8,128)(2,1)S(1)}, u32[]{:S(2)}, u32[]{:S(2)}) collective-permute-start(bf16[16,112,128]{2,1,0:T(8,128)(2,1)} %get-tuple-element.66), channel_id=1, source_target_pairs={{0,4},{1,5},{2,6},{3,7},{4,0},{5,1},{6,2},{7,3},{8,12},{9,13},{10,... | collective-permute-start | bytes 1376264 | tf_op jit(solution)/shard_map/ppermute | solution.py:609
  81.7 9.1 %collective-permute-start.7 = (bf16[16,112,128]{2,1,0:T(8,128)(2,1)}, bf16[16,112,128]{2,1,0:T(8,128)(2,1)S(1)}, u32[]{:S(2)}, u32[]{:S(2)}) collective-permute-start(bf16[16,112,128]{2,1,0:T(8,128)(2,1)} %get-tuple-element.67), channel_id=1, source_target_pairs={{0,4},{1,5},{2,6},{3,7},{4,0},{5,1},{6,2},{7,3},{8,12},{9,13},{10,... | collective-permute-start | bytes 1376264 | tf_op jit(solution)/shard_map/ppermute | solution.py:609
  81.8 18.6 %all-to-all-start.2 = ((f32[128,1,128]{2,1,0:T(1,128)}), f32[128,1,128]{2,1,0:T(1,128)S(1)}, u32[]{:S(2)}, u32[]{:S(2)}) async-start(f32[128,1,128]{2,1,0:T(1,128)} %bitcast.109), calls=%async_computation.2 | async-start | bytes 131072 | tf_op jit(solution)/shard_map/all_to_all | solution.py:530
  90.7 0.8 copy-start.14
  90.8 0.9 copy-start.15
  90.8 1.0 copy-start.17
  90.8 1.2 copy-start.18
  100.4 0.6 copy-start.19
  101.0 38.7 %all-to-all-start.4 = ((bf16[64,112,128]{2,1,0:T(8,128)(2,1)}), bf16[64,112,128]{2,1,0:T(8,128)(2,1)S(1)}, u32[]{:S(2)}, u32[]{:S(2)}) async-start(bf16[64,112,128]{2,1,0:T(8,128)(2,1)} %shard_map.157), calls=%async_computation.4 | async-start | bytes 3670016 | tf_op jit(solution)/shard_map/all_to_all | solution.py:616
  117.7 17.9 %collective-permute-start.8 = (bf16[2,8,80,256]{3,2,1,0:T(8,128)(2,1)}, bf16[2,8,80,256]{3,2,1,0:T(8,128)(2,1)S(1)}, u32[]{:S(2)}, u32[]{:S(2)}) collective-permute-start(bf16[2,8,80,256]{3,2,1,0:T(8,128)(2,1)} %bitcast.93), channel_id=1, source_target_pairs={{4,0},{8,4},{12,8},{16,12},{20,16},{24,20},{28,24},{32,28},{36,32}... | collective-permute-start | bytes 1966088 | tf_op jit(solution)/shard_map/ppermute | solution.py:552
  121.2 9.4 %collective-permute-start.10 = (bf16[2,80,256]{2,1,0:T(8,128)(2,1)S(1)}, bf16[2,80,256]{2,1,0:T(8,128)(2,1)S(1)}, u32[]{:S(2)}, u32[]{:S(2)}) collective-permute-start(bf16[2,80,256]{2,1,0:T(8,128)(2,1)S(1)} %get-tuple-element.97), channel_id=1, source_target_pairs={{5,0},{6,1},{7,2},{9,4},{10,5},{11,6},{13,8},{14,9},{15,10},{17,12... | collective-permute-start | bytes 245768 | tf_op jit(solution)/shard_map/ppermute | solution.py:556
  122.5 8.2 %collective-permute-start.11 = (bf16[2,80,256]{2,1,0:T(8,128)(2,1)S(1)}, bf16[2,80,256]{2,1,0:T(8,128)(2,1)S(1)}, u32[]{:S(2)}, u32[]{:S(2)}) collective-permute-start(bf16[2,80,256]{2,1,0:T(8,128)(2,1)S(1)} %get-tuple-element.98), channel_id=1, source_target_pairs={{0,1},{1,2},{2,3},{4,5},{5,6},{6,7},{8,9},{9,10},{10,11},{12,13},{... | collective-permute-start | bytes 245768 | tf_op jit(solution)/shard_map/ppermute | solution.py:544
  126.1 5.9 %collective-permute-start.12 = (bf16[2,80,256]{2,1,0:T(8,128)(2,1)S(1)}, bf16[2,80,256]{2,1,0:T(8,128)(2,1)S(1)}, u32[]{:S(2)}, u32[]{:S(2)}) collective-permute-start(bf16[2,80,256]{2,1,0:T(8,128)(2,1)S(1)} %get-tuple-element.97), channel_id=1, source_target_pairs={{1,0},{2,1},{3,2},{5,4},{6,5},{7,6},{9,8},{10,9},{11,10},{13,12},{... | collective-permute-start | bytes 245768 | tf_op jit(solution)/shard_map/ppermute | solution.py:544
  127.4 5.2 %collective-permute-start.9 = (bf16[2,80,256]{2,1,0:T(8,128)(2,1)S(1)}, bf16[2,80,256]{2,1,0:T(8,128)(2,1)S(1)}, u32[]{:S(2)}, u32[]{:S(2)}) collective-permute-start(bf16[2,80,256]{2,1,0:T(8,128)(2,1)S(1)} %get-tuple-element.98), channel_id=1, source_target_pairs={{4,1},{5,2},{6,3},{8,5},{9,6},{10,7},{12,9},{13,10},{14,11},{16,13... | collective-permute-start | bytes 245768 | tf_op jit(solution)/shard_map/ppermute | solution.py:556
  130.6 27.1 %copy-start.20 = (bf16[2,80,256]{2,1,0:T(8,128)(2,1)}, bf16[2,80,256]{2,1,0:T(8,128)(2,1)S(1)}, u32[]{:S(2)}) copy-start(bf16[2,80,256]{2,1,0:T(8,128)(2,1)S(1)} %collective-permute-done.10) | copy-start | bytes 245764
  130.6 5.0 %collective-permute-start.13 = (bf16[16,112,128]{2,1,0:T(8,128)(2,1)}, bf16[16,112,128]{2,1,0:T(8,128)(2,1)S(1)}, u32[]{:S(2)}, u32[]{:S(2)}) collective-permute-start(bf16[16,112,128]{2,1,0:T(8,128)(2,1)} %get-tuple-element.77), channel_id=1, source_target_pairs={{0,4},{1,5},{2,6},{3,7},{4,0},{5,1},{6,2},{7,3},{8,12},{9,13},{10,... | collective-permute-start | bytes 1376264 | tf_op jit(solution)/shard_map/ppermute | solution.py:609
  130.7 0.6 copy-start.21
  131.4 4.3 %collective-permute-start.14 = (bf16[16,112,128]{2,1,0:T(8,128)(2,1)}, bf16[16,112,128]{2,1,0:T(8,128)(2,1)S(1)}, u32[]{:S(2)}, u32[]{:S(2)}) collective-permute-start(bf16[16,112,128]{2,1,0:T(8,128)(2,1)} %get-tuple-element.78), channel_id=1, source_target_pairs={{0,4},{1,5},{2,6},{3,7},{4,0},{5,1},{6,2},{7,3},{8,12},{9,13},{10,... | collective-permute-start | bytes 1376264 | tf_op jit(solution)/shard_map/ppermute | solution.py:609
  132.0 0.6 copy-start.22
  132.6 3.0 %collective-permute-start.15 = (bf16[16,112,128]{2,1,0:T(8,128)(2,1)}, bf16[16,112,128]{2,1,0:T(8,128)(2,1)S(1)}, u32[]{:S(2)}, u32[]{:S(2)}) collective-permute-start(bf16[16,112,128]{2,1,0:T(8,128)(2,1)} %get-tuple-element.79), channel_id=1, source_target_pairs={{0,4},{1,5},{2,6},{3,7},{4,0},{5,1},{6,2},{7,3},{8,12},{9,13},{10,... | collective-permute-start | bytes 1376264 | tf_op jit(solution)/shard_map/ppermute | solution.py:609
  132.6 3.0 %copy-start.23 = (bf16[2,80,256]{2,1,0:T(8,128)(2,1)}, bf16[2,80,256]{2,1,0:T(8,128)(2,1)S(1)}, u32[]{:S(2)}) copy-start(bf16[2,80,256]{2,1,0:T(8,128)(2,1)S(1)} %collective-permute-done.9) | copy-start | bytes 245764
  132.6 3.1 %collective-permute-start.16 = (bf16[16,112,128]{2,1,0:T(8,128)(2,1)}, bf16[16,112,128]{2,1,0:T(8,128)(2,1)}, u32[]{:S(2)}, u32[]{:S(2)}) collective-permute-start(bf16[16,112,128]{2,1,0:T(8,128)(2,1)} %get-tuple-element.80), channel_id=1, source_target_pairs={{0,4},{1,5},{2,6},{3,7},{4,0},{5,1},{6,2},{7,3},{8,12},{9,13},{10,... | collective-permute-start | bytes 1376264 | tf_op jit(solution)/shard_map/ppermute | solution.py:609
  135.6 4.1 %copy-start.10 = (bf16[2,8,80,256]{3,2,1,0:T(8,128)(2,1)}, bf16[2,8,80,256]{3,2,1,0:T(8,128)(2,1)S(1)}, u32[]{:S(2)}) copy-start(bf16[2,8,80,256]{3,2,1,0:T(8,128)(2,1)S(1)} %collective-permute-done.8) | copy-start | bytes 1966084
  135.6 0.8 copy-start.12
  135.6 1.0 copy-start.13
  135.6 1.1 copy-start.16
  139.8 1.2 copy-start.8
  141.0 39.3 %all-to-all-start.3 = ((bf16[64,112,128]{2,1,0:T(8,128)(2,1)}), bf16[64,112,128]{2,1,0:T(8,128)(2,1)S(1)}, u32[]{:S(2)}, u32[]{:S(2)}) async-start(bf16[64,112,128]{2,1,0:T(8,128)(2,1)} %shard_map.159), calls=%async_computation.3 | async-start | bytes 3670016 | tf_op jit(solution)/shard_map/all_to_all | solution.py:616
  157.8 17.7 %collective-permute-start.17 = (bf16[1,112,128]{2,1,0:T(8,128)(2,1)}, bf16[1,112,128]{2,1,0:T(8,128)(2,1)S(1)}, u32[]{:S(2)}, u32[]{:S(2)}) collective-permute-start(bf16[1,112,128]{2,1,0:T(8,128)(2,1)} %get-tuple-element.82), channel_id=1, source_target_pairs={{0,3},{1,0},{2,1},{3,2},{4,7},{5,4},{6,5},{7,6},{8,11},{9,8},{10,9... | collective-permute-start | bytes 86024 | tf_op jit(solution)/shard_map/ppermute | solution.py:579
  160.1 16.9 %collective-permute-start.18 = (bf16[1,112,128]{2,1,0:T(8,128)(2,1)}, bf16[1,112,128]{2,1,0:T(8,128)(2,1)S(1)}, u32[]{:S(2)}, u32[]{:S(2)}) collective-permute-start(bf16[1,112,128]{2,1,0:T(8,128)(2,1)} %get-tuple-element.82), channel_id=1, source_target_pairs={{0,2},{1,3},{2,0},{3,1},{4,6},{5,7},{6,4},{7,5},{8,10},{9,11},{10,... | collective-permute-start | bytes 86024 | tf_op jit(solution)/shard_map/ppermute | solution.py:579
  160.6 16.4 %collective-permute-start.19 = (bf16[1,112,128]{2,1,0:T(8,128)(2,1)}, bf16[1,112,128]{2,1,0:T(8,128)(2,1)S(1)}, u32[]{:S(2)}, u32[]{:S(2)}) collective-permute-start(bf16[1,112,128]{2,1,0:T(8,128)(2,1)} %get-tuple-element.82), channel_id=1, source_target_pairs={{0,1},{1,2},{2,3},{3,0},{4,5},{5,6},{6,7},{7,4},{8,9},{9,10},{10,1... | collective-permute-start | bytes 86024 | tf_op jit(solution)/shard_map/ppermute | solution.py:579
  162.7 14.3 %copy-start.24 = (bf16[1,112,128]{2,1,0:T(8,128)(2,1)S(1)}, bf16[1,112,128]{2,1,0:T(8,128)(2,1)}, u32[]{:S(2)}) copy-start(bf16[1,112,128]{2,1,0:T(8,128)(2,1)} %get-tuple-element.82) | copy-start | bytes 86020
  180.3 1.2 copy-start.7
  199.3 26.8 %all-to-all-start.6 = ((bf16[16,448,128]{2,1,0:T(8,128)(2,1)}), bf16[16,448,128]{2,1,0:T(8,128)(2,1)S(1)}, u32[]{:S(2)}, u32[]{:S(2)}) async-start(bf16[16,448,128]{2,1,0:T(8,128)(2,1)} %broadcast_in_dim.24), calls=%async_computation.6 | async-start | bytes 3670016 | tf_op jit(solution)/shard_map/all_to_all | solution.py:573
  203.0 9.9 %collective-permute-start.20 = (bf16[16,112,128]{2,1,0:T(8,128)(2,1)S(1)}, bf16[16,112,128]{2,1,0:T(8,128)(2,1)S(1)}, u32[]{:S(2)}, u32[]{:S(2)}) collective-permute-start(bf16[16,112,128]{2,1,0:T(8,128)(2,1)S(1)} %all_to_all.53.refs_2_), channel_id=1, source_target_pairs={{0,1},{1,2},{2,3},{3,0},{4,5},{5,6},{6,7},{7,4},{8,9},{9,10},{10,1... | collective-permute-start | bytes 1376264 | tf_op jit(solution)/shard_map/ppermute | solution.py:579
  203.7 20.1 %collective-permute-start.21 = (bf16[16,112,128]{2,1,0:T(8,128)(2,1)S(1)}, bf16[16,112,128]{2,1,0:T(8,128)(2,1)S(1)}, u32[]{:S(2)}, u32[]{:S(2)}) collective-permute-start(bf16[16,112,128]{2,1,0:T(8,128)(2,1)S(1)} %all_to_all.53.refs_2_), channel_id=1, source_target_pairs={{0,2},{1,3},{2,0},{3,1},{4,6},{5,7},{6,4},{7,5},{8,10},{9,11},{10,... | collective-permute-start | bytes 1376264 | tf_op jit(solution)/shard_map/ppermute | solution.py:579
  206.1 20.1 %collective-permute-start.22 = (bf16[16,112,128]{2,1,0:T(8,128)(2,1)S(1)}, bf16[16,112,128]{2,1,0:T(8,128)(2,1)}, u32[]{:S(2)}, u32[]{:S(2)}) collective-permute-start(bf16[16,112,128]{2,1,0:T(8,128)(2,1)S(1)} %all_to_all.53.refs_2_), channel_id=1, source_target_pairs={{0,3},{1,0},{2,1},{3,2},{4,7},{5,4},{6,5},{7,6},{8,11},{9,8},{10,9... | collective-permute-start | bytes 1376264 | tf_op jit(solution)/shard_map/ppermute | solution.py:579
  226.1 8.3 %collective-permute-start.27 = (bf16[16,448,128]{2,1,0:T(8,128)(2,1)S(1)}, bf16[16,448,128]{2,1,0:T(8,128)(2,1)S(1)}, u32[]{:S(2)}, u32[]{:S(2)}) collective-permute-start(bf16[16,448,128]{2,1,0:T(8,128)(2,1)S(1)} %all-to-all-done.6), channel_id=1, source_target_pairs={{0,4},{1,5},{2,6},{3,7},{4,0},{5,1},{6,2},{7,3},{8,12},{9,13},{10,... | collective-permute-start | bytes 5505032 | tf_op jit(solution)/shard_map/ppermute | solution.py:749
  231.1 7.7 %collective-permute-start.23 = (bf16[16,112,128]{2,1,0:T(8,128)(2,1)S(1)}, bf16[16,112,128]{2,1,0:T(8,128)(2,1)S(1)}, u32[]{:S(2)}, u32[]{:S(2)}) collective-permute-start(bf16[16,112,128]{2,1,0:T(8,128)(2,1)S(1)} %all_to_all.53.refs_2_), channel_id=1, source_target_pairs={{0,4},{1,5},{2,6},{3,7},{4,0},{5,1},{6,2},{7,3},{8,12},{9,13},{10,... | collective-permute-start | bytes 1376264 | tf_op jit(solution)/shard_map/ppermute | solution.py:750
  231.1 7.7 %collective-permute-start.24 = (bf16[16,112,128]{2,1,0:T(8,128)(2,1)S(1)}, bf16[16,112,128]{2,1,0:T(8,128)(2,1)S(1)}, u32[]{:S(2)}, u32[]{:S(2)}) collective-permute-start(bf16[16,112,128]{2,1,0:T(8,128)(2,1)S(1)} %collective-permute-done.20.refs_3_), channel_id=1, source_target_pairs={{0,4},{1,5},{2,6},{3,7},{4,0},{5,1},{6,2},{7,3},{8,12},{9,13},{10,... | collective-permute-start | bytes 1376264 | tf_op jit(solution)/shard_map/ppermute | solution.py:750
  231.6 7.2 %collective-permute-start.25 = (bf16[16,112,128]{2,1,0:T(8,128)(2,1)S(1)}, bf16[16,112,128]{2,1,0:T(8,128)(2,1)S(1)}, u32[]{:S(2)}, u32[]{:S(2)}) collective-permute-start(bf16[16,112,128]{2,1,0:T(8,128)(2,1)S(1)} %collective-permute-done.21.refs_4_), channel_id=1, source_target_pairs={{0,4},{1,5},{2,6},{3,7},{4,0},{5,1},{6,2},{7,3},{8,12},{9,13},{10,... | collective-permute-start | bytes 1376264 | tf_op jit(solution)/shard_map/ppermute | solution.py:750
  231.6 7.2 %collective-permute-start.26 = (bf16[16,112,128]{2,1,0:T(8,128)(2,1)}, bf16[16,112,128]{2,1,0:T(8,128)(2,1)S(1)}, u32[]{:S(2)}, u32[]{:S(2)}) collective-permute-start(bf16[16,112,128]{2,1,0:T(8,128)(2,1)} %collective-permute-done.22.refs_5_), channel_id=1, source_target_pairs={{0,4},{1,5},{2,6},{3,7},{4,0},{5,1},{6,2},{7,3},{8,12},{9,13},{10,... | collective-permute-start | bytes 1376264 | tf_op jit(solution)/shard_map/ppermute | solution.py:750
  234.5 4.3 %copy-start.1 = (bf16[2,8,80,256]{3,2,1,0:T(8,128)(2,1)S(1)}, bf16[2,8,80,256]{3,2,1,0:T(8,128)(2,1)}, u32[]{:S(2)}) copy-start(bf16[2,8,80,256]{3,2,1,0:T(8,128)(2,1)} %param.10) | copy-start | bytes 1966084
  234.5 4.3 %copy-start.3 = (bf16[2,8,80,256]{3,2,1,0:T(8,128)(2,1)S(1)}, bf16[2,8,80,256]{3,2,1,0:T(8,128)(2,1)}, u32[]{:S(2)}) copy-start(bf16[2,8,80,256]{3,2,1,0:T(8,128)(2,1)} %param.11) | copy-start | bytes 1966084
  234.5 4.3 %copy-start.4 = (f32[1280,256]{1,0:T(8,128)S(1)}, f32[1280,256]{1,0:T(8,128)}, u32[]{:S(2)}) copy-start(f32[1280,256]{1,0:T(8,128)} %get-tuple-element.90.refs_10_) | copy-start | bytes 3932164
  234.5 4.3 %copy-start.6 = (f32[128,1,128]{2,1,0:T(1,128)S(1)}, f32[128,1,128]{2,1,0:T(1,128)}, u32[]{:S(2)}) copy-start(f32[128,1,128]{2,1,0:T(1,128)} %copy-done.5) | copy-start | bytes 196612

commit v6 on v5

--- a/solution.py
+++ b/solution.py
@@ -189,34 +189,29 @@
     return jnp.concatenate([patches[at : at + BAND, :] for at in starts], axis=0)
 
 
-def wgrad(patches, grad, whole):
+def cut_blocks(blocks, whole, core, kept, given):
+    for i in blocks:
+        for side, outs in ((1 - core, given), (core, kept)):
+            at = pl.multiple_of(i * BLOCK + side * (BLOCK // 2), 8)
+            slab = whole[pl.ds(at, BLOCK // 2 + 8), :]
+            for x in range(4):
+                rows = slab[x * (SHARE // 2) : x * (SHARE // 2) + PIECE // 2, :]
+                piece = jnp.concatenate([rows[:, :128], rows[:, 128:]], axis=0)
+                outs[i // 4].ref[i % 4 * 4 + x] = piece.astype(BF16)
+            if i % 4 == 3:
+                outs[i // 4].send()
+
+
+def wgrad(product, whole, core, kept, given):
+    done = 0
+    whole[27 * C :, :] = jnp.zeros((8, C), F32)
     for a in range(3):
-        ready = patches.get(a + FR - 1)
         for b in range(3):
-            left = both_frames(ready, lambda t: (t + a, b))
-            total = lax.dot_general(
-                left, grad[...], (((0,), (0,)), ((), ())), preferred_element_type=F32
-            )
             tap = (9 * a + 3 * b) * C
-            whole[tap : tap + 3 * C, :] = total * SCALE
-
-
-def cut_pieces(whole, core, kept, given):
-    whole[27 * C :, :] = jnp.zeros((8, C), F32)
-    for side, outs in ((1 - core, given), (core, kept)):
-        for k, out in enumerate(outs):
-
-            def block(i, _):
-                at = pl.multiple_of((4 * k + i) * BLOCK + side * (BLOCK // 2), 8)
-                slab = whole[pl.ds(at, BLOCK // 2 + 8), :]
-                for x in range(4):
-                    rows = slab[x * (SHARE // 2) : x * (SHARE // 2) + PIECE // 2, :]
-                    piece = jnp.concatenate([rows[:, :128], rows[:, 128:]], axis=0)
-                    out.ref[i * 4 + x] = piece.astype(BF16)
-                return 0
-
-            lax.fori_loop(0, 4, block, 0)
-            out.send()
+            product(a, b, whole.at[tap : tap + 3 * C, :])
+            ready = (tap + 3 * C) // BLOCK
+            cut_blocks(range(done, ready), whole, core, kept, given)
+            done = ready
 
 
 def silu_parts(value, center, inverse, gain):
@@ -283,16 +278,15 @@
     row.ref[...] = slopes(read, back.get(), center, inverse, gain.get()[...], slope.ref, hidden)
     slope.send()
     turned = hidden[...].astype(F32).T.astype(BF16)
-    for a in (2, 1, 0):
-        ready = patches.get(FR + 1 - a)
-        for b in range(3):
-            right = both_frames(ready, lambda t: (t + 2 - a, 2 - b))
-            total = jnp.dot(turned, right, preferred_element_type=F32)
-            total = total * SCALE
-            for c in range(3):
-                tap = (9 * a + 3 * b + c) * C
-                whole[tap : tap + C, :] = total[:, c * C : (c + 1) * C]
-    cut_pieces(whole, core[0], kept, given)
+    patches = patches.get()
+
+    def product(a, b, rows):
+        right = both_frames(patches, lambda t: (t + 2 - a, 2 - b))
+        total = jnp.dot(turned, right, preferred_element_type=F32) * SCALE
+        for c in range(3):
+            rows[c * C : (c + 1) * C, :] = total[:, c * C : (c + 1) * C]
+
+    wgrad(product, whole, core[0], kept, given)
 
 
 def grad_one_kernel(core, slope, middle, patches, table, sums, mid_grad, *refs):
@@ -308,8 +302,14 @@
 
     lax.fori_loop(0, FR * ROWS, step, 0, unroll=2)
     mid_grad.send()
-    wgrad(patches, mid_grad.ref, whole)
-    cut_pieces(whole, core[0], kept, given)
+
+    def product(a, b, rows):
+        left = both_frames(patches.get(a + FR - 1), lambda t: (t + a, b))
+        grad = mid_grad.ref[...]
+        total = lax.dot_general(left, grad, (((0,), (0,)), ((), ())), preferred_element_type=F32)
+        rows[...] = total * SCALE
+
+    wgrad(product, whole, core[0], kept, given)
 
 
 def back_one_kernel(
@@ -608,7 +608,7 @@
 def pair_sum(kept, given):
     taken = [lax.ppermute(part, BOTH, CORE_PAIRS) for part in given]
     whole = jax.ShapeDtypeStruct((64, PIECE, 128), BF16)
-    (total,) = run(pair_kernel, (), (*kept, *taken), (whole,), parts={8: 4})
+    (total,) = run(pair_kernel, (), (*kept, *taken), (whole,), parts={8: 4}, mib=63)
     return total
 
 

time: 246 us -> 243 us (0.988)
  local copies, waits for them, and re-layouts: 17.4 us -> 13.6 us
    unnamed x50 -> x38, local copies, waits for them, and re-layouts: 8.74 us -> 4.93 us
  transfers between devices with their start and end apart: 34 -> 34, of which waited for: 12 -> 13; matrix products, arithmetic and copies ran while one was open for 2% -> 2% of each run, Pallas kernels for 23% -> 23%
where the time goes in v6:
time: 243 us; the launch traced here: 242 us
  starting transfers between devices  88 us (36%)
  Pallas kernels  76.5 us (31%)
  waiting for transfers between devices  48.6 us (20%)
  local copies, waits for them, and re-layouts  13.6 us (6%)
  blocking collectives  12.3 us (5%)
    pallas_call x12, Pallas kernels, run(): pl.pallas_call(body, out_shape=tuple((jax.ShapeDtypeStruct(x.shape, x.dty...  76.5 us
    all_to_all x3, starting transfers between devices, everyone(): return lax.all_to_all(row, BOTH, 0, 0, tiled=True)  23.6 us
    ppermute x6, waiting for transfers between devices, over_line(): lax.ppermute(piece, 'rows', [(i, (i + k) % bands) for i in range(bands)])  21.6 us
    all_to_all x2, starting transfers between devices, over_chips(): lax.all_to_all(pieces, BOTH, 0, 0, axis_index_groups=CHIP_GROUPS, tiled=T...  19.3 us
    all_to_all x3, waiting for transfers between devices, everyone(): return lax.all_to_all(row, BOTH, 0, 0, tiled=True)  14.7 us
    all_to_all x1, blocking collectives, over_plane(): lax.all_to_all(pieces, BOTH, 0, 0, axis_index_groups=PLANE_GROUPS, tiled=...  12.3 us
    ppermute x6, starting transfers between devices, over_line(): lax.ppermute(piece, 'rows', [(i, (i + k) % bands) for i in range(bands)])  8.43 us
    ppermute x2, starting transfers between devices, edge_rows(): lax.ppermute(last, 'rows', down)  7.4 us
  transfers between devices with their start and end apart: 34, of which 13 were waited for; matrix products, arithmetic and copies ran while one was open for 2% of the time, Pallas kernels for 23%

profile of v6, /device:TPU:1, one launch (start us, length us, event | category | flops | bytes accessed | tf_op | source)
XLA Modules:
  0.0 242.0 jit_solution(6231448295738122763)
XLA Ops:
  0.6 1.0 slice_bitcast_fusion.3
  1.7 0.9 slice_bitcast_fusion.2
  2.6 4.0 %collective-permute-start = (bf16[4,80,256]{2,1,0:T(8,128)(2,1)S(1)}, bf16[4,80,256]{2,1,0:T(8,128)(2,1)S(1)}, u32[]{:S(2)}, u32[]{:S(2)}) collective-permute-start(bf16[4,80,256]{2,1,0:T(8,128)(2,1)S(1)} %pad_maximum_fusion.2), channel_id=1, source_target_pairs={{0,1},{1,2},{2,3},{4,5},{5,6},{6,7},{8,9},{9,10},{10,11},{12,13},{... | collective-permute-start | bytes 491528 | tf_op jit(solution)/shard_map/ppermute | solution.py:544
  6.6 1.4 collective-permute-start.1
  8.1 2.4 shard_map.153
  10.5 0.7 slice_bitcast_fusion.7
  11.2 2.2 collective-permute-done.1
  13.4 0.7 slice_bitcast_fusion.6
  14.2 5.0 %collective-permute-start.2 = (bf16[2,10,80,256]{3,2,1,0:T(8,128)(2,1)S(1)}, bf16[2,10,80,256]{3,2,1,0:T(8,128)(2,1)}, u32[]{:S(2)}, u32[]{:S(2)}) collective-permute-start(bf16[2,10,80,256]{3,2,1,0:T(8,128)(2,1)S(1)} %pad_maximum_fusion), channel_id=1, source_target_pairs={{0,4},{4,8},{8,12},{12,16},{16,20},{20,24},{24,28},{28,32},{32,36}... | collective-permute-start | bytes 2457608 | tf_op jit(solution)/shard_map/ppermute | solution.py:565
  19.3 1.9 collective-permute-start.3
  21.2 10.3 %all-to-all-start = ((f32[128,1,128]{2,1,0:T(1,128)}), f32[128,1,128]{2,1,0:T(1,128)S(1)}, u32[]{:S(2)}, u32[]{:S(2)}) async-start(f32[128,1,128]{2,1,0:T(1,128)} %bitcast.18), calls=%async_computation | async-start | bytes 131072 | tf_op jit(solution)/shard_map/all_to_all | solution.py:530
  31.5 0.6 maximum_maximum_fusion.refs_0_
  32.1 9.0 %all-to-all-done = f32[128,1,128]{2,1,0:T(1,128)S(1)} async-done(((f32[128,1,128]{2,1,0:T(1,128)}), f32[128,1,128]{2,1,0:T(1,128)S(1)}, u32[]{:S(2)}, u32[]{:S(2)}) %all-to-all-start) | async-done | bytes 65568 | tf_op jit(solution)/shard_map/all_to_all | solution.py:530
  41.1 0.6 copy-done.5
  41.7 10.0 %shard_map.154 = (bf16[3200,768]{1,0:T(8,128)(2,1)}, bf16[1280,256]{1,0:T(8,128)(2,1)}, f32[128,128]{1,0:T(8,128)}) custom-call(f32[3]{0:T(128)} %maximum_maximum_fusion.refs_0_, bf16[1280,256]{1,0:T(8,128)(2,1)} %bitcast.83, bf16[160,256]{1,0:T(8,128)(2,1)} %bitcast.102, bf16[160,256]{1,0:T(8,128)(2,1)} %bitcast.103, bf16[1600,256]{1,0:T(8,128)(2,1)} %bitcast.16.refs_4_, ...), custom_call_target="tpu_custom_call" | custom-call | flops 1024 | bytes 1024 | tf_op jit(solution)/shard_map/pallas_call | solution.py:517
  51.7 4.4 %all-to-all-start.1 = ((f32[128,1,128]{2,1,0:T(1,128)}), f32[128,1,128]{2,1,0:T(1,128)S(1)}, u32[]{:S(2)}, u32[]{:S(2)}) async-start(f32[128,1,128]{2,1,0:T(1,128)} %bitcast.110), calls=%async_computation.1 | async-start | bytes 131072 | tf_op jit(solution)/shard_map/all_to_all | solution.py:530
  56.2 0.6 maximum_maximum_fusion.1.refs_0_
  56.8 0.9 copy-done.8
  57.6 9.0 %shard_map.155 = (f32[1280,256]{1,0:T(8,128)}, bf16[3200,768]{1,0:T(8,128)(2,1)}) custom-call(f32[3]{0:T(128)} %maximum_maximum_fusion.1.refs_0_, bf16[1280,256]{1,0:T(8,128)(2,1)} %bitcast.87, bf16[160,256]{1,0:T(8,128)(2,1)} %bitcast.100, bf16[160,256]{1,0:T(8,128)(2,1)} %bitcast.101, bf16[1600,256]{1,0:T(8,128)(2,1)} %bitcast.95, bf16[6912,256]{1,0:T(8,128)(2,1)} %refs_5_.1), custom_call_target="tpu_custom_call" | custom-call | flops 1024 | bytes 1024 | tf_op jit(solution)/shard_map/pallas_call | solution.py:517
  66.7 0.6 copy-done.10
  67.3 11.3 %shard_map.156 = (f32[1280,256]{1,0:T(8,128)}, f32[128,128]{1,0:T(8,128)}, bf16[16,112,128]{2,1,0:T(8,128)(2,1)}, bf16[16,112,128]{2,1,0:T(8,128)(2,1)}, bf16[16...) custom-call(s32[1]{0:T(128)} %bitcast.refs_0_, ...), custom_call_target="tpu_custom_call" | custom-call | flops 1024 | bytes 1024 | tf_op jit(solution)/shard_map/pallas_call | solution.py:517
  78.6 1.4 collective-permute-start.4
  80.6 8.9 %all-to-all-start.2 = ((f32[128,1,128]{2,1,0:T(1,128)}), f32[128,1,128]{2,1,0:T(1,128)S(1)}, u32[]{:S(2)}, u32[]{:S(2)}) async-start(f32[128,1,128]{2,1,0:T(1,128)} %bitcast.109), calls=%async_computation.2 | async-start | bytes 131072 | tf_op jit(solution)/shard_map/all_to_all | solution.py:530
  89.6 0.7 copy-done.11
  90.5 3.0 %shard_map.157 = bf16[64,112,128]{2,1,0:T(8,128)(2,1)} custom-call(bf16[16,112,128]{2,1,0:T(8,128)(2,1)} %get-tuple-element.60.refs_0_, bf16[16,112,128]{2,1,0:T(8,128)(2,1)} %get-tuple-element.61.refs_1_, bf16[16,112,128]{2,1,0:T(8,128)(2,1)} %get-tuple-element.62.refs_2_, bf16[16,112,128]{2,1,0:T(8,128)(2,1)} %get-tuple-element.63.refs_3_, ...), custom_call_target="tpu_custom_call" | custom-call | flops 1024 | bytes 1024 | tf_op jit(solution)/shard_map/pallas_call | solution.py:517
  93.5 5.7 %all-to-all-done.2 = f32[128,1,128]{2,1,0:T(1,128)S(1)} async-done(((f32[128,1,128]{2,1,0:T(1,128)}), f32[128,1,128]{2,1,0:T(1,128)S(1)}, u32[]{:S(2)}, u32[]{:S(2)}) %all-to-all-start.2) | async-done | bytes 65568 | tf_op jit(solution)/shard_map/all_to_all | solution.py:530
  99.2 0.6 copy-done.13
  99.8 5.7 %all-to-all-start.4 = ((bf16[64,112,128]{2,1,0:T(8,128)(2,1)}), bf16[64,112,128]{2,1,0:T(8,128)(2,1)}, u32[]{:S(2)}, u32[]{:S(2)}) async-start(bf16[64,112,128]{2,1,0:T(8,128)(2,1)} %shard_map.157), calls=%async_computation.4 | async-start | bytes 3670016 | tf_op jit(solution)/shard_map/all_to_all | solution.py:616
  105.6 10.6 %shard_map.158 = (bf16[1280,256]{1,0:T(8,128)(2,1)}, bf16[16,112,128]{2,1,0:T(8,128)(2,1)}, bf16[16,112,128]{2,1,0:T(8,128)(2,1)}, bf16[16,112,128]{2,1,0:T(8,12...) custom-call(s32[1]{0:T(128)} %bitcast.refs_0_, ...), custom_call_target="tpu_custom_call" | custom-call | flops 1024 | bytes 1024 | tf_op jit(solution)/shard_map/pallas_call | solution.py:517
  116.2 2.6 %collective-permute-start.8 = (bf16[2,8,80,256]{3,2,1,0:T(8,128)(2,1)}, bf16[2,8,80,256]{3,2,1,0:T(8,128)(2,1)S(1)}, u32[]{:S(2)}, u32[]{:S(2)}) collective-permute-start(bf16[2,8,80,256]{3,2,1,0:T(8,128)(2,1)} %bitcast.93), channel_id=1, source_target_pairs={{4,0},{8,4},{12,8},{16,12},{20,16},{24,20},{28,24},{32,28},{36,32}... | collective-permute-start | bytes 1966088 | tf_op jit(solution)/shard_map/ppermute | solution.py:552
  118.8 0.9 slice_bitcast_fusion
  119.7 1.3 collective-permute-start.10
  121.0 3.4 %collective-permute-start.11 = (bf16[2,80,256]{2,1,0:T(8,128)(2,1)S(1)}, bf16[2,80,256]{2,1,0:T(8,128)(2,1)S(1)}, u32[]{:S(2)}, u32[]{:S(2)}) collective-permute-start(bf16[2,80,256]{2,1,0:T(8,128)(2,1)S(1)} %get-tuple-element.98), channel_id=1, source_target_pairs={{0,1},{1,2},{2,3},{4,5},{5,6},{6,7},{8,9},{9,10},{10,11},{12,13},{... | collective-permute-start | bytes 245768 | tf_op jit(solution)/shard_map/ppermute | solution.py:544
  124.5 1.3 collective-permute-start.12
  125.8 3.2 %collective-permute-start.9 = (bf16[2,80,256]{2,1,0:T(8,128)(2,1)S(1)}, bf16[2,80,256]{2,1,0:T(8,128)(2,1)S(1)}, u32[]{:S(2)}, u32[]{:S(2)}) collective-permute-start(bf16[2,80,256]{2,1,0:T(8,128)(2,1)S(1)} %get-tuple-element.98), channel_id=1, source_target_pairs={{4,1},{5,2},{6,3},{8,5},{9,6},{10,7},{12,9},{13,10},{14,11},{16,13... | collective-permute-start | bytes 245768 | tf_op jit(solution)/shard_map/ppermute | solution.py:556
  131.0 3.4 %collective-permute-done.8 = bf16[2,8,80,256]{3,2,1,0:T(8,128)(2,1)S(1)} collective-permute-done((bf16[2,8,80,256]{3,2,1,0:T(8,128)(2,1)}, bf16[2,8,80,256]{3,2,1,0:T(8,128)(2,1)S(1)}, u32[]{:S(2)}, u32[]{:S(2)}) %collective-permute-start.8) | collective-permute-done | bytes 655392 | tf_op jit(solution)/shard_map/ppermute | solution.py:552
  134.4 3.2 %shard_map.159 = bf16[64,112,128]{2,1,0:T(8,128)(2,1)} custom-call(bf16[16,112,128]{2,1,0:T(8,128)(2,1)} %get-tuple-element.73.refs_0_, bf16[16,112,128]{2,1,0:T(8,128)(2,1)} %get-tuple-element.74.refs_1_, bf16[16,112,128]{2,1,0:T(8,128)(2,1)} %get-tuple-element.75.refs_2_, bf16[16,112,128]{2,1,0:T(8,128)(2,1)} %get-tuple-element.76.refs_3_, ...), custom_call_target="tpu_custom_call" | custom-call | flops 1024 | bytes 1024 | tf_op jit(solution)/shard_map/pallas_call | solution.py:517
  137.7 13.5 %all-to-all-start.3 = ((bf16[64,112,128]{2,1,0:T(8,128)(2,1)}), bf16[64,112,128]{2,1,0:T(8,128)(2,1)S(1)}, u32[]{:S(2)}, u32[]{:S(2)}) async-start(bf16[64,112,128]{2,1,0:T(8,128)(2,1)} %shard_map.159), calls=%async_computation.3 | async-start | bytes 3670016 | tf_op jit(solution)/shard_map/all_to_all | solution.py:616
  151.3 0.8 constant_dynamic-slice_fusion.1
  152.1 0.6 reshape.128.refs_1_
  152.7 2.3 shard_map.160
  155.0 2.3 collective-permute-start.17
  157.9 0.6 collective-permute-start.19
  158.5 0.8 constant_dynamic-slice_fusion
  159.3 0.6 reshape.131.refs_1_
  160.0 10.8 %shard_map.161 = (f32[1280,256]{1,0:T(8,128)}, f32[8,128]{1,0:T(8,128)}) custom-call(f32[3]{0:T(128)} %maximum_maximum_fusion.1.refs_0_, bf16[1280,256]{1,0:T(8,128)(2,1)} %get-tuple-element.84.refs_1_, bf16[160,256]{1,0:T(8,128)(2,1)} %bitcast.106, bf16[160,256]{1,0:T(8,128)(2,1)} %bitcast.107, bf16[1280,256]{1,0:T(8,128)(2,1)} %bitcast.96, ...), custom_call_target="tpu_custom_call" | custom-call | flops 1024 | bytes 1024 | tf_op jit(solution)/shard_map/pallas_call | solution.py:517
  170.8 2.0 collective-permute-done.17
  172.8 1.5 collective-permute-done.18
  174.3 3.2 %all-to-all-done.3.refs_0_ = bf16[64,112,128]{2,1,0:T(8,128)(2,1)S(1)} async-done(((bf16[64,112,128]{2,1,0:T(8,128)(2,1)}), bf16[64,112,128]{2,1,0:T(8,128)(2,1)S(1)}, u32[]{:S(2)}, u32[]{:S(2)}) %all-to-all-start.3) | async-done | bytes 1835040 | tf_op jit(solution)/shard_map/all_to_all | solution.py:616
  177.5 1.2 copy-done.7
  178.8 3.9 %shard_map.162 = (f32[108,128]{1,0:T(8,128)}, f32[108,128]{1,0:T(8,128)}, bf16[16,112,128]{2,1,0:T(8,128)(2,1)}) custom-call(bf16[64,112,128]{2,1,0:T(8,128)(2,1)} %copy-done.7, bf16[108,128]{1,0:T(8,128)(2,1)} %reshape.131.refs_1_, f32[108,128]{1,0:T(8,128)} %bitcast.113, f32[108,128]{1,0:T(8,128)} %bitcast.114, f32[8,128]{1,0:T(8,128)} %get-tuple-element.85.refs_4_), custom_call_target="tpu_custom_call" | custom-call | flops 1024 | bytes 1024 | tf_op jit(solution)/shard_map/pallas_call | solution.py:517
  182.7 12.3 %all_to_all.53.refs_2_ = bf16[16,112,128]{2,1,0:T(8,128)(2,1)S(1)} all-to-all(bf16[16,112,128]{2,1,0:T(8,128)(2,1)} %get-tuple-element.86), channel_id=1, replica_groups={{0,8,16,24,32,40,48,56,64,72,80,88,96,104,112,120},{1,9,17,25,33,41,49,..., dimensions={0} | all-to-all | bytes 917504 | tf_op jit(solution)/shard_map/all_to_all | solution.py:573
  195.0 1.6 broadcast_in_dim.24
  196.5 3.7 %all-to-all-start.6 = ((bf16[16,448,128]{2,1,0:T(8,128)(2,1)}), bf16[16,448,128]{2,1,0:T(8,128)(2,1)S(1)}, u32[]{:S(2)}, u32[]{:S(2)}) async-start(bf16[16,448,128]{2,1,0:T(8,128)(2,1)} %broadcast_in_dim.24), calls=%async_computation.6 | async-start | bytes 3670016 | tf_op jit(solution)/shard_map/all_to_all | solution.py:573
  200.3 0.7 collective-permute-start.20
  201.0 2.4 collective-permute-start.21
  203.3 1.9 collective-permute-start.22
  205.3 4.9 %collective-permute-done.20.refs_3_ = bf16[16,112,128]{2,1,0:T(8,128)(2,1)S(1)} collective-permute-done((bf16[16,112,128]{2,1,0:T(8,128)(2,1)S(1)}, bf16[16,112,128]{2,1,0:T(8,128)(2,1)S(1)}, u32[]{:S(2)}, u32[]{:S(2)}) %collective-permute-start.20) | collective-permute-done | bytes 458784 | tf_op jit(solution)/shard_map/ppermute | solution.py:579
  210.1 10.9 %collective-permute-done.21.refs_4_ = bf16[16,112,128]{2,1,0:T(8,128)(2,1)S(1)} collective-permute-done((bf16[16,112,128]{2,1,0:T(8,128)(2,1)S(1)}, bf16[16,112,128]{2,1,0:T(8,128)(2,1)S(1)}, u32[]{:S(2)}, u32[]{:S(2)}) %collective-permute-start.21) | collective-permute-done | bytes 458784 | tf_op jit(solution)/shard_map/ppermute | solution.py:579
  221.0 2.3 collective-permute-done.22.refs_5_
  223.4 5.0 %collective-permute-start.27 = (bf16[16,448,128]{2,1,0:T(8,128)(2,1)S(1)}, bf16[16,448,128]{2,1,0:T(8,128)(2,1)S(1)}, u32[]{:S(2)}, u32[]{:S(2)}) collective-permute-start(bf16[16,448,128]{2,1,0:T(8,128)(2,1)S(1)} %all-to-all-done.6), channel_id=1, source_target_pairs={{0,4},{1,5},{2,6},{3,7},{4,0},{5,1},{6,2},{7,3},{8,12},{9,13},{10,... | collective-permute-start | bytes 5505032 | tf_op jit(solution)/shard_map/ppermute | solution.py:749
  229.4 2.4 collective-permute-done.27
  231.8 4.2 %shard_map.163 = bf16[6912,256]{1,0:T(8,128)(2,1)} custom-call(s32[1]{0:T(128)} %bitcast.refs_0_, bf16[64,112,128]{2,1,0:T(8,128)(2,1)S(1)} %bitcast.86, bf16[64,112,128]{2,1,0:T(8,128)(2,1)S(1)} %bitcast.89), custom_call_target="tpu_custom_call" | custom-call | flops 1024 | bytes 1024 | tf_op jit(solution)/shard_map/pallas_call | solution.py:517
  236.1 5.7 %shard_map.164 = (bf16[6912,256]{1,0:T(8,128)(2,1)}, bf16[1280,256]{1,0:T(8,128)(2,1)}) custom-call(s32[1]{0:T(128)} %bitcast.refs_0_, s32[1]{0:T(128)} %bitcast.1.refs_1_, bf16[16,112,128]{2,1,0:T(8,128)(2,1)S(1)} %all_to_all.53.refs_2_, bf16[16,112,128]{2,1,0:T(8,128)(2,1)S(1)} %collective-permute-done.20.refs_3_, ...), custom_call_target="tpu_custom_call" | custom-call | flops 1024 | bytes 1024 | tf_op jit(solution)/shard_map/pallas_call | solution.py:517
  (73 shorter events, 4.7 us)
Async XLA Ops:
  0.6 13.5 %copy-start = (bf16[2,8,80,256]{3,2,1,0:T(8,128)(2,1)S(1)}, bf16[2,8,80,256]{3,2,1,0:T(8,128)(2,1)}, u32[]{:S(2)}) copy-start(bf16[2,8,80,256]{3,2,1,0:T(8,128)(2,1)} %param.10) | copy-start | bytes 1966084
  2.6 7.8 %collective-permute-start = (bf16[4,80,256]{2,1,0:T(8,128)(2,1)S(1)}, bf16[4,80,256]{2,1,0:T(8,128)(2,1)S(1)}, u32[]{:S(2)}, u32[]{:S(2)}) collective-permute-start(bf16[4,80,256]{2,1,0:T(8,128)(2,1)S(1)} %pad_maximum_fusion.2), channel_id=1, source_target_pairs={{0,1},{1,2},{2,3},{4,5},{5,6},{6,7},{8,9},{9,10},{10,11},{12,13},{... | collective-permute-start | bytes 491528 | tf_op jit(solution)/shard_map/ppermute | solution.py:544
  6.6 12.6 %copy-start.2 = (bf16[2,8,80,256]{3,2,1,0:T(8,128)(2,1)S(1)}, bf16[2,8,80,256]{3,2,1,0:T(8,128)(2,1)}, u32[]{:S(2)}) copy-start(bf16[2,8,80,256]{3,2,1,0:T(8,128)(2,1)} %param.11) | copy-start | bytes 1966084
  6.6 6.8 %collective-permute-start.1 = (bf16[4,80,256]{2,1,0:T(8,128)(2,1)S(1)}, bf16[4,80,256]{2,1,0:T(8,128)(2,1)S(1)}, u32[]{:S(2)}, u32[]{:S(2)}) collective-permute-start(bf16[4,80,256]{2,1,0:T(8,128)(2,1)S(1)} %pad_maximum_fusion.3), channel_id=1, source_target_pairs={{1,0},{2,1},{3,2},{5,4},{6,5},{7,6},{9,8},{10,9},{11,10},{13,12},{... | collective-permute-start | bytes 491528 | tf_op jit(solution)/shard_map/ppermute | solution.py:544
  14.2 26.9 %collective-permute-start.2 = (bf16[2,10,80,256]{3,2,1,0:T(8,128)(2,1)S(1)}, bf16[2,10,80,256]{3,2,1,0:T(8,128)(2,1)}, u32[]{:S(2)}, u32[]{:S(2)}) collective-permute-start(bf16[2,10,80,256]{3,2,1,0:T(8,128)(2,1)S(1)} %pad_maximum_fusion), channel_id=1, source_target_pairs={{0,4},{4,8},{8,12},{12,16},{16,20},{20,24},{24,28},{28,32},{32,36}... | collective-permute-start | bytes 2457608 | tf_op jit(solution)/shard_map/ppermute | solution.py:565
  19.3 37.5 %collective-permute-start.3 = (bf16[2,10,80,256]{3,2,1,0:T(8,128)(2,1)S(1)}, bf16[2,10,80,256]{3,2,1,0:T(8,128)(2,1)S(1)}, u32[]{:S(2)}, u32[]{:S(2)}) collective-permute-start(bf16[2,10,80,256]{3,2,1,0:T(8,128)(2,1)S(1)} %pad_maximum_fusion.1), channel_id=1, source_target_pairs={{4,0},{8,4},{12,8},{16,12},{20,16},{24,20},{28,24},{32,28},{36,32}... | collective-permute-start | bytes 2457608 | tf_op jit(solution)/shard_map/ppermute | solution.py:565
  21.2 19.9 %all-to-all-start = ((f32[128,1,128]{2,1,0:T(1,128)}), f32[128,1,128]{2,1,0:T(1,128)S(1)}, u32[]{:S(2)}, u32[]{:S(2)}) async-start(f32[128,1,128]{2,1,0:T(1,128)} %bitcast.18), calls=%async_computation | async-start | bytes 131072 | tf_op jit(solution)/shard_map/all_to_all | solution.py:530
  41.1 0.6 copy-start.5
  51.7 15.0 %all-to-all-start.1 = ((f32[128,1,128]{2,1,0:T(1,128)}), f32[128,1,128]{2,1,0:T(1,128)S(1)}, u32[]{:S(2)}, u32[]{:S(2)}) async-start(f32[128,1,128]{2,1,0:T(1,128)} %bitcast.110), calls=%async_computation.1 | async-start | bytes 131072 | tf_op jit(solution)/shard_map/all_to_all | solution.py:530
  56.8 0.9 copy-start.8
  66.7 0.6 copy-start.10
  78.6 10.9 %collective-permute-start.4 = (bf16[16,112,128]{2,1,0:T(8,128)(2,1)}, bf16[16,112,128]{2,1,0:T(8,128)(2,1)S(1)}, u32[]{:S(2)}, u32[]{:S(2)}) collective-permute-start(bf16[16,112,128]{2,1,0:T(8,128)(2,1)} %get-tuple-element.64), channel_id=1, source_target_pairs={{0,4},{1,5},{2,6},{3,7},{4,0},{5,1},{6,2},{7,3},{8,12},{9,13},{10,... | collective-permute-start | bytes 1376264 | tf_op jit(solution)/shard_map/ppermute | solution.py:609
  80.0 9.6 %collective-permute-start.5 = (bf16[16,112,128]{2,1,0:T(8,128)(2,1)}, bf16[16,112,128]{2,1,0:T(8,128)(2,1)S(1)}, u32[]{:S(2)}, u32[]{:S(2)}) collective-permute-start(bf16[16,112,128]{2,1,0:T(8,128)(2,1)} %get-tuple-element.65), channel_id=1, source_target_pairs={{0,4},{1,5},{2,6},{3,7},{4,0},{5,1},{6,2},{7,3},{8,12},{9,13},{10,... | collective-permute-start | bytes 1376264 | tf_op jit(solution)/shard_map/ppermute | solution.py:609
  80.1 9.5 %collective-permute-start.6 = (bf16[16,112,128]{2,1,0:T(8,128)(2,1)}, bf16[16,112,128]{2,1,0:T(8,128)(2,1)}, u32[]{:S(2)}, u32[]{:S(2)}) collective-permute-start(bf16[16,112,128]{2,1,0:T(8,128)(2,1)} %get-tuple-element.66), channel_id=1, source_target_pairs={{0,4},{1,5},{2,6},{3,7},{4,0},{5,1},{6,2},{7,3},{8,12},{9,13},{10,... | collective-permute-start | bytes 1376264 | tf_op jit(solution)/shard_map/ppermute | solution.py:609
  80.5 9.1 %collective-permute-start.7 = (bf16[16,112,128]{2,1,0:T(8,128)(2,1)}, bf16[16,112,128]{2,1,0:T(8,128)(2,1)}, u32[]{:S(2)}, u32[]{:S(2)}) collective-permute-start(bf16[16,112,128]{2,1,0:T(8,128)(2,1)} %get-tuple-element.67), channel_id=1, source_target_pairs={{0,4},{1,5},{2,6},{3,7},{4,0},{5,1},{6,2},{7,3},{8,12},{9,13},{10,... | collective-permute-start | bytes 1376264 | tf_op jit(solution)/shard_map/ppermute | solution.py:609
  80.6 18.6 %all-to-all-start.2 = ((f32[128,1,128]{2,1,0:T(1,128)}), f32[128,1,128]{2,1,0:T(1,128)S(1)}, u32[]{:S(2)}, u32[]{:S(2)}) async-start(f32[128,1,128]{2,1,0:T(1,128)} %bitcast.109), calls=%async_computation.2 | async-start | bytes 131072 | tf_op jit(solution)/shard_map/all_to_all | solution.py:530
  89.5 0.8 copy-start.11
  89.6 0.9 copy-start.12
  99.2 0.6 copy-start.13
  99.8 37.9 %all-to-all-start.4 = ((bf16[64,112,128]{2,1,0:T(8,128)(2,1)}), bf16[64,112,128]{2,1,0:T(8,128)(2,1)}, u32[]{:S(2)}, u32[]{:S(2)}) async-start(bf16[64,112,128]{2,1,0:T(8,128)(2,1)} %shard_map.157), calls=%async_computation.4 | async-start | bytes 3670016 | tf_op jit(solution)/shard_map/all_to_all | solution.py:616
  116.2 18.2 %collective-permute-start.8 = (bf16[2,8,80,256]{3,2,1,0:T(8,128)(2,1)}, bf16[2,8,80,256]{3,2,1,0:T(8,128)(2,1)S(1)}, u32[]{:S(2)}, u32[]{:S(2)}) collective-permute-start(bf16[2,8,80,256]{3,2,1,0:T(8,128)(2,1)} %bitcast.93), channel_id=1, source_target_pairs={{4,0},{8,4},{12,8},{16,12},{20,16},{24,20},{28,24},{32,28},{36,32}... | collective-permute-start | bytes 1966088 | tf_op jit(solution)/shard_map/ppermute | solution.py:552
  119.7 9.8 %collective-permute-start.10 = (bf16[2,80,256]{2,1,0:T(8,128)(2,1)S(1)}, bf16[2,80,256]{2,1,0:T(8,128)(2,1)S(1)}, u32[]{:S(2)}, u32[]{:S(2)}) collective-permute-start(bf16[2,80,256]{2,1,0:T(8,128)(2,1)S(1)} %get-tuple-element.97), channel_id=1, source_target_pairs={{5,0},{6,1},{7,2},{9,4},{10,5},{11,6},{13,8},{14,9},{15,10},{17,12... | collective-permute-start | bytes 245768 | tf_op jit(solution)/shard_map/ppermute | solution.py:556
  121.0 8.5 %collective-permute-start.11 = (bf16[2,80,256]{2,1,0:T(8,128)(2,1)S(1)}, bf16[2,80,256]{2,1,0:T(8,128)(2,1)S(1)}, u32[]{:S(2)}, u32[]{:S(2)}) collective-permute-start(bf16[2,80,256]{2,1,0:T(8,128)(2,1)S(1)} %get-tuple-element.98), channel_id=1, source_target_pairs={{0,1},{1,2},{2,3},{4,5},{5,6},{6,7},{8,9},{9,10},{10,11},{12,13},{... | collective-permute-start | bytes 245768 | tf_op jit(solution)/shard_map/ppermute | solution.py:544
  124.5 6.0 %collective-permute-start.12 = (bf16[2,80,256]{2,1,0:T(8,128)(2,1)S(1)}, bf16[2,80,256]{2,1,0:T(8,128)(2,1)S(1)}, u32[]{:S(2)}, u32[]{:S(2)}) collective-permute-start(bf16[2,80,256]{2,1,0:T(8,128)(2,1)S(1)} %get-tuple-element.97), channel_id=1, source_target_pairs={{1,0},{2,1},{3,2},{5,4},{6,5},{7,6},{9,8},{10,9},{11,10},{13,12},{... | collective-permute-start | bytes 245768 | tf_op jit(solution)/shard_map/ppermute | solution.py:544
  125.8 4.7 %collective-permute-start.9 = (bf16[2,80,256]{2,1,0:T(8,128)(2,1)S(1)}, bf16[2,80,256]{2,1,0:T(8,128)(2,1)S(1)}, u32[]{:S(2)}, u32[]{:S(2)}) collective-permute-start(bf16[2,80,256]{2,1,0:T(8,128)(2,1)S(1)} %get-tuple-element.98), channel_id=1, source_target_pairs={{4,1},{5,2},{6,3},{8,5},{9,6},{10,7},{12,9},{13,10},{14,11},{16,13... | collective-permute-start | bytes 245768 | tf_op jit(solution)/shard_map/ppermute | solution.py:556
  129.6 8.1 %copy-start.14 = (bf16[2,80,256]{2,1,0:T(8,128)(2,1)}, bf16[2,80,256]{2,1,0:T(8,128)(2,1)S(1)}, u32[]{:S(2)}) copy-start(bf16[2,80,256]{2,1,0:T(8,128)(2,1)S(1)} %collective-permute-done.10) | copy-start | bytes 245764
  129.6 4.8 %collective-permute-start.13 = (bf16[16,112,128]{2,1,0:T(8,128)(2,1)}, bf16[16,112,128]{2,1,0:T(8,128)(2,1)}, u32[]{:S(2)}, u32[]{:S(2)}) collective-permute-start(bf16[16,112,128]{2,1,0:T(8,128)(2,1)} %get-tuple-element.77), channel_id=1, source_target_pairs={{0,4},{1,5},{2,6},{3,7},{4,0},{5,1},{6,2},{7,3},{8,12},{9,13},{10,... | collective-permute-start | bytes 1376264 | tf_op jit(solution)/shard_map/ppermute | solution.py:609
  129.6 8.1 %copy-start.15 = (bf16[2,80,256]{2,1,0:T(8,128)(2,1)}, bf16[2,80,256]{2,1,0:T(8,128)(2,1)S(1)}, u32[]{:S(2)}) copy-start(bf16[2,80,256]{2,1,0:T(8,128)(2,1)S(1)} %collective-permute-done.11) | copy-start | bytes 245764
  129.6 4.8 %collective-permute-start.14 = (bf16[16,112,128]{2,1,0:T(8,128)(2,1)}, bf16[16,112,128]{2,1,0:T(8,128)(2,1)}, u32[]{:S(2)}, u32[]{:S(2)}) collective-permute-start(bf16[16,112,128]{2,1,0:T(8,128)(2,1)} %get-tuple-element.78), channel_id=1, source_target_pairs={{0,4},{1,5},{2,6},{3,7},{4,0},{5,1},{6,2},{7,3},{8,12},{9,13},{10,... | collective-permute-start | bytes 1376264 | tf_op jit(solution)/shard_map/ppermute | solution.py:609
  130.4 7.2 %copy-start.16 = (bf16[2,80,256]{2,1,0:T(8,128)(2,1)}, bf16[2,80,256]{2,1,0:T(8,128)(2,1)S(1)}, u32[]{:S(2)}) copy-start(bf16[2,80,256]{2,1,0:T(8,128)(2,1)S(1)} %collective-permute-done.12) | copy-start | bytes 245764
  130.4 4.0 %collective-permute-start.15 = (bf16[16,112,128]{2,1,0:T(8,128)(2,1)}, bf16[16,112,128]{2,1,0:T(8,128)(2,1)}, u32[]{:S(2)}, u32[]{:S(2)}) collective-permute-start(bf16[16,112,128]{2,1,0:T(8,128)(2,1)} %get-tuple-element.79), channel_id=1, source_target_pairs={{0,4},{1,5},{2,6},{3,7},{4,0},{5,1},{6,2},{7,3},{8,12},{9,13},{10,... | collective-permute-start | bytes 1376264 | tf_op jit(solution)/shard_map/ppermute | solution.py:609
  130.5 7.2 %copy-start.17 = (bf16[2,80,256]{2,1,0:T(8,128)(2,1)}, bf16[2,80,256]{2,1,0:T(8,128)(2,1)S(1)}, u32[]{:S(2)}) copy-start(bf16[2,80,256]{2,1,0:T(8,128)(2,1)S(1)} %collective-permute-done.9) | copy-start | bytes 245764
  130.5 4.0 %collective-permute-start.16 = (bf16[16,112,128]{2,1,0:T(8,128)(2,1)}, bf16[16,112,128]{2,1,0:T(8,128)(2,1)}, u32[]{:S(2)}, u32[]{:S(2)}) collective-permute-start(bf16[16,112,128]{2,1,0:T(8,128)(2,1)} %get-tuple-element.80), channel_id=1, source_target_pairs={{0,4},{1,5},{2,6},{3,7},{4,0},{5,1},{6,2},{7,3},{8,12},{9,13},{10,... | collective-permute-start | bytes 1376264 | tf_op jit(solution)/shard_map/ppermute | solution.py:609
  134.4 3.3 %copy-start.9 = (bf16[2,8,80,256]{3,2,1,0:T(8,128)(2,1)}, bf16[2,8,80,256]{3,2,1,0:T(8,128)(2,1)S(1)}, u32[]{:S(2)}) copy-start(bf16[2,8,80,256]{3,2,1,0:T(8,128)(2,1)S(1)} %collective-permute-done.8) | copy-start | bytes 1966084
  137.7 39.8 %all-to-all-start.3 = ((bf16[64,112,128]{2,1,0:T(8,128)(2,1)}), bf16[64,112,128]{2,1,0:T(8,128)(2,1)S(1)}, u32[]{:S(2)}, u32[]{:S(2)}) async-start(bf16[64,112,128]{2,1,0:T(8,128)(2,1)} %shard_map.159), calls=%async_computation.3 | async-start | bytes 3670016 | tf_op jit(solution)/shard_map/all_to_all | solution.py:616
  155.0 17.7 %collective-permute-start.17 = (bf16[1,112,128]{2,1,0:T(8,128)(2,1)}, bf16[1,112,128]{2,1,0:T(8,128)(2,1)S(1)}, u32[]{:S(2)}, u32[]{:S(2)}) collective-permute-start(bf16[1,112,128]{2,1,0:T(8,128)(2,1)} %get-tuple-element.82), channel_id=1, source_target_pairs={{0,3},{1,0},{2,1},{3,2},{4,7},{5,4},{6,5},{7,6},{8,11},{9,8},{10,9... | collective-permute-start | bytes 86024 | tf_op jit(solution)/shard_map/ppermute | solution.py:579
  157.3 16.9 %collective-permute-start.18 = (bf16[1,112,128]{2,1,0:T(8,128)(2,1)}, bf16[1,112,128]{2,1,0:T(8,128)(2,1)S(1)}, u32[]{:S(2)}, u32[]{:S(2)}) collective-permute-start(bf16[1,112,128]{2,1,0:T(8,128)(2,1)} %get-tuple-element.82), channel_id=1, source_target_pairs={{0,2},{1,3},{2,0},{3,1},{4,6},{5,7},{6,4},{7,5},{8,10},{9,11},{10,... | collective-permute-start | bytes 86024 | tf_op jit(solution)/shard_map/ppermute | solution.py:579
  157.9 16.4 %collective-permute-start.19 = (bf16[1,112,128]{2,1,0:T(8,128)(2,1)}, bf16[1,112,128]{2,1,0:T(8,128)(2,1)S(1)}, u32[]{:S(2)}, u32[]{:S(2)}) collective-permute-start(bf16[1,112,128]{2,1,0:T(8,128)(2,1)} %get-tuple-element.82), channel_id=1, source_target_pairs={{0,1},{1,2},{2,3},{3,0},{4,5},{5,6},{6,7},{7,4},{8,9},{9,10},{10,1... | collective-permute-start | bytes 86024 | tf_op jit(solution)/shard_map/ppermute | solution.py:579
  160.0 14.3 %copy-start.18 = (bf16[1,112,128]{2,1,0:T(8,128)(2,1)S(1)}, bf16[1,112,128]{2,1,0:T(8,128)(2,1)}, u32[]{:S(2)}) copy-start(bf16[1,112,128]{2,1,0:T(8,128)(2,1)} %get-tuple-element.82) | copy-start | bytes 86020
  177.5 1.2 copy-start.7
  196.5 26.8 %all-to-all-start.6 = ((bf16[16,448,128]{2,1,0:T(8,128)(2,1)}), bf16[16,448,128]{2,1,0:T(8,128)(2,1)S(1)}, u32[]{:S(2)}, u32[]{:S(2)}) async-start(bf16[16,448,128]{2,1,0:T(8,128)(2,1)} %broadcast_in_dim.24), calls=%async_computation.6 | async-start | bytes 3670016 | tf_op jit(solution)/shard_map/all_to_all | solution.py:573
  200.3 9.8 %collective-permute-start.20 = (bf16[16,112,128]{2,1,0:T(8,128)(2,1)S(1)}, bf16[16,112,128]{2,1,0:T(8,128)(2,1)S(1)}, u32[]{:S(2)}, u32[]{:S(2)}) collective-permute-start(bf16[16,112,128]{2,1,0:T(8,128)(2,1)S(1)} %all_to_all.53.refs_2_), channel_id=1, source_target_pairs={{0,1},{1,2},{2,3},{3,0},{4,5},{5,6},{6,7},{7,4},{8,9},{9,10},{10,1... | collective-permute-start | bytes 1376264 | tf_op jit(solution)/shard_map/ppermute | solution.py:579
  201.0 20.1 %collective-permute-start.21 = (bf16[16,112,128]{2,1,0:T(8,128)(2,1)S(1)}, bf16[16,112,128]{2,1,0:T(8,128)(2,1)S(1)}, u32[]{:S(2)}, u32[]{:S(2)}) collective-permute-start(bf16[16,112,128]{2,1,0:T(8,128)(2,1)S(1)} %all_to_all.53.refs_2_), channel_id=1, source_target_pairs={{0,2},{1,3},{2,0},{3,1},{4,6},{5,7},{6,4},{7,5},{8,10},{9,11},{10,... | collective-permute-start | bytes 1376264 | tf_op jit(solution)/shard_map/ppermute | solution.py:579
  203.3 20.1 %collective-permute-start.22 = (bf16[16,112,128]{2,1,0:T(8,128)(2,1)S(1)}, bf16[16,112,128]{2,1,0:T(8,128)(2,1)}, u32[]{:S(2)}, u32[]{:S(2)}) collective-permute-start(bf16[16,112,128]{2,1,0:T(8,128)(2,1)S(1)} %all_to_all.53.refs_2_), channel_id=1, source_target_pairs={{0,3},{1,0},{2,1},{3,2},{4,7},{5,4},{6,5},{7,6},{8,11},{9,8},{10,9... | collective-permute-start | bytes 1376264 | tf_op jit(solution)/shard_map/ppermute | solution.py:579
  223.4 8.4 %collective-permute-start.27 = (bf16[16,448,128]{2,1,0:T(8,128)(2,1)S(1)}, bf16[16,448,128]{2,1,0:T(8,128)(2,1)S(1)}, u32[]{:S(2)}, u32[]{:S(2)}) collective-permute-start(bf16[16,448,128]{2,1,0:T(8,128)(2,1)S(1)} %all-to-all-done.6), channel_id=1, source_target_pairs={{0,4},{1,5},{2,6},{3,7},{4,0},{5,1},{6,2},{7,3},{8,12},{9,13},{10,... | collective-permute-start | bytes 5505032 | tf_op jit(solution)/shard_map/ppermute | solution.py:749
  228.3 7.7 %collective-permute-start.23 = (bf16[16,112,128]{2,1,0:T(8,128)(2,1)S(1)}, bf16[16,112,128]{2,1,0:T(8,128)(2,1)S(1)}, u32[]{:S(2)}, u32[]{:S(2)}) collective-permute-start(bf16[16,112,128]{2,1,0:T(8,128)(2,1)S(1)} %all_to_all.53.refs_2_), channel_id=1, source_target_pairs={{0,4},{1,5},{2,6},{3,7},{4,0},{5,1},{6,2},{7,3},{8,12},{9,13},{10,... | collective-permute-start | bytes 1376264 | tf_op jit(solution)/shard_map/ppermute | solution.py:750
  228.3 7.7 %collective-permute-start.24 = (bf16[16,112,128]{2,1,0:T(8,128)(2,1)S(1)}, bf16[16,112,128]{2,1,0:T(8,128)(2,1)S(1)}, u32[]{:S(2)}, u32[]{:S(2)}) collective-permute-start(bf16[16,112,128]{2,1,0:T(8,128)(2,1)S(1)} %collective-permute-done.20.refs_3_), channel_id=1, source_target_pairs={{0,4},{1,5},{2,6},{3,7},{4,0},{5,1},{6,2},{7,3},{8,12},{9,13},{10,... | collective-permute-start | bytes 1376264 | tf_op jit(solution)/shard_map/ppermute | solution.py:750
  228.8 7.2 %collective-permute-start.25 = (bf16[16,112,128]{2,1,0:T(8,128)(2,1)S(1)}, bf16[16,112,128]{2,1,0:T(8,128)(2,1)S(1)}, u32[]{:S(2)}, u32[]{:S(2)}) collective-permute-start(bf16[16,112,128]{2,1,0:T(8,128)(2,1)S(1)} %collective-permute-done.21.refs_4_), channel_id=1, source_target_pairs={{0,4},{1,5},{2,6},{3,7},{4,0},{5,1},{6,2},{7,3},{8,12},{9,13},{10,... | collective-permute-start | bytes 1376264 | tf_op jit(solution)/shard_map/ppermute | solution.py:750
  228.8 7.2 %collective-permute-start.26 = (bf16[16,112,128]{2,1,0:T(8,128)(2,1)}, bf16[16,112,128]{2,1,0:T(8,128)(2,1)S(1)}, u32[]{:S(2)}, u32[]{:S(2)}) collective-permute-start(bf16[16,112,128]{2,1,0:T(8,128)(2,1)} %collective-permute-done.22.refs_5_), channel_id=1, source_target_pairs={{0,4},{1,5},{2,6},{3,7},{4,0},{5,1},{6,2},{7,3},{8,12},{9,13},{10,... | collective-permute-start | bytes 1376264 | tf_op jit(solution)/shard_map/ppermute | solution.py:750
  231.7 4.3 %copy-start.1 = (bf16[2,8,80,256]{3,2,1,0:T(8,128)(2,1)S(1)}, bf16[2,8,80,256]{3,2,1,0:T(8,128)(2,1)}, u32[]{:S(2)}) copy-start(bf16[2,8,80,256]{3,2,1,0:T(8,128)(2,1)} %param.10) | copy-start | bytes 1966084
  231.7 4.3 %copy-start.3 = (bf16[2,8,80,256]{3,2,1,0:T(8,128)(2,1)S(1)}, bf16[2,8,80,256]{3,2,1,0:T(8,128)(2,1)}, u32[]{:S(2)}) copy-start(bf16[2,8,80,256]{3,2,1,0:T(8,128)(2,1)} %param.11) | copy-start | bytes 1966084
  231.8 4.3 %copy-start.4 = (f32[1280,256]{1,0:T(8,128)S(1)}, f32[1280,256]{1,0:T(8,128)}, u32[]{:S(2)}) copy-start(f32[1280,256]{1,0:T(8,128)} %get-tuple-element.90.refs_10_) | copy-start | bytes 3932164
  231.8 4.3 %copy-start.6 = (f32[128,1,128]{2,1,0:T(1,128)S(1)}, f32[128,1,128]{2,1,0:T(1,128)}, u32[]{:S(2)}) copy-start(f32[128,1,128]{2,1,0:T(1,128)} %copy-done.5) | copy-start | bytes 196612

commit v7 on v6

--- a/solution.py
+++ b/solution.py
@@ -659,6 +659,7 @@
             (moment_type, moment_type, *part_types),
             (pltpu.VMEM((PIECE, 128), F32),),
             parts={0: 4},
+            mib=16,
         )
         return part, first_new.reshape(-1), second_new.reshape(-1)
 

time: 243 us -> 241 us (level)
    unnamed x38 -> x44, local copies, waits for them, and re-layouts: 4.93 us -> 4.37 us
where the time goes in v7:
time: 241 us; the launch traced here: 240 us
  starting transfers between devices  87.8 us (36%)
  Pallas kernels  75.6 us (31%)
  waiting for transfers between devices  49.4 us (20%)
  blocking collectives  12.1 us (5%)
  local copies, waits for them, and re-layouts  11.8 us (5%)
    pallas_call x12, Pallas kernels, run(): pl.pallas_call(body, out_shape=tuple((jax.ShapeDtypeStruct(x.shape, x.dty...  75.6 us
    all_to_all x3, starting transfers between devices, everyone(): return lax.all_to_all(row, BOTH, 0, 0, tiled=True)  23.6 us
    ppermute x6, waiting for transfers between devices, over_line(): lax.ppermute(piece, 'rows', [(i, (i + k) % bands) for i in range(bands)])  22.4 us
    all_to_all x2, starting transfers between devices, over_chips(): lax.all_to_all(pieces, BOTH, 0, 0, axis_index_groups=CHIP_GROUPS, tiled=T...  19.4 us
    all_to_all x3, waiting for transfers between devices, everyone(): return lax.all_to_all(row, BOTH, 0, 0, tiled=True)  14.7 us
    all_to_all x1, blocking collectives, over_plane(): lax.all_to_all(pieces, BOTH, 0, 0, axis_index_groups=PLANE_GROUPS, tiled=...  12.1 us
    ppermute x6, starting transfers between devices, over_line(): lax.ppermute(piece, 'rows', [(i, (i + k) % bands) for i in range(bands)])  8.67 us
    ppermute x2, starting transfers between devices, edge_rows(): lax.ppermute(last, 'rows', down)  7.39 us
  transfers between devices with their start and end apart: 34, of which 13 were waited for; matrix products, arithmetic and copies ran while one was open for 2% of the time, Pallas kernels for 23%

profile of v7, /device:TPU:1, one launch (start us, length us, event | category | flops | bytes accessed | tf_op | source)
XLA Modules:
  0.0 239.8 jit_solution(551513242181686009)
XLA Ops:
  0.6 1.0 slice_bitcast_fusion.3
  1.7 0.9 slice_bitcast_fusion.2
  2.6 4.0 %collective-permute-start = (bf16[4,80,256]{2,1,0:T(8,128)(2,1)S(1)}, bf16[4,80,256]{2,1,0:T(8,128)(2,1)S(1)}, u32[]{:S(2)}, u32[]{:S(2)}) collective-permute-start(bf16[4,80,256]{2,1,0:T(8,128)(2,1)S(1)} %pad_maximum_fusion.2), channel_id=1, source_target_pairs={{0,1},{1,2},{2,3},{4,5},{5,6},{6,7},{8,9},{9,10},{10,11},{12,13},{... | collective-permute-start | bytes 491528 | tf_op jit(solution)/shard_map/ppermute | solution.py:544
  6.6 1.4 collective-permute-start.1
  8.1 2.4 shard_map.153
  10.5 0.7 slice_bitcast_fusion.7
  11.2 2.2 collective-permute-done.1
  13.4 0.7 slice_bitcast_fusion.6
  14.2 5.0 %collective-permute-start.2 = (bf16[2,10,80,256]{3,2,1,0:T(8,128)(2,1)S(1)}, bf16[2,10,80,256]{3,2,1,0:T(8,128)(2,1)}, u32[]{:S(2)}, u32[]{:S(2)}) collective-permute-start(bf16[2,10,80,256]{3,2,1,0:T(8,128)(2,1)S(1)} %pad_maximum_fusion), channel_id=1, source_target_pairs={{0,4},{4,8},{8,12},{12,16},{16,20},{20,24},{24,28},{28,32},{32,36}... | collective-permute-start | bytes 2457608 | tf_op jit(solution)/shard_map/ppermute | solution.py:565
  19.3 1.9 collective-permute-start.3
  21.2 10.3 %all-to-all-start = ((f32[128,1,128]{2,1,0:T(1,128)}), f32[128,1,128]{2,1,0:T(1,128)S(1)}, u32[]{:S(2)}, u32[]{:S(2)}) async-start(f32[128,1,128]{2,1,0:T(1,128)} %bitcast.18), calls=%async_computation | async-start | bytes 131072 | tf_op jit(solution)/shard_map/all_to_all | solution.py:530
  31.5 0.6 maximum_maximum_fusion.refs_0_
  32.1 9.0 %all-to-all-done = f32[128,1,128]{2,1,0:T(1,128)S(1)} async-done(((f32[128,1,128]{2,1,0:T(1,128)}), f32[128,1,128]{2,1,0:T(1,128)S(1)}, u32[]{:S(2)}, u32[]{:S(2)}) %all-to-all-start) | async-done | bytes 65568 | tf_op jit(solution)/shard_map/all_to_all | solution.py:530
  41.1 0.6 copy-done.5
  41.7 10.0 %shard_map.154 = (bf16[3200,768]{1,0:T(8,128)(2,1)}, bf16[1280,256]{1,0:T(8,128)(2,1)}, f32[128,128]{1,0:T(8,128)}) custom-call(f32[3]{0:T(128)} %maximum_maximum_fusion.refs_0_, bf16[1280,256]{1,0:T(8,128)(2,1)} %bitcast.83, bf16[160,256]{1,0:T(8,128)(2,1)} %bitcast.106, bf16[160,256]{1,0:T(8,128)(2,1)} %bitcast.107, bf16[1600,256]{1,0:T(8,128)(2,1)} %bitcast.16.refs_4_, ...), custom_call_target="tpu_custom_call" | custom-call | flops 1024 | bytes 1024 | tf_op jit(solution)/shard_map/pallas_call | solution.py:517
  51.7 4.4 %all-to-all-start.1 = ((f32[128,1,128]{2,1,0:T(1,128)}), f32[128,1,128]{2,1,0:T(1,128)S(1)}, u32[]{:S(2)}, u32[]{:S(2)}) async-start(f32[128,1,128]{2,1,0:T(1,128)} %bitcast.114), calls=%async_computation.1 | async-start | bytes 131072 | tf_op jit(solution)/shard_map/all_to_all | solution.py:530
  56.1 0.6 maximum_maximum_fusion.1.refs_0_
  56.7 0.9 copy-done.12
  57.6 9.0 %shard_map.155 = (f32[1280,256]{1,0:T(8,128)}, bf16[3200,768]{1,0:T(8,128)(2,1)}) custom-call(f32[3]{0:T(128)} %maximum_maximum_fusion.1.refs_0_, bf16[1280,256]{1,0:T(8,128)(2,1)} %bitcast.87, bf16[160,256]{1,0:T(8,128)(2,1)} %bitcast.104, bf16[160,256]{1,0:T(8,128)(2,1)} %bitcast.105, bf16[1600,256]{1,0:T(8,128)(2,1)} %bitcast.99, bf16[6912,256]{1,0:T(8,128)(2,1)} %refs_5_.1), custom_call_target="tpu_custom_call" | custom-call | flops 1024 | bytes 1024 | tf_op jit(solution)/shard_map/pallas_call | solution.py:517
  66.7 0.6 copy-done.14
  67.3 11.2 %shard_map.156 = (f32[1280,256]{1,0:T(8,128)}, f32[128,128]{1,0:T(8,128)}, bf16[16,112,128]{2,1,0:T(8,128)(2,1)}, bf16[16,112,128]{2,1,0:T(8,128)(2,1)}, bf16[16...) custom-call(s32[1]{0:T(128)} %bitcast.refs_0_, ...), custom_call_target="tpu_custom_call" | custom-call | flops 1024 | bytes 1024 | tf_op jit(solution)/shard_map/pallas_call | solution.py:517
  78.5 1.4 collective-permute-start.4
  80.5 9.0 %all-to-all-start.2 = ((f32[128,1,128]{2,1,0:T(1,128)}), f32[128,1,128]{2,1,0:T(1,128)S(1)}, u32[]{:S(2)}, u32[]{:S(2)}) async-start(f32[128,1,128]{2,1,0:T(1,128)} %bitcast.113), calls=%async_computation.2 | async-start | bytes 131072 | tf_op jit(solution)/shard_map/all_to_all | solution.py:530
  89.5 0.7 copy-done.15
  90.4 3.0 %shard_map.157 = bf16[64,112,128]{2,1,0:T(8,128)(2,1)} custom-call(bf16[16,112,128]{2,1,0:T(8,128)(2,1)} %get-tuple-element.60.refs_0_, bf16[16,112,128]{2,1,0:T(8,128)(2,1)} %get-tuple-element.61.refs_1_, bf16[16,112,128]{2,1,0:T(8,128)(2,1)} %get-tuple-element.62.refs_2_, bf16[16,112,128]{2,1,0:T(8,128)(2,1)} %get-tuple-element.63.refs_3_, ...), custom_call_target="tpu_custom_call" | custom-call | flops 1024 | bytes 1024 | tf_op jit(solution)/shard_map/pallas_call | solution.py:517
  93.4 5.7 %all-to-all-done.2 = f32[128,1,128]{2,1,0:T(1,128)S(1)} async-done(((f32[128,1,128]{2,1,0:T(1,128)}), f32[128,1,128]{2,1,0:T(1,128)S(1)}, u32[]{:S(2)}, u32[]{:S(2)}) %all-to-all-start.2) | async-done | bytes 65568 | tf_op jit(solution)/shard_map/all_to_all | solution.py:530
  99.2 0.6 copy-done.17
  99.8 5.7 %all-to-all-start.4 = ((bf16[64,112,128]{2,1,0:T(8,128)(2,1)}), bf16[64,112,128]{2,1,0:T(8,128)(2,1)}, u32[]{:S(2)}, u32[]{:S(2)}) async-start(bf16[64,112,128]{2,1,0:T(8,128)(2,1)} %shard_map.157), calls=%async_computation.4 | async-start | bytes 3670016 | tf_op jit(solution)/shard_map/all_to_all | solution.py:616
  105.5 10.6 %shard_map.158 = (bf16[1280,256]{1,0:T(8,128)(2,1)}, bf16[16,112,128]{2,1,0:T(8,128)(2,1)}, bf16[16,112,128]{2,1,0:T(8,128)(2,1)}, bf16[16,112,128]{2,1,0:T(8,12...) custom-call(s32[1]{0:T(128)} %bitcast.refs_0_, ...), custom_call_target="tpu_custom_call" | custom-call | flops 1024 | bytes 1024 | tf_op jit(solution)/shard_map/pallas_call | solution.py:517
  116.1 2.6 %collective-permute-start.8 = (bf16[2,8,80,256]{3,2,1,0:T(8,128)(2,1)}, bf16[2,8,80,256]{3,2,1,0:T(8,128)(2,1)S(1)}, u32[]{:S(2)}, u32[]{:S(2)}) collective-permute-start(bf16[2,8,80,256]{3,2,1,0:T(8,128)(2,1)} %bitcast.97), channel_id=1, source_target_pairs={{4,0},{8,4},{12,8},{16,12},{20,16},{24,20},{28,24},{32,28},{36,32}... | collective-permute-start | bytes 1966088 | tf_op jit(solution)/shard_map/ppermute | solution.py:552
  118.7 0.9 slice_bitcast_fusion
  119.7 1.3 collective-permute-start.10
  121.0 3.4 %collective-permute-start.11 = (bf16[2,80,256]{2,1,0:T(8,128)(2,1)S(1)}, bf16[2,80,256]{2,1,0:T(8,128)(2,1)S(1)}, u32[]{:S(2)}, u32[]{:S(2)}) collective-permute-start(bf16[2,80,256]{2,1,0:T(8,128)(2,1)S(1)} %get-tuple-element.98), channel_id=1, source_target_pairs={{0,1},{1,2},{2,3},{4,5},{5,6},{6,7},{8,9},{9,10},{10,11},{12,13},{... | collective-permute-start | bytes 245768 | tf_op jit(solution)/shard_map/ppermute | solution.py:544
  124.4 1.3 collective-permute-start.12
  125.7 3.2 %collective-permute-start.9 = (bf16[2,80,256]{2,1,0:T(8,128)(2,1)S(1)}, bf16[2,80,256]{2,1,0:T(8,128)(2,1)S(1)}, u32[]{:S(2)}, u32[]{:S(2)}) collective-permute-start(bf16[2,80,256]{2,1,0:T(8,128)(2,1)S(1)} %get-tuple-element.98), channel_id=1, source_target_pairs={{4,1},{5,2},{6,3},{8,5},{9,6},{10,7},{12,9},{13,10},{14,11},{16,13... | collective-permute-start | bytes 245768 | tf_op jit(solution)/shard_map/ppermute | solution.py:556
  128.9 0.6 collective-permute-done.10
  130.9 3.4 %collective-permute-done.8 = bf16[2,8,80,256]{3,2,1,0:T(8,128)(2,1)S(1)} collective-permute-done((bf16[2,8,80,256]{3,2,1,0:T(8,128)(2,1)}, bf16[2,8,80,256]{3,2,1,0:T(8,128)(2,1)S(1)}, u32[]{:S(2)}, u32[]{:S(2)}) %collective-permute-start.8) | collective-permute-done | bytes 655392 | tf_op jit(solution)/shard_map/ppermute | solution.py:552
  134.4 3.2 %shard_map.159 = bf16[64,112,128]{2,1,0:T(8,128)(2,1)} custom-call(bf16[16,112,128]{2,1,0:T(8,128)(2,1)} %get-tuple-element.73.refs_0_, bf16[16,112,128]{2,1,0:T(8,128)(2,1)} %get-tuple-element.74.refs_1_, bf16[16,112,128]{2,1,0:T(8,128)(2,1)} %get-tuple-element.75.refs_2_, bf16[16,112,128]{2,1,0:T(8,128)(2,1)} %get-tuple-element.76.refs_3_, ...), custom_call_target="tpu_custom_call" | custom-call | flops 1024 | bytes 1024 | tf_op jit(solution)/shard_map/pallas_call | solution.py:517
  137.7 13.7 %all-to-all-start.3 = ((bf16[64,112,128]{2,1,0:T(8,128)(2,1)}), bf16[64,112,128]{2,1,0:T(8,128)(2,1)S(1)}, u32[]{:S(2)}, u32[]{:S(2)}) async-start(bf16[64,112,128]{2,1,0:T(8,128)(2,1)} %shard_map.159), calls=%async_computation.3 | async-start | bytes 3670016 | tf_op jit(solution)/shard_map/all_to_all | solution.py:616
  151.4 0.8 constant_dynamic-slice_fusion.1
  152.2 2.5 %shard_map.160 = (f32[108,128]{1,0:T(8,128)}, f32[108,128]{1,0:T(8,128)}, bf16[1,112,128]{2,1,0:T(8,128)(2,1)S(1)}) custom-call(bf16[64,112,128]{2,1,0:T(8,128)(2,1)} %all-to-all-done.4.refs_0_, bf16[108,128]{1,0:T(8,128)(2,1)S(1)} %reshape.128.refs_1_, f32[108,128]{1,0:T(8,128)S(1)} %bitcast.93, f32[108,128]{1,0:T(8,128)S(1)} %bitcast.94), custom_call_target="tpu_custom_call" | custom-call | flops 1024 | bytes 1024 | tf_op jit(solution)/shard_map/pallas_call | solution.py:517
  154.7 2.3 collective-permute-start.17
  157.0 0.6 collective-permute-start.18
  157.5 0.6 collective-permute-start.19
  158.1 0.8 constant_dynamic-slice_fusion
  159.0 10.8 %shard_map.161 = (f32[1280,256]{1,0:T(8,128)}, f32[8,128]{1,0:T(8,128)}) custom-call(f32[3]{0:T(128)} %maximum_maximum_fusion.1.refs_0_, bf16[1280,256]{1,0:T(8,128)(2,1)} %get-tuple-element.84.refs_1_, bf16[160,256]{1,0:T(8,128)(2,1)} %bitcast.110, bf16[160,256]{1,0:T(8,128)(2,1)} %bitcast.111, bf16[1280,256]{1,0:T(8,128)(2,1)} %bitcast.100, ...), custom_call_target="tpu_custom_call" | custom-call | flops 1024 | bytes 1024 | tf_op jit(solution)/shard_map/pallas_call | solution.py:517
  169.8 3.1 %collective-permute-done.17 = bf16[1,112,128]{2,1,0:T(8,128)(2,1)S(1)} collective-permute-done((bf16[1,112,128]{2,1,0:T(8,128)(2,1)S(1)}, bf16[1,112,128]{2,1,0:T(8,128)(2,1)S(1)}, u32[]{:S(2)}, u32[]{:S(2)}) %collective-permute-start.17) | collective-permute-done | bytes 28704 | tf_op jit(solution)/shard_map/ppermute | solution.py:579
  172.9 1.5 collective-permute-done.18
  174.4 3.2 %all-to-all-done.3.refs_0_ = bf16[64,112,128]{2,1,0:T(8,128)(2,1)S(1)} async-done(((bf16[64,112,128]{2,1,0:T(8,128)(2,1)}), bf16[64,112,128]{2,1,0:T(8,128)(2,1)S(1)}, u32[]{:S(2)}, u32[]{:S(2)}) %all-to-all-start.3) | async-done | bytes 1835040 | tf_op jit(solution)/shard_map/all_to_all | solution.py:616
  177.6 0.7 copy-done.11
  178.3 2.9 %shard_map.162 = (f32[108,128]{1,0:T(8,128)}, f32[108,128]{1,0:T(8,128)}, bf16[16,112,128]{2,1,0:T(8,128)(2,1)S(1)}) custom-call(bf16[64,112,128]{2,1,0:T(8,128)(2,1)S(1)} %all-to-all-done.3.refs_0_, bf16[108,128]{1,0:T(8,128)(2,1)S(1)} %reshape.131.refs_1_, f32[108,128]{1,0:T(8,128)S(1)} %bitcast.95, f32[108,128]{1,0:T(8,128)S(1)} %bitcast.96, ...), custom_call_target="tpu_custom_call" | custom-call | flops 1024 | bytes 1024 | tf_op jit(solution)/shard_map/pallas_call | solution.py:517
  181.2 12.1 %all_to_all.53.refs_2_ = bf16[16,112,128]{2,1,0:T(8,128)(2,1)S(1)} all-to-all(bf16[16,112,128]{2,1,0:T(8,128)(2,1)S(1)} %get-tuple-element.86), channel_id=1, replica_groups={{0,8,16,24,32,40,48,56,64,72,80,88,96,104,112,120},{1,9,17,25,33,41,49,..., dimensions={0} | all-to-all | bytes 917504 | tf_op jit(solution)/shard_map/all_to_all | solution.py:573
  193.3 1.6 broadcast_in_dim.24
  194.9 3.7 %all-to-all-start.6 = ((bf16[16,448,128]{2,1,0:T(8,128)(2,1)}), bf16[16,448,128]{2,1,0:T(8,128)(2,1)S(1)}, u32[]{:S(2)}, u32[]{:S(2)}) async-start(bf16[16,448,128]{2,1,0:T(8,128)(2,1)} %broadcast_in_dim.24), calls=%async_computation.6 | async-start | bytes 3670016 | tf_op jit(solution)/shard_map/all_to_all | solution.py:573
  198.7 1.1 collective-permute-start.20
  199.7 2.2 collective-permute-start.21
  201.9 2.0 collective-permute-start.22
  203.9 5.1 %collective-permute-done.20.refs_3_ = bf16[16,112,128]{2,1,0:T(8,128)(2,1)S(1)} collective-permute-done((bf16[16,112,128]{2,1,0:T(8,128)(2,1)S(1)}, bf16[16,112,128]{2,1,0:T(8,128)(2,1)S(1)}, u32[]{:S(2)}, u32[]{:S(2)}) %collective-permute-start.20) | collective-permute-done | bytes 458784 | tf_op jit(solution)/shard_map/ppermute | solution.py:579
  209.0 10.7 %collective-permute-done.21.refs_4_ = bf16[16,112,128]{2,1,0:T(8,128)(2,1)S(1)} collective-permute-done((bf16[16,112,128]{2,1,0:T(8,128)(2,1)S(1)}, bf16[16,112,128]{2,1,0:T(8,128)(2,1)S(1)}, u32[]{:S(2)}, u32[]{:S(2)}) %collective-permute-start.21) | collective-permute-done | bytes 458784 | tf_op jit(solution)/shard_map/ppermute | solution.py:579
  219.7 2.1 collective-permute-done.22.refs_5_
  221.8 4.3 %collective-permute-start.27 = (bf16[16,448,128]{2,1,0:T(8,128)(2,1)S(1)}, bf16[16,448,128]{2,1,0:T(8,128)(2,1)S(1)}, u32[]{:S(2)}, u32[]{:S(2)}) collective-permute-start(bf16[16,448,128]{2,1,0:T(8,128)(2,1)S(1)} %all-to-all-done.6), channel_id=1, source_target_pairs={{0,4},{1,5},{2,6},{3,7},{4,0},{5,1},{6,2},{7,3},{8,12},{9,13},{10,... | collective-permute-start | bytes 5505032 | tf_op jit(solution)/shard_map/ppermute | solution.py:750
  227.1 2.4 collective-permute-done.27
  229.5 4.2 %shard_map.163 = bf16[6912,256]{1,0:T(8,128)(2,1)} custom-call(s32[1]{0:T(128)} %bitcast.refs_0_, bf16[64,112,128]{2,1,0:T(8,128)(2,1)S(1)} %bitcast.86, bf16[64,112,128]{2,1,0:T(8,128)(2,1)S(1)} %bitcast.89), custom_call_target="tpu_custom_call" | custom-call | flops 1024 | bytes 1024 | tf_op jit(solution)/shard_map/pallas_call | solution.py:517
  233.9 5.7 %shard_map.164 = (bf16[6912,256]{1,0:T(8,128)(2,1)}, bf16[1280,256]{1,0:T(8,128)(2,1)}) custom-call(s32[1]{0:T(128)} %bitcast.refs_0_, s32[1]{0:T(128)} %bitcast.1.refs_1_, bf16[16,112,128]{2,1,0:T(8,128)(2,1)S(1)} %all_to_all.53.refs_2_, bf16[16,112,128]{2,1,0:T(8,128)(2,1)S(1)} %collective-permute-done.20.refs_3_, ...), custom_call_target="tpu_custom_call" | custom-call | flops 1024 | bytes 1024 | tf_op jit(solution)/shard_map/pallas_call | solution.py:517
  (79 shorter events, 3.6 us)
Async XLA Ops:
  0.6 13.5 %copy-start = (bf16[2,8,80,256]{3,2,1,0:T(8,128)(2,1)S(1)}, bf16[2,8,80,256]{3,2,1,0:T(8,128)(2,1)}, u32[]{:S(2)}) copy-start(bf16[2,8,80,256]{3,2,1,0:T(8,128)(2,1)} %param.10) | copy-start | bytes 1966084
  2.6 7.8 %collective-permute-start = (bf16[4,80,256]{2,1,0:T(8,128)(2,1)S(1)}, bf16[4,80,256]{2,1,0:T(8,128)(2,1)S(1)}, u32[]{:S(2)}, u32[]{:S(2)}) collective-permute-start(bf16[4,80,256]{2,1,0:T(8,128)(2,1)S(1)} %pad_maximum_fusion.2), channel_id=1, source_target_pairs={{0,1},{1,2},{2,3},{4,5},{5,6},{6,7},{8,9},{9,10},{10,11},{12,13},{... | collective-permute-start | bytes 491528 | tf_op jit(solution)/shard_map/ppermute | solution.py:544
  6.6 12.6 %copy-start.2 = (bf16[2,8,80,256]{3,2,1,0:T(8,128)(2,1)S(1)}, bf16[2,8,80,256]{3,2,1,0:T(8,128)(2,1)}, u32[]{:S(2)}) copy-start(bf16[2,8,80,256]{3,2,1,0:T(8,128)(2,1)} %param.11) | copy-start | bytes 1966084
  6.6 6.8 %collective-permute-start.1 = (bf16[4,80,256]{2,1,0:T(8,128)(2,1)S(1)}, bf16[4,80,256]{2,1,0:T(8,128)(2,1)S(1)}, u32[]{:S(2)}, u32[]{:S(2)}) collective-permute-start(bf16[4,80,256]{2,1,0:T(8,128)(2,1)S(1)} %pad_maximum_fusion.3), channel_id=1, source_target_pairs={{1,0},{2,1},{3,2},{5,4},{6,5},{7,6},{9,8},{10,9},{11,10},{13,12},{... | collective-permute-start | bytes 491528 | tf_op jit(solution)/shard_map/ppermute | solution.py:544
  14.2 26.9 %collective-permute-start.2 = (bf16[2,10,80,256]{3,2,1,0:T(8,128)(2,1)S(1)}, bf16[2,10,80,256]{3,2,1,0:T(8,128)(2,1)}, u32[]{:S(2)}, u32[]{:S(2)}) collective-permute-start(bf16[2,10,80,256]{3,2,1,0:T(8,128)(2,1)S(1)} %pad_maximum_fusion), channel_id=1, source_target_pairs={{0,4},{4,8},{8,12},{12,16},{16,20},{20,24},{24,28},{28,32},{32,36}... | collective-permute-start | bytes 2457608 | tf_op jit(solution)/shard_map/ppermute | solution.py:565
  19.3 37.5 %collective-permute-start.3 = (bf16[2,10,80,256]{3,2,1,0:T(8,128)(2,1)S(1)}, bf16[2,10,80,256]{3,2,1,0:T(8,128)(2,1)S(1)}, u32[]{:S(2)}, u32[]{:S(2)}) collective-permute-start(bf16[2,10,80,256]{3,2,1,0:T(8,128)(2,1)S(1)} %pad_maximum_fusion.1), channel_id=1, source_target_pairs={{4,0},{8,4},{12,8},{16,12},{20,16},{24,20},{28,24},{32,28},{36,32}... | collective-permute-start | bytes 2457608 | tf_op jit(solution)/shard_map/ppermute | solution.py:565
  21.2 19.9 %all-to-all-start = ((f32[128,1,128]{2,1,0:T(1,128)}), f32[128,1,128]{2,1,0:T(1,128)S(1)}, u32[]{:S(2)}, u32[]{:S(2)}) async-start(f32[128,1,128]{2,1,0:T(1,128)} %bitcast.18), calls=%async_computation | async-start | bytes 131072 | tf_op jit(solution)/shard_map/all_to_all | solution.py:530
  41.1 0.6 copy-start.5
  51.7 15.0 %all-to-all-start.1 = ((f32[128,1,128]{2,1,0:T(1,128)}), f32[128,1,128]{2,1,0:T(1,128)S(1)}, u32[]{:S(2)}, u32[]{:S(2)}) async-start(f32[128,1,128]{2,1,0:T(1,128)} %bitcast.114), calls=%async_computation.1 | async-start | bytes 131072 | tf_op jit(solution)/shard_map/all_to_all | solution.py:530
  56.7 0.9 copy-start.12
  66.7 0.6 copy-start.14
  78.5 10.9 %collective-permute-start.4 = (bf16[16,112,128]{2,1,0:T(8,128)(2,1)}, bf16[16,112,128]{2,1,0:T(8,128)(2,1)S(1)}, u32[]{:S(2)}, u32[]{:S(2)}) collective-permute-start(bf16[16,112,128]{2,1,0:T(8,128)(2,1)} %get-tuple-element.64), channel_id=1, source_target_pairs={{0,4},{1,5},{2,6},{3,7},{4,0},{5,1},{6,2},{7,3},{8,12},{9,13},{10,... | collective-permute-start | bytes 1376264 | tf_op jit(solution)/shard_map/ppermute | solution.py:609
  79.9 9.6 %collective-permute-start.5 = (bf16[16,112,128]{2,1,0:T(8,128)(2,1)}, bf16[16,112,128]{2,1,0:T(8,128)(2,1)S(1)}, u32[]{:S(2)}, u32[]{:S(2)}) collective-permute-start(bf16[16,112,128]{2,1,0:T(8,128)(2,1)} %get-tuple-element.65), channel_id=1, source_target_pairs={{0,4},{1,5},{2,6},{3,7},{4,0},{5,1},{6,2},{7,3},{8,12},{9,13},{10,... | collective-permute-start | bytes 1376264 | tf_op jit(solution)/shard_map/ppermute | solution.py:609
  80.0 9.5 %collective-permute-start.6 = (bf16[16,112,128]{2,1,0:T(8,128)(2,1)}, bf16[16,112,128]{2,1,0:T(8,128)(2,1)}, u32[]{:S(2)}, u32[]{:S(2)}) collective-permute-start(bf16[16,112,128]{2,1,0:T(8,128)(2,1)} %get-tuple-element.66), channel_id=1, source_target_pairs={{0,4},{1,5},{2,6},{3,7},{4,0},{5,1},{6,2},{7,3},{8,12},{9,13},{10,... | collective-permute-start | bytes 1376264 | tf_op jit(solution)/shard_map/ppermute | solution.py:609
  80.4 9.1 %collective-permute-start.7 = (bf16[16,112,128]{2,1,0:T(8,128)(2,1)}, bf16[16,112,128]{2,1,0:T(8,128)(2,1)}, u32[]{:S(2)}, u32[]{:S(2)}) collective-permute-start(bf16[16,112,128]{2,1,0:T(8,128)(2,1)} %get-tuple-element.67), channel_id=1, source_target_pairs={{0,4},{1,5},{2,6},{3,7},{4,0},{5,1},{6,2},{7,3},{8,12},{9,13},{10,... | collective-permute-start | bytes 1376264 | tf_op jit(solution)/shard_map/ppermute | solution.py:609
  80.5 18.6 %all-to-all-start.2 = ((f32[128,1,128]{2,1,0:T(1,128)}), f32[128,1,128]{2,1,0:T(1,128)S(1)}, u32[]{:S(2)}, u32[]{:S(2)}) async-start(f32[128,1,128]{2,1,0:T(1,128)} %bitcast.113), calls=%async_computation.2 | async-start | bytes 131072 | tf_op jit(solution)/shard_map/all_to_all | solution.py:530
  89.5 0.8 copy-start.15
  89.5 0.9 copy-start.16
  99.1 0.6 copy-start.17
  99.8 37.9 %all-to-all-start.4 = ((bf16[64,112,128]{2,1,0:T(8,128)(2,1)}), bf16[64,112,128]{2,1,0:T(8,128)(2,1)}, u32[]{:S(2)}, u32[]{:S(2)}) async-start(bf16[64,112,128]{2,1,0:T(8,128)(2,1)} %shard_map.157), calls=%async_computation.4 | async-start | bytes 3670016 | tf_op jit(solution)/shard_map/all_to_all | solution.py:616
  116.1 18.2 %collective-permute-start.8 = (bf16[2,8,80,256]{3,2,1,0:T(8,128)(2,1)}, bf16[2,8,80,256]{3,2,1,0:T(8,128)(2,1)S(1)}, u32[]{:S(2)}, u32[]{:S(2)}) collective-permute-start(bf16[2,8,80,256]{3,2,1,0:T(8,128)(2,1)} %bitcast.97), channel_id=1, source_target_pairs={{4,0},{8,4},{12,8},{16,12},{20,16},{24,20},{28,24},{32,28},{36,32}... | collective-permute-start | bytes 1966088 | tf_op jit(solution)/shard_map/ppermute | solution.py:552
  119.7 9.8 %collective-permute-start.10 = (bf16[2,80,256]{2,1,0:T(8,128)(2,1)S(1)}, bf16[2,80,256]{2,1,0:T(8,128)(2,1)S(1)}, u32[]{:S(2)}, u32[]{:S(2)}) collective-permute-start(bf16[2,80,256]{2,1,0:T(8,128)(2,1)S(1)} %get-tuple-element.97), channel_id=1, source_target_pairs={{5,0},{6,1},{7,2},{9,4},{10,5},{11,6},{13,8},{14,9},{15,10},{17,12... | collective-permute-start | bytes 245768 | tf_op jit(solution)/shard_map/ppermute | solution.py:556
  121.0 8.5 %collective-permute-start.11 = (bf16[2,80,256]{2,1,0:T(8,128)(2,1)S(1)}, bf16[2,80,256]{2,1,0:T(8,128)(2,1)S(1)}, u32[]{:S(2)}, u32[]{:S(2)}) collective-permute-start(bf16[2,80,256]{2,1,0:T(8,128)(2,1)S(1)} %get-tuple-element.98), channel_id=1, source_target_pairs={{0,1},{1,2},{2,3},{4,5},{5,6},{6,7},{8,9},{9,10},{10,11},{12,13},{... | collective-permute-start | bytes 245768 | tf_op jit(solution)/shard_map/ppermute | solution.py:544
  124.4 6.0 %collective-permute-start.12 = (bf16[2,80,256]{2,1,0:T(8,128)(2,1)S(1)}, bf16[2,80,256]{2,1,0:T(8,128)(2,1)S(1)}, u32[]{:S(2)}, u32[]{:S(2)}) collective-permute-start(bf16[2,80,256]{2,1,0:T(8,128)(2,1)S(1)} %get-tuple-element.97), channel_id=1, source_target_pairs={{1,0},{2,1},{3,2},{5,4},{6,5},{7,6},{9,8},{10,9},{11,10},{13,12},{... | collective-permute-start | bytes 245768 | tf_op jit(solution)/shard_map/ppermute | solution.py:544
  125.7 4.7 %collective-permute-start.9 = (bf16[2,80,256]{2,1,0:T(8,128)(2,1)S(1)}, bf16[2,80,256]{2,1,0:T(8,128)(2,1)S(1)}, u32[]{:S(2)}, u32[]{:S(2)}) collective-permute-start(bf16[2,80,256]{2,1,0:T(8,128)(2,1)S(1)} %get-tuple-element.98), channel_id=1, source_target_pairs={{4,1},{5,2},{6,3},{8,5},{9,6},{10,7},{12,9},{13,10},{14,11},{16,13... | collective-permute-start | bytes 245768 | tf_op jit(solution)/shard_map/ppermute | solution.py:556
  129.5 8.1 %copy-start.18 = (bf16[2,80,256]{2,1,0:T(8,128)(2,1)}, bf16[2,80,256]{2,1,0:T(8,128)(2,1)S(1)}, u32[]{:S(2)}) copy-start(bf16[2,80,256]{2,1,0:T(8,128)(2,1)S(1)} %collective-permute-done.10) | copy-start | bytes 245764
  129.5 4.8 %collective-permute-start.13 = (bf16[16,112,128]{2,1,0:T(8,128)(2,1)}, bf16[16,112,128]{2,1,0:T(8,128)(2,1)}, u32[]{:S(2)}, u32[]{:S(2)}) collective-permute-start(bf16[16,112,128]{2,1,0:T(8,128)(2,1)} %get-tuple-element.77), channel_id=1, source_target_pairs={{0,4},{1,5},{2,6},{3,7},{4,0},{5,1},{6,2},{7,3},{8,12},{9,13},{10,... | collective-permute-start | bytes 1376264 | tf_op jit(solution)/shard_map/ppermute | solution.py:609
  129.5 8.1 %copy-start.19 = (bf16[2,80,256]{2,1,0:T(8,128)(2,1)}, bf16[2,80,256]{2,1,0:T(8,128)(2,1)S(1)}, u32[]{:S(2)}) copy-start(bf16[2,80,256]{2,1,0:T(8,128)(2,1)S(1)} %collective-permute-done.11) | copy-start | bytes 245764
  129.5 4.8 %collective-permute-start.14 = (bf16[16,112,128]{2,1,0:T(8,128)(2,1)}, bf16[16,112,128]{2,1,0:T(8,128)(2,1)}, u32[]{:S(2)}, u32[]{:S(2)}) collective-permute-start(bf16[16,112,128]{2,1,0:T(8,128)(2,1)} %get-tuple-element.78), channel_id=1, source_target_pairs={{0,4},{1,5},{2,6},{3,7},{4,0},{5,1},{6,2},{7,3},{8,12},{9,13},{10,... | collective-permute-start | bytes 1376264 | tf_op jit(solution)/shard_map/ppermute | solution.py:609
  130.4 7.2 %copy-start.20 = (bf16[2,80,256]{2,1,0:T(8,128)(2,1)}, bf16[2,80,256]{2,1,0:T(8,128)(2,1)S(1)}, u32[]{:S(2)}) copy-start(bf16[2,80,256]{2,1,0:T(8,128)(2,1)S(1)} %collective-permute-done.12) | copy-start | bytes 245764
  130.4 4.0 %collective-permute-start.15 = (bf16[16,112,128]{2,1,0:T(8,128)(2,1)}, bf16[16,112,128]{2,1,0:T(8,128)(2,1)}, u32[]{:S(2)}, u32[]{:S(2)}) collective-permute-start(bf16[16,112,128]{2,1,0:T(8,128)(2,1)} %get-tuple-element.79), channel_id=1, source_target_pairs={{0,4},{1,5},{2,6},{3,7},{4,0},{5,1},{6,2},{7,3},{8,12},{9,13},{10,... | collective-permute-start | bytes 1376264 | tf_op jit(solution)/shard_map/ppermute | solution.py:609
  130.4 7.2 %copy-start.21 = (bf16[2,80,256]{2,1,0:T(8,128)(2,1)}, bf16[2,80,256]{2,1,0:T(8,128)(2,1)S(1)}, u32[]{:S(2)}) copy-start(bf16[2,80,256]{2,1,0:T(8,128)(2,1)S(1)} %collective-permute-done.9) | copy-start | bytes 245764
  130.4 4.0 %collective-permute-start.16 = (bf16[16,112,128]{2,1,0:T(8,128)(2,1)}, bf16[16,112,128]{2,1,0:T(8,128)(2,1)}, u32[]{:S(2)}, u32[]{:S(2)}) collective-permute-start(bf16[16,112,128]{2,1,0:T(8,128)(2,1)} %get-tuple-element.80), channel_id=1, source_target_pairs={{0,4},{1,5},{2,6},{3,7},{4,0},{5,1},{6,2},{7,3},{8,12},{9,13},{10,... | collective-permute-start | bytes 1376264 | tf_op jit(solution)/shard_map/ppermute | solution.py:609
  134.3 3.3 %copy-start.13 = (bf16[2,8,80,256]{3,2,1,0:T(8,128)(2,1)}, bf16[2,8,80,256]{3,2,1,0:T(8,128)(2,1)S(1)}, u32[]{:S(2)}) copy-start(bf16[2,8,80,256]{3,2,1,0:T(8,128)(2,1)S(1)} %collective-permute-done.8) | copy-start | bytes 1966084
  137.6 14.5 %copy-start.7 = (f32[13824]{0:T(1024)S(1)}, f32[13824]{0:T(1024)}, u32[]{:S(2)}) copy-start(f32[13824]{0:T(1024)} %param.18) | copy-start | bytes 165892
  137.7 14.5 %copy-start.8 = (f32[13824]{0:T(1024)S(1)}, f32[13824]{0:T(1024)}, u32[]{:S(2)}) copy-start(f32[13824]{0:T(1024)} %param.19) | copy-start | bytes 165892
  137.7 40.0 %all-to-all-start.3 = ((bf16[64,112,128]{2,1,0:T(8,128)(2,1)}), bf16[64,112,128]{2,1,0:T(8,128)(2,1)S(1)}, u32[]{:S(2)}, u32[]{:S(2)}) async-start(bf16[64,112,128]{2,1,0:T(8,128)(2,1)} %shard_map.159), calls=%async_computation.3 | async-start | bytes 3670016 | tf_op jit(solution)/shard_map/all_to_all | solution.py:616
  154.7 18.2 %collective-permute-start.17 = (bf16[1,112,128]{2,1,0:T(8,128)(2,1)S(1)}, bf16[1,112,128]{2,1,0:T(8,128)(2,1)S(1)}, u32[]{:S(2)}, u32[]{:S(2)}) collective-permute-start(bf16[1,112,128]{2,1,0:T(8,128)(2,1)S(1)} %get-tuple-element.82), channel_id=1, source_target_pairs={{0,3},{1,0},{2,1},{3,2},{4,7},{5,4},{6,5},{7,6},{8,11},{9,8},{10,9... | collective-permute-start | bytes 86024 | tf_op jit(solution)/shard_map/ppermute | solution.py:579
  157.0 17.4 %collective-permute-start.18 = (bf16[1,112,128]{2,1,0:T(8,128)(2,1)S(1)}, bf16[1,112,128]{2,1,0:T(8,128)(2,1)S(1)}, u32[]{:S(2)}, u32[]{:S(2)}) collective-permute-start(bf16[1,112,128]{2,1,0:T(8,128)(2,1)S(1)} %get-tuple-element.82), channel_id=1, source_target_pairs={{0,2},{1,3},{2,0},{3,1},{4,6},{5,7},{6,4},{7,5},{8,10},{9,11},{10,... | collective-permute-start | bytes 86024 | tf_op jit(solution)/shard_map/ppermute | solution.py:579
  157.5 16.8 %collective-permute-start.19 = (bf16[1,112,128]{2,1,0:T(8,128)(2,1)S(1)}, bf16[1,112,128]{2,1,0:T(8,128)(2,1)S(1)}, u32[]{:S(2)}, u32[]{:S(2)}) collective-permute-start(bf16[1,112,128]{2,1,0:T(8,128)(2,1)S(1)} %get-tuple-element.82), channel_id=1, source_target_pairs={{0,1},{1,2},{2,3},{3,0},{4,5},{5,6},{6,7},{7,4},{8,9},{9,10},{10,1... | collective-permute-start | bytes 86024 | tf_op jit(solution)/shard_map/ppermute | solution.py:579
  159.0 18.6 %copy-start.9 = (f32[13824]{0:T(1024)S(1)}, f32[13824]{0:T(1024)}, u32[]{:S(2)}) copy-start(f32[13824]{0:T(1024)} %param.16) | copy-start | bytes 165892
  159.0 18.6 %copy-start.10 = (f32[13824]{0:T(1024)S(1)}, f32[13824]{0:T(1024)}, u32[]{:S(2)}) copy-start(f32[13824]{0:T(1024)} %param.17) | copy-start | bytes 165892
  177.6 0.7 copy-start.11
  194.9 26.8 %all-to-all-start.6 = ((bf16[16,448,128]{2,1,0:T(8,128)(2,1)}), bf16[16,448,128]{2,1,0:T(8,128)(2,1)S(1)}, u32[]{:S(2)}, u32[]{:S(2)}) async-start(bf16[16,448,128]{2,1,0:T(8,128)(2,1)} %broadcast_in_dim.24), calls=%async_computation.6 | async-start | bytes 3670016 | tf_op jit(solution)/shard_map/all_to_all | solution.py:573
  198.7 10.4 %collective-permute-start.20 = (bf16[16,112,128]{2,1,0:T(8,128)(2,1)S(1)}, bf16[16,112,128]{2,1,0:T(8,128)(2,1)S(1)}, u32[]{:S(2)}, u32[]{:S(2)}) collective-permute-start(bf16[16,112,128]{2,1,0:T(8,128)(2,1)S(1)} %all_to_all.53.refs_2_), channel_id=1, source_target_pairs={{0,1},{1,2},{2,3},{3,0},{4,5},{5,6},{6,7},{7,4},{8,9},{9,10},{10,1... | collective-permute-start | bytes 1376264 | tf_op jit(solution)/shard_map/ppermute | solution.py:579
  199.7 20.0 %collective-permute-start.21 = (bf16[16,112,128]{2,1,0:T(8,128)(2,1)S(1)}, bf16[16,112,128]{2,1,0:T(8,128)(2,1)S(1)}, u32[]{:S(2)}, u32[]{:S(2)}) collective-permute-start(bf16[16,112,128]{2,1,0:T(8,128)(2,1)S(1)} %all_to_all.53.refs_2_), channel_id=1, source_target_pairs={{0,2},{1,3},{2,0},{3,1},{4,6},{5,7},{6,4},{7,5},{8,10},{9,11},{10,... | collective-permute-start | bytes 1376264 | tf_op jit(solution)/shard_map/ppermute | solution.py:579
  201.9 19.9 %collective-permute-start.22 = (bf16[16,112,128]{2,1,0:T(8,128)(2,1)S(1)}, bf16[16,112,128]{2,1,0:T(8,128)(2,1)}, u32[]{:S(2)}, u32[]{:S(2)}) collective-permute-start(bf16[16,112,128]{2,1,0:T(8,128)(2,1)S(1)} %all_to_all.53.refs_2_), channel_id=1, source_target_pairs={{0,3},{1,0},{2,1},{3,2},{4,7},{5,4},{6,5},{7,6},{8,11},{9,8},{10,9... | collective-permute-start | bytes 1376264 | tf_op jit(solution)/shard_map/ppermute | solution.py:579
  221.8 7.7 %collective-permute-start.27 = (bf16[16,448,128]{2,1,0:T(8,128)(2,1)S(1)}, bf16[16,448,128]{2,1,0:T(8,128)(2,1)S(1)}, u32[]{:S(2)}, u32[]{:S(2)}) collective-permute-start(bf16[16,448,128]{2,1,0:T(8,128)(2,1)S(1)} %all-to-all-done.6), channel_id=1, source_target_pairs={{0,4},{1,5},{2,6},{3,7},{4,0},{5,1},{6,2},{7,3},{8,12},{9,13},{10,... | collective-permute-start | bytes 5505032 | tf_op jit(solution)/shard_map/ppermute | solution.py:750
  226.1 7.7 %collective-permute-start.23 = (bf16[16,112,128]{2,1,0:T(8,128)(2,1)S(1)}, bf16[16,112,128]{2,1,0:T(8,128)(2,1)S(1)}, u32[]{:S(2)}, u32[]{:S(2)}) collective-permute-start(bf16[16,112,128]{2,1,0:T(8,128)(2,1)S(1)} %all_to_all.53.refs_2_), channel_id=1, source_target_pairs={{0,4},{1,5},{2,6},{3,7},{4,0},{5,1},{6,2},{7,3},{8,12},{9,13},{10,... | collective-permute-start | bytes 1376264 | tf_op jit(solution)/shard_map/ppermute | solution.py:751
  226.1 7.7 %collective-permute-start.24 = (bf16[16,112,128]{2,1,0:T(8,128)(2,1)S(1)}, bf16[16,112,128]{2,1,0:T(8,128)(2,1)S(1)}, u32[]{:S(2)}, u32[]{:S(2)}) collective-permute-start(bf16[16,112,128]{2,1,0:T(8,128)(2,1)S(1)} %collective-permute-done.20.refs_3_), channel_id=1, source_target_pairs={{0,4},{1,5},{2,6},{3,7},{4,0},{5,1},{6,2},{7,3},{8,12},{9,13},{10,... | collective-permute-start | bytes 1376264 | tf_op jit(solution)/shard_map/ppermute | solution.py:751
  226.6 7.2 %collective-permute-start.25 = (bf16[16,112,128]{2,1,0:T(8,128)(2,1)S(1)}, bf16[16,112,128]{2,1,0:T(8,128)(2,1)S(1)}, u32[]{:S(2)}, u32[]{:S(2)}) collective-permute-start(bf16[16,112,128]{2,1,0:T(8,128)(2,1)S(1)} %collective-permute-done.21.refs_4_), channel_id=1, source_target_pairs={{0,4},{1,5},{2,6},{3,7},{4,0},{5,1},{6,2},{7,3},{8,12},{9,13},{10,... | collective-permute-start | bytes 1376264 | tf_op jit(solution)/shard_map/ppermute | solution.py:751
  226.6 7.2 %collective-permute-start.26 = (bf16[16,112,128]{2,1,0:T(8,128)(2,1)}, bf16[16,112,128]{2,1,0:T(8,128)(2,1)S(1)}, u32[]{:S(2)}, u32[]{:S(2)}) collective-permute-start(bf16[16,112,128]{2,1,0:T(8,128)(2,1)} %collective-permute-done.22.refs_5_), channel_id=1, source_target_pairs={{0,4},{1,5},{2,6},{3,7},{4,0},{5,1},{6,2},{7,3},{8,12},{9,13},{10,... | collective-permute-start | bytes 1376264 | tf_op jit(solution)/shard_map/ppermute | solution.py:751
  229.5 4.3 %copy-start.1 = (bf16[2,8,80,256]{3,2,1,0:T(8,128)(2,1)S(1)}, bf16[2,8,80,256]{3,2,1,0:T(8,128)(2,1)}, u32[]{:S(2)}) copy-start(bf16[2,8,80,256]{3,2,1,0:T(8,128)(2,1)} %param.10) | copy-start | bytes 1966084
  229.5 4.3 %copy-start.3 = (bf16[2,8,80,256]{3,2,1,0:T(8,128)(2,1)S(1)}, bf16[2,8,80,256]{3,2,1,0:T(8,128)(2,1)}, u32[]{:S(2)}) copy-start(bf16[2,8,80,256]{3,2,1,0:T(8,128)(2,1)} %param.11) | copy-start | bytes 1966084
  229.5 4.3 %copy-start.4 = (f32[1280,256]{1,0:T(8,128)S(1)}, f32[1280,256]{1,0:T(8,128)}, u32[]{:S(2)}) copy-start(f32[1280,256]{1,0:T(8,128)} %get-tuple-element.90.refs_10_) | copy-start | bytes 3932164
  229.5 4.3 %copy-start.6 = (f32[128,1,128]{2,1,0:T(1,128)S(1)}, f32[128,1,128]{2,1,0:T(1,128)}, u32[]{:S(2)}) copy-start(f32[128,1,128]{2,1,0:T(1,128)} %copy-done.5) | copy-start | bytes 196612
